TPU v7x, 256 devices: a whole 4x4x8 slice. The times are simulated.
256 devices in a mesh: batch: 2 (over x_lo), ctx: 16 (over z, x_hi), tp: 8 (over y, core).
Axes of the slice: x: 4 (x_hi: 2, x_lo: 2; x = x_hi * 2 + x_lo), y: 4, z: 8, core: 2. Of those that a mesh axis runs over, the one named last changes fastest.
Arguments:
- tokens: bfloat16 [2, 4096, 1024], P('batch', 'ctx'), may hold values from -10.5 to 10.5
- query_weight: bfloat16 [1024, 1024], P(None, 'tp'), may hold values from -0.1875 to 0.1875
- key_weight: bfloat16 [1024, 1024], P(None, 'tp'), may hold values from -0.1875 to 0.1875
- value_weight: bfloat16 [1024, 1024], P(None, 'tp'), may hold values from -0.1875 to 0.1875
- cotangent: bfloat16 [2, 4096, 1024], P('batch', 'ctx', 'tp'), may hold values from -6 to 6
- doc_lengths: int32 [2, 8], P('batch'), may hold values from 1 to 3072, 4096 in all within a row
- global_positions: int32 [2, 256], P('batch'), may hold values from 0 to 4095, as said below
Outputs:
- attended: bfloat16 [2, 4096, 1024], P('batch', 'ctx', 'tp')
- grad_tokens: bfloat16 [2, 4096, 1024], P('batch', ('ctx', 'tp'))
- grad_query_weight: float32 [1024, 1024], P(None, 'tp')
- grad_key_weight: float32 [1024, 1024], P(None, 'tp')
- grad_value_weight: float32 [1024, 1024], P(None, 'tp')
Inputs may be any that keep to these rules, and one draw needn't show every extreme that they name: `global_positions`: distinct positions of the sequence in ascending order; the first position 0 and the last position 4095 are always among them.
All inputs are finite; a program needn't handle non-finite values.
Results may differ from a plain program's by a relative error of at most 0.022.
The roundings to bfloat16 on the way count: a program that leaves them out, or rounds other values in their place, can miss the bound.
Values may be sent and summed in bfloat16 or wider, within the bound.
No kernel may reach another device: no remote copies, remote signals or barrier semaphores. Data moves between devices by JAX's collectives and lax.ppermute only.
A program may use at most 64 MiB of HBM per device.

v0:
```python
import math

import jax
import jax.numpy as jnp
from jax import lax
from jax.sharding import PartitionSpec as P

WINDOW = 512
HD = 64


NEGATIVE = -1e30


def with_halo(block, sides, width):
    for axis, dim in sides:
        count = lax.axis_size(axis)
        forward = [(i, i + 1) for i in range(count - 1)]
        backward = [(target, source) for source, target in forward]
        low = lax.ppermute(
            lax.slice_in_dim(block, block.shape[dim] - width, None, axis=dim), axis, forward
        )
        high = lax.ppermute(lax.slice_in_dim(block, 0, width, axis=dim), axis, backward)
        block = jnp.concatenate([low, block, high], axis=dim)
    return block


def merged_2(part, axis, combine):
    gathered = jax.tree.map(lambda a: lax.all_gather(a, axis), part)

    def take(source):
        return jax.tree.map(lambda a: lax.dynamic_index_in_dim(a, source, 0, False), gathered)

    return lax.fori_loop(
        1, lax.axis_size(axis), lambda source, state: combine(state, take(source)), take(0)
    )


def document_of(positions, lengths):
    ends = jnp.cumsum(lengths)
    return jnp.sum((positions[:, None] >= ends[None, :]).astype(jnp.int32), axis=1)


def combine(earlier, latter):
    row_peak = jnp.maximum(earlier[0], latter[0])
    scale_first = jnp.exp(earlier[0] - row_peak)
    scale_second = jnp.exp(latter[0] - row_peak)
    row_total = scale_first * earlier[1] + scale_second * latter[1]
    weighted = scale_first[..., None] * earlier[2] + scale_second[..., None] * latter[2]
    return (row_peak, row_total, weighted)


def group_stats(scores, allowed, value_rows):
    masked = jnp.where(allowed[:, None, :], scores, NEGATIVE)
    row_peak = jnp.max(masked, axis=2)
    expon_terms = jnp.where(allowed[:, None, :], jnp.exp(masked - row_peak[:, :, None]), 0.0)
    row_total = jnp.sum(expon_terms, axis=2)
    weighted = jnp.einsum(
        "qhk,khd->qhd",
        expon_terms.astype(jnp.bfloat16),
        value_rows,
        preferred_element_type=jnp.float32,
    )
    return (row_peak, row_total, weighted)


def group_grads(
    scores, allowed, log_total, row_delta, out_grad, queries, key_rows, value_rows, score_scale
):
    prob_terms = jnp.where(allowed[:, None, :], jnp.exp(scores - log_total[:, :, None]), 0.0)
    value_grad = jnp.einsum(
        "qhk,qhd->khd",
        prob_terms.astype(jnp.bfloat16),
        out_grad,
        preferred_element_type=jnp.float32,
    )
    prob_grad = jnp.einsum("qhd,khd->qhk", out_grad, value_rows, preferred_element_type=jnp.float32)
    score_grad = (prob_terms * (prob_grad - row_delta[:, :, None])).astype(jnp.bfloat16)
    query_grad = score_scale * jnp.einsum(
        "qhk,khd->qhd", score_grad, key_rows, preferred_element_type=jnp.float32
    )
    key_grad = score_scale * jnp.einsum(
        "qhk,qhd->khd", score_grad, queries, preferred_element_type=jnp.float32
    )
    return (query_grad, key_grad, value_grad)


def on_device(
    tokens, query_weight, key_weight, value_weight, cotangent, doc_lengths, global_positions
):
    token_rows = tokens[0]
    local_len = token_rows.shape[0]
    width = query_weight.shape[1]
    head_count = width // HD
    half_span = WINDOW // 2
    block_len = min(local_len, 512)
    key_span = block_len + 2 * half_span
    score_scale = 1.0 / math.sqrt(HD)
    lengths = doc_lengths[0]
    global_spots = global_positions[0]
    global_count = global_spots.shape[0]
    seq_len = local_len * lax.axis_size("ctx")
    first_place = lax.axis_index("ctx") * local_len
    query_proj = jnp.dot(token_rows, query_weight, preferred_element_type=jnp.float32).astype(
        jnp.bfloat16
    )
    key_proj = jnp.dot(token_rows, key_weight, preferred_element_type=jnp.float32).astype(
        jnp.bfloat16
    )
    value_proj = jnp.dot(token_rows, value_weight, preferred_element_type=jnp.float32).astype(
        jnp.bfloat16
    )
    cot_rows = cotangent[0]
    positions = first_place + jnp.arange(local_len, dtype=jnp.int32)
    doc_ids = document_of(positions, lengths)
    global_docs = document_of(global_spots, lengths)
    own_global = positions[:, None] == global_spots[None, :]
    is_global = jnp.any(own_global, axis=1)
    select = own_global.astype(jnp.bfloat16)
    local_slot = global_spots - first_place
    slot_owned = (local_slot >= 0) & (local_slot < local_len)
    target_slot = jnp.where(slot_owned, local_slot, local_len)
    packed = jnp.concatenate([query_proj, key_proj, value_proj, cot_rows], axis=1)
    picked = lax.dot_general(
        select, packed, (((0,), (0,)), ((), ())), preferred_element_type=jnp.float32
    )
    picked = lax.psum(picked.astype(jnp.bfloat16), "ctx")
    global_queries = picked[:, :width].reshape(global_count, head_count, HD)
    global_keys = picked[:, width : 2 * width].reshape(global_count, head_count, HD)
    global_values = picked[:, 2 * width : 3 * width].reshape(global_count, head_count, HD)
    global_cotangent = picked[:, 3 * width :].reshape(global_count, head_count, HD)
    pair = jnp.stack([key_proj, value_proj])
    widened = with_halo(pair, (("ctx", 1),), half_span)
    ext_keys = widened[0].reshape(local_len + 2 * half_span, head_count, HD)
    ext_values = widened[1].reshape(local_len + 2 * half_span, head_count, HD)
    ext_places = first_place - half_span + jnp.arange(local_len + 2 * half_span, dtype=jnp.int32)
    inside = (ext_places >= 0) & (ext_places < seq_len)
    ext_docs = jnp.where(inside, document_of(ext_places, lengths), -1)
    ext_global = jnp.any(ext_places[:, None] == global_spots[None, :], axis=1)
    queries3 = query_proj.reshape(local_len, head_count, HD)
    keys3 = key_proj.reshape(local_len, head_count, HD)
    values3 = value_proj.reshape(local_len, head_count, HD)
    cot3 = cot_rows.reshape(local_len, head_count, HD)
    offsets = jnp.arange(key_span)[None, :] - half_span - jnp.arange(block_len)[:, None]
    near_mask = jnp.abs(offsets) <= half_span
    block_ids = jnp.arange(local_len // block_len, dtype=jnp.int32)

    def block_parts():
        band_mask = (
            (ext_docs[None, :] == doc_ids[:, None])
            & near_mask
            & jnp.logical_not(ext_global)[None, :]
            & jnp.logical_not(is_global)[:, None]
        )
        global_mask = (global_docs[None, :] == doc_ids[:, None]) & jnp.logical_not(is_global)[
            :, None
        ]
        band_scores = (
            jnp.einsum("qhd,khd->qhk", queries3, ext_keys, preferred_element_type=jnp.float32)
            * score_scale
        )
        global_scores = (
            jnp.einsum("qhd,khd->qhk", queries3, global_keys, preferred_element_type=jnp.float32)
            * score_scale
        )
        return (
            queries3,
            ext_keys,
            ext_values,
            is_global,
            band_mask,
            global_mask,
            band_scores,
            global_scores,
        )

    def forward_block(block_index):
        (
            query_block,
            key_block,
            value_block,
            query_global,
            band_mask,
            global_mask,
            band_scores,
            global_scores,
        ) = block_parts()
        row_peak, row_total, weighted = combine(
            group_stats(band_scores, band_mask, value_block),
            group_stats(global_scores, global_mask, global_values),
        )
        safe_total = jnp.where(query_global[:, None], 1.0, row_total)
        return (weighted / safe_total[:, :, None], row_peak + jnp.log(safe_total))

    block_outputs, block_totals = lax.map(forward_block, block_ids)
    local_out = block_outputs.reshape(local_len, width)
    log_total = block_totals.reshape(local_len, head_count)
    own_mask = global_docs[:, None] == doc_ids[None, :]
    own_scores = (
        jnp.einsum("ghd,khd->ghk", global_queries, keys3, preferred_element_type=jnp.float32)
        * score_scale
    )
    merged = merged_2(group_stats(own_scores, own_mask, values3), "ctx", combine)
    global_peak, global_total, global_weighted = merged
    global_out = (global_weighted / global_total[:, :, None]).astype(jnp.bfloat16)
    global_log_total = global_peak + jnp.log(global_total)
    spread = jnp.dot(
        select, global_out.reshape(global_count, width), preferred_element_type=jnp.float32
    ).astype(jnp.bfloat16)
    attended = jnp.where(is_global[:, None], spread, local_out.astype(jnp.bfloat16))
    attended3 = attended.reshape(local_len, head_count, HD)
    row_delta = jnp.sum(cot3.astype(jnp.float32) * attended3.astype(jnp.float32), axis=2)
    global_delta = jnp.sum(
        global_cotangent.astype(jnp.float32) * global_out.astype(jnp.float32), axis=2
    )

    def backward_block(running, block_index):
        key_grads, value_grads, gkey_grads, gvalue_grads = running
        (
            query_block,
            key_block,
            value_block,
            query_global,
            band_mask,
            global_mask,
            band_scores,
            global_scores,
        ) = block_parts()
        band_q, band_k, band_v = group_grads(
            band_scores,
            band_mask,
            log_total,
            row_delta,
            cot3,
            query_block,
            key_block,
            value_block,
            score_scale,
        )
        glob_q, glob_k, glob_v = group_grads(
            global_scores,
            global_mask,
            log_total,
            row_delta,
            cot3,
            query_block,
            global_keys,
            global_values,
            score_scale,
        )
        key_grads = key_grads + band_k
        value_grads = value_grads + band_v
        return (
            (key_grads, value_grads, gkey_grads + glob_k, gvalue_grads + glob_v),
            band_q + glob_q,
        )

    zero_ext = jnp.zeros((local_len + 2 * half_span, head_count, HD), jnp.float32)
    zero_global = jnp.zeros((global_count, head_count, HD), jnp.float32)
    (key_grads, value_grads, gkey_part, gvalue_part), query_blocks = lax.scan(
        backward_block, (zero_ext, zero_ext, zero_global, zero_global), block_ids
    )
    gquery_part, from_key, from_value = group_grads(
        own_scores,
        own_mask,
        global_log_total,
        global_delta,
        global_cotangent,
        global_queries,
        keys3,
        values3,
        score_scale,
    )

    def rim_rows(grads):
        return jnp.concatenate([grads[:half_span], grads[-half_span:]], axis=0).reshape(
            2 * half_span, width
        )

    rim_pair = jnp.stack([rim_rows(key_grads), rim_rows(value_grads)])
    returned = with_halo(rim_pair, (("ctx", 1),), half_span)
    from_lower = returned[:, :half_span]
    from_upper = returned[:, 3 * half_span :]
    gquery_total, gkey_total, gvalue_total = lax.psum(
        (
            gquery_part.reshape(global_count, width),
            gkey_part.reshape(global_count, width),
            gvalue_part.reshape(global_count, width),
        ),
        "ctx",
    )

    def add_global(rows_sum, global_total_rows):
        return rows_sum.at[target_slot].add(global_total_rows, mode="drop")

    def own_total(ext_grads, from_global, rim_index, global_total_rows):
        inner = ext_grads[half_span : half_span + local_len].reshape(local_len, width)
        inner = (
            inner.at[:half_span]
            .add(from_lower[rim_index])
            .at[local_len - half_span :]
            .add(from_upper[rim_index])
        )
        inner = inner + from_global.reshape(local_len, width)
        return add_global(inner, global_total_rows)

    key_bf = own_total(key_grads, from_key, 0, gkey_total).astype(jnp.bfloat16)
    value_bf = own_total(value_grads, from_value, 1, gvalue_total).astype(jnp.bfloat16)
    query_bf = add_global(query_blocks.reshape(local_len, width), gquery_total).astype(jnp.bfloat16)

    def weight_grad(grad_rows):
        return lax.dot_general(
            token_rows, grad_rows, (((0,), (0,)), ((), ())), preferred_element_type=jnp.float32
        )

    local_grads = (weight_grad(query_bf), weight_grad(key_bf), weight_grad(value_bf))
    totals = (
        lax.psum(local_grads[0].astype(jnp.bfloat16), ("batch", "ctx")).astype(jnp.float32),
        lax.psum(local_grads[1].astype(jnp.bfloat16), ("batch", "ctx")).astype(jnp.float32),
        lax.psum(local_grads[2].astype(jnp.bfloat16), ("batch", "ctx")).astype(jnp.float32),
    )
    contract = (((1,), (1,)), ((), ()))
    result = lax.dot_general(query_bf, query_weight, contract, preferred_element_type=jnp.float32)
    result = result + lax.dot_general(
        key_bf, key_weight, contract, preferred_element_type=jnp.float32
    )
    result = result + lax.dot_general(
        value_bf, value_weight, contract, preferred_element_type=jnp.float32
    )
    share_rows = lax.psum_scatter(result, "tp", scatter_dimension=0, tiled=True)
    return (attended[None], share_rows.astype(jnp.bfloat16)[None], totals[0], totals[1], totals[2])


def solution(mesh):
    in_specs = (
        P("batch", "ctx", None),
        P(None, "tp"),
        P(None, "tp"),
        P(None, "tp"),
        P("batch", "ctx", "tp"),
        P("batch", None),
        P("batch", None),
    )
    out_specs = (
        P("batch", "ctx", "tp"),
        P("batch", ("ctx", "tp"), None),
        P(None, "tp"),
        P(None, "tp"),
        P(None, "tp"),
    )
    return jax.shard_map(
        on_device, mesh=mesh, in_specs=in_specs, out_specs=out_specs, check_vma=False
    )
```

profile of v0, /device:TPU:8, one launch (start us, length us, event | category | flops | bytes accessed | tf_op | source)
XLA Modules:
  0.0 718.2 jit_solution(1137973450989035679)
XLA Ops:
  8.2 1.3 convolution_convert_fusion.4
  9.5 1.3 convolution_convert_fusion.6
  10.8 1.3 collective-permute-start.1
  12.1 6.1 collective-permute-start
  21.4 159.3 %all-reduce.6.cloned.1.call-done = bf16[256,512]{1,0:T(8,128)(2,1)} async-done(((bf16[256,512]{1,0:T(8,128)(2,1)}), bf16[256,512]{1,0:T(8,128)(2,1)}) %all-reduce.6.cloned.1.call-update) | async-done | bytes 262160 | tf_op jit(solution)/shard_map/psum | solution.py:127
  188.9 42.9 %all-gather = f32[4096,2]{0,1:T(2,128)} all-gather(f32[256,2]{0,1:T(2,128)S(1)} %get-tuple-element.458), channel_id=2, replica_groups=mesh['batch'=2,'ctx'=16,'tp'=8] {'ctx'}, dimensions={0}, use_global_device_ids=true | all-gather | bytes 34816 | tf_op jit(solution)/shard_map/all_gather | solution.py:29
  232.7 38.2 %all-gather.1 = f32[4096,2]{0,1:T(2,128)} all-gather(f32[256,2]{0,1:T(2,128)S(1)} %fusion.50), channel_id=3, replica_groups=mesh['batch'=2,'ctx'=16,'tp'=8] {'ctx'}, dimensions={0}, use_global_device_ids=true | all-gather | bytes 34816 | tf_op jit(solution)/shard_map/all_gather | solution.py:29
  271.5 1.2 select_reduce_fusion
  273.8 1.3 log_add_fusion.1
  275.1 1.8 fusion.58
  276.9 1.7 copy.116
  278.5 1.3 convolution_bitcast_fusion.2
  281.2 1.8 copy.106
  283.0 1.7 copy.112
  284.7 1.1 fusion.26
  285.8 2.0 fusion.28
  288.9 6.1 copy.133
  295.1 52.5 %while.40 = (s32[]{:T(128)}, f32[256,2]{0,1:T(2,128)S(1)}, f32[256,2]{0,1:T(2,128)S(1)}, f32[256,2,64]{2,1,0:T(2,128)S(1)}, f32[16,256,2]{1,2,0:T(2,128)}, /*ind...) while((s32[]{:T(128)}, f32[256,2]{0,1:T(2,128)S(1)}, ...), condition=%wide.region_8.9_spmd, body=%wide.region_7.8_spmd.sunk | while | flops 101381 | bytes 422039 | solution.py:34
  296.0 2.5 fusion.156
  299.5 2.5 fusion.156
  303.0 2.5 fusion.156
  306.5 2.5 fusion.156
  310.0 2.5 fusion.156
  313.5 2.5 fusion.156
  317.1 2.5 fusion.156
  320.6 2.5 fusion.156
  324.1 2.5 fusion.156
  327.6 2.5 fusion.156
  331.1 2.5 fusion.156
  334.6 2.5 fusion.156
  338.1 2.5 fusion.156
  341.6 2.5 fusion.156
  345.1 2.5 fusion.156
  348.7 1.2 fusion.88
  349.9 1.4 fusion.16
  354.4 1.4 collective-permute-start.3
  355.9 6.1 collective-permute-start.2
  364.4 3.2 collective-permute-done.2
  367.6 154.5 %all-reduce.8.cloned.1.call-done = (f32[256,128]{1,0:T(8,128)}, f32[256,128]{1,0:T(8,128)}, f32[256,128]{1,0:T(8,128)}) async-done(((f32[256,128]{1,0:T(8,128)}, f32[256,128]{1,0:T(8,128)}, f32[256,128]{1,0:T(8,128)}), (f32[256,128]{1,0:T(8,128)}, f32[256,128]{1,0:T(8,128)}, f32[256,128]{1,0:T(8,128)})) %all-reduce.8.cloned.1.call-update) | async-done | bytes 393232 | tf_op jit(solution)/shard_map/psum | solution.py:284
  522.1 2.4 scatter_fusion
  525.5 2.2 scatter_fusion.1
  528.6 2.0 scatter_fusion.2
  532.9 1.3 convolution_add_fusion
  535.0 144.1 %all-reduce.10.cloned.1.call-done = (bf16[1024,128]{0,1:T(8,128)(2,1)}, bf16[1024,128]{0,1:T(8,128)(2,1)}, bf16[1024,128]{0,1:T(8,128)(2,1)}) async-done(((bf16[1024,128]{0,1:T(8,128)(2,1)}, bf16[1024,128]{0,1:T(8,128)(2,1)}, bf16[1024,128]{0,1:T(8,128)(2,1)}), (bf16[1024,128]{0,1:T(8,128)(2,1)}, bf16[1024,128]{0,1:T(8,128)(2,1)}, bf16[1024,128]{0,1:T(8,128)(2,1)})) %all-reduce.10.cloned.1.call-update) | async-done | bytes 786448 | tf_op jit(solution)/shard_map/psum | solution.py:318
  679.1 1.9 copy.118
  681.0 1.9 copy.119
  683.9 26.3 %reduce-scatter.2.cloned.1.call-done = f32[32,1024]{1,0:T(8,128)} async-done(((f32[256,1024]{1,0:T(8,128)}), f32[32,1024]{1,0:T(8,128)}) %reduce-scatter.2.cloned.1.call-update) | async-done | bytes 131088 | tf_op jit(solution)/shard_map/reduce_scatter | solution.py:330
  710.1 1.5 convert_bitcast_fusion
  (194 shorter events, 44.2 us)
Async XLA Ops:
  7.2 1.0 copy-start
  7.2 11.0 %copy-start.26 = (bf16[1,256,128]{2,1,0:T(8,128)(2,1)S(1)}, bf16[1,256,128]{2,1,0:T(8,128)(2,1)}, u32[]{:S(2)}) copy-start(bf16[1,256,128]{2,1,0:T(8,128)(2,1)} %param.29) | copy-start | bytes 196612
  7.2 11.1 %copy-start.10 = (bf16[1024,128]{1,0:T(8,128)(2,1)S(1)}, bf16[1024,128]{1,0:T(8,128)(2,1)}, u32[]{:S(2)}) copy-start(bf16[1024,128]{1,0:T(8,128)(2,1)} %param.26) | copy-start | bytes 786436
  7.2 11.5 %copy-start.29 = (s32[1,256]{1,0:T(1,128)S(1)}, s32[1,256]{1,0:T(1,128)}, u32[]{:S(2)}) copy-start(s32[1,256]{1,0:T(1,128)} %param.31) | copy-start | bytes 3076
  7.2 173.5 %all-reduce.6.cloned.1.call-start = ((), (), s32[]{:S(2)}) async-start(), calls=%async_computation.1 | async-start | bytes 524288 | tf_op jit(solution)/shard_map/psum | solution.py:127
  9.5 175.1 %copy-start.19 = (bf16[256,128]{0,1:T(8,128)(2,1)}, bf16[256,128]{0,1:T(8,128)(2,1)S(1)}, u32[]{:S(2)}) copy-start(bf16[256,128]{0,1:T(8,128)(2,1)S(1)} %convolution_convert_fusion.4) | copy-start | bytes 196612
  9.5 10.9 %copy-start.33 = (s32[1,8]{1,0:T(1,128)S(1)}, s32[1,8]{1,0:T(1,128)}, u32[]{:S(2)}) copy-start(s32[1,8]{1,0:T(1,128)} %param.30) | copy-start | bytes 100
  10.8 173.8 %copy-start.4 = (bf16[256,128]{0,1:T(8,128)(2,1)}, bf16[256,128]{0,1:T(8,128)(2,1)S(1)}, u32[]{:S(2)}) copy-start(bf16[256,128]{0,1:T(8,128)(2,1)S(1)} %convolution_convert_fusion.6) | copy-start | bytes 196612
  10.8 173.7 %collective-permute-start.1 = (bf16[2,256,128]{1,2,0:T(8,128)(2,1)S(1)}, bf16[2,256,128]{1,2,0:T(8,128)(2,1)S(1)}, u32[]{:S(2)}, u32[]{:S(2)}) collective-permute-start(bf16[2,256,128]{1,2,0:T(8,128)(2,1)S(1)} %pad_maximum_fusion.4), channel_id=1, source_target_pairs={{8,0},{16,8},{24,16},{32,24},{40,32},{48,40},{56,48},{64,56},{72,6... | collective-permute-start | bytes 393224 | tf_op jit(solution)/shard_map/ppermute | solution.py:23
  12.1 172.4 %collective-permute-start = (bf16[2,256,128]{1,2,0:T(8,128)(2,1)S(1)}, bf16[2,256,128]{1,2,0:T(8,128)(2,1)S(1)}, u32[]{:S(2)}, u32[]{:S(2)}) collective-permute-start(bf16[2,256,128]{1,2,0:T(8,128)(2,1)S(1)} %pad_maximum_fusion.4), channel_id=1, source_target_pairs={{0,8},{8,16},{16,24},{24,32},{32,40},{40,48},{48,56},{56,64},{64,7... | collective-permute-start | bytes 393224 | tf_op jit(solution)/shard_map/ppermute | solution.py:20
  18.3 163.5 %copy-start.13 = (bf16[1,256,128]{1,2,0:T(8,128)(2,1)}, bf16[1,256,128]{1,2,0:T(8,128)(2,1)S(1)}, u32[]{:S(2)}) copy-start(bf16[1,256,128]{1,2,0:T(8,128)(2,1)S(1)} %copy.86) | copy-start | bytes 196612
  18.7 166.6 %copy-start.2 = (bf16[256,128]{0,1:T(8,128)(2,1)}, bf16[256,128]{0,1:T(8,128)(2,1)S(1)}, u32[]{:S(2)}) copy-start(bf16[256,128]{0,1:T(8,128)(2,1)S(1)} %convolution_convert_fusion.5) | copy-start | bytes 196612
  18.7 164.3 %copy-start.31 = (s32[256]{0:T(256)}, s32[256]{0:T(256)S(1)}, u32[]{:S(2)}) copy-start(s32[256]{0:T(256)S(1)} %iota_add_fusion.2) | copy-start | bytes 3076
  19.8 268.0 %all-gather.5.cloned.1.call-start = ((), (), s32[]{:S(2)}) async-start(), calls=%async_computation.3 | async-start | bytes 2228224 | tf_op jit(solution)/shard_map/all_gather | solution.py:29
  20.0 163.1 %copy-start.32 = (pred[256]{0:T(512)(128)(4,1)}, pred[256]{0:T(512)(128)(4,1)S(1)}, u32[]{:S(2)}) copy-start(pred[256]{0:T(512)(128)(4,1)S(1)} %compare_reduce_fusion.1) | copy-start | bytes 772
  21.4 211.1 %copy-start.8 = (pred[256,256]{0,1:T(8,128)(4,1)}, pred[256,256]{0,1:T(8,128)(4,1)S(1)}, u32[]{:S(2)}) copy-start(pred[256,256]{0,1:T(8,128)(4,1)S(1)} %get-tuple-element.452) | copy-start | bytes 196612
  181.8 1.4 copy-start.16
  183.0 339.1 %all-reduce.8.cloned.1.call-start = ((), (), s32[]{:S(2)}) async-start(), calls=%async_computation.4 | async-start | bytes 786432 | tf_op jit(solution)/shard_map/psum | solution.py:284
  188.9 84.9 %copy-start.30 = (f32[256,2]{0,1:T(2,128)S(1)}, f32[256,2]{0,1:T(2,128)}, u32[]{:S(2)}) copy-start(f32[256,2]{0,1:T(2,128)} %fusion.18) | copy-start | bytes 6148
  272.7 1.1 copy-start.27
  272.7 12.0 %copy-start.1 = (f32[256,2,256]{0,2,1:T(8,128)}, f32[256,2,256]{0,2,1:T(8,128)S(1)}, u32[]{:S(2)}) copy-start(f32[256,2,256]{0,2,1:T(8,128)S(1)} %get-tuple-element.455) | copy-start | bytes 1572868
  347.6 3.7 copy-start.14
  347.7 3.5 copy-start.23
  351.3 0.8 copy-start.18
  351.3 1.0 copy-start.3
  352.3 0.9 copy-start.9
  352.3 0.9 copy-start.15
  352.5 0.9 copy-start.20
  353.4 1.0 copy-start.12
  353.8 8.2 %copy-start.5 = (bf16[256,128]{0,1:T(8,128)(2,1)S(1)}, bf16[256,128]{0,1:T(8,128)(2,1)}, u32[]{:S(2)}) copy-start(bf16[256,128]{0,1:T(8,128)(2,1)} %copy-done.4) | copy-start | bytes 196612
  354.4 9.5 %copy-start.17 = (bf16[256,128]{0,1:T(8,128)(2,1)S(1)}, bf16[256,128]{0,1:T(8,128)(2,1)}, u32[]{:S(2)}) copy-start(bf16[256,128]{0,1:T(8,128)(2,1)} %copy-done.16) | copy-start | bytes 196612
  354.4 13.2 %copy-start.21 = (f32[256,128]{1,0:T(8,128)S(1)}, f32[256,128]{1,0:T(8,128)}, u32[]{:S(2)}) copy-start(f32[256,128]{1,0:T(8,128)} %copy.112) | copy-start | bytes 393220
  354.4 9.9 %collective-permute-start.3 = (f32[2,256,128]{2,1,0:T(8,128)S(1)}, f32[2,256,128]{2,1,0:T(8,128)S(1)}, u32[]{:S(2)}, u32[]{:S(2)}) collective-permute-start(f32[2,256,128]{2,1,0:T(8,128)S(1)} %get-tuple-element.439), channel_id=1, source_target_pairs={{8,0},{16,8},{24,16},{32,24},{40,32},{48,40},{56,48},{64,56},{72,6... | collective-permute-start | bytes 786440 | tf_op jit(solution)/shard_map/ppermute | solution.py:23
  355.9 11.7 %collective-permute-start.2 = (f32[2,256,128]{2,1,0:T(8,128)S(1)}, f32[2,256,128]{2,1,0:T(8,128)S(1)}, u32[]{:S(2)}, u32[]{:S(2)}) collective-permute-start(f32[2,256,128]{2,1,0:T(8,128)S(1)} %get-tuple-element.438), channel_id=1, source_target_pairs={{0,8},{8,16},{16,24},{24,32},{32,40},{40,48},{48,56},{56,64},{64,7... | collective-permute-start | bytes 786440 | tf_op jit(solution)/shard_map/ppermute | solution.py:20
  363.0 159.1 %copy-start.28 = (s32[256,1]{0,1:T(1,128)S(1)}, s32[256,1]{0,1:T(1,128)}, u32[]{:S(2)}) copy-start(s32[256,1]{0,1:T(1,128)} %compare_select_fusion) | copy-start | bytes 3076
  363.9 315.2 %all-reduce.10.cloned.1.call-start = ((), (), s32[]{:S(2)}) async-start(), calls=%async_computation.5 | async-start | bytes 1572864 | tf_op jit(solution)/shard_map/psum | solution.py:318
  522.1 3.4 copy-start.25
  525.5 3.1 copy-start.24
  528.6 3.1 copy-start.11
  530.6 1.4 copy-start.6
  531.6 178.5 %reduce-scatter.2.cloned.1.call-start = ((), (), s32[]{:S(2)}) async-start(), calls=%async_computation.2 | async-start | bytes 1179648 | tf_op jit(solution)/shard_map/reduce_scatter | solution.py:330
  532.0 1.0 copy-start.7
  679.1 3.8 copy-start.22
Sparse Core Ops, SparseCore 0:
  19.9 160.7 all-reduce.5
  183.5 83.5 all-gather.4
  364.0 158.0 all-reduce.7
  531.7 147.3 all-reduce.9
  681.5 28.5 reduce-scatter.1
where the time goes:
time: 723 us; the launch traced here: 718 us
  waiting for transfers between devices  488 us (67%)
  blocking collectives  81.2 us (11%)
  other arithmetic  64.2 us (9%)
  local copies, waits for them, and re-layouts  32.5 us (4%)
  matrix products  22.7 us (3%)
  starting transfers between devices  15.1 us (2%)
  between operations  14.5 us (2%)
    psum x1, waiting for transfers between devices, on_device(): picked = lax.psum(picked.astype(jnp.bfloat16), 'ctx')  159 us
    psum x1, waiting for transfers between devices, on_device(): lax.psum((gquery_part.reshape(global_count, width), gkey_part.reshape(glo...  154 us
    psum x1, waiting for transfers between devices, on_device(): lax.psum(local_grads[0].astype(jnp.bfloat16), ('batch', 'ctx'))  144 us
    all_gather x2, blocking collectives, merged_2(): gathered = jax.tree.map(lambda a: lax.all_gather(a, axis), part)  81.2 us
    add x15, other arithmetic, combine(): scale_first[..., None] * earlier[2] + scale_second[..., None] * latter[2]  37.3 us
    reduce_scatter x1, waiting for transfers between devices, on_device(): share_rows = lax.psum_scatter(result, 'tp', scatter_dimension=0, tiled=True)  26.3 us
  transfers between devices with their start and end apart: 9, of which 5 were waited for; matrix products, arithmetic and copies ran while one was open for 5% of the time, Pallas kernels for 0%

commit v1 on v0

v1 whole, which is shorter than its diff:
```python
import functools
import math

import jax
import jax.numpy as jnp
from jax import lax
from jax.experimental import pallas as pl
from jax.experimental.pallas import tpu as pltpu
from jax.sharding import Mesh
from jax.sharding import PartitionSpec as P

HALF = 256
HD = 64
RUN = 256
SEC = 512
NSEC = 8
NEG = -1e30
BF = jnp.bfloat16
F32 = jnp.float32

Z = ("z2", "z1", "z0")
CTX = Z + ("xh",)
TP = ("y", "core")

OFFSETS = (0, -1, 1, -2, 2, -3, 3, 4)

NN = (((1,), (0,)), ((), ()))
NT = (((1,), (1,)), ((), ()))
TN = (((0,), (0,)), ((), ()))


def dot(a, b, dims=NN):
    return lax.dot_general(a, b, dims, preferred_element_type=F32)


def full_spec(memory_space=pltpu.VMEM):
    return pl.BlockSpec(memory_space=memory_space)


def call(kernel, outs, args, scratch=(), flops=0, transcendentals=0, smem=1, limit=48 << 20):
    specs = [full_spec(pltpu.SMEM)] * smem + [full_spec()] * (len(args) - smem)
    moved = sum(a.size * a.dtype.itemsize for a in args)
    return pl.pallas_call(
        kernel,
        out_shape=outs,
        in_specs=specs,
        out_specs=jax.tree.map(lambda _: full_spec(), outs),
        scratch_shapes=list(scratch),
        compiler_params=pltpu.CompilerParams(vmem_limit_bytes=limit),
        cost_estimate=pl.CostEstimate(
            flops=flops, bytes_accessed=moved, transcendentals=transcendentals
        ),
    )(*args)


def low_lanes(rows):
    return lax.broadcasted_iota(jnp.int32, (rows, 128), 1) < HD


def project_kernel(place, tok, wq, wk, wv, cot, mine, theirs):
    first = place[0] == 0
    t = tok[...]
    q = dot(t, wq[...]).astype(BF)
    k = dot(t, wk[...]).astype(BF)
    v = dot(t, wv[...]).astype(BF)
    c = cot[...]
    kv0 = jnp.concatenate([k[:, :HD], v[:, :HD]], axis=1)
    kv1 = jnp.concatenate([k[:, HD:], v[:, HD:]], axis=1)
    qc0 = jnp.concatenate([q[:, :HD], c[:, :HD]], axis=1)
    qc1 = jnp.concatenate([q[:, HD:], c[:, HD:]], axis=1)

    @pl.when(first)
    def _():
        mine[:RUN] = kv0
        mine[RUN:] = qc0
        theirs[:RUN] = kv1
        theirs[RUN:] = qc1

    @pl.when(jnp.logical_not(first))
    def _():
        mine[:RUN] = kv1
        mine[RUN:] = qc1
        theirs[:RUN] = kv0
        theirs[RUN:] = qc0


def feature_kernel(place, spots, starts, ends, key_feat, row_feat):
    flip = place[0]
    lane = lax.broadcasted_iota(jnp.int32, (RUN, 128), 1)
    inside = (lane >= HD) & (lane < HD + 8)
    last = lane == HD + 8

    def one(block, carry):
        half = lax.rem(block, 2)
        run = (block - half) + jnp.where(half == flip, 0, 1)
        pos = run * RUN + lax.broadcasted_iota(jnp.int32, (RUN, RUN), 0)
        hit = jnp.max(jnp.where(pos == spots[...], 1.0, 0.0), axis=1, keepdims=True)
        other = 1.0 - hit
        pos128 = run * RUN + lax.broadcasted_iota(jnp.int32, (RUN, 128), 0)
        member = (pos128 >= starts[...]) & (pos128 < ends[...])
        row = jnp.where(last, other, jnp.where(member, 1.0, 0.0))
        key = jnp.where(last, other, jnp.where(inside & jnp.logical_not(member), 1.0, 0.0))
        at = pl.ds(pl.multiple_of(block * RUN, RUN), RUN)
        row_feat[at, :] = row.astype(BF)
        key_feat[at, :] = (key * NEG).astype(BF)
        return carry

    lax.fori_loop(0, 2 * NSEC, one, 0)


def places(section, flip, along):
    shape = (1, SEC) if along == 1 else (SEC, 1)
    i = lax.broadcasted_iota(jnp.int32, shape, along)
    half = jnp.where(i >= RUN, 1 - flip, flip)
    return section * SEC + half * RUN + lax.bitwise_and(i, RUN - 1)


def rows_kernel(chunk, place, *refs):
    pieces, rest = refs[: 2 * NSEC], refs[2 * NSEC :]
    key_feat, row_feat, packed, stats, kv_s, kp_s, q_s, qn_s, c_s = rest
    flip, own = place[0], place[1]
    low = low_lanes(RUN)
    lane = lax.broadcasted_iota(jnp.int32, (RUN, 128), 1)
    for r in range(NSEC):
        section = lax.rem(own + OFFSETS[r] + NSEC, NSEC)
        for half in range(2):
            kv = pieces[2 * r + half][:RUN]
            at = r * SEC + half * RUN
            kv_s[at : at + RUN] = kv
            feat = key_feat[pl.ds(pl.multiple_of(section * SEC + half * RUN, RUN), RUN), :]
            kp_s[at : at + RUN] = jnp.where(low, kv, feat)
    for half in range(2):
        qc = pieces[half][RUN:]
        feat = row_feat[pl.ds(pl.multiple_of(own * SEC + half * RUN, RUN), RUN), :]
        at = half * RUN
        scaled = qc * jnp.asarray(1.0 / math.sqrt(HD), BF)
        joined = jnp.where(low, scaled, feat)
        zero = jnp.zeros_like(qc)
        q_s[at : at + RUN] = joined
        qn_s[at : at + RUN] = jnp.where(lane == HD + 8, zero, joined)
        c_s[at : at + RUN] = jnp.where(low, zero, qc)
    row_places = places(own, flip, 0)
    for c in range(SEC // chunk):
        rows = slice(c * chunk, (c + 1) * chunk)
        q, qn, cot = q_s[rows], qn_s[rows], c_s[rows]

        def scores(r, at, q=q, qn=qn, rows=rows):
            s = dot(q, kp_s[at, :], NT)
            if r is not None:
                section = lax.rem(own + OFFSETS[r] + NSEC, NSEC)
                away = row_places[rows] - places(section, flip, 1)
                s = jnp.where(jnp.abs(away) <= HALF, dot(qn, kp_s[at, :], NT), s)
            return s

        def forward(r, at, state, scores=scores):
            peak, total, acc = state
            s = scores(r, at)
            new_peak = jnp.maximum(peak, jnp.max(s, axis=1, keepdims=True))
            keep = jnp.exp(peak - new_peak)
            e = jnp.exp(s - new_peak)
            total = keep * total + jnp.sum(e, axis=1, keepdims=True)
            acc = keep * acc + dot(e.astype(BF), kv_s[at, :])
            return new_peak, total, acc

        state = (
            jnp.full((chunk, 1), NEG, F32),
            jnp.zeros((chunk, 1), F32),
            jnp.zeros((chunk, 128), F32),
        )
        for r in range(3):
            state = forward(r, slice(r * SEC, (r + 1) * SEC), state)
        state = lax.fori_loop(
            3,
            NSEC,
            lambda r, st, forward=forward: forward(
                None, pl.ds(pl.multiple_of(r * SEC, SEC), SEC), st
            ),
            state,
        )
        peak, total, acc = state
        att = (acc / total).astype(BF)
        log_total = peak + jnp.log(total)
        delta = jnp.sum(att.astype(F32) * cot.astype(F32), axis=1, keepdims=True)

        def backward(r, at, acc, scores=scores, log_total=log_total, delta=delta, cot=cot):
            p = jnp.exp(scores(r, at) - log_total)
            kv = kv_s[at, :]
            ds = p * (dot(cot, kv, NT) - delta)
            return acc + dot(ds.astype(BF), kv)

        grad = jnp.zeros((chunk, 128), F32)
        for r in range(3):
            grad = backward(r, slice(r * SEC, (r + 1) * SEC), grad)
        grad = lax.fori_loop(
            3,
            NSEC,
            lambda r, acc, backward=backward: backward(
                None, pl.ds(pl.multiple_of(r * SEC, SEC), SEC), acc
            ),
            grad,
        )
        grad = (grad * (1.0 / math.sqrt(HD))).astype(BF)
        packed[rows] = jnp.where(low_lanes(chunk), grad, att)
        lanes = lax.broadcasted_iota(jnp.int32, (chunk, 128), 1)
        turned = jnp.where(lanes == 0, log_total, delta).T
        for k in range(chunk // 128):
            at = c * (chunk // 128) + k
            stats[at : at + 1] = turned[0:1, k * 128 : (k + 1) * 128]
            stats[4 + at : 5 + at] = turned[1:2, k * 128 : (k + 1) * 128]


def keys_kernel(chunk, place, *refs):
    pieces, rest = refs[: 2 * NSEC], refs[2 * NSEC :]
    own_a, own_b, key_feat, row_feat, stats, packed, qc_s, q_s, k_s, kn_s, v_s = rest
    flip, own = place[0], place[1]
    low = low_lanes(RUN)
    lane = lax.broadcasted_iota(jnp.int32, (RUN, 128), 1)
    for r in range(NSEC):
        section = lax.rem(own + OFFSETS[r] + NSEC, NSEC)
        for half in range(2):
            piece = pieces[2 * r + half]
            qc = piece[piece.shape[0] - RUN :]
            at = r * SEC + half * RUN
            qc_s[at : at + RUN] = qc
            feat = row_feat[pl.ds(pl.multiple_of(section * SEC + half * RUN, RUN), RUN), :]
            q_s[at : at + RUN] = jnp.where(low, qc * jnp.asarray(1.0 / math.sqrt(HD), BF), feat)
    for half, piece in enumerate((own_a, own_b)):
        kv = piece[:RUN]
        feat = key_feat[pl.ds(pl.multiple_of(own * SEC + half * RUN, RUN), RUN), :]
        at = half * RUN
        joined = jnp.where(low, kv, feat)
        zero = jnp.zeros_like(kv)
        k_s[at : at + RUN] = joined
        kn_s[at : at + RUN] = jnp.where(lane == HD + 8, zero, joined)
        v_s[at : at + RUN] = jnp.where(low, zero, kv)
    key_places = places(own, flip, 0)
    for c in range(SEC // chunk):
        rows = slice(c * chunk, (c + 1) * chunk)
        k, kn, v = k_s[rows], kn_s[rows], v_s[rows]

        def backward(band, r, section, at, state):
            key_acc, value_acc = state
            st = stats[pl.ds(pl.multiple_of(section * 8, 8), 8), :]
            log_total = jnp.concatenate([st[i : i + 1] for i in range(4)], axis=1)
            delta = jnp.concatenate([st[i : i + 1] for i in range(4, 8)], axis=1)
            qc = qc_s[at, :]
            s = dot(k, q_s[at, :], NT)
            if band:
                away = key_places[rows] - places(section, flip, 1)
                s = jnp.where(jnp.abs(away) <= HALF, dot(kn, q_s[at, :], NT), s)
            p = jnp.exp(s - log_total)
            ds = p * (dot(v, qc, NT) - delta)
            key_acc = key_acc + dot(ds.astype(BF), qc)
            value_acc = value_acc + dot(p.astype(BF), qc)
            return key_acc, value_acc

        state = (jnp.zeros((chunk, 128), F32), jnp.zeros((chunk, 128), F32))
        for r in range(3):
            section = lax.rem(own + OFFSETS[r] + NSEC, NSEC)
            state = backward(True, r, section, slice(r * SEC, (r + 1) * SEC), state)

        def far(r, st):
            size = lax.div(r + 1, 2)
            offset = jnp.where(lax.rem(r, 2) == 1, jnp.where(r == 7, size, -size), size)
            section = lax.rem(own + offset + NSEC, NSEC)
            return backward(False, r, section, pl.ds(pl.multiple_of(r * SEC, SEC), SEC), st)

        key_acc, value_acc = lax.fori_loop(3, NSEC, far, state)
        joined = jnp.where(low_lanes(chunk), key_acc * (1.0 / math.sqrt(HD)), value_acc)
        packed[rows] = joined.astype(BF)


def weights_kernel(tok, tok_other, first, second, out):
    qa = dot(tok[...], first[:RUN], TN) + dot(tok_other[...], first[RUN:], TN)
    kv = dot(tok[...], second[:RUN], TN) + dot(tok_other[...], second[RUN:], TN)
    for p in range(16):
        out[p, :64] = kv[p * 64 : (p + 1) * 64].astype(BF)
        upper = qa[p * 32 : (p + 1) * 32, :HD]
        lower = qa[512 + p * 32 : 512 + (p + 1) * 32, :HD]
        out[p, 64:96] = jnp.concatenate([upper, lower], axis=1).astype(BF)


def sum_kernel(parts, out):
    total = parts[0].astype(F32)
    for p in range(1, 16):
        total = total + parts[p].astype(F32)
    total = total.astype(BF)
    for p in range(32):
        out[p] = total


def input_kernel(place, first, first_other, second, second_other, wq, wk, wv, att, keep, send):
    swap = place[0] != 0
    core = place[2]
    a, b, c, d = first[:RUN], first_other[...], second[:RUN], second_other[...]
    a, b = jnp.where(swap, b, a), jnp.where(swap, a, b)
    c, d = jnp.where(swap, d, c), jnp.where(swap, c, d)
    dq = jnp.concatenate([a[:, :HD], b[:, :HD]], axis=1)
    att[...] = jnp.concatenate([a[:, HD:], b[:, HD:]], axis=1)
    dk = jnp.concatenate([c[:, :HD], d[:, :HD]], axis=1)
    dv = jnp.concatenate([c[:, HD:], d[:, HD:]], axis=1)
    grad = dot(dq, wq[...], NT) + dot(dk, wk[...], NT) + dot(dv, wv[...], NT)
    for y in range(4):
        low, high = grad[y * 64 : y * 64 + 32], grad[y * 64 + 32 : y * 64 + 64]
        keep[y] = jnp.where(core == 0, low, high)
        send[y] = jnp.where(core == 0, high, low).astype(BF)


def assemble_kernel(parts, gq, gk, gv):
    for p in range(16):
        a, b = parts[2 * p].astype(F32), parts[2 * p + 1].astype(F32)
        low = jnp.concatenate([a[:, :HD], b[:, :HD]], axis=1)
        high = jnp.concatenate([a[:, HD:], b[:, HD:]], axis=1)
        gk[p * 64 : (p + 1) * 64] = low[:64]
        gv[p * 64 : (p + 1) * 64] = high[:64]
        gq[p * 32 : (p + 1) * 32] = low[64:]
        gq[512 + p * 32 : 512 + (p + 1) * 32] = high[64:]


def shift(a, step):
    return lax.ppermute(a, Z, [(i, (i + step) % NSEC) for i in range(NSEC)])


def swap(a):
    return lax.ppermute(a, "xh", [(0, 1), (1, 0)])


def ring(block):
    lower, upper = [block], [block]
    for _ in range(3):
        lower.append(shift(lower[-1], 1))
        upper.append(shift(upper[-1], -1))
    far_kv = shift(lower[3][:RUN], 1)
    far_qc = shift(upper[3][RUN:], -1)
    near = [block, lower[1], upper[1], lower[2], upper[2], lower[3], upper[3]]
    return near + [far_kv], near + [far_qc]


def on_device(tokens, wq, wk, wv, cotangent, doc_lengths, global_positions):
    shape = jax.ShapeDtypeStruct
    tok, cot = tokens[0], cotangent[0]
    xh, z, y, core = (lax.axis_index(a) for a in ("xh", Z, "y", "core"))
    place = jnp.stack([xh, z, core]).astype(jnp.int32)
    ends = jnp.cumsum(doc_lengths[0])
    starts_row = jnp.zeros((1, 128), jnp.int32).at[0, HD : HD + 8].set(ends - doc_lengths[0])
    ends_row = jnp.zeros((1, 128), jnp.int32).at[0, HD : HD + 8].set(ends)
    mine, theirs = call(
        project_kernel,
        (shape((SEC, 128), BF),) * 2,
        (place, tok, wq, wk, wv, cot),
        flops=6 * 256 * 1024 * 128,
    )
    other = swap(theirs)
    tok_other = swap(tok)
    key_feat, row_feat = call(
        feature_kernel,
        (shape((NSEC * SEC, 128), BF),) * 2,
        (place, global_positions, starts_row, ends_row),
    )
    kv_a, qc_a = ring(mine)
    kv_b, qc_b = ring(other)
    kv = [x for pair in zip(kv_a, kv_b) for x in pair]
    qc = [x for pair in zip(qc_a, qc_b) for x in pair]
    whole, part = pltpu.VMEM((NSEC * SEC, 128), BF), pltpu.VMEM((SEC, 128), BF)
    pairs = SEC * NSEC * SEC
    first, stats = call(
        functools.partial(rows_kernel, 256),
        (shape((SEC, 128), BF), shape((8, 128), F32)),
        (place, *kv, key_feat, row_feat),
        scratch=(whole, whole, part, part, part),
        flops=2 * 128 * 5 * pairs,
        transcendentals=2 * pairs,
    )
    first_other = swap(first[RUN:])
    all_stats = lax.all_to_all(
        jnp.broadcast_to(stats[None], (NSEC, 8, 128)), Z, 0, 0, tiled=True
    ).reshape(NSEC * 8, 128)
    second = call(
        functools.partial(keys_kernel, 256),
        shape((SEC, 128), BF),
        (place, *qc, mine, other, key_feat, row_feat, all_stats),
        scratch=(whole, whole, part, part, part),
        flops=2 * 128 * 4 * pairs,
        transcendentals=pairs,
    )
    second_other = swap(second[RUN:])
    partial = call(
        weights_kernel,
        shape((16, 96, 128), BF),
        (tok, tok_other, first, second),
        flops=2 * 512 * 1024 * 256,
        smem=0,
    )
    partial = lax.all_to_all(partial, ("b",) + Z, 0, 0, tiled=True)
    total = call(sum_kernel, shape((32, 96, 128), BF), (partial,), smem=0)
    att, keep, send = call(
        input_kernel,
        (shape((RUN, 128), BF), shape((4, 32, 1024), F32), shape((4, 32, 1024), BF)),
        (place, first, first_other, second, second_other, wq, wk, wv),
        flops=6 * 256 * 1024 * 128,
    )
    arrived = lax.ppermute(send, "core", [(0, 1), (1, 0)])
    both = keep + arrived.astype(F32)
    share = lax.dynamic_index_in_dim(both, y, 0, False)
    both_bf = both.astype(BF)
    for k in (1, 2, 3):
        out = lax.dynamic_index_in_dim(both_bf, lax.bitwise_xor(y, k), 0, False)
        share = share + lax.ppermute(out, "y", [(i, i ^ k) for i in range(4)]).astype(F32)
    total = lax.all_to_all(total, ("b",) + CTX, 0, 0, tiled=True)
    gq, gk, gv = call(assemble_kernel, (shape((1024, 128), F32),) * 3, (total,), smem=0)
    return att[None], share.astype(BF)[None], gq, gk, gv


def solution(mesh):
    devices = mesh.devices.reshape(2, 2, 2, 2, 2, 4, 2)
    fine = Mesh(devices, ("b",) + CTX + TP)
    in_specs = (
        P("b", CTX, None),
        P(None, TP),
        P(None, TP),
        P(None, TP),
        P("b", CTX, TP),
        P("b", None),
        P("b", None),
    )
    out_specs = (
        P("b", CTX, TP),
        P("b", CTX + TP, None),
        P(None, TP),
        P(None, TP),
        P(None, TP),
    )
    return jax.shard_map(
        on_device, mesh=fine, in_specs=in_specs, out_specs=out_specs, check_vma=False
    )
```

time: 723 us -> 141 us (0.20)
  waiting for transfers between devices: 488 us -> 22.3 us
  blocking collectives: 81.2 us -> 12.9 us
  other arithmetic: 64.2 us -> 2.28 us
  starting transfers between devices: 15.1 us -> 51.5 us
  Pallas kernels: 0 us -> 34.6 us
  matrix products: 22.7 us -> 0 us
  local copies, waits for them, and re-layouts: 32.5 us -> 13.8 us
  between operations: 14.5 us -> 0.85 us
    psum x3 -> x0, waiting for transfers between devices: 458 us -> none  [the longest x1 159 us: on_device(): picked = lax.psum(picked.astype(jnp.bfloat16), 'ctx')]
    all_gather x2 -> x0, blocking collectives: 81.2 us -> none  [merged_2(): gathered = jax.tree.map(lambda a: lax.all_gather(a, axis), part)]
    add x35 -> x0, other arithmetic: 49.3 us -> none  [the longest x15 37.3 us: combine(): scale_first[..., None] * earlier[2] + scale_second[..., None] * latter[2]]
    pallas_call x0 -> x8, Pallas kernels: none -> 34.6 us  [call(): pl.pallas_call(kernel, out_shape=outs, in_specs=specs, out_specs=jax.tree...]
    reduce_scatter x1 -> x0, waiting for transfers between devices: 26.3 us -> none  [on_device(): share_rows = lax.psum_scatter(result, 'tp', scatter_dimension=0, tiled=True)]
    ppermute x4 -> x24, starting transfers between devices: 14.8 us -> 39.5 us  [the longest x16 26.2 us: shift(): return lax.ppermute(a, Z, [(i, (i + step) % NSEC) for i in range(NSEC)])]
    dot_general x29 -> x0, matrix products: 22.7 us -> none  [the longest x3 4.03 us: group_stats(): jnp.einsum('qhk,khd->qhd', expon_terms.astype(jnp.bfloat16), value_rows,...]
    all_to_all x0 -> x1, blocking collectives: none -> 12.9 us  [on_device(): partial = lax.all_to_all(partial, ('b',) + Z, 0, 0, tiled=True)]
  transfers between devices with their start and end apart: 9 -> 26, of which waited for: 5 -> 9; matrix products, arithmetic and copies ran while one was open for 5% -> 6% of each run, Pallas kernels for 0% -> 21%
where the time goes in v1:
time: 141 us; the launch traced here: 138 us
  starting transfers between devices  51.5 us (37%)
  Pallas kernels  34.6 us (25%)
  waiting for transfers between devices  22.3 us (16%)
  local copies, waits for them, and re-layouts  13.8 us (10%)
  blocking collectives  12.9 us (9%)
  other arithmetic  2.28 us (2%)
    pallas_call x8, Pallas kernels, call(): pl.pallas_call(kernel, out_shape=outs, in_specs=specs, out_specs=jax.tree...  34.6 us
    ppermute x16, starting transfers between devices, shift(): return lax.ppermute(a, Z, [(i, (i + step) % NSEC) for i in range(NSEC)])  26.2 us
    all_to_all x1, blocking collectives, on_device(): partial = lax.all_to_all(partial, ('b',) + Z, 0, 0, tiled=True)  12.9 us
    ppermute x4, starting transfers between devices, swap(): return lax.ppermute(a, 'xh', [(0, 1), (1, 0)])  9.8 us
    unnamed x36, local copies, waits for them, and re-layouts  8.23 us
    all_to_all x1, waiting for transfers between devices, on_device(): lax.all_to_all(jnp.broadcast_to(stats[None], (NSEC, 8, 128)), Z, 0, 0, ti...  8.01 us
    all_to_all x1, starting transfers between devices, on_device(): lax.all_to_all(jnp.broadcast_to(stats[None], (NSEC, 8, 128)), Z, 0, 0, ti...  6.89 us
    ppermute x4, waiting for transfers between devices, swap(): return lax.ppermute(a, 'xh', [(0, 1), (1, 0)])  6.57 us
  transfers between devices with their start and end apart: 26, of which 9 were waited for; matrix products, arithmetic and copies ran while one was open for 6% of the time, Pallas kernels for 21%

profile of v1, /device:TPU:8, one launch (start us, length us, event | category | flops | bytes accessed | tf_op | source)
XLA Modules:
  0.0 138.2 jit_solution(3501358191174397661)
XLA Ops:
  0.7 0.9 copy-done
  1.7 0.9 copy-done.2
  2.6 0.9 copy-done.4
  3.6 0.8 copy-done.6
  4.4 1.7 %shard_map.110 = (bf16[512,128]{1,0:T(8,128)(2,1)S(1)}, bf16[512,128]{1,0:T(8,128)(2,1)S(1)}) custom-call(s32[3]{0:T(128)S(1)} %pad_add_fusion.place, bf16[256,1024]{1,0:T(8,128)(2,1)} %bitcast.3.tok, bf16[1024,128]{1,0:T(8,128)(2,1)S(1)} %copy-done, bf16[1024,128]{1,0:T(8,128)(2,1)S(1)} %copy-done.2, bf16[1024,128]{1,0:T(8,128)(2,1)S(1)} %copy-done.4, ...), custom_call_target="tpu_custom_call" | custom-call | flops 201326592 | bytes 1376268 | tf_op jit(solution)/shard_map/pallas_call | solution.py:43
  6.1 3.1 %collective-permute-start = (bf16[512,128]{1,0:T(8,128)(2,1)S(1)}, bf16[512,128]{1,0:T(8,128)(2,1)S(1)}, u32[]{:S(2)}, u32[]{:S(2)}) collective-permute-start(bf16[512,128]{1,0:T(8,128)(2,1)S(1)} %get-tuple-element.42), channel_id=1, source_target_pairs={{0,8},{8,0},{1,9},{9,1},{2,10},{10,2},{3,11},{11,3},{4,12},{12,4},... | collective-permute-start | bytes 393224 | tf_op jit(solution)/shard_map/ppermute | solution.py:325
  9.3 1.9 %collective-permute-start.1 = (bf16[512,128]{1,0:T(8,128)(2,1)S(1)}, bf16[512,128]{1,0:T(8,128)(2,1)S(1)}, u32[]{:S(2)}, u32[]{:S(2)}) collective-permute-start(bf16[512,128]{1,0:T(8,128)(2,1)S(1)} %get-tuple-element.41.refs_0_.refs_16_), channel_id=1, source_target_pairs={{0,16},{16,32},{32,48},{48,64},{64,80},{80,96},{96,112},{112,0},{1... | collective-permute-start | bytes 393224 | tf_op jit(solution)/shard_map/ppermute | solution.py:321
  11.2 3.9 %collective-permute-start.3 = (bf16[512,128]{1,0:T(8,128)(2,1)S(1)}, bf16[512,128]{1,0:T(8,128)(2,1)S(1)}, u32[]{:S(2)}, u32[]{:S(2)}) collective-permute-start(bf16[512,128]{1,0:T(8,128)(2,1)S(1)} %get-tuple-element.41.refs_0_.refs_16_), channel_id=1, source_target_pairs={{0,112},{16,0},{32,16},{48,32},{64,48},{80,64},{96,80},{112,96},{1... | collective-permute-start | bytes 393224 | tf_op jit(solution)/shard_map/ppermute | solution.py:321
  15.1 3.7 %collective-permute-start.4 = (bf16[512,128]{1,0:T(8,128)(2,1)S(1)}, bf16[512,128]{1,0:T(8,128)(2,1)S(1)}, u32[]{:S(2)}, u32[]{:S(2)}) collective-permute-start(bf16[512,128]{1,0:T(8,128)(2,1)S(1)} %collective-permute-done.refs_1_.refs_17_), channel_id=1, source_target_pairs={{0,112},{16,0},{32,16},{48,32},{64,48},{80,64},{96,80},{112,96},{1... | collective-permute-start | bytes 393224 | tf_op jit(solution)/shard_map/ppermute | solution.py:321
  18.8 3.2 %collective-permute-start.7 = (bf16[512,128]{1,0:T(8,128)(2,1)S(1)}, bf16[512,128]{1,0:T(8,128)(2,1)S(1)}, u32[]{:S(2)}, u32[]{:S(2)}) collective-permute-start(bf16[512,128]{1,0:T(8,128)(2,1)S(1)} %collective-permute-done.3.refs_4_), channel_id=1, source_target_pairs={{0,112},{16,0},{32,16},{48,32},{64,48},{80,64},{96,80},{112,96},{1... | collective-permute-start | bytes 393224 | tf_op jit(solution)/shard_map/ppermute | solution.py:321
  22.2 3.5 %collective-permute-start.8 = (bf16[512,128]{1,0:T(8,128)(2,1)S(1)}, bf16[512,128]{1,0:T(8,128)(2,1)S(1)}, u32[]{:S(2)}, u32[]{:S(2)}) collective-permute-start(bf16[512,128]{1,0:T(8,128)(2,1)S(1)} %collective-permute-done.4.refs_5_), channel_id=1, source_target_pairs={{0,112},{16,0},{32,16},{48,32},{64,48},{80,64},{96,80},{112,96},{1... | collective-permute-start | bytes 393224 | tf_op jit(solution)/shard_map/ppermute | solution.py:321
  25.8 3.0 %collective-permute-start.23 = (bf16[256,1024]{1,0:T(8,128)(2,1)}, bf16[256,1024]{1,0:T(8,128)(2,1)S(1)}, u32[]{:S(2)}, u32[]{:S(2)}) collective-permute-start(bf16[256,1024]{1,0:T(8,128)(2,1)} %bitcast.3.tok), channel_id=1, source_target_pairs={{0,8},{8,0},{1,9},{9,1},{2,10},{10,2},{3,11},{11,3},{4,12},{12,4},... | collective-permute-start | bytes 1572872 | tf_op jit(solution)/shard_map/ppermute | solution.py:325
  29.0 0.6 and_reduce_fusion
  29.6 3.2 %collective-permute-start.11 = (bf16[512,128]{1,0:T(8,128)(2,1)S(1)}, bf16[512,128]{1,0:T(8,128)(2,1)S(1)}, u32[]{:S(2)}, u32[]{:S(2)}) collective-permute-start(bf16[512,128]{1,0:T(8,128)(2,1)S(1)} %collective-permute-done.7.refs_8_), channel_id=1, source_target_pairs={{0,112},{16,0},{32,16},{48,32},{64,48},{80,64},{96,80},{112,96},{1... | collective-permute-start | bytes 393224 | tf_op jit(solution)/shard_map/ppermute | solution.py:321
  32.9 3.2 %collective-permute-start.12 = (bf16[512,128]{1,0:T(8,128)(2,1)S(1)}, bf16[512,128]{1,0:T(8,128)(2,1)S(1)}, u32[]{:S(2)}, u32[]{:S(2)}) collective-permute-start(bf16[512,128]{1,0:T(8,128)(2,1)S(1)} %collective-permute-done.8.refs_9_), channel_id=1, source_target_pairs={{0,112},{16,0},{32,16},{48,32},{64,48},{80,64},{96,80},{112,96},{1... | collective-permute-start | bytes 393224 | tf_op jit(solution)/shard_map/ppermute | solution.py:321
  36.1 0.6 broadcast_select_fusion
  36.8 0.6 slice.61
  37.4 1.9 %collective-permute-done.10.refs_11_ = bf16[512,128]{1,0:T(8,128)(2,1)S(1)} collective-permute-done((bf16[512,128]{1,0:T(8,128)(2,1)S(1)}, bf16[512,128]{1,0:T(8,128)(2,1)S(1)}, u32[]{:S(2)}, u32[]{:S(2)}) %collective-permute-start.10) | collective-permute-done | bytes 131104 | tf_op jit(solution)/shard_map/ppermute | solution.py:321
  39.3 0.6 slice.62
  40.5 0.9 scatter.6.starts
  41.5 0.9 scatter.9.ends
  42.4 2.8 %shard_map.111 = (bf16[4096,128]{1,0:T(8,128)(2,1)S(1)}, bf16[4096,128]{1,0:T(8,128)(2,1)S(1)}) custom-call(s32[3]{0:T(128)S(1)} %pad_add_fusion.place, s32[1,256]{1,0:T(1,128)S(1)} %copy-done.7, s32[1,128]{1,0:T(1,128)S(1)} %scatter.6.starts, s32[1,128]{1,0:T(1,128)S(1)} %scatter.9.ends), custom_call_target="tpu_custom_call" | custom-call | bytes 2060 | tf_op jit(solution)/shard_map/pallas_call | solution.py:43
  45.2 0.6 slice.63
  45.8 3.2 %collective-permute-start.16 = (bf16[256,128]{1,0:T(8,128)(2,1)}, bf16[256,128]{1,0:T(8,128)(2,1)}, u32[]{:S(2)}, u32[]{:S(2)}) collective-permute-start(bf16[256,128]{1,0:T(8,128)(2,1)} %slice.63), channel_id=1, source_target_pairs={{0,112},{16,0},{32,16},{48,32},{64,48},{80,64},{96,80},{112,96},{1... | collective-permute-start | bytes 196616 | tf_op jit(solution)/shard_map/ppermute | solution.py:321
  50.5 0.8 copy-done.16
  51.3 14.8 %shard_map.112 = (bf16[512,128]{1,0:T(8,128)(2,1)S(1)}, f32[8,128]{1,0:T(8,128)S(1)}) custom-call(s32[3]{0:T(128)S(1)} %pad_add_fusion.place, bf16[512,128]{1,0:T(8,128)(2,1)S(1)} %get-tuple-element.41.refs_0_.refs_16_, bf16[512,128]{1,0:T(8,128)(2,1)S(1)} %collective-permute-done.refs_1_.refs_17_, bf16[512,128]{1,0:T(8,128)(2,1)S(1)} %collective-permute-done.1.refs_2_, ...), custom_call_target="tpu_custom_call" | custom-call | flops 2684354560 | bytes 4063244 | tf_op jit(solution)/shard_map/pallas_call | solution.py:43
  66.1 0.6 broadcast_in_dim.12
  66.7 6.9 %all-to-all-start = ((f32[8,8,128]{2,1,0:T(8,128)}), f32[8,8,128]{2,1,0:T(8,128)S(1)}, u32[]{:S(2)}, u32[]{:S(2)}) async-start(f32[8,8,128]{2,1,0:T(8,128)} %broadcast_in_dim.12), calls=%async_computation | async-start | bytes 65536 | tf_op jit(solution)/shard_map/all_to_all | solution.py:375
  73.6 8.0 %all-to-all-done = f32[8,8,128]{2,1,0:T(8,128)S(1)} async-done(((f32[8,8,128]{2,1,0:T(8,128)}), f32[8,8,128]{2,1,0:T(8,128)S(1)}, u32[]{:S(2)}, u32[]{:S(2)}) %all-to-all-start) | async-done | bytes 32800 | tf_op jit(solution)/shard_map/all_to_all | solution.py:375
  81.6 1.2 copy-done.9
  82.9 0.9 copy-done.11
  83.8 0.9 copy-done.14
  84.7 9.4 %shard_map.113.second = bf16[512,128]{1,0:T(8,128)(2,1)S(1)} custom-call(s32[3]{0:T(128)S(1)} %pad_add_fusion.place, bf16[512,128]{1,0:T(8,128)(2,1)S(1)} %get-tuple-element.41.refs_0_.refs_16_, bf16[512,128]{1,0:T(8,128)(2,1)S(1)} %collective-permute-done.refs_1_.refs_17_, bf16[512,128]{1,0:T(8,128)(2,1)S(1)} %collective-permute-done.1.refs_2_, ...), custom_call_target="tpu_custom_call" | custom-call | flops 2147483648 | bytes 4358156 | tf_op jit(solution)/shard_map/pallas_call | solution.py:43
  94.1 1.9 %shard_map.115 = bf16[16,96,128]{2,1,0:T(8,128)(2,1)S(1)} custom-call(bf16[256,1024]{1,0:T(8,128)(2,1)} %bitcast.3.tok, bf16[256,1024]{1,0:T(8,128)(2,1)S(1)} %collective-permute-done.23.tok_other, bf16[512,128]{1,0:T(8,128)(2,1)S(1)} %get-tuple-element.45.first, bf16[512,128]{1,0:T(8,128)(2,1)S(1)} %shard_map.113.second), custom_call_target="tpu_custom_call" | custom-call | flops 268435456 | bytes 1310720 | tf_op jit(solution)/shard_map/pallas_call | solution.py:43
  95.9 12.9 %all_to_all.15.parts = bf16[16,96,128]{2,1,0:T(8,128)(2,1)S(1)} all-to-all(bf16[16,96,128]{2,1,0:T(8,128)(2,1)S(1)} %shard_map.115), channel_id=1, replica_groups=mesh['b'=2,'z2'=2,'z1'=2,'z0'=2,'xh'=2,'y'=4,'core'=2] {'b','z2','z1','z0'}, dimensions={0} | all-to-all | bytes 786432 | tf_op jit(solution)/shard_map/all_to_all | solution.py:394
  108.8 1.0 shard_map.116
  109.8 5.1 %all-to-all-start.2 = ((bf16[32,96,128]{2,1,0:T(8,128)(2,1)}), bf16[32,96,128]{2,1,0:T(8,128)(2,1)S(1)}, u32[]{:S(2)}, u32[]{:S(2)}) async-start(bf16[32,96,128]{2,1,0:T(8,128)(2,1)} %shard_map.116), calls=%async_computation.2 | async-start | bytes 1572864 | tf_op jit(solution)/shard_map/all_to_all | solution.py:409
  114.9 3.4 %collective-permute-start.15 = (bf16[256,128]{1,0:T(8,128)(2,1)S(1)}, bf16[256,128]{1,0:T(8,128)(2,1)S(1)}, u32[]{:S(2)}, u32[]{:S(2)}) collective-permute-start(bf16[256,128]{1,0:T(8,128)(2,1)S(1)} %slice.57), channel_id=1, source_target_pairs={{0,8},{8,0},{1,9},{9,1},{2,10},{10,2},{3,11},{11,3},{4,12},{12,4},... | collective-permute-start | bytes 196616 | tf_op jit(solution)/shard_map/ppermute | solution.py:325
  118.5 3.4 %collective-permute-done.15.first_other = bf16[256,128]{1,0:T(8,128)(2,1)S(1)} collective-permute-done((bf16[256,128]{1,0:T(8,128)(2,1)S(1)}, bf16[256,128]{1,0:T(8,128)(2,1)S(1)}, u32[]{:S(2)}, u32[]{:S(2)}) %collective-permute-start.15) | collective-permute-done | bytes 65568 | tf_op jit(solution)/shard_map/ppermute | solution.py:325
  121.9 3.1 %collective-permute-done.18.second_other = bf16[256,128]{1,0:T(8,128)(2,1)S(1)} collective-permute-done((bf16[256,128]{1,0:T(8,128)(2,1)S(1)}, bf16[256,128]{1,0:T(8,128)(2,1)S(1)}, u32[]{:S(2)}, u32[]{:S(2)}) %collective-permute-start.18) | collective-permute-done | bytes 65568 | tf_op jit(solution)/shard_map/ppermute | solution.py:325
  125.1 1.8 %shard_map.114 = (bf16[256,128]{1,0:T(8,128)(2,1)}, f32[4,32,1024]{2,1,0:T(8,128)S(1)}, bf16[4,32,1024]{2,1,0:T(8,128)(2,1)S(1)}) custom-call(s32[3]{0:T(128)S(1)} %pad_add_fusion.place, bf16[512,128]{1,0:T(8,128)(2,1)S(1)} %get-tuple-element.45.first, bf16[256,128]{1,0:T(8,128)(2,1)S(1)} %collective-permute-done.15.first_other, ...), custom_call_target="tpu_custom_call" | custom-call | flops 201326592 | bytes 1179660 | tf_op jit(solution)/shard_map/pallas_call | solution.py:43
  126.8 1.5 %collective-permute-done.19 = bf16[4,32,1024]{2,1,0:T(8,128)(2,1)S(1)} collective-permute-done((bf16[4,32,1024]{2,1,0:T(8,128)(2,1)S(1)}, bf16[4,32,1024]{2,1,0:T(8,128)(2,1)S(1)}, u32[]{:S(2)}, u32[]{:S(2)}) %collective-permute-start.19) | collective-permute-done | bytes 262176 | tf_op jit(solution)/shard_map/ppermute | solution.py:402
  129.0 2.6 %collective-permute-start.21 = (bf16[32,1024]{1,0:T(8,128)(2,1)S(1)}, bf16[32,1024]{1,0:T(8,128)(2,1)S(1)}, u32[]{:S(2)}, u32[]{:S(2)}) collective-permute-start(bf16[32,1024]{1,0:T(8,128)(2,1)S(1)} %get-tuple-element.57), channel_id=1, source_target_pairs={{0,4},{2,6},{4,0},{6,2},{1,5},{3,7},{5,1},{7,3},{8,12},{10,14},{12... | collective-permute-start | bytes 196616 | tf_op jit(solution)/shard_map/ppermute | solution.py:408
  132.0 0.8 collective-permute-done.20
  132.8 2.4 %collective-permute-done.21 = bf16[32,1024]{1,0:T(8,128)(2,1)S(1)} collective-permute-done((bf16[32,1024]{1,0:T(8,128)(2,1)S(1)}, bf16[32,1024]{1,0:T(8,128)(2,1)S(1)}, u32[]{:S(2)}, u32[]{:S(2)}) %collective-permute-start.21) | collective-permute-done | bytes 65568 | tf_op jit(solution)/shard_map/ppermute | solution.py:408
  135.2 0.9 collective-permute-done.22
  136.2 0.7 fusion.3
  136.8 1.4 %shard_map.117 = (f32[1024,128]{1,0:T(8,128)}, f32[1024,128]{1,0:T(8,128)}, f32[1024,128]{1,0:T(8,128)}) custom-call(bf16[32,96,128]{2,1,0:T(8,128)(2,1)S(1)} %all-to-all-done.2.parts), custom_call_target="tpu_custom_call" | custom-call | bytes 786432 | tf_op jit(solution)/shard_map/pallas_call | solution.py:43
  (69 shorter events, 3.8 us)
Async XLA Ops:
  0.7 1.0 copy-start
  1.7 0.9 copy-start.2
  2.6 0.9 copy-start.4
  3.6 0.8 copy-start.6
  6.1 9.0 %collective-permute-start = (bf16[512,128]{1,0:T(8,128)(2,1)S(1)}, bf16[512,128]{1,0:T(8,128)(2,1)S(1)}, u32[]{:S(2)}, u32[]{:S(2)}) collective-permute-start(bf16[512,128]{1,0:T(8,128)(2,1)S(1)} %get-tuple-element.42), channel_id=1, source_target_pairs={{0,8},{8,0},{1,9},{9,1},{2,10},{10,2},{3,11},{11,3},{4,12},{12,4},... | collective-permute-start | bytes 393224 | tf_op jit(solution)/shard_map/ppermute | solution.py:325
  9.3 19.6 %copy-start.17 = (s32[1,8]{1,0:T(1,128)S(1)}, s32[1,8]{1,0:T(1,128)}, u32[]{:S(2)}) copy-start(s32[1,8]{1,0:T(1,128)} %param.16) | copy-start | bytes 100
  9.3 9.6 %collective-permute-start.1 = (bf16[512,128]{1,0:T(8,128)(2,1)S(1)}, bf16[512,128]{1,0:T(8,128)(2,1)S(1)}, u32[]{:S(2)}, u32[]{:S(2)}) collective-permute-start(bf16[512,128]{1,0:T(8,128)(2,1)S(1)} %get-tuple-element.41.refs_0_.refs_16_), channel_id=1, source_target_pairs={{0,16},{16,32},{32,48},{48,64},{64,80},{80,96},{96,112},{112,0},{1... | collective-permute-start | bytes 393224 | tf_op jit(solution)/shard_map/ppermute | solution.py:321
  11.2 7.6 %collective-permute-start.3 = (bf16[512,128]{1,0:T(8,128)(2,1)S(1)}, bf16[512,128]{1,0:T(8,128)(2,1)S(1)}, u32[]{:S(2)}, u32[]{:S(2)}) collective-permute-start(bf16[512,128]{1,0:T(8,128)(2,1)S(1)} %get-tuple-element.41.refs_0_.refs_16_), channel_id=1, source_target_pairs={{0,112},{16,0},{32,16},{48,32},{64,48},{80,64},{96,80},{112,96},{1... | collective-permute-start | bytes 393224 | tf_op jit(solution)/shard_map/ppermute | solution.py:321
  15.1 7.1 %collective-permute-start.2 = (bf16[512,128]{1,0:T(8,128)(2,1)S(1)}, bf16[512,128]{1,0:T(8,128)(2,1)S(1)}, u32[]{:S(2)}, u32[]{:S(2)}) collective-permute-start(bf16[512,128]{1,0:T(8,128)(2,1)S(1)} %collective-permute-done.refs_1_.refs_17_), channel_id=1, source_target_pairs={{0,16},{16,32},{32,48},{48,64},{64,80},{80,96},{96,112},{112,0},{1... | collective-permute-start | bytes 393224 | tf_op jit(solution)/shard_map/ppermute | solution.py:321
  15.1 7.1 %collective-permute-start.4 = (bf16[512,128]{1,0:T(8,128)(2,1)S(1)}, bf16[512,128]{1,0:T(8,128)(2,1)S(1)}, u32[]{:S(2)}, u32[]{:S(2)}) collective-permute-start(bf16[512,128]{1,0:T(8,128)(2,1)S(1)} %collective-permute-done.refs_1_.refs_17_), channel_id=1, source_target_pairs={{0,112},{16,0},{32,16},{48,32},{64,48},{80,64},{96,80},{112,96},{1... | collective-permute-start | bytes 393224 | tf_op jit(solution)/shard_map/ppermute | solution.py:321
  18.8 10.8 %collective-permute-start.5 = (bf16[512,128]{1,0:T(8,128)(2,1)S(1)}, bf16[512,128]{1,0:T(8,128)(2,1)S(1)}, u32[]{:S(2)}, u32[]{:S(2)}) collective-permute-start(bf16[512,128]{1,0:T(8,128)(2,1)S(1)} %collective-permute-done.1.refs_2_), channel_id=1, source_target_pairs={{0,16},{16,32},{32,48},{48,64},{64,80},{80,96},{96,112},{112,0},{1... | collective-permute-start | bytes 393224 | tf_op jit(solution)/shard_map/ppermute | solution.py:321
  18.8 10.8 %collective-permute-start.7 = (bf16[512,128]{1,0:T(8,128)(2,1)S(1)}, bf16[512,128]{1,0:T(8,128)(2,1)S(1)}, u32[]{:S(2)}, u32[]{:S(2)}) collective-permute-start(bf16[512,128]{1,0:T(8,128)(2,1)S(1)} %collective-permute-done.3.refs_4_), channel_id=1, source_target_pairs={{0,112},{16,0},{32,16},{48,32},{64,48},{80,64},{96,80},{112,96},{1... | collective-permute-start | bytes 393224 | tf_op jit(solution)/shard_map/ppermute | solution.py:321
  22.2 10.7 %collective-permute-start.6 = (bf16[512,128]{1,0:T(8,128)(2,1)S(1)}, bf16[512,128]{1,0:T(8,128)(2,1)S(1)}, u32[]{:S(2)}, u32[]{:S(2)}) collective-permute-start(bf16[512,128]{1,0:T(8,128)(2,1)S(1)} %collective-permute-done.2.refs_3_), channel_id=1, source_target_pairs={{0,16},{16,32},{32,48},{48,64},{64,80},{80,96},{96,112},{112,0},{1... | collective-permute-start | bytes 393224 | tf_op jit(solution)/shard_map/ppermute | solution.py:321
  22.2 10.7 %collective-permute-start.8 = (bf16[512,128]{1,0:T(8,128)(2,1)S(1)}, bf16[512,128]{1,0:T(8,128)(2,1)S(1)}, u32[]{:S(2)}, u32[]{:S(2)}) collective-permute-start(bf16[512,128]{1,0:T(8,128)(2,1)S(1)} %collective-permute-done.4.refs_5_), channel_id=1, source_target_pairs={{0,112},{16,0},{32,16},{48,32},{64,48},{80,64},{96,80},{112,96},{1... | collective-permute-start | bytes 393224 | tf_op jit(solution)/shard_map/ppermute | solution.py:321
  25.8 68.3 %collective-permute-start.23 = (bf16[256,1024]{1,0:T(8,128)(2,1)}, bf16[256,1024]{1,0:T(8,128)(2,1)S(1)}, u32[]{:S(2)}, u32[]{:S(2)}) collective-permute-start(bf16[256,1024]{1,0:T(8,128)(2,1)} %bitcast.3.tok), channel_id=1, source_target_pairs={{0,8},{8,0},{1,9},{9,1},{2,10},{10,2},{3,11},{11,3},{4,12},{12,4},... | collective-permute-start | bytes 1572872 | tf_op jit(solution)/shard_map/ppermute | solution.py:325
  29.6 7.1 %collective-permute-start.9 = (bf16[512,128]{1,0:T(8,128)(2,1)S(1)}, bf16[512,128]{1,0:T(8,128)(2,1)S(1)}, u32[]{:S(2)}, u32[]{:S(2)}) collective-permute-start(bf16[512,128]{1,0:T(8,128)(2,1)S(1)} %collective-permute-done.5.refs_6_), channel_id=1, source_target_pairs={{0,16},{16,32},{32,48},{48,64},{64,80},{80,96},{96,112},{112,0},{1... | collective-permute-start | bytes 393224 | tf_op jit(solution)/shard_map/ppermute | solution.py:321
  29.6 15.5 %collective-permute-start.11 = (bf16[512,128]{1,0:T(8,128)(2,1)S(1)}, bf16[512,128]{1,0:T(8,128)(2,1)S(1)}, u32[]{:S(2)}, u32[]{:S(2)}) collective-permute-start(bf16[512,128]{1,0:T(8,128)(2,1)S(1)} %collective-permute-done.7.refs_8_), channel_id=1, source_target_pairs={{0,112},{16,0},{32,16},{48,32},{64,48},{80,64},{96,80},{112,96},{1... | collective-permute-start | bytes 393224 | tf_op jit(solution)/shard_map/ppermute | solution.py:321
  32.9 17.6 %copy-start.10 = (bf16[512,128]{1,0:T(8,128)(2,1)}, bf16[512,128]{1,0:T(8,128)(2,1)S(1)}, u32[]{:S(2)}) copy-start(bf16[512,128]{1,0:T(8,128)(2,1)S(1)} %collective-permute-done.6.refs_7_) | copy-start | bytes 393220
  32.9 6.4 %collective-permute-start.10 = (bf16[512,128]{1,0:T(8,128)(2,1)S(1)}, bf16[512,128]{1,0:T(8,128)(2,1)S(1)}, u32[]{:S(2)}, u32[]{:S(2)}) collective-permute-start(bf16[512,128]{1,0:T(8,128)(2,1)S(1)} %collective-permute-done.6.refs_7_), channel_id=1, source_target_pairs={{0,16},{16,32},{32,48},{48,64},{64,80},{80,96},{96,112},{112,0},{1... | collective-permute-start | bytes 393224 | tf_op jit(solution)/shard_map/ppermute | solution.py:321
  32.9 7.1 %copy-start.12 = (bf16[512,128]{1,0:T(8,128)(2,1)}, bf16[512,128]{1,0:T(8,128)(2,1)S(1)}, u32[]{:S(2)}) copy-start(bf16[512,128]{1,0:T(8,128)(2,1)S(1)} %collective-permute-done.8.refs_9_) | copy-start | bytes 393220
  32.9 16.1 %collective-permute-start.12 = (bf16[512,128]{1,0:T(8,128)(2,1)S(1)}, bf16[512,128]{1,0:T(8,128)(2,1)S(1)}, u32[]{:S(2)}, u32[]{:S(2)}) collective-permute-start(bf16[512,128]{1,0:T(8,128)(2,1)S(1)} %collective-permute-done.8.refs_9_), channel_id=1, source_target_pairs={{0,112},{16,0},{32,16},{48,32},{64,48},{80,64},{96,80},{112,96},{1... | collective-permute-start | bytes 393224 | tf_op jit(solution)/shard_map/ppermute | solution.py:321
  37.4 12.4 %collective-permute-start.13 = (bf16[256,128]{1,0:T(8,128)(2,1)}, bf16[256,128]{1,0:T(8,128)(2,1)S(1)}, u32[]{:S(2)}, u32[]{:S(2)}) collective-permute-start(bf16[256,128]{1,0:T(8,128)(2,1)} %slice.61), channel_id=1, source_target_pairs={{0,16},{16,32},{32,48},{48,64},{64,80},{80,96},{96,112},{112,0},{1... | collective-permute-start | bytes 196616 | tf_op jit(solution)/shard_map/ppermute | solution.py:321
  40.0 10.5 %collective-permute-start.14 = (bf16[256,128]{1,0:T(8,128)(2,1)}, bf16[256,128]{1,0:T(8,128)(2,1)}, u32[]{:S(2)}, u32[]{:S(2)}) collective-permute-start(bf16[256,128]{1,0:T(8,128)(2,1)} %slice.62), channel_id=1, source_target_pairs={{0,16},{16,32},{32,48},{48,64},{64,80},{80,96},{96,112},{112,0},{1... | collective-permute-start | bytes 196616 | tf_op jit(solution)/shard_map/ppermute | solution.py:321
  41.4 0.9 copy-start.7
  45.1 20.9 %copy-start.8 = (bf16[4096,128]{1,0:T(8,128)(2,1)}, bf16[4096,128]{1,0:T(8,128)(2,1)S(1)}, u32[]{:S(2)}) copy-start(bf16[4096,128]{1,0:T(8,128)(2,1)S(1)} %get-tuple-element.44.refs_17_.refs_19_) | copy-start | bytes 3145732
  45.2 5.3 %copy-start.13 = (bf16[512,128]{1,0:T(8,128)(2,1)S(1)}, bf16[512,128]{1,0:T(8,128)(2,1)}, u32[]{:S(2)}) copy-start(bf16[512,128]{1,0:T(8,128)(2,1)} %copy-done.12) | copy-start | bytes 393220
  45.8 27.8 %collective-permute-start.16 = (bf16[256,128]{1,0:T(8,128)(2,1)}, bf16[256,128]{1,0:T(8,128)(2,1)}, u32[]{:S(2)}, u32[]{:S(2)}) collective-permute-start(bf16[256,128]{1,0:T(8,128)(2,1)} %slice.63), channel_id=1, source_target_pairs={{0,112},{16,0},{32,16},{48,32},{64,48},{80,64},{96,80},{112,96},{1... | collective-permute-start | bytes 196616 | tf_op jit(solution)/shard_map/ppermute | solution.py:321
  49.7 23.9 %collective-permute-start.17 = (bf16[256,128]{1,0:T(8,128)(2,1)}, bf16[256,128]{1,0:T(8,128)(2,1)}, u32[]{:S(2)}, u32[]{:S(2)}) collective-permute-start(bf16[256,128]{1,0:T(8,128)(2,1)} %slice.64), channel_id=1, source_target_pairs={{0,112},{16,0},{32,16},{48,32},{64,48},{80,64},{96,80},{112,96},{1... | collective-permute-start | bytes 196616 | tf_op jit(solution)/shard_map/ppermute | solution.py:321
  49.8 0.6 copy-start.15
  50.5 0.8 copy-start.16
  66.7 14.9 %all-to-all-start = ((f32[8,8,128]{2,1,0:T(8,128)}), f32[8,8,128]{2,1,0:T(8,128)S(1)}, u32[]{:S(2)}, u32[]{:S(2)}) async-start(f32[8,8,128]{2,1,0:T(8,128)} %broadcast_in_dim.12), calls=%async_computation | async-start | bytes 65536 | tf_op jit(solution)/shard_map/all_to_all | solution.py:375
  81.6 1.2 copy-start.9
  82.9 0.9 copy-start.11
  83.8 0.9 copy-start.14
  109.8 15.3 %copy-start.1 = (bf16[1024,128]{1,0:T(8,128)(2,1)S(1)}, bf16[1024,128]{1,0:T(8,128)(2,1)}, u32[]{:S(2)}) copy-start(bf16[1024,128]{1,0:T(8,128)(2,1)} %wq.3) | copy-start | bytes 786436
  109.8 15.3 %copy-start.3 = (bf16[1024,128]{1,0:T(8,128)(2,1)S(1)}, bf16[1024,128]{1,0:T(8,128)(2,1)}, u32[]{:S(2)}) copy-start(bf16[1024,128]{1,0:T(8,128)(2,1)} %wk.3) | copy-start | bytes 786436
  109.8 15.3 %copy-start.5 = (bf16[1024,128]{1,0:T(8,128)(2,1)S(1)}, bf16[1024,128]{1,0:T(8,128)(2,1)}, u32[]{:S(2)}) copy-start(bf16[1024,128]{1,0:T(8,128)(2,1)} %wv.3) | copy-start | bytes 786436
  109.8 27.0 %all-to-all-start.2 = ((bf16[32,96,128]{2,1,0:T(8,128)(2,1)}), bf16[32,96,128]{2,1,0:T(8,128)(2,1)S(1)}, u32[]{:S(2)}, u32[]{:S(2)}) async-start(bf16[32,96,128]{2,1,0:T(8,128)(2,1)} %shard_map.116), calls=%async_computation.2 | async-start | bytes 1572864 | tf_op jit(solution)/shard_map/all_to_all | solution.py:409
  114.9 7.1 %collective-permute-start.15 = (bf16[256,128]{1,0:T(8,128)(2,1)S(1)}, bf16[256,128]{1,0:T(8,128)(2,1)S(1)}, u32[]{:S(2)}, u32[]{:S(2)}) collective-permute-start(bf16[256,128]{1,0:T(8,128)(2,1)S(1)} %slice.57), channel_id=1, source_target_pairs={{0,8},{8,0},{1,9},{9,1},{2,10},{10,2},{3,11},{11,3},{4,12},{12,4},... | collective-permute-start | bytes 196616 | tf_op jit(solution)/shard_map/ppermute | solution.py:325
  118.3 6.8 %collective-permute-start.18 = (bf16[256,128]{1,0:T(8,128)(2,1)S(1)}, bf16[256,128]{1,0:T(8,128)(2,1)S(1)}, u32[]{:S(2)}, u32[]{:S(2)}) collective-permute-start(bf16[256,128]{1,0:T(8,128)(2,1)S(1)} %slice.65), channel_id=1, source_target_pairs={{0,8},{8,0},{1,9},{9,1},{2,10},{10,2},{3,11},{11,3},{4,12},{12,4},... | collective-permute-start | bytes 196616 | tf_op jit(solution)/shard_map/ppermute | solution.py:325
  126.8 1.5 %collective-permute-start.19 = (bf16[4,32,1024]{2,1,0:T(8,128)(2,1)S(1)}, bf16[4,32,1024]{2,1,0:T(8,128)(2,1)S(1)}, u32[]{:S(2)}, u32[]{:S(2)}) collective-permute-start(bf16[4,32,1024]{2,1,0:T(8,128)(2,1)S(1)} %get-tuple-element.49), channel_id=1, source_target_pairs={{0,1},{1,0},{2,3},{3,2},{4,5},{5,4},{6,7},{7,6},{8,9},{9,8},{10,11... | collective-permute-start | bytes 786440 | tf_op jit(solution)/shard_map/ppermute | solution.py:402
  128.5 4.4 %collective-permute-start.20 = (bf16[32,1024]{1,0:T(8,128)(2,1)S(1)}, bf16[32,1024]{1,0:T(8,128)(2,1)S(1)}, u32[]{:S(2)}, u32[]{:S(2)}) collective-permute-start(bf16[32,1024]{1,0:T(8,128)(2,1)S(1)} %get-tuple-element.55), channel_id=1, source_target_pairs={{0,2},{2,0},{4,6},{6,4},{1,3},{3,1},{5,7},{7,5},{8,10},{10,8},{12,... | collective-permute-start | bytes 196616 | tf_op jit(solution)/shard_map/ppermute | solution.py:408
  129.0 6.2 %collective-permute-start.21 = (bf16[32,1024]{1,0:T(8,128)(2,1)S(1)}, bf16[32,1024]{1,0:T(8,128)(2,1)S(1)}, u32[]{:S(2)}, u32[]{:S(2)}) collective-permute-start(bf16[32,1024]{1,0:T(8,128)(2,1)S(1)} %get-tuple-element.57), channel_id=1, source_target_pairs={{0,4},{2,6},{4,0},{6,2},{1,5},{3,7},{5,1},{7,3},{8,12},{10,14},{12... | collective-permute-start | bytes 196616 | tf_op jit(solution)/shard_map/ppermute | solution.py:408
  131.6 4.5 %collective-permute-start.22 = (bf16[32,1024]{1,0:T(8,128)(2,1)S(1)}, bf16[32,1024]{1,0:T(8,128)(2,1)S(1)}, u32[]{:S(2)}, u32[]{:S(2)}) collective-permute-start(bf16[32,1024]{1,0:T(8,128)(2,1)S(1)} %get-tuple-element.56), channel_id=1, source_target_pairs={{0,6},{2,4},{4,2},{6,0},{1,7},{3,5},{5,3},{7,1},{8,14},{10,12},{12... | collective-permute-start | bytes 196616 | tf_op jit(solution)/shard_map/ppermute | solution.py:408

commit v2 on v1

v2 whole, which is shorter than its diff:
```python
import functools
import math

import jax
import jax.numpy as jnp
from jax import lax
from jax.experimental import pallas as pl
from jax.experimental.pallas import tpu as pltpu
from jax.sharding import Mesh
from jax.sharding import PartitionSpec as P

HALF = 256
HD = 64
RUN = 256
SEC = 512
NSEC = 8
NEG = -1e30
LIMIT = 64 << 20
BF = jnp.bfloat16
F32 = jnp.float32

Z = ("z2", "z1", "z0")
CTX = Z + ("xh",)
TP = ("y", "core")

OFFSETS = (0, -1, 1, -2, 2, -3, 3, 4)

NN = (((1,), (0,)), ((), ()))
NT = (((1,), (1,)), ((), ()))
TN = (((0,), (0,)), ((), ()))


def dot(a, b, dims=NN):
    return lax.dot_general(a, b, dims, preferred_element_type=F32)


def call(kernel, outs, args, scratch=(), flops=0, transcendentals=0, smem=1, manual=0):
    specs = [pl.BlockSpec(memory_space=pltpu.SMEM)] * smem
    specs += [pl.BlockSpec(memory_space=pl.ANY)] * manual
    specs += [pl.BlockSpec(memory_space=pltpu.VMEM)] * (len(args) - smem - manual)
    moved = sum(a.size * a.dtype.itemsize for a in args)
    return pl.pallas_call(
        kernel,
        out_shape=outs,
        in_specs=specs,
        out_specs=jax.tree.map(lambda _: pl.BlockSpec(memory_space=pltpu.VMEM), outs),
        scratch_shapes=list(scratch),
        compiler_params=pltpu.CompilerParams(vmem_limit_bytes=LIMIT),
        cost_estimate=pl.CostEstimate(
            flops=flops, bytes_accessed=moved, transcendentals=transcendentals
        ),
    )(*args)


def low_lanes(rows):
    return lax.broadcasted_iota(jnp.int32, (rows, 128), 1) < HD


def project_kernel(place, tok, wq, wk, wv, cot, mine, theirs, tok_v, wk_v, wv_v, wq_v, cot_v, sems):
    pairs = ((tok, tok_v), (wk, wk_v), (wv, wv_v), (wq, wq_v), (cot, cot_v))
    copies = [pltpu.make_async_copy(a, b, sems.at[i]) for i, (a, b) in enumerate(pairs)]
    for copy in copies:
        copy.start()
    first = place[0] == 0
    copies[0].wait()
    t = tok_v[...]
    copies[1].wait()
    k = dot(t, wk_v[...]).astype(BF)
    copies[2].wait()
    v = dot(t, wv_v[...]).astype(BF)
    copies[3].wait()
    q = dot(t, wq_v[...]).astype(BF)
    copies[4].wait()
    c = cot_v[...]
    kv0 = jnp.concatenate([k[:, :HD], v[:, :HD]], axis=1)
    kv1 = jnp.concatenate([k[:, HD:], v[:, HD:]], axis=1)
    qc0 = jnp.concatenate([q[:, :HD], c[:, :HD]], axis=1)
    qc1 = jnp.concatenate([q[:, HD:], c[:, HD:]], axis=1)

    @pl.when(first)
    def _():
        mine[:RUN] = kv0
        mine[RUN:] = qc0
        theirs[:RUN] = kv1
        theirs[RUN:] = qc1

    @pl.when(jnp.logical_not(first))
    def _():
        mine[:RUN] = kv1
        mine[RUN:] = qc1
        theirs[:RUN] = kv0
        theirs[RUN:] = qc0


def feature_kernel(place, lengths, spots, key_feat, row_feat):
    flip = place[0]
    lane = lax.broadcasted_iota(jnp.int32, (RUN, 128), 1)
    inside = (lane >= HD) & (lane < HD + 8)
    last = lane == HD + 8
    lane_row = lax.broadcasted_iota(jnp.int32, (1, 128), 1)
    starts, ends = jnp.zeros((1, 128), jnp.int32), jnp.zeros((1, 128), jnp.int32)
    start = jnp.int32(0)
    for d in range(8):
        end = start + lengths[0, d]
        starts = jnp.where(lane_row == HD + d, start, starts)
        ends = jnp.where(lane_row == HD + d, end, ends)
        start = end

    def one(block, carry):
        half = lax.rem(block, 2)
        run = (block - half) + jnp.where(half == flip, 0, 1)
        pos = run * RUN + lax.broadcasted_iota(jnp.int32, (RUN, RUN), 0)
        hit = jnp.max(jnp.where(pos == spots[...], 1.0, 0.0), axis=1, keepdims=True)
        other = 1.0 - hit
        pos128 = run * RUN + lax.broadcasted_iota(jnp.int32, (RUN, 128), 0)
        member = (pos128 >= starts) & (pos128 < ends)
        row = jnp.where(last, other, jnp.where(member, 1.0, 0.0))
        key = jnp.where(last, other, jnp.where(inside & jnp.logical_not(member), 1.0, 0.0))
        at = pl.ds(pl.multiple_of(block * RUN, RUN), RUN)
        row_feat[at, :] = row.astype(BF)
        key_feat[at, :] = (key * NEG).astype(BF)
        return carry

    lax.fori_loop(0, 2 * NSEC, one, 0)


def places(section, flip, along):
    shape = (1, SEC) if along == 1 else (SEC, 1)
    i = lax.broadcasted_iota(jnp.int32, shape, along)
    half = jnp.where(i >= RUN, 1 - flip, flip)
    return section * SEC + half * RUN + lax.bitwise_and(i, RUN - 1)


def section_at(own, offset):
    return lax.rem(own + offset + NSEC, NSEC)


def bring(own, offsets, pieces, part, feat, rows, joined, sems):
    copies = []
    for r, offset in enumerate(offsets):
        for half in range(2):
            to = rows.at[pl.ds(r * SEC + half * RUN, RUN)]
            copies.append((pieces[2 * r + half].at[pl.ds(part * RUN, RUN)], to))
        at = pl.multiple_of(section_at(own, offset) * SEC, SEC)
        copies.append((feat.at[pl.ds(at, SEC)], joined.at[pl.ds(r * SEC, SEC)]))
    copies = [pltpu.make_async_copy(a, b, sems.at[i]) for i, (a, b) in enumerate(copies)]
    for copy in copies:
        copy.start()
    return copies


def join_keys(count, kv_s, kp_s):
    low = low_lanes(SEC)
    for r in range(count):
        at = slice(r * SEC, (r + 1) * SEC)
        kp_s[at] = jnp.where(low, kv_s[at], kp_s[at])


def join_queries(count, qc_s, q_s):
    low = low_lanes(SEC)
    for r in range(count):
        at = slice(r * SEC, (r + 1) * SEC)
        scaled = qc_s[at] * jnp.asarray(1.0 / math.sqrt(HD), BF)
        q_s[at] = jnp.where(low, scaled, q_s[at])


def upper_only(rows_s, joined_s, near_s):
    rows = rows_s[...]
    rows_s[...] = jnp.where(low_lanes(SEC), jnp.zeros_like(rows), rows)
    lane = lax.broadcasted_iota(jnp.int32, (SEC, 128), 1)
    joined = joined_s[...]
    near_s[...] = jnp.where(lane == HD + 8, jnp.zeros_like(joined), joined)


def bring_both(own, offsets, pieces, mine, other, key_feat, row_feat, scratch):
    kv_s, kp_s, q_s, qn_s, c_s, sems, own_sems = scratch
    copies = bring(own, offsets, pieces, 0, key_feat, kv_s, kp_s, sems)
    copies += bring(own, (0,), (mine, other), 1, row_feat, c_s, q_s, own_sems)
    for copy in copies:
        copy.wait()
    join_keys(len(offsets), kv_s, kp_s)
    join_queries(1, c_s, q_s)
    upper_only(c_s, q_s, qn_s)


def scores_of(own, flip, chunk, c, offset, at, row_places, q_s, qn_s, kp_s):
    rows = slice(c * chunk, (c + 1) * chunk)
    s = dot(q_s[rows], kp_s[at, :], NT)
    if offset in (0, -1, 1):
        away = row_places[rows] - places(section_at(own, offset), flip, 1)
        s = jnp.where(jnp.abs(away) <= HALF, dot(qn_s[rows], kp_s[at, :], NT), s)
    return s


def forward_kernel(chunk, offsets, first, last, place, mine, other, key_feat, row_feat, *refs):
    pieces, rest = refs[: 2 * len(offsets)], list(refs[2 * len(offsets) :])
    acc_in, peak_in = (None, None) if first else (rest.pop(0), rest.pop(0))
    if last:
        att_out, column_out, stats, *scratch = rest
    else:
        acc_out, peak_out, *scratch = rest
    kv_s, kp_s, q_s, qn_s, c_s = scratch[:5]
    flip, own = place[0], place[1]
    bring_both(own, offsets, pieces, mine, other, key_feat, row_feat, scratch)
    row_places = places(own, flip, 0)
    for c in range(SEC // chunk):
        rows = slice(c * chunk, (c + 1) * chunk)
        if first:
            peak = jnp.full((chunk, 1), NEG, F32)
            total = jnp.zeros((chunk, 1), F32)
            acc = jnp.zeros((chunk, 128), F32)
        else:
            peak, total, acc = peak_in[rows, 0:1], peak_in[rows, 1:2], acc_in[rows]
        for r, offset in enumerate(offsets):
            at = slice(r * SEC, (r + 1) * SEC)
            s = scores_of(own, flip, chunk, c, offset, at, row_places, q_s, qn_s, kp_s)
            new_peak = jnp.maximum(peak, jnp.max(s, axis=1, keepdims=True))
            keep = jnp.exp(peak - new_peak)
            e = jnp.exp(s - new_peak)
            total = keep * total + jnp.sum(e, axis=1, keepdims=True)
            acc = keep * acc + dot(e.astype(BF), kv_s[at, :])
            peak = new_peak
        lanes = lax.broadcasted_iota(jnp.int32, (chunk, 128), 1)
        if not last:
            acc_out[rows] = acc
            peak_out[rows] = jnp.where(lanes == 0, peak, total)
            continue
        att = (acc / total).astype(BF)
        att_out[rows] = att
        log_total = peak + jnp.log(total)
        cot = c_s[rows].astype(F32)
        delta = jnp.sum(att.astype(F32) * cot, axis=1, keepdims=True)
        column = jnp.where(lanes == 0, log_total, delta)
        column_out[rows] = column
        turned = column.T
        for k in range(chunk // 128):
            at = c * (chunk // 128) + k
            stats[at : at + 1] = turned[0:1, k * 128 : (k + 1) * 128]
            stats[4 + at : 5 + at] = turned[1:2, k * 128 : (k + 1) * 128]


def queries_kernel(chunk, place, *refs):
    pieces, rest = refs[: 2 * NSEC], refs[2 * NSEC :]
    key_feat, row_feat, att, column, packed, packed_other, *scratch = rest
    kv_s, kp_s, q_s, qn_s, c_s = scratch[:5]
    flip, own = place[0], place[1]
    bring_both(own, OFFSETS, pieces, pieces[0], pieces[1], key_feat, row_feat, scratch)
    row_places = places(own, flip, 0)
    for c in range(SEC // chunk):
        rows = slice(c * chunk, (c + 1) * chunk)
        log_total, delta, cot = column[rows, 0:1], column[rows, 1:2], c_s[rows]

        def backward(offset, at, acc, c=c, log_total=log_total, delta=delta, cot=cot):
            s = scores_of(own, flip, chunk, c, offset, at, row_places, q_s, qn_s, kp_s)
            p = jnp.exp(s - log_total)
            kv = kv_s[at, :]
            ds = p * (dot(cot, kv, NT) - delta)
            return acc + dot(ds.astype(BF), kv)

        grad = jnp.zeros((chunk, 128), F32)
        for r in range(3):
            grad = backward(OFFSETS[r], slice(r * SEC, (r + 1) * SEC), grad)
        grad = lax.fori_loop(
            3,
            NSEC,
            lambda r, acc, backward=backward: backward(
                None, pl.ds(pl.multiple_of(r * SEC, SEC), SEC), acc
            ),
            grad,
        )
        grad = (grad * (1.0 / math.sqrt(HD))).astype(BF)
        joined = jnp.where(low_lanes(chunk), grad, att[rows])
        out = packed if c * chunk < RUN else packed_other
        at = (c * chunk) % RUN
        out[at : at + chunk] = joined


def keys_kernel(chunk, place, *refs):
    pieces, rest = refs[: 2 * NSEC], refs[2 * NSEC :]
    key_feat, row_feat, stats, packed, packed_other, *scratch = rest
    qc_s, q_s, k_s, kn_s, v_s, sems, own_sems, stats_s, stats_sems = scratch
    flip, own = place[0], place[1]
    copies = bring(own, OFFSETS, pieces, 1, row_feat, qc_s, q_s, sems)
    copies += bring(own, (0,), pieces[:2], 0, key_feat, v_s, k_s, own_sems)
    for r, offset in enumerate(OFFSETS):
        at = pl.multiple_of(section_at(own, offset) * 8, 8)
        to = stats_s.at[pl.ds(r * 8, 8)]
        copies.append(pltpu.make_async_copy(stats.at[pl.ds(at, 8)], to, stats_sems.at[r]))
        copies[-1].start()
    for copy in copies:
        copy.wait()
    join_queries(NSEC, qc_s, q_s)
    join_keys(1, v_s, k_s)
    upper_only(v_s, k_s, kn_s)
    key_places = places(own, flip, 0)
    for c in range(SEC // chunk):
        rows = slice(c * chunk, (c + 1) * chunk)
        k, kn, v = k_s[rows], kn_s[rows], v_s[rows]

        def backward(near, r, at, state):
            key_acc, value_acc = state
            st = stats_s[pl.ds(pl.multiple_of(r * 8, 8), 8), :]
            log_total = jnp.concatenate([st[i : i + 1] for i in range(4)], axis=1)
            delta = jnp.concatenate([st[i : i + 1] for i in range(4, 8)], axis=1)
            qc = qc_s[at, :]
            s = dot(k, q_s[at, :], NT)
            if near:
                section = section_at(own, OFFSETS[r])
                away = key_places[rows] - places(section, flip, 1)
                s = jnp.where(jnp.abs(away) <= HALF, dot(kn, q_s[at, :], NT), s)
            p = jnp.exp(s - log_total)
            ds = p * (dot(v, qc, NT) - delta)
            key_acc = key_acc + dot(ds.astype(BF), qc)
            value_acc = value_acc + dot(p.astype(BF), qc)
            return key_acc, value_acc

        state = (jnp.zeros((chunk, 128), F32), jnp.zeros((chunk, 128), F32))
        for r in range(3):
            state = backward(True, r, slice(r * SEC, (r + 1) * SEC), state)

        def far(r, st, backward=backward):
            return backward(False, r, pl.ds(pl.multiple_of(r * SEC, SEC), SEC), st)

        key_acc, value_acc = lax.fori_loop(3, NSEC, far, state)
        joined = jnp.where(low_lanes(chunk), key_acc * (1.0 / math.sqrt(HD)), value_acc)
        out = packed if c * chunk < RUN else packed_other
        at = (c * chunk) % RUN
        out[at : at + chunk] = joined.astype(BF)


def weights_kernel(tok, tok_other, first, first_sent, second, second_sent, out):
    qa = dot(tok[...], first[...], TN) + dot(tok_other[...], first_sent[...], TN)
    kv = dot(tok[...], second[...], TN) + dot(tok_other[...], second_sent[...], TN)
    for p in range(16):
        out[p, :64] = kv[p * 64 : (p + 1) * 64].astype(BF)
        upper = qa[p * 32 : (p + 1) * 32, :HD]
        lower = qa[512 + p * 32 : 512 + (p + 1) * 32, :HD]
        out[p, 64:96] = jnp.concatenate([upper, lower], axis=1).astype(BF)


def sum_kernel(parts, out):
    total = parts[0].astype(F32)
    for p in range(1, 16):
        total = total + parts[p].astype(F32)
    total = total.astype(BF)
    for p in range(32):
        out[p] = total


def input_kernel(place, first, first_other, second, second_other, wq, wk, wv, att, keep, send):
    swap = place[0] != 0
    core = place[2]
    a, b, c, d = first[...], first_other[...], second[...], second_other[...]
    a, b = jnp.where(swap, b, a), jnp.where(swap, a, b)
    c, d = jnp.where(swap, d, c), jnp.where(swap, c, d)
    dq = jnp.concatenate([a[:, :HD], b[:, :HD]], axis=1)
    att[...] = jnp.concatenate([a[:, HD:], b[:, HD:]], axis=1)
    dk = jnp.concatenate([c[:, :HD], d[:, :HD]], axis=1)
    dv = jnp.concatenate([c[:, HD:], d[:, HD:]], axis=1)
    grad = dot(dq, wq[...], NT) + dot(dk, wk[...], NT) + dot(dv, wv[...], NT)
    for y in range(4):
        low, high = grad[y * 64 : y * 64 + 32], grad[y * 64 + 32 : y * 64 + 64]
        keep[y] = jnp.where(core == 0, low, high)
        send[y] = jnp.where(core == 0, high, low).astype(BF)


def assemble_kernel(parts, gq, gk, gv):
    for p in range(16):
        a, b = parts[2 * p].astype(F32), parts[2 * p + 1].astype(F32)
        low = jnp.concatenate([a[:, :HD], b[:, :HD]], axis=1)
        high = jnp.concatenate([a[:, HD:], b[:, HD:]], axis=1)
        gk[p * 64 : (p + 1) * 64] = low[:64]
        gv[p * 64 : (p + 1) * 64] = high[:64]
        gq[p * 32 : (p + 1) * 32] = low[64:]
        gq[512 + p * 32 : 512 + (p + 1) * 32] = high[64:]


def shift(a, step):
    return lax.ppermute(a, Z, [(i, (i + step) % NSEC) for i in range(NSEC)])


def swap(a):
    return lax.ppermute(a, "xh", [(0, 1), (1, 0)])


def on_device(tokens, wq, wk, wv, cotangent, doc_lengths, global_positions):
    shape = jax.ShapeDtypeStruct
    tok, cot = tokens[0], cotangent[0]
    xh, z, y, core = (lax.axis_index(a) for a in ("xh", Z, "y", "core"))
    place = jnp.stack([xh, z, core]).astype(jnp.int32)
    weight = pltpu.VMEM((1024, 128), BF)
    mine, theirs = call(
        project_kernel,
        (shape((SEC, 128), BF),) * 2,
        (place, tok, wq, wk, wv, cot),
        scratch=(
            pltpu.VMEM((RUN, 1024), BF),
            weight,
            weight,
            weight,
            pltpu.VMEM((RUN, 128), BF),
            pltpu.SemaphoreType.DMA((5,)),
        ),
        flops=6 * 256 * 1024 * 128,
        manual=5,
    )
    other = swap(theirs)
    tok_other = swap(tok)
    part, own_sems = pltpu.VMEM((SEC, 128), BF), pltpu.SemaphoreType.DMA((3,))
    pairs = SEC * SEC
    wide = shape((SEC, 128), F32)

    def forward(lo, hi, place, pieces, state):
        n, last = hi - lo, hi == NSEC
        outs = (shape((SEC, 128), BF), wide, shape((8, 128), F32)) if last else (wide, wide)
        keys = pltpu.VMEM((n * SEC, 128), BF)
        return call(
            functools.partial(forward_kernel, 256, OFFSETS[lo:hi], lo == 0, last),
            outs,
            (place, mine, other, key_feat, row_feat, *pieces, *state),
            scratch=(keys, keys, part, part, part, pltpu.SemaphoreType.DMA((3 * n,)), own_sems),
            flops=2 * 128 * 2 * n * pairs,
            transcendentals=n * pairs,
            manual=4 + 2 * n,
        )

    tie = lax.optimization_barrier
    lower_a, upper_a = [mine, shift(mine, 1)], [mine, shift(mine, -1)]
    lower_b, upper_b = [other, shift(other, 1)], [other, shift(other, -1)]
    late, upper_a[1] = tie((place, upper_a[1]))
    key_feat, row_feat = call(
        feature_kernel,
        (shape((NSEC * SEC, 128), BF),) * 2,
        (late, doc_lengths, global_positions),
        smem=2,
    )
    lower_b[1], key_feat, row_feat = tie((lower_b[1], key_feat, row_feat))
    for x, step in ((lower_a, 1), (upper_a, -1), (lower_b, 1), (upper_b, -1)):
        x.append(shift(x[1], step))
    late, upper_a[2] = tie((place, upper_a[2]))
    state = forward(0, 1, late, (mine, other), ())
    lower_b[2], *state = tie((lower_b[2], *state))
    for x, step in ((lower_a, 1), (upper_a, -1), (lower_b, 1), (upper_b, -1)):
        x.append(shift(x[2], step))
    late, upper_a[3] = tie((place, upper_a[3]))
    near = (lower_a[1], lower_b[1], upper_a[1], upper_b[1])
    state = forward(1, 3, late, near, state)
    upper_b[3], *state = tie((upper_b[3], *state))
    far = (shift(lower_a[3], 1), shift(upper_b[3], -1))
    near2 = (lower_a[2], lower_b[2], upper_a[2], upper_b[2])
    state = forward(3, 5, place, near2, state)
    rest = (lower_a[3], lower_b[3], upper_a[3], upper_b[3]) + far
    pieces = (mine, other) + near + near2 + rest
    att_rows, column, stats = forward(5, 8, place, rest, state)
    all_stats = lax.all_to_all(
        jnp.broadcast_to(stats[None], (NSEC, 8, 128)), Z, 0, 0, tiled=True
    ).reshape(NSEC * 8, 128)
    whole = pltpu.VMEM((NSEC * SEC, 128), BF)
    half = shape((RUN, 128), BF)
    first, first_sent = call(
        functools.partial(queries_kernel, 256),
        (half, half),
        (place, *pieces, key_feat, row_feat, att_rows, column),
        scratch=(whole, whole, part, part, part, pltpu.SemaphoreType.DMA((24,)), own_sems),
        flops=2 * 128 * 3 * NSEC * pairs,
        manual=18,
        transcendentals=NSEC * pairs,
    )
    all_stats, first, first_sent = lax.optimization_barrier((all_stats, first, first_sent))
    first_other = swap(first_sent)
    stats_scratch = (pltpu.VMEM((NSEC * 8, 128), F32), pltpu.SemaphoreType.DMA((NSEC,)))
    second, second_sent = call(
        functools.partial(keys_kernel, 256),
        (half, half),
        (place, *pieces, key_feat, row_feat, all_stats),
        scratch=(whole, whole, part, part, part, pltpu.SemaphoreType.DMA((24,)), own_sems) + stats_scratch,
        flops=2 * 128 * 4 * NSEC * pairs,
        manual=19,
        transcendentals=NSEC * pairs,
    )
    second, second_sent, first_other = lax.optimization_barrier((second, second_sent, first_other))
    second_other = swap(second_sent)
    partial = call(
        weights_kernel,
        shape((16, 96, 128), BF),
        (tok, tok_other, first, first_sent, second, second_sent),
        flops=2 * 512 * 1024 * 256,
        smem=0,
    )
    partial = lax.all_to_all(partial, ("b",) + Z, 0, 0, tiled=True)
    att, keep, send = call(
        input_kernel,
        (half, shape((4, 32, 1024), F32), shape((4, 32, 1024), BF)),
        (place, first, first_other, second, second_other, wq, wk, wv),
        flops=6 * 256 * 1024 * 128,
    )
    arrived = lax.ppermute(send, "core", [(0, 1), (1, 0)])
    partial, arrived = lax.optimization_barrier((partial, arrived))
    total = call(sum_kernel, shape((32, 96, 128), BF), (partial,), smem=0)
    both = keep + arrived.astype(F32)
    share = lax.dynamic_index_in_dim(both, y, 0, False)
    both_bf = both.astype(BF)
    for k in (1, 2, 3):
        out = lax.dynamic_index_in_dim(both_bf, lax.bitwise_xor(y, k), 0, False)
        share = share + lax.ppermute(out, "y", [(i, i ^ k) for i in range(4)]).astype(F32)
    total = lax.all_to_all(total, ("b",) + CTX, 0, 0, tiled=True)
    gq, gk, gv = call(assemble_kernel, (shape((1024, 128), F32),) * 3, (total,), smem=0)
    return att[None], share.astype(BF)[None], gq, gk, gv


def solution(mesh):
    devices = mesh.devices.reshape(2, 2, 2, 2, 2, 4, 2)
    fine = Mesh(devices, ("b",) + CTX + TP)
    in_specs = (
        P("b", CTX, None),
        P(None, TP),
        P(None, TP),
        P(None, TP),
        P("b", CTX, TP),
        P("b", None),
        P("b", None),
    )
    out_specs = (
        P("b", CTX, TP),
        P("b", CTX + TP, None),
        P(None, TP),
        P(None, TP),
        P(None, TP),
    )
    return jax.shard_map(
        on_device, mesh=fine, in_specs=in_specs, out_specs=out_specs, check_vma=False
    )
```

time: 141 us -> 152 us (1.078); the launches traced: 138 us -> 151 us
  Pallas kernels: 34.6 us -> 59.8 us
  blocking collectives: 12.9 us -> 0 us
  local copies, waits for them, and re-layouts: 13.8 us -> 1.34 us
  starting transfers between devices: 51.5 us -> 63.4 us
    pallas_call x8 -> x12, Pallas kernels: 34.6 us -> 59.8 us  [call(): pl.pallas_call(kernel, out_shape=outs, in_specs=specs, out_specs=jax.tree...]
    all_to_all x1, waiting for transfers between devices: 0.01 us -> 14.2 us  [on_device(): total = lax.all_to_all(total, ('b',) + CTX, 0, 0, tiled=True)]
    all_to_all x1 -> x0, blocking collectives: 12.9 us -> none  [on_device(): partial = lax.all_to_all(partial, ('b',) + Z, 0, 0, tiled=True)]
    all_to_all x0 -> x1, starting transfers between devices: none -> 8.3 us  [on_device(): partial = lax.all_to_all(partial, ('b',) + Z, 0, 0, tiled=True)]
    unnamed x36 -> x4, local copies, waits for them, and re-layouts: 8.23 us -> 0.01 us
    all_to_all x1, waiting for transfers between devices: 8.01 us -> 0.01 us  [on_device(): lax.all_to_all(jnp.broadcast_to(stats[None], (NSEC, 8, 128)), Z, 0, 0, ti...]
    all_to_all x1, starting transfers between devices: 5.06 us -> 10.9 us  [on_device(): total = lax.all_to_all(total, ('b',) + CTX, 0, 0, tiled=True)]
    ppermute x4, waiting for transfers between devices: 6.57 us -> 3.17 us  [swap(): return lax.ppermute(a, 'xh', [(0, 1), (1, 0)])]
  transfers between devices with their start and end apart: 26 -> 25, of which waited for: 9 -> 7; matrix products, arithmetic and copies ran while one was open for 6% -> 2% of each run, Pallas kernels for 21% -> 32%
where the time goes in v2:
time: 152 us; the launch traced here: 151 us
  starting transfers between devices  63.4 us (42%)
  Pallas kernels  59.8 us (39%)
  waiting for transfers between devices  23.4 us (15%)
  other arithmetic  2.35 us (2%)
    pallas_call x12, Pallas kernels, call(): pl.pallas_call(kernel, out_shape=outs, in_specs=specs, out_specs=jax.tree...  59.8 us
    ppermute x14, starting transfers between devices, shift(): return lax.ppermute(a, Z, [(i, (i + step) % NSEC) for i in range(NSEC)])  26.9 us
    all_to_all x1, waiting for transfers between devices, on_device(): total = lax.all_to_all(total, ('b',) + CTX, 0, 0, tiled=True)  14.2 us
    all_to_all x1, starting transfers between devices, on_device(): total = lax.all_to_all(total, ('b',) + CTX, 0, 0, tiled=True)  10.9 us
    ppermute x4, starting transfers between devices, swap(): return lax.ppermute(a, 'xh', [(0, 1), (1, 0)])  9.76 us
    all_to_all x1, starting transfers between devices, on_device(): partial = lax.all_to_all(partial, ('b',) + Z, 0, 0, tiled=True)  8.3 us
    all_to_all x1, starting transfers between devices, on_device(): lax.all_to_all(jnp.broadcast_to(stats[None], (NSEC, 8, 128)), Z, 0, 0, ti...  3.96 us
    ppermute x3, waiting for transfers between devices, on_device(): lax.ppermute(out, 'y', [(i, i ^ k) for i in range(4)]).astype(F32)  3.81 us
  transfers between devices with their start and end apart: 25, of which 7 were waited for; matrix products, arithmetic and copies ran while one was open for 2% of the time, Pallas kernels for 32%

profile of v2, /device:TPU:8, one launch (start us, length us, event | category | flops | bytes accessed | tf_op | source)
XLA Modules:
  0.0 151.2 jit_solution(13074629175112762276)
XLA Ops:
  0.6 0.7 pad_add_fusion.place
  1.3 3.5 %shard_map.110 = (bf16[512,128]{1,0:T(8,128)(2,1)}, bf16[512,128]{1,0:T(8,128)(2,1)}) custom-call(s32[3]{0:T(128)} %pad_add_fusion.place, bf16[256,1024]{1,0:T(8,128)(2,1)} %bitcast.25, bf16[1024,128]{1,0:T(8,128)(2,1)} %wq.3, bf16[1024,128]{1,0:T(8,128)(2,1)} %wk.3, bf16[1024,128]{1,0:T(8,128)(2,1)} %wv.3, bf16[256,128]{1,0:T(8,128)(2,1)} %bitcast.28), custom_call_target="tpu_custom_call" | custom-call | flops 201326592 | bytes 1376268 | tf_op jit(solution)/shard_map/pallas_call | solution.py:42
  4.9 3.1 %collective-permute-start = (bf16[512,128]{1,0:T(8,128)(2,1)}, bf16[512,128]{1,0:T(8,128)(2,1)}, u32[]{:S(2)}, u32[]{:S(2)}) collective-permute-start(bf16[512,128]{1,0:T(8,128)(2,1)} %get-tuple-element.52), channel_id=1, source_target_pairs={{0,8},{8,0},{1,9},{9,1},{2,10},{10,2},{3,11},{11,3},{4,12},{12,4},... | collective-permute-start | bytes 393224 | tf_op jit(solution)/shard_map/ppermute | solution.py:383
  8.0 5.9 %collective-permute-start.2 = (bf16[512,128]{1,0:T(8,128)(2,1)}, bf16[512,128]{1,0:T(8,128)(2,1)}, u32[]{:S(2)}, u32[]{:S(2)}) collective-permute-start(bf16[512,128]{1,0:T(8,128)(2,1)} %get-tuple-element.51.mine.refs_0_), channel_id=1, source_target_pairs={{0,112},{16,0},{32,16},{48,32},{64,48},{80,64},{96,80},{112,96},{1... | collective-permute-start | bytes 393224 | tf_op jit(solution)/shard_map/ppermute | solution.py:379
  13.8 4.0 %collective-permute-start.10 = (bf16[512,128]{1,0:T(8,128)(2,1)}, bf16[512,128]{1,0:T(8,128)(2,1)}, u32[]{:S(2)}, u32[]{:S(2)}) collective-permute-start(bf16[512,128]{1,0:T(8,128)(2,1)} %collective-permute-done.other.refs_1_), channel_id=1, source_target_pairs={{0,112},{16,0},{32,16},{48,32},{64,48},{80,64},{96,80},{112,96},{1... | collective-permute-start | bytes 393224 | tf_op jit(solution)/shard_map/ppermute | solution.py:379
  17.9 3.2 %collective-permute-start.7 = (bf16[512,128]{1,0:T(8,128)(2,1)}, bf16[512,128]{1,0:T(8,128)(2,1)}, u32[]{:S(2)}, u32[]{:S(2)}) collective-permute-start(bf16[512,128]{1,0:T(8,128)(2,1)} %collective-permute-done.2.refs_2_.refs_4_), channel_id=1, source_target_pairs={{0,112},{16,0},{32,16},{48,32},{64,48},{80,64},{96,80},{112,96},{1... | collective-permute-start | bytes 393224 | tf_op jit(solution)/shard_map/ppermute | solution.py:379
  21.1 0.0 collective-permute-done.3.refs_0_.refs_2_
  21.1 0.0 collective-permute-start.4
  21.1 0.3 collective-permute-done.10.refs_3_.refs_5_
  21.4 3.7 %collective-permute-start.11 = (bf16[512,128]{1,0:T(8,128)(2,1)}, bf16[512,128]{1,0:T(8,128)(2,1)}, u32[]{:S(2)}, u32[]{:S(2)}) collective-permute-start(bf16[512,128]{1,0:T(8,128)(2,1)} %collective-permute-done.10.refs_3_.refs_5_), channel_id=1, source_target_pairs={{0,112},{16,0},{32,16},{48,32},{64,48},{80,64},{96,80},{112,96},{1... | collective-permute-start | bytes 393224 | tf_op jit(solution)/shard_map/ppermute | solution.py:379
  25.1 4.3 %shard_map.111 = (bf16[4096,128]{1,0:T(8,128)(2,1)}, bf16[4096,128]{1,0:T(8,128)(2,1)}) custom-call(s32[3]{0:T(128)} %pad_add_fusion.place, s32[1,8]{1,0:T(1,128)} %lengths.1, s32[1,256]{1,0:T(1,128)} %spots.1), custom_call_target="tpu_custom_call" | custom-call | bytes 1068 | tf_op jit(solution)/shard_map/pallas_call | solution.py:42
  29.4 0.0 collective-permute-done.7.refs_2_.refs_8_
  29.4 3.2 %collective-permute-start.9 = (bf16[512,128]{1,0:T(8,128)(2,1)}, bf16[512,128]{1,0:T(8,128)(2,1)}, u32[]{:S(2)}, u32[]{:S(2)}) collective-permute-start(bf16[512,128]{1,0:T(8,128)(2,1)} %collective-permute-done.7.refs_2_.refs_8_), channel_id=1, source_target_pairs={{0,112},{16,0},{32,16},{48,32},{64,48},{80,64},{96,80},{112,96},{1... | collective-permute-start | bytes 393224 | tf_op jit(solution)/shard_map/ppermute | solution.py:379
  32.6 0.0 collective-permute-done.4.refs_0_.refs_6_
  32.6 0.0 collective-permute-start.5
  32.6 3.2 %collective-permute-start.12 = (bf16[512,128]{1,0:T(8,128)(2,1)}, bf16[512,128]{1,0:T(8,128)(2,1)}, u32[]{:S(2)}, u32[]{:S(2)}) collective-permute-start(bf16[512,128]{1,0:T(8,128)(2,1)} %collective-permute-done.11.refs_3_.refs_9_), channel_id=1, source_target_pairs={{0,112},{16,0},{32,16},{48,32},{64,48},{80,64},{96,80},{112,96},{1... | collective-permute-start | bytes 393224 | tf_op jit(solution)/shard_map/ppermute | solution.py:379
  35.9 3.0 %collective-permute-start.17 = (bf16[256,1024]{1,0:T(8,128)(2,1)}, bf16[256,1024]{1,0:T(8,128)(2,1)}, u32[]{:S(2)}, u32[]{:S(2)}) collective-permute-start(bf16[256,1024]{1,0:T(8,128)(2,1)} %bitcast.26), channel_id=1, source_target_pairs={{0,8},{8,0},{1,9},{9,1},{2,10},{10,2},{3,11},{11,3},{4,12},{12,4},... | collective-permute-start | bytes 1572872 | tf_op jit(solution)/shard_map/ppermute | solution.py:383
  38.9 3.5 %shard_map.112 = (f32[512,128]{1,0:T(8,128)}, f32[512,128]{1,0:T(8,128)}) custom-call(s32[3]{0:T(128)} %pad_add_fusion.place, bf16[512,128]{1,0:T(8,128)(2,1)} %get-tuple-element.51.mine.refs_0_, bf16[512,128]{1,0:T(8,128)(2,1)} %collective-permute-done.other.refs_1_, bf16[4096,128]{1,0:T(8,128)(2,1)} %get-tuple-element.56.key_feat.refs_16_, ...), custom_call_target="tpu_custom_call" | custom-call | flops 134217728 | bytes 2621452 | tf_op jit(solution)/shard_map/pallas_call | solution.py:42
  42.4 0.0 collective-permute-done.6.refs_1_.refs_7_
  42.5 0.3 collective-permute-start.8
  42.8 0.1 collective-permute-start.13
  42.8 5.3 %shard_map.113 = (f32[512,128]{1,0:T(8,128)}, f32[512,128]{1,0:T(8,128)}) custom-call(s32[3]{0:T(128)} %pad_add_fusion.place, bf16[512,128]{1,0:T(8,128)(2,1)} %get-tuple-element.51.mine.refs_0_, bf16[512,128]{1,0:T(8,128)(2,1)} %collective-permute-done.other.refs_1_, bf16[4096,128]{1,0:T(8,128)(2,1)} %get-tuple-element.56.key_feat.refs_16_, ...), custom_call_target="tpu_custom_call" | custom-call | flops 268435456 | bytes 3407884 | tf_op jit(solution)/shard_map/pallas_call | solution.py:42
  48.2 3.3 %collective-permute-start.14 = (bf16[512,128]{1,0:T(8,128)(2,1)}, bf16[512,128]{1,0:T(8,128)(2,1)}, u32[]{:S(2)}, u32[]{:S(2)}) collective-permute-start(bf16[512,128]{1,0:T(8,128)(2,1)} %collective-permute-done.12.refs_3_.refs_13_), channel_id=1, source_target_pairs={{0,112},{16,0},{32,16},{48,32},{64,48},{80,64},{96,80},{112,96},{1... | collective-permute-start | bytes 393224 | tf_op jit(solution)/shard_map/ppermute | solution.py:379
  51.5 4.8 %shard_map.114 = (f32[512,128]{1,0:T(8,128)}, f32[512,128]{1,0:T(8,128)}) custom-call(s32[3]{0:T(128)} %pad_add_fusion.place, bf16[512,128]{1,0:T(8,128)(2,1)} %get-tuple-element.51.mine.refs_0_, bf16[512,128]{1,0:T(8,128)(2,1)} %collective-permute-done.other.refs_1_, bf16[4096,128]{1,0:T(8,128)(2,1)} %get-tuple-element.56.key_feat.refs_16_, ...), custom_call_target="tpu_custom_call" | custom-call | flops 268435456 | bytes 3407884 | tf_op jit(solution)/shard_map/pallas_call | solution.py:42
  56.3 5.8 %shard_map.115 = (bf16[512,128]{1,0:T(8,128)(2,1)}, f32[512,128]{1,0:T(8,128)}, f32[8,128]{1,0:T(8,128)}) custom-call(s32[3]{0:T(128)} %pad_add_fusion.place, bf16[512,128]{1,0:T(8,128)(2,1)} %get-tuple-element.51.mine.refs_0_, bf16[512,128]{1,0:T(8,128)(2,1)} %collective-permute-done.other.refs_1_, bf16[4096,128]{1,0:T(8,128)(2,1)} %get-tuple-element.56.key_feat.refs_16_, ...), custom_call_target="tpu_custom_call" | custom-call | flops 402653184 | bytes 3670028 | tf_op jit(solution)/shard_map/pallas_call | solution.py:42
  62.1 1.3 broadcast_in_dim.12
  63.4 4.0 %all-to-all-start = ((f32[8,8,128]{2,1,0:T(8,128)}), f32[8,8,128]{2,1,0:T(8,128)}, u32[]{:S(2)}, u32[]{:S(2)}) async-start(f32[8,8,128]{2,1,0:T(8,128)} %broadcast_in_dim.12), calls=%async_computation | async-start | bytes 65536 | tf_op jit(solution)/shard_map/all_to_all | solution.py:455
  67.4 10.8 %shard_map.116 = (bf16[256,128]{1,0:T(8,128)(2,1)}, bf16[256,128]{1,0:T(8,128)(2,1)}) custom-call(s32[3]{0:T(128)} %pad_add_fusion.place, bf16[512,128]{1,0:T(8,128)(2,1)} %get-tuple-element.51.mine.refs_0_, bf16[512,128]{1,0:T(8,128)(2,1)} %collective-permute-done.other.refs_1_, bf16[512,128]{1,0:T(8,128)(2,1)} %collective-permute-done.3.refs_0_.refs_2_, ...), custom_call_target="tpu_custom_call" | custom-call | flops 1610612736 | bytes 4587532 | tf_op jit(solution)/shard_map/pallas_call | solution.py:42
  78.2 0.8 collective-permute-start.15
  79.0 11.7 %shard_map.117 = (bf16[256,128]{1,0:T(8,128)(2,1)}, bf16[256,128]{1,0:T(8,128)(2,1)}) custom-call(s32[3]{0:T(128)} %pad_add_fusion.place, bf16[512,128]{1,0:T(8,128)(2,1)} %get-tuple-element.51.mine.refs_0_, bf16[512,128]{1,0:T(8,128)(2,1)} %collective-permute-done.other.refs_1_, bf16[512,128]{1,0:T(8,128)(2,1)} %collective-permute-done.3.refs_0_.refs_2_, ...), custom_call_target="tpu_custom_call" | custom-call | flops 2147483648 | bytes 4227084 | tf_op jit(solution)/shard_map/pallas_call | solution.py:42
  90.7 2.8 %shard_map.119 = bf16[16,96,128]{2,1,0:T(8,128)(2,1)} custom-call(bf16[256,1024]{1,0:T(8,128)(2,1)} %bitcast.27, bf16[256,1024]{1,0:T(8,128)(2,1)} %collective-permute-done.17.tok_other, bf16[256,128]{1,0:T(8,128)(2,1)} %get-tuple-element.81.first, bf16[256,128]{1,0:T(8,128)(2,1)} %get-tuple-element.85.first_sent, ...), custom_call_target="tpu_custom_call" | custom-call | flops 268435456 | bytes 1310720 | tf_op jit(solution)/shard_map/pallas_call | solution.py:42
  93.5 8.3 %all-to-all-start.1 = ((bf16[16,96,128]{2,1,0:T(8,128)(2,1)}), bf16[16,96,128]{2,1,0:T(8,128)(2,1)}, u32[]{:S(2)}, u32[]{:S(2)}) async-start(bf16[16,96,128]{2,1,0:T(8,128)(2,1)} %shard_map.119), calls=%async_computation.1 | async-start | bytes 786432 | tf_op jit(solution)/shard_map/all_to_all | solution.py:490
  101.8 2.8 %collective-permute-start.16 = (bf16[256,128]{1,0:T(8,128)(2,1)S(1)}, bf16[256,128]{1,0:T(8,128)(2,1)}, u32[]{:S(2)}, u32[]{:S(2)}) collective-permute-start(bf16[256,128]{1,0:T(8,128)(2,1)S(1)} %copy-done.1), channel_id=1, source_target_pairs={{0,8},{8,0},{1,9},{9,1},{2,10},{10,2},{3,11},{11,3},{4,12},{12,4},... | collective-permute-start | bytes 196616 | tf_op jit(solution)/shard_map/ppermute | solution.py:383
  104.6 3.2 %collective-permute-done.16.second_other = bf16[256,128]{1,0:T(8,128)(2,1)} collective-permute-done((bf16[256,128]{1,0:T(8,128)(2,1)S(1)}, bf16[256,128]{1,0:T(8,128)(2,1)}, u32[]{:S(2)}, u32[]{:S(2)}) %collective-permute-start.16) | collective-permute-done | bytes 65568 | tf_op jit(solution)/shard_map/ppermute | solution.py:383
  107.8 2.8 %shard_map.118 = (bf16[256,128]{1,0:T(8,128)(2,1)}, f32[4,32,1024]{2,1,0:T(8,128)}, bf16[4,32,1024]{2,1,0:T(8,128)(2,1)}) custom-call(s32[3]{0:T(128)} %pad_add_fusion.place, bf16[256,128]{1,0:T(8,128)(2,1)} %get-tuple-element.81.first, bf16[256,128]{1,0:T(8,128)(2,1)} %collective-permute-done.15.first_other, bf16[256,128]{1,0:T(8,128)(2,1)} %get-tuple-element.87.second, ...), custom_call_target="tpu_custom_call" | custom-call | flops 201326592 | bytes 1048588 | tf_op jit(solution)/shard_map/pallas_call | solution.py:42
  110.6 1.9 %collective-permute-done.18 = bf16[4,32,1024]{2,1,0:T(8,128)(2,1)} collective-permute-done((bf16[4,32,1024]{2,1,0:T(8,128)(2,1)}, bf16[4,32,1024]{2,1,0:T(8,128)(2,1)}, u32[]{:S(2)}, u32[]{:S(2)}) %collective-permute-start.18) | collective-permute-done | bytes 262176 | tf_op jit(solution)/shard_map/ppermute | solution.py:497
  112.4 2.0 %shard_map.120 = bf16[32,96,128]{2,1,0:T(8,128)(2,1)} custom-call(bf16[16,96,128]{2,1,0:T(8,128)(2,1)} %all-to-all-done.1.parts), custom_call_target="tpu_custom_call" | custom-call | bytes 393216 | tf_op jit(solution)/shard_map/pallas_call | solution.py:42
  114.4 10.9 %all-to-all-start.2 = ((bf16[32,96,128]{2,1,0:T(8,128)(2,1)}), bf16[32,96,128]{2,1,0:T(8,128)(2,1)}, u32[]{:S(2)}, u32[]{:S(2)}) async-start(bf16[32,96,128]{2,1,0:T(8,128)(2,1)} %shard_map.120), calls=%async_computation.2 | async-start | bytes 1572864 | tf_op jit(solution)/shard_map/all_to_all | solution.py:506
  125.3 1.0 fusion.4
  126.4 0.5 collective-permute-start.19
  126.9 2.6 %collective-permute-start.20 = (bf16[32,1024]{1,0:T(8,128)(2,1)S(1)}, bf16[32,1024]{1,0:T(8,128)(2,1)S(1)}, u32[]{:S(2)}, u32[]{:S(2)}) collective-permute-start(bf16[32,1024]{1,0:T(8,128)(2,1)S(1)} %get-tuple-element.101), channel_id=1, source_target_pairs={{0,4},{2,6},{4,0},{6,2},{1,5},{3,7},{5,1},{7,3},{8,12},{10,14},{12... | collective-permute-start | bytes 196616 | tf_op jit(solution)/shard_map/ppermute | solution.py:505
  129.5 0.5 collective-permute-start.21
  130.0 0.8 collective-permute-done.19
  130.8 2.1 %collective-permute-done.20 = bf16[32,1024]{1,0:T(8,128)(2,1)S(1)} collective-permute-done((bf16[32,1024]{1,0:T(8,128)(2,1)S(1)}, bf16[32,1024]{1,0:T(8,128)(2,1)S(1)}, u32[]{:S(2)}, u32[]{:S(2)}) %collective-permute-start.20) | collective-permute-done | bytes 65568 | tf_op jit(solution)/shard_map/ppermute | solution.py:505
  132.9 0.9 collective-permute-done.21
  133.8 0.7 fusion.3
  134.5 14.2 %all-to-all-done.2.parts = bf16[32,96,128]{2,1,0:T(8,128)(2,1)} async-done(((bf16[32,96,128]{2,1,0:T(8,128)(2,1)}), bf16[32,96,128]{2,1,0:T(8,128)(2,1)}, u32[]{:S(2)}, u32[]{:S(2)}) %all-to-all-start.2) | async-done | bytes 786464 | tf_op jit(solution)/shard_map/all_to_all | solution.py:506
  148.6 2.6 %shard_map.121 = (f32[1024,128]{1,0:T(8,128)}, f32[1024,128]{1,0:T(8,128)}, f32[1024,128]{1,0:T(8,128)}) custom-call(bf16[32,96,128]{2,1,0:T(8,128)(2,1)} %all-to-all-done.2.parts), custom_call_target="tpu_custom_call" | custom-call | bytes 786432 | tf_op jit(solution)/shard_map/pallas_call | solution.py:42
  (23 shorter events, 0.1 us)
Async XLA Ops:
  4.9 9.0 %collective-permute-start = (bf16[512,128]{1,0:T(8,128)(2,1)}, bf16[512,128]{1,0:T(8,128)(2,1)}, u32[]{:S(2)}, u32[]{:S(2)}) collective-permute-start(bf16[512,128]{1,0:T(8,128)(2,1)} %get-tuple-element.52), channel_id=1, source_target_pairs={{0,8},{8,0},{1,9},{9,1},{2,10},{10,2},{3,11},{11,3},{4,12},{12,4},... | collective-permute-start | bytes 393224 | tf_op jit(solution)/shard_map/ppermute | solution.py:383
  8.0 9.9 %collective-permute-start.2 = (bf16[512,128]{1,0:T(8,128)(2,1)}, bf16[512,128]{1,0:T(8,128)(2,1)}, u32[]{:S(2)}, u32[]{:S(2)}) collective-permute-start(bf16[512,128]{1,0:T(8,128)(2,1)} %get-tuple-element.51.mine.refs_0_), channel_id=1, source_target_pairs={{0,112},{16,0},{32,16},{48,32},{64,48},{80,64},{96,80},{112,96},{1... | collective-permute-start | bytes 393224 | tf_op jit(solution)/shard_map/ppermute | solution.py:379
  13.8 7.3 %collective-permute-start.3 = (bf16[512,128]{1,0:T(8,128)(2,1)}, bf16[512,128]{1,0:T(8,128)(2,1)}, u32[]{:S(2)}, u32[]{:S(2)}) collective-permute-start(bf16[512,128]{1,0:T(8,128)(2,1)} %get-tuple-element.51.mine.refs_0_), channel_id=1, source_target_pairs={{0,16},{16,32},{32,48},{48,64},{64,80},{80,96},{96,112},{112,0},{1... | collective-permute-start | bytes 393224 | tf_op jit(solution)/shard_map/ppermute | solution.py:379
  13.8 7.6 %collective-permute-start.10 = (bf16[512,128]{1,0:T(8,128)(2,1)}, bf16[512,128]{1,0:T(8,128)(2,1)}, u32[]{:S(2)}, u32[]{:S(2)}) collective-permute-start(bf16[512,128]{1,0:T(8,128)(2,1)} %collective-permute-done.other.refs_1_), channel_id=1, source_target_pairs={{0,112},{16,0},{32,16},{48,32},{64,48},{80,64},{96,80},{112,96},{1... | collective-permute-start | bytes 393224 | tf_op jit(solution)/shard_map/ppermute | solution.py:379
  17.9 11.5 %collective-permute-start.1 = (bf16[512,128]{1,0:T(8,128)(2,1)}, bf16[512,128]{1,0:T(8,128)(2,1)}, u32[]{:S(2)}, u32[]{:S(2)}) collective-permute-start(bf16[512,128]{1,0:T(8,128)(2,1)} %collective-permute-done.other.refs_1_), channel_id=1, source_target_pairs={{0,16},{16,32},{32,48},{48,64},{64,80},{80,96},{96,112},{112,0},{1... | collective-permute-start | bytes 393224 | tf_op jit(solution)/shard_map/ppermute | solution.py:379
  17.9 11.5 %collective-permute-start.7 = (bf16[512,128]{1,0:T(8,128)(2,1)}, bf16[512,128]{1,0:T(8,128)(2,1)}, u32[]{:S(2)}, u32[]{:S(2)}) collective-permute-start(bf16[512,128]{1,0:T(8,128)(2,1)} %collective-permute-done.2.refs_2_.refs_4_), channel_id=1, source_target_pairs={{0,112},{16,0},{32,16},{48,32},{64,48},{80,64},{96,80},{112,96},{1... | collective-permute-start | bytes 393224 | tf_op jit(solution)/shard_map/ppermute | solution.py:379
  21.1 11.5 %collective-permute-start.4 = (bf16[512,128]{1,0:T(8,128)(2,1)}, bf16[512,128]{1,0:T(8,128)(2,1)}, u32[]{:S(2)}, u32[]{:S(2)}) collective-permute-start(bf16[512,128]{1,0:T(8,128)(2,1)} %collective-permute-done.3.refs_0_.refs_2_), channel_id=1, source_target_pairs={{0,16},{16,32},{32,48},{48,64},{64,80},{80,96},{96,112},{112,0},{1... | collective-permute-start | bytes 393224 | tf_op jit(solution)/shard_map/ppermute | solution.py:379
  21.4 11.2 %collective-permute-start.11 = (bf16[512,128]{1,0:T(8,128)(2,1)}, bf16[512,128]{1,0:T(8,128)(2,1)}, u32[]{:S(2)}, u32[]{:S(2)}) collective-permute-start(bf16[512,128]{1,0:T(8,128)(2,1)} %collective-permute-done.10.refs_3_.refs_5_), channel_id=1, source_target_pairs={{0,112},{16,0},{32,16},{48,32},{64,48},{80,64},{96,80},{112,96},{1... | collective-permute-start | bytes 393224 | tf_op jit(solution)/shard_map/ppermute | solution.py:379
  29.4 13.1 %collective-permute-start.6 = (bf16[512,128]{1,0:T(8,128)(2,1)}, bf16[512,128]{1,0:T(8,128)(2,1)}, u32[]{:S(2)}, u32[]{:S(2)}) collective-permute-start(bf16[512,128]{1,0:T(8,128)(2,1)} %collective-permute-done.1.refs_1_.refs_3_), channel_id=1, source_target_pairs={{0,16},{16,32},{32,48},{48,64},{64,80},{80,96},{96,112},{112,0},{1... | collective-permute-start | bytes 393224 | tf_op jit(solution)/shard_map/ppermute | solution.py:379
  29.4 13.0 %collective-permute-start.9 = (bf16[512,128]{1,0:T(8,128)(2,1)}, bf16[512,128]{1,0:T(8,128)(2,1)}, u32[]{:S(2)}, u32[]{:S(2)}) collective-permute-start(bf16[512,128]{1,0:T(8,128)(2,1)} %collective-permute-done.7.refs_2_.refs_8_), channel_id=1, source_target_pairs={{0,112},{16,0},{32,16},{48,32},{64,48},{80,64},{96,80},{112,96},{1... | collective-permute-start | bytes 393224 | tf_op jit(solution)/shard_map/ppermute | solution.py:379
  32.6 10.1 %collective-permute-start.5 = (bf16[512,128]{1,0:T(8,128)(2,1)}, bf16[512,128]{1,0:T(8,128)(2,1)}, u32[]{:S(2)}, u32[]{:S(2)}) collective-permute-start(bf16[512,128]{1,0:T(8,128)(2,1)} %collective-permute-done.4.refs_0_.refs_6_), channel_id=1, source_target_pairs={{0,16},{16,32},{32,48},{48,64},{64,80},{80,96},{96,112},{112,0},{1... | collective-permute-start | bytes 393224 | tf_op jit(solution)/shard_map/ppermute | solution.py:379
  32.6 15.6 %collective-permute-start.12 = (bf16[512,128]{1,0:T(8,128)(2,1)}, bf16[512,128]{1,0:T(8,128)(2,1)}, u32[]{:S(2)}, u32[]{:S(2)}) collective-permute-start(bf16[512,128]{1,0:T(8,128)(2,1)} %collective-permute-done.11.refs_3_.refs_9_), channel_id=1, source_target_pairs={{0,112},{16,0},{32,16},{48,32},{64,48},{80,64},{96,80},{112,96},{1... | collective-permute-start | bytes 393224 | tf_op jit(solution)/shard_map/ppermute | solution.py:379
  35.9 54.8 %collective-permute-start.17 = (bf16[256,1024]{1,0:T(8,128)(2,1)}, bf16[256,1024]{1,0:T(8,128)(2,1)}, u32[]{:S(2)}, u32[]{:S(2)}) collective-permute-start(bf16[256,1024]{1,0:T(8,128)(2,1)} %bitcast.26), channel_id=1, source_target_pairs={{0,8},{8,0},{1,9},{9,1},{2,10},{10,2},{3,11},{11,3},{4,12},{12,4},... | collective-permute-start | bytes 1572872 | tf_op jit(solution)/shard_map/ppermute | solution.py:383
  42.5 13.8 %collective-permute-start.8 = (bf16[512,128]{1,0:T(8,128)(2,1)}, bf16[512,128]{1,0:T(8,128)(2,1)}, u32[]{:S(2)}, u32[]{:S(2)}) collective-permute-start(bf16[512,128]{1,0:T(8,128)(2,1)} %collective-permute-done.6.refs_1_.refs_7_), channel_id=1, source_target_pairs={{0,16},{16,32},{32,48},{48,64},{64,80},{80,96},{96,112},{112,0},{1... | collective-permute-start | bytes 393224 | tf_op jit(solution)/shard_map/ppermute | solution.py:379
  42.8 13.6 %collective-permute-start.13 = (bf16[512,128]{1,0:T(8,128)(2,1)}, bf16[512,128]{1,0:T(8,128)(2,1)}, u32[]{:S(2)}, u32[]{:S(2)}) collective-permute-start(bf16[512,128]{1,0:T(8,128)(2,1)} %collective-permute-done.5.refs_0_.refs_10_), channel_id=1, source_target_pairs={{0,16},{16,32},{32,48},{48,64},{64,80},{80,96},{96,112},{112,0},{1... | collective-permute-start | bytes 393224 | tf_op jit(solution)/shard_map/ppermute | solution.py:379
  48.2 8.1 %collective-permute-start.14 = (bf16[512,128]{1,0:T(8,128)(2,1)}, bf16[512,128]{1,0:T(8,128)(2,1)}, u32[]{:S(2)}, u32[]{:S(2)}) collective-permute-start(bf16[512,128]{1,0:T(8,128)(2,1)} %collective-permute-done.12.refs_3_.refs_13_), channel_id=1, source_target_pairs={{0,112},{16,0},{32,16},{48,32},{64,48},{80,64},{96,80},{112,96},{1... | collective-permute-start | bytes 393224 | tf_op jit(solution)/shard_map/ppermute | solution.py:379
  63.4 14.7 %all-to-all-start = ((f32[8,8,128]{2,1,0:T(8,128)}), f32[8,8,128]{2,1,0:T(8,128)}, u32[]{:S(2)}, u32[]{:S(2)}) async-start(f32[8,8,128]{2,1,0:T(8,128)} %broadcast_in_dim.12), calls=%async_computation | async-start | bytes 65536 | tf_op jit(solution)/shard_map/all_to_all | solution.py:455
  78.2 12.6 %collective-permute-start.15 = (bf16[256,128]{1,0:T(8,128)(2,1)}, bf16[256,128]{1,0:T(8,128)(2,1)}, u32[]{:S(2)}, u32[]{:S(2)}) collective-permute-start(bf16[256,128]{1,0:T(8,128)(2,1)} %get-tuple-element.85.first_sent), channel_id=1, source_target_pairs={{0,8},{8,0},{1,9},{9,1},{2,10},{10,2},{3,11},{11,3},{4,12},{12,4},... | collective-permute-start | bytes 196616 | tf_op jit(solution)/shard_map/ppermute | solution.py:383
  93.5 8.3 %copy-start.1 = (bf16[256,128]{1,0:T(8,128)(2,1)S(1)}, bf16[256,128]{1,0:T(8,128)(2,1)}, u32[]{:S(2)}) copy-start(bf16[256,128]{1,0:T(8,128)(2,1)} %get-tuple-element.88.second_sent) | copy-start | bytes 196612
  93.5 18.9 %all-to-all-start.1 = ((bf16[16,96,128]{2,1,0:T(8,128)(2,1)}), bf16[16,96,128]{2,1,0:T(8,128)(2,1)}, u32[]{:S(2)}, u32[]{:S(2)}) async-start(bf16[16,96,128]{2,1,0:T(8,128)(2,1)} %shard_map.119), calls=%async_computation.1 | async-start | bytes 786432 | tf_op jit(solution)/shard_map/all_to_all | solution.py:490
  101.8 6.0 %collective-permute-start.16 = (bf16[256,128]{1,0:T(8,128)(2,1)S(1)}, bf16[256,128]{1,0:T(8,128)(2,1)}, u32[]{:S(2)}, u32[]{:S(2)}) collective-permute-start(bf16[256,128]{1,0:T(8,128)(2,1)S(1)} %copy-done.1), channel_id=1, source_target_pairs={{0,8},{8,0},{1,9},{9,1},{2,10},{10,2},{3,11},{11,3},{4,12},{12,4},... | collective-permute-start | bytes 196616 | tf_op jit(solution)/shard_map/ppermute | solution.py:383
  110.6 1.9 %collective-permute-start.18 = (bf16[4,32,1024]{2,1,0:T(8,128)(2,1)}, bf16[4,32,1024]{2,1,0:T(8,128)(2,1)}, u32[]{:S(2)}, u32[]{:S(2)}) collective-permute-start(bf16[4,32,1024]{2,1,0:T(8,128)(2,1)} %get-tuple-element.91), channel_id=1, source_target_pairs={{0,1},{1,0},{2,3},{3,2},{4,5},{5,4},{6,7},{7,6},{8,9},{9,8},{10,11... | collective-permute-start | bytes 786440 | tf_op jit(solution)/shard_map/ppermute | solution.py:497
  114.4 10.9 %copy-start = (f32[4,32,1024]{2,1,0:T(8,128)S(1)}, f32[4,32,1024]{2,1,0:T(8,128)}, u32[]{:S(2)}) copy-start(f32[4,32,1024]{2,1,0:T(8,128)} %get-tuple-element.90) | copy-start | bytes 1572868
  114.4 34.2 %all-to-all-start.2 = ((bf16[32,96,128]{2,1,0:T(8,128)(2,1)}), bf16[32,96,128]{2,1,0:T(8,128)(2,1)}, u32[]{:S(2)}, u32[]{:S(2)}) async-start(bf16[32,96,128]{2,1,0:T(8,128)(2,1)} %shard_map.120), calls=%async_computation.2 | async-start | bytes 1572864 | tf_op jit(solution)/shard_map/all_to_all | solution.py:506
  126.4 4.4 %collective-permute-start.19 = (bf16[32,1024]{1,0:T(8,128)(2,1)S(1)}, bf16[32,1024]{1,0:T(8,128)(2,1)S(1)}, u32[]{:S(2)}, u32[]{:S(2)}) collective-permute-start(bf16[32,1024]{1,0:T(8,128)(2,1)S(1)} %get-tuple-element.99), channel_id=1, source_target_pairs={{0,2},{2,0},{4,6},{6,4},{1,3},{3,1},{5,7},{7,5},{8,10},{10,8},{12,... | collective-permute-start | bytes 196616 | tf_op jit(solution)/shard_map/ppermute | solution.py:505
  126.9 5.9 %collective-permute-start.20 = (bf16[32,1024]{1,0:T(8,128)(2,1)S(1)}, bf16[32,1024]{1,0:T(8,128)(2,1)S(1)}, u32[]{:S(2)}, u32[]{:S(2)}) collective-permute-start(bf16[32,1024]{1,0:T(8,128)(2,1)S(1)} %get-tuple-element.101), channel_id=1, source_target_pairs={{0,4},{2,6},{4,0},{6,2},{1,5},{3,7},{5,1},{7,3},{8,12},{10,14},{12... | collective-permute-start | bytes 196616 | tf_op jit(solution)/shard_map/ppermute | solution.py:505
  129.5 4.3 %collective-permute-start.21 = (bf16[32,1024]{1,0:T(8,128)(2,1)S(1)}, bf16[32,1024]{1,0:T(8,128)(2,1)S(1)}, u32[]{:S(2)}, u32[]{:S(2)}) collective-permute-start(bf16[32,1024]{1,0:T(8,128)(2,1)S(1)} %get-tuple-element.100), channel_id=1, source_target_pairs={{0,6},{2,4},{4,2},{6,0},{1,7},{3,5},{5,3},{7,1},{8,14},{10,12},{12... | collective-permute-start | bytes 196616 | tf_op jit(solution)/shard_map/ppermute | solution.py:505

commit v3 on v2

--- a/solution.py
+++ b/solution.py
@@ -15,7 +15,8 @@
 SEC = 512
 NSEC = 8
 NEG = -1e30
-LIMIT = 64 << 20
+LIMIT = 51 << 20
+CALLS = ((0, 8),)
 BF = jnp.bfloat16
 F32 = jnp.float32
 
@@ -34,7 +35,7 @@
     return lax.dot_general(a, b, dims, preferred_element_type=F32)
 
 
-def call(kernel, outs, args, scratch=(), flops=0, transcendentals=0, smem=1, manual=0):
+def call(kernel, outs, args, scratch=(), flops=0, transcendentals=0, smem=1, manual=0, limit=None):
     specs = [pl.BlockSpec(memory_space=pltpu.SMEM)] * smem
     specs += [pl.BlockSpec(memory_space=pl.ANY)] * manual
     specs += [pl.BlockSpec(memory_space=pltpu.VMEM)] * (len(args) - smem - manual)
@@ -45,7 +46,7 @@
         in_specs=specs,
         out_specs=jax.tree.map(lambda _: pl.BlockSpec(memory_space=pltpu.VMEM), outs),
         scratch_shapes=list(scratch),
-        compiler_params=pltpu.CompilerParams(vmem_limit_bytes=LIMIT),
+        compiler_params=pltpu.CompilerParams(vmem_limit_bytes=limit or LIMIT),
         cost_estimate=pl.CostEstimate(
             flops=flops, bytes_accessed=moved, transcendentals=transcendentals
         ),
@@ -56,11 +57,42 @@
     return lax.broadcasted_iota(jnp.int32, (rows, 128), 1) < HD
 
 
-def project_kernel(place, tok, wq, wk, wv, cot, mine, theirs, tok_v, wk_v, wv_v, wq_v, cot_v, sems):
+def document_features(place, lengths, spots, feat):
+    flip = place[0]
+    lane = lax.broadcasted_iota(jnp.int32, (RUN, 128), 1)
+    last = lane == HD + 8
+    lane_row = lax.broadcasted_iota(jnp.int32, (1, 128), 1)
+    starts, ends = jnp.zeros((1, 128), jnp.int32), jnp.zeros((1, 128), jnp.int32)
+    start = jnp.int32(0)
+    for d in range(8):
+        end = start + lengths[0, d]
+        starts = jnp.where(lane_row == HD + d, start, starts)
+        ends = jnp.where(lane_row == HD + d, end, ends)
+        start = end
+
+    def one(block, carry):
+        half = lax.rem(block, 2)
+        run = (block - half) + jnp.where(half == flip, 0, 1)
+        pos = run * RUN + lax.broadcasted_iota(jnp.int32, (RUN, RUN), 0)
+        hit = jnp.max(jnp.where(pos == spots[...], 1.0, 0.0), axis=1, keepdims=True)
+        other = 1.0 - hit
+        pos128 = run * RUN + lax.broadcasted_iota(jnp.int32, (RUN, 128), 0)
+        member = (pos128 >= starts) & (pos128 < ends)
+        row = jnp.where(last, other, jnp.where(member, 1.0, 0.0))
+        at = pl.ds(pl.multiple_of(block * RUN, RUN), RUN)
+        feat[at, :] = row.astype(BF)
+        return carry
+
+    lax.fori_loop(0, 2 * NSEC, one, 0)
+
+
+def project_kernel(place, lengths, tok, wq, wk, wv, cot, spots, mine, theirs, feat, *scratch):
+    tok_v, wk_v, wv_v, wq_v, cot_v, sems = scratch
     pairs = ((tok, tok_v), (wk, wk_v), (wv, wv_v), (wq, wq_v), (cot, cot_v))
     copies = [pltpu.make_async_copy(a, b, sems.at[i]) for i, (a, b) in enumerate(pairs)]
     for copy in copies:
         copy.start()
+    document_features(place, lengths, spots, feat)
     first = place[0] == 0
     copies[0].wait()
     t = tok_v[...]
@@ -92,38 +124,6 @@
         theirs[RUN:] = qc0
 
 
-def feature_kernel(place, lengths, spots, key_feat, row_feat):
-    flip = place[0]
-    lane = lax.broadcasted_iota(jnp.int32, (RUN, 128), 1)
-    inside = (lane >= HD) & (lane < HD + 8)
-    last = lane == HD + 8
-    lane_row = lax.broadcasted_iota(jnp.int32, (1, 128), 1)
-    starts, ends = jnp.zeros((1, 128), jnp.int32), jnp.zeros((1, 128), jnp.int32)
-    start = jnp.int32(0)
-    for d in range(8):
-        end = start + lengths[0, d]
-        starts = jnp.where(lane_row == HD + d, start, starts)
-        ends = jnp.where(lane_row == HD + d, end, ends)
-        start = end
-
-    def one(block, carry):
-        half = lax.rem(block, 2)
-        run = (block - half) + jnp.where(half == flip, 0, 1)
-        pos = run * RUN + lax.broadcasted_iota(jnp.int32, (RUN, RUN), 0)
-        hit = jnp.max(jnp.where(pos == spots[...], 1.0, 0.0), axis=1, keepdims=True)
-        other = 1.0 - hit
-        pos128 = run * RUN + lax.broadcasted_iota(jnp.int32, (RUN, 128), 0)
-        member = (pos128 >= starts) & (pos128 < ends)
-        row = jnp.where(last, other, jnp.where(member, 1.0, 0.0))
-        key = jnp.where(last, other, jnp.where(inside & jnp.logical_not(member), 1.0, 0.0))
-        at = pl.ds(pl.multiple_of(block * RUN, RUN), RUN)
-        row_feat[at, :] = row.astype(BF)
-        key_feat[at, :] = (key * NEG).astype(BF)
-        return carry
-
-    lax.fori_loop(0, 2 * NSEC, one, 0)
-
-
 def places(section, flip, along):
     shape = (1, SEC) if along == 1 else (SEC, 1)
     i = lax.broadcasted_iota(jnp.int32, shape, along)
@@ -150,10 +150,14 @@
 
 
 def join_keys(count, kv_s, kp_s):
-    low = low_lanes(SEC)
+    lane = lax.broadcasted_iota(jnp.int32, (SEC, 128), 1)
+    low, last = lane < HD, lane == HD + 8
+    base = jnp.where(lane < HD + 8, 1.0, 0.0).astype(BF)
+    sign = jnp.where(last, 1.0, jnp.where(lane < HD + 8, -1.0, 0.0)).astype(BF)
     for r in range(count):
         at = slice(r * SEC, (r + 1) * SEC)
-        kp_s[at] = jnp.where(low, kv_s[at], kp_s[at])
+        feat = (base + sign * kp_s[at]) * jnp.asarray(NEG, BF)
+        kp_s[at] = jnp.where(low, kv_s[at], feat)
 
 
 def join_queries(count, qc_s, q_s):
@@ -172,10 +176,10 @@
     near_s[...] = jnp.where(lane == HD + 8, jnp.zeros_like(joined), joined)
 
 
-def bring_both(own, offsets, pieces, mine, other, key_feat, row_feat, scratch):
+def bring_both(own, offsets, pieces, mine, other, feat, scratch):
     kv_s, kp_s, q_s, qn_s, c_s, sems, own_sems = scratch
-    copies = bring(own, offsets, pieces, 0, key_feat, kv_s, kp_s, sems)
-    copies += bring(own, (0,), (mine, other), 1, row_feat, c_s, q_s, own_sems)
+    copies = bring(own, offsets, pieces, 0, feat, kv_s, kp_s, sems)
+    copies += bring(own, (0,), (mine, other), 1, feat, c_s, q_s, own_sems)
     for copy in copies:
         copy.wait()
     join_keys(len(offsets), kv_s, kp_s)
@@ -192,7 +196,7 @@
     return s
 
 
-def forward_kernel(chunk, offsets, first, last, place, mine, other, key_feat, row_feat, *refs):
+def forward_kernel(chunk, offsets, first, last, place, mine, other, feat, *refs):
     pieces, rest = refs[: 2 * len(offsets)], list(refs[2 * len(offsets) :])
     acc_in, peak_in = (None, None) if first else (rest.pop(0), rest.pop(0))
     if last:
@@ -201,7 +205,7 @@
         acc_out, peak_out, *scratch = rest
     kv_s, kp_s, q_s, qn_s, c_s = scratch[:5]
     flip, own = place[0], place[1]
-    bring_both(own, offsets, pieces, mine, other, key_feat, row_feat, scratch)
+    bring_both(own, offsets, pieces, mine, other, feat, scratch)
     row_places = places(own, flip, 0)
     for c in range(SEC // chunk):
         rows = slice(c * chunk, (c + 1) * chunk)
@@ -241,10 +245,10 @@
 
 def queries_kernel(chunk, place, *refs):
     pieces, rest = refs[: 2 * NSEC], refs[2 * NSEC :]
-    key_feat, row_feat, att, column, packed, packed_other, *scratch = rest
+    feat, att, column, packed, packed_other, *scratch = rest
     kv_s, kp_s, q_s, qn_s, c_s = scratch[:5]
     flip, own = place[0], place[1]
-    bring_both(own, OFFSETS, pieces, pieces[0], pieces[1], key_feat, row_feat, scratch)
+    bring_both(own, OFFSETS, pieces, pieces[0], pieces[1], feat, scratch)
     row_places = places(own, flip, 0)
     for c in range(SEC // chunk):
         rows = slice(c * chunk, (c + 1) * chunk)
@@ -277,11 +281,11 @@
 
 def keys_kernel(chunk, place, *refs):
     pieces, rest = refs[: 2 * NSEC], refs[2 * NSEC :]
-    key_feat, row_feat, stats, packed, packed_other, *scratch = rest
+    feat, stats, packed, packed_other, *scratch = rest
     qc_s, q_s, k_s, kn_s, v_s, sems, own_sems, stats_s, stats_sems = scratch
     flip, own = place[0], place[1]
-    copies = bring(own, OFFSETS, pieces, 1, row_feat, qc_s, q_s, sems)
-    copies += bring(own, (0,), pieces[:2], 0, key_feat, v_s, k_s, own_sems)
+    copies = bring(own, OFFSETS, pieces, 1, feat, qc_s, q_s, sems)
+    copies += bring(own, (0,), pieces[:2], 0, feat, v_s, k_s, own_sems)
     for r, offset in enumerate(OFFSETS):
         at = pl.multiple_of(section_at(own, offset) * 8, 8)
         to = stats_s.at[pl.ds(r * 8, 8)]
@@ -389,10 +393,10 @@
     xh, z, y, core = (lax.axis_index(a) for a in ("xh", Z, "y", "core"))
     place = jnp.stack([xh, z, core]).astype(jnp.int32)
     weight = pltpu.VMEM((1024, 128), BF)
-    mine, theirs = call(
+    mine, theirs, feat = call(
         project_kernel,
-        (shape((SEC, 128), BF),) * 2,
-        (place, tok, wq, wk, wv, cot),
+        (shape((SEC, 128), BF),) * 2 + (shape((NSEC * SEC, 128), BF),),
+        (place, doc_lengths, tok, wq, wk, wv, cot, global_positions),
         scratch=(
             pltpu.VMEM((RUN, 1024), BF),
             weight,
@@ -402,7 +406,9 @@
             pltpu.SemaphoreType.DMA((5,)),
         ),
         flops=6 * 256 * 1024 * 128,
+        smem=2,
         manual=5,
+        limit=64 << 20,
     )
     other = swap(theirs)
     tok_other = swap(tok)
@@ -417,41 +423,29 @@
         return call(
             functools.partial(forward_kernel, 256, OFFSETS[lo:hi], lo == 0, last),
             outs,
-            (place, mine, other, key_feat, row_feat, *pieces, *state),
+            (place, mine, other, feat, *pieces, *state),
             scratch=(keys, keys, part, part, part, pltpu.SemaphoreType.DMA((3 * n,)), own_sems),
             flops=2 * 128 * 2 * n * pairs,
             transcendentals=n * pairs,
-            manual=4 + 2 * n,
+            manual=3 + 2 * n,
         )
 
     tie = lax.optimization_barrier
     lower_a, upper_a = [mine, shift(mine, 1)], [mine, shift(mine, -1)]
     lower_b, upper_b = [other, shift(other, 1)], [other, shift(other, -1)]
-    late, upper_a[1] = tie((place, upper_a[1]))
-    key_feat, row_feat = call(
-        feature_kernel,
-        (shape((NSEC * SEC, 128), BF),) * 2,
-        (late, doc_lengths, global_positions),
-        smem=2,
-    )
-    lower_b[1], key_feat, row_feat = tie((lower_b[1], key_feat, row_feat))
     for x, step in ((lower_a, 1), (upper_a, -1), (lower_b, 1), (upper_b, -1)):
         x.append(shift(x[1], step))
-    late, upper_a[2] = tie((place, upper_a[2]))
-    state = forward(0, 1, late, (mine, other), ())
-    lower_b[2], *state = tie((lower_b[2], *state))
     for x, step in ((lower_a, 1), (upper_a, -1), (lower_b, 1), (upper_b, -1)):
         x.append(shift(x[2], step))
-    late, upper_a[3] = tie((place, upper_a[3]))
-    near = (lower_a[1], lower_b[1], upper_a[1], upper_b[1])
-    state = forward(1, 3, late, near, state)
-    upper_b[3], *state = tie((upper_b[3], *state))
     far = (shift(lower_a[3], 1), shift(upper_b[3], -1))
-    near2 = (lower_a[2], lower_b[2], upper_a[2], upper_b[2])
-    state = forward(3, 5, place, near2, state)
-    rest = (lower_a[3], lower_b[3], upper_a[3], upper_b[3]) + far
-    pieces = (mine, other) + near + near2 + rest
-    att_rows, column, stats = forward(5, 8, place, rest, state)
+    pieces = (mine, other)
+    for i in (1, 2, 3):
+        pieces += (lower_a[i], lower_b[i], upper_a[i], upper_b[i])
+    pieces += far
+    state = ()
+    for lo, hi in CALLS:
+        state = forward(lo, hi, place, pieces[2 * lo : 2 * hi], state)
+    att_rows, column, stats = state
     all_stats = lax.all_to_all(
         jnp.broadcast_to(stats[None], (NSEC, 8, 128)), Z, 0, 0, tiled=True
     ).reshape(NSEC * 8, 128)
@@ -460,10 +454,10 @@
     first, first_sent = call(
         functools.partial(queries_kernel, 256),
         (half, half),
-        (place, *pieces, key_feat, row_feat, att_rows, column),
+        (place, *pieces, feat, att_rows, column),
         scratch=(whole, whole, part, part, part, pltpu.SemaphoreType.DMA((24,)), own_sems),
         flops=2 * 128 * 3 * NSEC * pairs,
-        manual=18,
+        manual=17,
         transcendentals=NSEC * pairs,
     )
     all_stats, first, first_sent = lax.optimization_barrier((all_stats, first, first_sent))
@@ -472,10 +466,10 @@
     second, second_sent = call(
         functools.partial(keys_kernel, 256),
         (half, half),
-        (place, *pieces, key_feat, row_feat, all_stats),
+        (place, *pieces, feat, all_stats),
         scratch=(whole, whole, part, part, part, pltpu.SemaphoreType.DMA((24,)), own_sems) + stats_scratch,
         flops=2 * 128 * 4 * NSEC * pairs,
-        manual=19,
+        manual=18,
         transcendentals=NSEC * pairs,
     )
     second, second_sent, first_other = lax.optimization_barrier((second, second_sent, first_other))
@@ -488,6 +482,8 @@
         smem=0,
     )
     partial = lax.all_to_all(partial, ("b",) + Z, 0, 0, tiled=True)
+    partial, second_other = tie((partial, second_other))
+    total = call(sum_kernel, shape((32, 96, 128), BF), (partial,), smem=0)
     att, keep, send = call(
         input_kernel,
         (half, shape((4, 32, 1024), F32), shape((4, 32, 1024), BF)),
@@ -495,8 +491,6 @@
         flops=6 * 256 * 1024 * 128,
     )
     arrived = lax.ppermute(send, "core", [(0, 1), (1, 0)])
-    partial, arrived = lax.optimization_barrier((partial, arrived))
-    total = call(sum_kernel, shape((32, 96, 128), BF), (partial,), smem=0)
     both = keep + arrived.astype(F32)
     share = lax.dynamic_index_in_dim(both, y, 0, False)
     both_bf = both.astype(BF)

time: 152 us -> 128 us (0.84)
  Pallas kernels: 59.8 us -> 42.5 us
  starting transfers between devices: 63.4 us -> 58.6 us
    pallas_call x12 -> x8, Pallas kernels: 59.8 us -> 42.5 us  [call(): pl.pallas_call(kernel, out_shape=outs, in_specs=specs, out_specs=jax.tree...]
    all_to_all x1, waiting for transfers between devices: 14.2 us -> 4.16 us  [on_device(): total = lax.all_to_all(total, ('b',) + CTX, 0, 0, tiled=True)]
    all_to_all x1, starting transfers between devices: 10.9 us -> 5.88 us  [on_device(): total = lax.all_to_all(total, ('b',) + CTX, 0, 0, tiled=True)]
    all_to_all x1, waiting for transfers between devices: 0.01 us -> 4.46 us  [on_device(): partial = lax.all_to_all(partial, ('b',) + Z, 0, 0, tiled=True)]
    ppermute x14, waiting for transfers between devices: 0.37 us -> 3.12 us  [shift(): return lax.ppermute(a, Z, [(i, (i + step) % NSEC) for i in range(NSEC)])]
    ppermute x4, waiting for transfers between devices: 3.17 us -> 5.77 us  [swap(): return lax.ppermute(a, 'xh', [(0, 1), (1, 0)])]
    ppermute x4, starting transfers between devices: 9.76 us -> 11.6 us  [swap(): return lax.ppermute(a, 'xh', [(0, 1), (1, 0)])]
  transfers between devices with their start and end apart: 25 -> 25, of which waited for: 7 -> 11; matrix products, arithmetic and copies ran while one was open for 2% -> 1% of each run, Pallas kernels for 32% -> 26%
where the time goes in v3:
time: 128 us
  starting transfers between devices  58.6 us (46%)
  Pallas kernels  42.5 us (33%)
  waiting for transfers between devices  23.1 us (18%)
  local copies, waits for them, and re-layouts  1.57 us (1%)
  other arithmetic  1.32 us (1%)
    pallas_call x8, Pallas kernels, call(): pl.pallas_call(kernel, out_shape=outs, in_specs=specs, out_specs=jax.tree...  42.5 us
    ppermute x14, starting transfers between devices, shift(): return lax.ppermute(a, Z, [(i, (i + step) % NSEC) for i in range(NSEC)])  25.8 us
    ppermute x4, starting transfers between devices, swap(): return lax.ppermute(a, 'xh', [(0, 1), (1, 0)])  11.6 us
    all_to_all x1, starting transfers between devices, on_device(): partial = lax.all_to_all(partial, ('b',) + Z, 0, 0, tiled=True)  7.32 us
    all_to_all x1, starting transfers between devices, on_device(): total = lax.all_to_all(total, ('b',) + CTX, 0, 0, tiled=True)  5.88 us
    ppermute x4, waiting for transfers between devices, swap(): return lax.ppermute(a, 'xh', [(0, 1), (1, 0)])  5.77 us
    all_to_all x1, waiting for transfers between devices, on_device(): partial = lax.all_to_all(partial, ('b',) + Z, 0, 0, tiled=True)  4.46 us
    all_to_all x1, starting transfers between devices, on_device(): lax.all_to_all(jnp.broadcast_to(stats[None], (NSEC, 8, 128)), Z, 0, 0, ti...  4.38 us
  transfers between devices with their start and end apart: 25, of which 11 were waited for; matrix products, arithmetic and copies ran while one was open for 1% of the time, Pallas kernels for 26%

profile of v3, /device:TPU:8, one launch (start us, length us, event | category | flops | bytes accessed | tf_op | source)
XLA Modules:
  0.0 127.9 jit_solution(5874378396699220278)
XLA Ops:
  0.6 0.6 pad_add_fusion.place
  1.2 4.8 %shard_map.110 = (bf16[512,128]{1,0:T(8,128)(2,1)}, bf16[512,128]{1,0:T(8,128)(2,1)}, bf16[4096,128]{1,0:T(8,128)(2,1)}) custom-call(s32[3]{0:T(128)} %pad_add_fusion.place, s32[1,8]{1,0:T(1,128)} %lengths.1, bf16[256,1024]{1,0:T(8,128)(2,1)} %bitcast.25, bf16[1024,128]{1,0:T(8,128)(2,1)} %wq.3, bf16[1024,128]{1,0:T(8,128)(2,1)} %wk.3, ...), custom_call_target="tpu_custom_call" | custom-call | flops 201326592 | bytes 1377324 | tf_op jit(solution)/shard_map/pallas_call | solution.py:43
  6.0 3.1 %collective-permute-start = (bf16[512,128]{1,0:T(8,128)(2,1)}, bf16[512,128]{1,0:T(8,128)(2,1)S(1)}, u32[]{:S(2)}, u32[]{:S(2)}) collective-permute-start(bf16[512,128]{1,0:T(8,128)(2,1)} %get-tuple-element.30), channel_id=1, source_target_pairs={{0,8},{8,0},{1,9},{9,1},{2,10},{10,2},{3,11},{11,3},{4,12},{12,4},... | collective-permute-start | bytes 393224 | tf_op jit(solution)/shard_map/ppermute | solution.py:387
  9.1 1.9 %collective-permute-start.1 = (bf16[512,128]{1,0:T(8,128)(2,1)}, bf16[512,128]{1,0:T(8,128)(2,1)S(1)}, u32[]{:S(2)}, u32[]{:S(2)}) collective-permute-start(bf16[512,128]{1,0:T(8,128)(2,1)} %get-tuple-element.29.mine.refs_0_), channel_id=1, source_target_pairs={{0,16},{16,32},{32,48},{48,64},{64,80},{80,96},{96,112},{112,0},{1... | collective-permute-start | bytes 393224 | tf_op jit(solution)/shard_map/ppermute | solution.py:383
  11.0 2.0 %collective-permute-done.other.refs_1_ = bf16[512,128]{1,0:T(8,128)(2,1)S(1)} collective-permute-done((bf16[512,128]{1,0:T(8,128)(2,1)}, bf16[512,128]{1,0:T(8,128)(2,1)S(1)}, u32[]{:S(2)}, u32[]{:S(2)}) %collective-permute-start) | collective-permute-done | bytes 131104 | tf_op jit(solution)/shard_map/ppermute | solution.py:387
  13.0 5.9 %collective-permute-start.4 = (bf16[512,128]{1,0:T(8,128)(2,1)S(1)}, bf16[512,128]{1,0:T(8,128)(2,1)S(1)}, u32[]{:S(2)}, u32[]{:S(2)}) collective-permute-start(bf16[512,128]{1,0:T(8,128)(2,1)S(1)} %collective-permute-done.other.refs_1_), channel_id=1, source_target_pairs={{0,112},{16,0},{32,16},{48,32},{64,48},{80,64},{96,80},{112,96},{1... | collective-permute-start | bytes 393224 | tf_op jit(solution)/shard_map/ppermute | solution.py:383
  18.9 1.0 collective-permute-start.3
  19.9 1.0 collective-permute-start.5
  20.9 0.0 collective-permute-start.2
  20.9 1.2 collective-permute-done.4.refs_5_
  22.2 3.7 %collective-permute-start.8 = (bf16[512,128]{1,0:T(8,128)(2,1)S(1)}, bf16[512,128]{1,0:T(8,128)(2,1)S(1)}, u32[]{:S(2)}, u32[]{:S(2)}) collective-permute-start(bf16[512,128]{1,0:T(8,128)(2,1)S(1)} %collective-permute-done.4.refs_5_), channel_id=1, source_target_pairs={{0,112},{16,0},{32,16},{48,32},{64,48},{80,64},{96,80},{112,96},{1... | collective-permute-start | bytes 393224 | tf_op jit(solution)/shard_map/ppermute | solution.py:383
  25.9 1.9 %collective-permute-start.7 = (bf16[512,128]{1,0:T(8,128)(2,1)S(1)}, bf16[512,128]{1,0:T(8,128)(2,1)S(1)}, u32[]{:S(2)}, u32[]{:S(2)}) collective-permute-start(bf16[512,128]{1,0:T(8,128)(2,1)S(1)} %collective-permute-done.3.refs_4_), channel_id=1, source_target_pairs={{0,112},{16,0},{32,16},{48,32},{64,48},{80,64},{96,80},{112,96},{1... | collective-permute-start | bytes 393224 | tf_op jit(solution)/shard_map/ppermute | solution.py:383
  27.8 0.1 collective-permute-start.9
  27.9 0.1 collective-permute-start.6
  28.0 0.4 collective-permute-done.8.refs_9_
  28.4 3.7 %collective-permute-start.12 = (bf16[512,128]{1,0:T(8,128)(2,1)S(1)}, bf16[512,128]{1,0:T(8,128)(2,1)S(1)}, u32[]{:S(2)}, u32[]{:S(2)}) collective-permute-start(bf16[512,128]{1,0:T(8,128)(2,1)S(1)} %collective-permute-done.8.refs_9_), channel_id=1, source_target_pairs={{0,112},{16,0},{32,16},{48,32},{64,48},{80,64},{96,80},{112,96},{1... | collective-permute-start | bytes 393224 | tf_op jit(solution)/shard_map/ppermute | solution.py:383
  32.0 3.3 %collective-permute-start.11 = (bf16[512,128]{1,0:T(8,128)(2,1)S(1)}, bf16[512,128]{1,0:T(8,128)(2,1)S(1)}, u32[]{:S(2)}, u32[]{:S(2)}) collective-permute-start(bf16[512,128]{1,0:T(8,128)(2,1)S(1)} %collective-permute-done.7.refs_8_), channel_id=1, source_target_pairs={{0,112},{16,0},{32,16},{48,32},{64,48},{80,64},{96,80},{112,96},{1... | collective-permute-start | bytes 393224 | tf_op jit(solution)/shard_map/ppermute | solution.py:383
  35.4 1.5 %collective-permute-done.6.refs_7_ = bf16[512,128]{1,0:T(8,128)(2,1)S(1)} collective-permute-done((bf16[512,128]{1,0:T(8,128)(2,1)S(1)}, bf16[512,128]{1,0:T(8,128)(2,1)S(1)}, u32[]{:S(2)}, u32[]{:S(2)}) %collective-permute-start.6) | collective-permute-done | bytes 131104 | tf_op jit(solution)/shard_map/ppermute | solution.py:383
  36.8 3.2 %collective-permute-start.14 = (bf16[512,128]{1,0:T(8,128)(2,1)S(1)}, bf16[512,128]{1,0:T(8,128)(2,1)S(1)}, u32[]{:S(2)}, u32[]{:S(2)}) collective-permute-start(bf16[512,128]{1,0:T(8,128)(2,1)S(1)} %collective-permute-done.12.refs_13_), channel_id=1, source_target_pairs={{0,112},{16,0},{32,16},{48,32},{64,48},{80,64},{96,80},{112,96},{1... | collective-permute-start | bytes 393224 | tf_op jit(solution)/shard_map/ppermute | solution.py:383
  40.1 3.0 %collective-permute-start.16 = (bf16[256,1024]{1,0:T(8,128)(2,1)}, bf16[256,1024]{1,0:T(8,128)(2,1)S(1)}, u32[]{:S(2)}, u32[]{:S(2)}) collective-permute-start(bf16[256,1024]{1,0:T(8,128)(2,1)} %bitcast.26), channel_id=1, source_target_pairs={{0,8},{8,0},{1,9},{9,1},{2,10},{10,2},{3,11},{11,3},{4,12},{12,4},... | collective-permute-start | bytes 1572872 | tf_op jit(solution)/shard_map/ppermute | solution.py:387
  43.1 0.0 copy-start.5
  43.2 0.9 copy-done.5
  44.1 9.4 %shard_map.111 = (bf16[512,128]{1,0:T(8,128)(2,1)S(1)}, f32[512,128]{1,0:T(8,128)S(1)}, f32[8,128]{1,0:T(8,128)S(1)}) custom-call(s32[3]{0:T(128)S(1)} %copy-done.4, bf16[512,128]{1,0:T(8,128)(2,1)S(1)} %copy-done.5, bf16[512,128]{1,0:T(8,128)(2,1)S(1)} %collective-permute-done.other.refs_1_, bf16[4096,128]{1,0:T(8,128)(2,1)} %get-tuple-element.31.feat.refs_16_, ...), custom_call_target="tpu_custom_call" | custom-call | flops 1073741824 | bytes 3407884 | tf_op jit(solution)/shard_map/pallas_call | solution.py:43
  53.4 0.6 broadcast_in_dim.12
  54.0 4.4 %all-to-all-start = ((f32[8,8,128]{2,1,0:T(8,128)}), f32[8,8,128]{2,1,0:T(8,128)S(1)}, u32[]{:S(2)}, u32[]{:S(2)}) async-start(f32[8,8,128]{2,1,0:T(8,128)} %broadcast_in_dim.12), calls=%async_computation | async-start | bytes 65536 | tf_op jit(solution)/shard_map/all_to_all | solution.py:449
  58.4 10.7 %shard_map.112 = (bf16[256,128]{1,0:T(8,128)(2,1)S(1)}, bf16[256,128]{1,0:T(8,128)(2,1)S(1)}) custom-call(s32[3]{0:T(128)S(1)} %copy-done.4, bf16[512,128]{1,0:T(8,128)(2,1)S(1)} %copy-done.6, bf16[512,128]{1,0:T(8,128)(2,1)S(1)} %collective-permute-done.other.refs_1_, bf16[512,128]{1,0:T(8,128)(2,1)S(1)} %collective-permute-done.1.refs_2_, ...), custom_call_target="tpu_custom_call" | custom-call | flops 1610612736 | bytes 3538956 | tf_op jit(solution)/shard_map/pallas_call | solution.py:43
  69.1 0.0 copy-start
  69.1 3.4 %collective-permute-start.15 = (bf16[256,128]{1,0:T(8,128)(2,1)S(1)}, bf16[256,128]{1,0:T(8,128)(2,1)S(1)}, u32[]{:S(2)}, u32[]{:S(2)}) collective-permute-start(bf16[256,128]{1,0:T(8,128)(2,1)S(1)} %get-tuple-element.41.first_sent), channel_id=1, source_target_pairs={{0,8},{8,0},{1,9},{9,1},{2,10},{10,2},{3,11},{11,3},{4,12},{12,4},... | collective-permute-start | bytes 196616 | tf_op jit(solution)/shard_map/ppermute | solution.py:387
  72.5 12.0 %shard_map.113 = (bf16[256,128]{1,0:T(8,128)(2,1)S(1)}, bf16[256,128]{1,0:T(8,128)(2,1)S(1)}) custom-call(s32[3]{0:T(128)S(1)} %copy-done.4, bf16[512,128]{1,0:T(8,128)(2,1)S(1)} %copy-done.6, bf16[512,128]{1,0:T(8,128)(2,1)S(1)} %collective-permute-done.other.refs_1_, bf16[512,128]{1,0:T(8,128)(2,1)S(1)} %collective-permute-done.1.refs_2_, ...), custom_call_target="tpu_custom_call" | custom-call | flops 2147483648 | bytes 3178508 | tf_op jit(solution)/shard_map/pallas_call | solution.py:43
  84.5 1.6 %shard_map.114 = bf16[16,96,128]{2,1,0:T(8,128)(2,1)} custom-call(bf16[256,1024]{1,0:T(8,128)(2,1)S(1)} %bitcast.27, bf16[256,1024]{1,0:T(8,128)(2,1)S(1)} %collective-permute-done.16.tok_other, bf16[256,128]{1,0:T(8,128)(2,1)S(1)} %get-tuple-element.37.first, bf16[256,128]{1,0:T(8,128)(2,1)S(1)} %get-tuple-element.41.first_sent, ...), custom_call_target="tpu_custom_call" | custom-call | flops 268435456 | bytes 1310720 | tf_op jit(solution)/shard_map/pallas_call | solution.py:43
  86.1 7.3 %all-to-all-start.1 = ((bf16[16,96,128]{2,1,0:T(8,128)(2,1)}), bf16[16,96,128]{2,1,0:T(8,128)(2,1)S(1)}, u32[]{:S(2)}, u32[]{:S(2)}) async-start(bf16[16,96,128]{2,1,0:T(8,128)(2,1)} %shard_map.114), calls=%async_computation.1 | async-start | bytes 786432 | tf_op jit(solution)/shard_map/all_to_all | solution.py:484
  93.4 2.1 %collective-permute-start.17 = (bf16[256,128]{1,0:T(8,128)(2,1)S(1)}, bf16[256,128]{1,0:T(8,128)(2,1)S(1)}, u32[]{:S(2)}, u32[]{:S(2)}) collective-permute-start(bf16[256,128]{1,0:T(8,128)(2,1)S(1)} %get-tuple-element.44.second_sent), channel_id=1, source_target_pairs={{0,8},{8,0},{1,9},{9,1},{2,10},{10,2},{3,11},{11,3},{4,12},{12,4},... | collective-permute-start | bytes 196616 | tf_op jit(solution)/shard_map/ppermute | solution.py:387
  95.5 3.8 %collective-permute-done.17.second_other = bf16[256,128]{1,0:T(8,128)(2,1)S(1)} collective-permute-done((bf16[256,128]{1,0:T(8,128)(2,1)S(1)}, bf16[256,128]{1,0:T(8,128)(2,1)S(1)}, u32[]{:S(2)}, u32[]{:S(2)}) %collective-permute-start.17) | collective-permute-done | bytes 65568 | tf_op jit(solution)/shard_map/ppermute | solution.py:387
  99.3 4.5 %all-to-all-done.1.parts = bf16[16,96,128]{2,1,0:T(8,128)(2,1)S(1)} async-done(((bf16[16,96,128]{2,1,0:T(8,128)(2,1)}), bf16[16,96,128]{2,1,0:T(8,128)(2,1)S(1)}, u32[]{:S(2)}, u32[]{:S(2)}) %all-to-all-start.1) | async-done | bytes 393248 | tf_op jit(solution)/shard_map/all_to_all | solution.py:484
  103.7 1.0 shard_map.116
  104.7 5.9 %all-to-all-start.2 = ((bf16[32,96,128]{2,1,0:T(8,128)(2,1)}), bf16[32,96,128]{2,1,0:T(8,128)(2,1)S(1)}, u32[]{:S(2)}, u32[]{:S(2)}) async-start(bf16[32,96,128]{2,1,0:T(8,128)(2,1)} %shard_map.116), calls=%async_computation.2 | async-start | bytes 1572864 | tf_op jit(solution)/shard_map/all_to_all | solution.py:500
  110.6 1.7 %shard_map.115 = (bf16[256,128]{1,0:T(8,128)(2,1)}, f32[4,32,1024]{2,1,0:T(8,128)S(1)}, bf16[4,32,1024]{2,1,0:T(8,128)(2,1)S(1)}) custom-call(s32[3]{0:T(128)S(1)} %copy-done.4, bf16[256,128]{1,0:T(8,128)(2,1)S(1)} %get-tuple-element.37.first, bf16[256,128]{1,0:T(8,128)(2,1)S(1)} %collective-permute-done.15.first_other, ...), custom_call_target="tpu_custom_call" | custom-call | flops 201326592 | bytes 1048588 | tf_op jit(solution)/shard_map/pallas_call | solution.py:43
  112.4 1.5 %collective-permute-done.18 = bf16[4,32,1024]{2,1,0:T(8,128)(2,1)S(1)} collective-permute-done((bf16[4,32,1024]{2,1,0:T(8,128)(2,1)S(1)}, bf16[4,32,1024]{2,1,0:T(8,128)(2,1)S(1)}, u32[]{:S(2)}, u32[]{:S(2)}) %collective-permute-start.18) | collective-permute-done | bytes 262176 | tf_op jit(solution)/shard_map/ppermute | solution.py:493
  113.9 0.1 fusion.4
  114.0 0.5 collective-permute-start.19
  114.5 2.6 %collective-permute-start.20 = (bf16[32,1024]{1,0:T(8,128)(2,1)S(1)}, bf16[32,1024]{1,0:T(8,128)(2,1)S(1)}, u32[]{:S(2)}, u32[]{:S(2)}) collective-permute-start(bf16[32,1024]{1,0:T(8,128)(2,1)S(1)} %get-tuple-element.57), channel_id=1, source_target_pairs={{0,4},{2,6},{4,0},{6,2},{1,5},{3,7},{5,1},{7,3},{8,12},{10,14},{12... | collective-permute-start | bytes 196616 | tf_op jit(solution)/shard_map/ppermute | solution.py:499
  117.1 0.4 collective-permute-start.21
  117.6 0.8 collective-permute-done.19
  118.4 2.4 %collective-permute-done.20 = bf16[32,1024]{1,0:T(8,128)(2,1)S(1)} collective-permute-done((bf16[32,1024]{1,0:T(8,128)(2,1)S(1)}, bf16[32,1024]{1,0:T(8,128)(2,1)S(1)}, u32[]{:S(2)}, u32[]{:S(2)}) %collective-permute-start.20) | collective-permute-done | bytes 65568 | tf_op jit(solution)/shard_map/ppermute | solution.py:499
  120.7 0.9 collective-permute-done.21
  121.7 0.7 fusion.3
  122.3 4.2 %all-to-all-done.2.parts = bf16[32,96,128]{2,1,0:T(8,128)(2,1)S(1)} async-done(((bf16[32,96,128]{2,1,0:T(8,128)(2,1)}), bf16[32,96,128]{2,1,0:T(8,128)(2,1)S(1)}, u32[]{:S(2)}, u32[]{:S(2)}) %all-to-all-start.2) | async-done | bytes 786464 | tf_op jit(solution)/shard_map/all_to_all | solution.py:500
  126.5 1.4 %shard_map.117 = (f32[1024,128]{1,0:T(8,128)}, f32[1024,128]{1,0:T(8,128)}, f32[1024,128]{1,0:T(8,128)}) custom-call(bf16[32,96,128]{2,1,0:T(8,128)(2,1)S(1)} %all-to-all-done.2.parts), custom_call_target="tpu_custom_call" | custom-call | bytes 786432 | tf_op jit(solution)/shard_map/pallas_call | solution.py:43
  (29 shorter events, 0.1 us)
Async XLA Ops:
  6.0 7.0 %collective-permute-start = (bf16[512,128]{1,0:T(8,128)(2,1)}, bf16[512,128]{1,0:T(8,128)(2,1)S(1)}, u32[]{:S(2)}, u32[]{:S(2)}) collective-permute-start(bf16[512,128]{1,0:T(8,128)(2,1)} %get-tuple-element.30), channel_id=1, source_target_pairs={{0,8},{8,0},{1,9},{9,1},{2,10},{10,2},{3,11},{11,3},{4,12},{12,4},... | collective-permute-start | bytes 393224 | tf_op jit(solution)/shard_map/ppermute | solution.py:387
  9.1 34.0 %copy-start.4 = (s32[3]{0:T(128)S(1)}, s32[3]{0:T(128)}, u32[]{:S(2)}) copy-start(s32[3]{0:T(128)} %pad_add_fusion.place) | copy-start | bytes 40
  9.1 10.8 %collective-permute-start.1 = (bf16[512,128]{1,0:T(8,128)(2,1)}, bf16[512,128]{1,0:T(8,128)(2,1)S(1)}, u32[]{:S(2)}, u32[]{:S(2)}) collective-permute-start(bf16[512,128]{1,0:T(8,128)(2,1)} %get-tuple-element.29.mine.refs_0_), channel_id=1, source_target_pairs={{0,16},{16,32},{32,48},{48,64},{64,80},{80,96},{96,112},{112,0},{1... | collective-permute-start | bytes 393224 | tf_op jit(solution)/shard_map/ppermute | solution.py:383
  13.0 9.1 %collective-permute-start.4 = (bf16[512,128]{1,0:T(8,128)(2,1)S(1)}, bf16[512,128]{1,0:T(8,128)(2,1)S(1)}, u32[]{:S(2)}, u32[]{:S(2)}) collective-permute-start(bf16[512,128]{1,0:T(8,128)(2,1)S(1)} %collective-permute-done.other.refs_1_), channel_id=1, source_target_pairs={{0,112},{16,0},{32,16},{48,32},{64,48},{80,64},{96,80},{112,96},{1... | collective-permute-start | bytes 393224 | tf_op jit(solution)/shard_map/ppermute | solution.py:383
  18.9 7.0 %collective-permute-start.3 = (bf16[512,128]{1,0:T(8,128)(2,1)}, bf16[512,128]{1,0:T(8,128)(2,1)S(1)}, u32[]{:S(2)}, u32[]{:S(2)}) collective-permute-start(bf16[512,128]{1,0:T(8,128)(2,1)} %get-tuple-element.29.mine.refs_0_), channel_id=1, source_target_pairs={{0,112},{16,0},{32,16},{48,32},{64,48},{80,64},{96,80},{112,96},{1... | collective-permute-start | bytes 393224 | tf_op jit(solution)/shard_map/ppermute | solution.py:383
  19.9 7.9 %collective-permute-start.5 = (bf16[512,128]{1,0:T(8,128)(2,1)S(1)}, bf16[512,128]{1,0:T(8,128)(2,1)S(1)}, u32[]{:S(2)}, u32[]{:S(2)}) collective-permute-start(bf16[512,128]{1,0:T(8,128)(2,1)S(1)} %collective-permute-done.1.refs_2_), channel_id=1, source_target_pairs={{0,16},{16,32},{32,48},{48,64},{64,80},{80,96},{96,112},{112,0},{1... | collective-permute-start | bytes 393224 | tf_op jit(solution)/shard_map/ppermute | solution.py:383
  20.9 7.0 %collective-permute-start.2 = (bf16[512,128]{1,0:T(8,128)(2,1)S(1)}, bf16[512,128]{1,0:T(8,128)(2,1)S(1)}, u32[]{:S(2)}, u32[]{:S(2)}) collective-permute-start(bf16[512,128]{1,0:T(8,128)(2,1)S(1)} %collective-permute-done.other.refs_1_), channel_id=1, source_target_pairs={{0,16},{16,32},{32,48},{48,64},{64,80},{80,96},{96,112},{112,0},{1... | collective-permute-start | bytes 393224 | tf_op jit(solution)/shard_map/ppermute | solution.py:383
  22.2 6.2 %collective-permute-start.8 = (bf16[512,128]{1,0:T(8,128)(2,1)S(1)}, bf16[512,128]{1,0:T(8,128)(2,1)S(1)}, u32[]{:S(2)}, u32[]{:S(2)}) collective-permute-start(bf16[512,128]{1,0:T(8,128)(2,1)S(1)} %collective-permute-done.4.refs_5_), channel_id=1, source_target_pairs={{0,112},{16,0},{32,16},{48,32},{64,48},{80,64},{96,80},{112,96},{1... | collective-permute-start | bytes 393224 | tf_op jit(solution)/shard_map/ppermute | solution.py:383
  25.9 6.2 %collective-permute-start.7 = (bf16[512,128]{1,0:T(8,128)(2,1)S(1)}, bf16[512,128]{1,0:T(8,128)(2,1)S(1)}, u32[]{:S(2)}, u32[]{:S(2)}) collective-permute-start(bf16[512,128]{1,0:T(8,128)(2,1)S(1)} %collective-permute-done.3.refs_4_), channel_id=1, source_target_pairs={{0,112},{16,0},{32,16},{48,32},{64,48},{80,64},{96,80},{112,96},{1... | collective-permute-start | bytes 393224 | tf_op jit(solution)/shard_map/ppermute | solution.py:383
  27.8 7.6 %collective-permute-start.9 = (bf16[512,128]{1,0:T(8,128)(2,1)S(1)}, bf16[512,128]{1,0:T(8,128)(2,1)S(1)}, u32[]{:S(2)}, u32[]{:S(2)}) collective-permute-start(bf16[512,128]{1,0:T(8,128)(2,1)S(1)} %collective-permute-done.5.refs_6_), channel_id=1, source_target_pairs={{0,16},{16,32},{32,48},{48,64},{64,80},{80,96},{96,112},{112,0},{1... | collective-permute-start | bytes 393224 | tf_op jit(solution)/shard_map/ppermute | solution.py:383
  27.9 8.9 %collective-permute-start.6 = (bf16[512,128]{1,0:T(8,128)(2,1)S(1)}, bf16[512,128]{1,0:T(8,128)(2,1)S(1)}, u32[]{:S(2)}, u32[]{:S(2)}) collective-permute-start(bf16[512,128]{1,0:T(8,128)(2,1)S(1)} %collective-permute-done.2.refs_3_), channel_id=1, source_target_pairs={{0,16},{16,32},{32,48},{48,64},{64,80},{80,96},{96,112},{112,0},{1... | collective-permute-start | bytes 393224 | tf_op jit(solution)/shard_map/ppermute | solution.py:383
  28.4 8.5 %collective-permute-start.12 = (bf16[512,128]{1,0:T(8,128)(2,1)S(1)}, bf16[512,128]{1,0:T(8,128)(2,1)S(1)}, u32[]{:S(2)}, u32[]{:S(2)}) collective-permute-start(bf16[512,128]{1,0:T(8,128)(2,1)S(1)} %collective-permute-done.8.refs_9_), channel_id=1, source_target_pairs={{0,112},{16,0},{32,16},{48,32},{64,48},{80,64},{96,80},{112,96},{1... | collective-permute-start | bytes 393224 | tf_op jit(solution)/shard_map/ppermute | solution.py:383
  32.0 11.1 %collective-permute-start.11 = (bf16[512,128]{1,0:T(8,128)(2,1)S(1)}, bf16[512,128]{1,0:T(8,128)(2,1)S(1)}, u32[]{:S(2)}, u32[]{:S(2)}) collective-permute-start(bf16[512,128]{1,0:T(8,128)(2,1)S(1)} %collective-permute-done.7.refs_8_), channel_id=1, source_target_pairs={{0,112},{16,0},{32,16},{48,32},{64,48},{80,64},{96,80},{112,96},{1... | collective-permute-start | bytes 393224 | tf_op jit(solution)/shard_map/ppermute | solution.py:383
  35.4 7.8 %collective-permute-start.13 = (bf16[512,128]{1,0:T(8,128)(2,1)S(1)}, bf16[512,128]{1,0:T(8,128)(2,1)S(1)}, u32[]{:S(2)}, u32[]{:S(2)}) collective-permute-start(bf16[512,128]{1,0:T(8,128)(2,1)S(1)} %collective-permute-done.9.refs_10_), channel_id=1, source_target_pairs={{0,16},{16,32},{32,48},{48,64},{64,80},{80,96},{96,112},{112,0},{1... | collective-permute-start | bytes 393224 | tf_op jit(solution)/shard_map/ppermute | solution.py:383
  36.8 6.3 %collective-permute-start.10 = (bf16[512,128]{1,0:T(8,128)(2,1)S(1)}, bf16[512,128]{1,0:T(8,128)(2,1)S(1)}, u32[]{:S(2)}, u32[]{:S(2)}) collective-permute-start(bf16[512,128]{1,0:T(8,128)(2,1)S(1)} %collective-permute-done.6.refs_7_), channel_id=1, source_target_pairs={{0,16},{16,32},{32,48},{48,64},{64,80},{80,96},{96,112},{112,0},{1... | collective-permute-start | bytes 393224 | tf_op jit(solution)/shard_map/ppermute | solution.py:383
  36.8 6.3 %collective-permute-start.14 = (bf16[512,128]{1,0:T(8,128)(2,1)S(1)}, bf16[512,128]{1,0:T(8,128)(2,1)S(1)}, u32[]{:S(2)}, u32[]{:S(2)}) collective-permute-start(bf16[512,128]{1,0:T(8,128)(2,1)S(1)} %collective-permute-done.12.refs_13_), channel_id=1, source_target_pairs={{0,112},{16,0},{32,16},{48,32},{64,48},{80,64},{96,80},{112,96},{1... | collective-permute-start | bytes 393224 | tf_op jit(solution)/shard_map/ppermute | solution.py:383
  40.1 44.4 %collective-permute-start.16 = (bf16[256,1024]{1,0:T(8,128)(2,1)}, bf16[256,1024]{1,0:T(8,128)(2,1)S(1)}, u32[]{:S(2)}, u32[]{:S(2)}) collective-permute-start(bf16[256,1024]{1,0:T(8,128)(2,1)} %bitcast.26), channel_id=1, source_target_pairs={{0,8},{8,0},{1,9},{9,1},{2,10},{10,2},{3,11},{11,3},{4,12},{12,4},... | collective-permute-start | bytes 1572872 | tf_op jit(solution)/shard_map/ppermute | solution.py:387
  43.1 0.9 copy-start.5
  44.1 14.4 %copy-start.6 = (bf16[512,128]{1,0:T(8,128)(2,1)S(1)}, bf16[512,128]{1,0:T(8,128)(2,1)}, u32[]{:S(2)}) copy-start(bf16[512,128]{1,0:T(8,128)(2,1)} %get-tuple-element.29.mine.refs_0_) | copy-start | bytes 393220
  54.0 15.1 %all-to-all-start = ((f32[8,8,128]{2,1,0:T(8,128)}), f32[8,8,128]{2,1,0:T(8,128)S(1)}, u32[]{:S(2)}, u32[]{:S(2)}) async-start(f32[8,8,128]{2,1,0:T(8,128)} %broadcast_in_dim.12), calls=%async_computation | async-start | bytes 65536 | tf_op jit(solution)/shard_map/all_to_all | solution.py:449
  69.1 15.4 %copy-start = (bf16[1,256,1024]{2,1,0:T(8,128)(2,1)S(1)}, bf16[1,256,1024]{2,1,0:T(8,128)(2,1)}, u32[]{:S(2)}) copy-start(bf16[1,256,1024]{2,1,0:T(8,128)(2,1)} %param.7) | copy-start | bytes 1572868
  69.1 15.3 %collective-permute-start.15 = (bf16[256,128]{1,0:T(8,128)(2,1)S(1)}, bf16[256,128]{1,0:T(8,128)(2,1)S(1)}, u32[]{:S(2)}, u32[]{:S(2)}) collective-permute-start(bf16[256,128]{1,0:T(8,128)(2,1)S(1)} %get-tuple-element.41.first_sent), channel_id=1, source_target_pairs={{0,8},{8,0},{1,9},{9,1},{2,10},{10,2},{3,11},{11,3},{4,12},{12,4},... | collective-permute-start | bytes 196616 | tf_op jit(solution)/shard_map/ppermute | solution.py:387
  86.1 17.6 %all-to-all-start.1 = ((bf16[16,96,128]{2,1,0:T(8,128)(2,1)}), bf16[16,96,128]{2,1,0:T(8,128)(2,1)S(1)}, u32[]{:S(2)}, u32[]{:S(2)}) async-start(bf16[16,96,128]{2,1,0:T(8,128)(2,1)} %shard_map.114), calls=%async_computation.1 | async-start | bytes 786432 | tf_op jit(solution)/shard_map/all_to_all | solution.py:484
  93.4 5.9 %collective-permute-start.17 = (bf16[256,128]{1,0:T(8,128)(2,1)S(1)}, bf16[256,128]{1,0:T(8,128)(2,1)S(1)}, u32[]{:S(2)}, u32[]{:S(2)}) collective-permute-start(bf16[256,128]{1,0:T(8,128)(2,1)S(1)} %get-tuple-element.44.second_sent), channel_id=1, source_target_pairs={{0,8},{8,0},{1,9},{9,1},{2,10},{10,2},{3,11},{11,3},{4,12},{12,4},... | collective-permute-start | bytes 196616 | tf_op jit(solution)/shard_map/ppermute | solution.py:387
  104.7 5.9 %copy-start.1 = (bf16[1024,128]{1,0:T(8,128)(2,1)S(1)}, bf16[1024,128]{1,0:T(8,128)(2,1)}, u32[]{:S(2)}) copy-start(bf16[1024,128]{1,0:T(8,128)(2,1)} %wq.3) | copy-start | bytes 786436
  104.7 5.9 %copy-start.2 = (bf16[1024,128]{1,0:T(8,128)(2,1)S(1)}, bf16[1024,128]{1,0:T(8,128)(2,1)}, u32[]{:S(2)}) copy-start(bf16[1024,128]{1,0:T(8,128)(2,1)} %wk.3) | copy-start | bytes 786436
  104.7 5.9 %copy-start.3 = (bf16[1024,128]{1,0:T(8,128)(2,1)S(1)}, bf16[1024,128]{1,0:T(8,128)(2,1)}, u32[]{:S(2)}) copy-start(bf16[1024,128]{1,0:T(8,128)(2,1)} %wv.3) | copy-start | bytes 786436
  104.7 21.8 %all-to-all-start.2 = ((bf16[32,96,128]{2,1,0:T(8,128)(2,1)}), bf16[32,96,128]{2,1,0:T(8,128)(2,1)S(1)}, u32[]{:S(2)}, u32[]{:S(2)}) async-start(bf16[32,96,128]{2,1,0:T(8,128)(2,1)} %shard_map.116), calls=%async_computation.2 | async-start | bytes 1572864 | tf_op jit(solution)/shard_map/all_to_all | solution.py:500
  112.4 1.5 %collective-permute-start.18 = (bf16[4,32,1024]{2,1,0:T(8,128)(2,1)S(1)}, bf16[4,32,1024]{2,1,0:T(8,128)(2,1)S(1)}, u32[]{:S(2)}, u32[]{:S(2)}) collective-permute-start(bf16[4,32,1024]{2,1,0:T(8,128)(2,1)S(1)} %get-tuple-element.48), channel_id=1, source_target_pairs={{0,1},{1,0},{2,3},{3,2},{4,5},{5,4},{6,7},{7,6},{8,9},{9,8},{10,11... | collective-permute-start | bytes 786440 | tf_op jit(solution)/shard_map/ppermute | solution.py:493
  114.0 4.4 %collective-permute-start.19 = (bf16[32,1024]{1,0:T(8,128)(2,1)S(1)}, bf16[32,1024]{1,0:T(8,128)(2,1)S(1)}, u32[]{:S(2)}, u32[]{:S(2)}) collective-permute-start(bf16[32,1024]{1,0:T(8,128)(2,1)S(1)} %get-tuple-element.55), channel_id=1, source_target_pairs={{0,2},{2,0},{4,6},{6,4},{1,3},{3,1},{5,7},{7,5},{8,10},{10,8},{12,... | collective-permute-start | bytes 196616 | tf_op jit(solution)/shard_map/ppermute | solution.py:499
  114.5 6.2 %collective-permute-start.20 = (bf16[32,1024]{1,0:T(8,128)(2,1)S(1)}, bf16[32,1024]{1,0:T(8,128)(2,1)S(1)}, u32[]{:S(2)}, u32[]{:S(2)}) collective-permute-start(bf16[32,1024]{1,0:T(8,128)(2,1)S(1)} %get-tuple-element.57), channel_id=1, source_target_pairs={{0,4},{2,6},{4,0},{6,2},{1,5},{3,7},{5,1},{7,3},{8,12},{10,14},{12... | collective-permute-start | bytes 196616 | tf_op jit(solution)/shard_map/ppermute | solution.py:499
  117.1 4.5 %collective-permute-start.21 = (bf16[32,1024]{1,0:T(8,128)(2,1)S(1)}, bf16[32,1024]{1,0:T(8,128)(2,1)S(1)}, u32[]{:S(2)}, u32[]{:S(2)}) collective-permute-start(bf16[32,1024]{1,0:T(8,128)(2,1)S(1)} %get-tuple-element.56), channel_id=1, source_target_pairs={{0,6},{2,4},{4,2},{6,0},{1,7},{3,5},{5,3},{7,1},{8,14},{10,12},{12... | collective-permute-start | bytes 196616 | tf_op jit(solution)/shard_map/ppermute | solution.py:499

commit v4 on v3

v4 whole, which is shorter than its diff:
```python
import functools
import math

import jax
import jax.numpy as jnp
from jax import lax
from jax.experimental import pallas as pl
from jax.experimental.pallas import tpu as pltpu
from jax.sharding import Mesh
from jax.sharding import PartitionSpec as P

HALF = 256
HD = 64
RUN = 256
SEC = 512
NSEC = 8
NEG = -1e30
LIMIT = 51 << 20
CHUNK = 512
BF = jnp.bfloat16
F32 = jnp.float32

Z = ("z2", "z1", "z0")
CTX = Z + ("xh",)
TP = ("y", "core")

OFFSETS = (0, -1, 1, -2, 2, -3, 3, 4)

NN = (((1,), (0,)), ((), ()))
NT = (((1,), (1,)), ((), ()))
TN = (((0,), (0,)), ((), ()))


def dot(a, b, dims=NN):
    return lax.dot_general(a, b, dims, preferred_element_type=F32)


def call(kernel, outs, args, scratch=(), flops=0, transcendentals=0, smem=1, manual=0, limit=None):
    specs = [pl.BlockSpec(memory_space=pltpu.SMEM)] * smem
    specs += [pl.BlockSpec(memory_space=pl.ANY)] * manual
    specs += [pl.BlockSpec(memory_space=pltpu.VMEM)] * (len(args) - smem - manual)
    moved = sum(a.size * a.dtype.itemsize for a in args)
    return pl.pallas_call(
        kernel,
        out_shape=outs,
        in_specs=specs,
        out_specs=jax.tree.map(lambda _: pl.BlockSpec(memory_space=pltpu.VMEM), outs),
        scratch_shapes=list(scratch),
        compiler_params=pltpu.CompilerParams(vmem_limit_bytes=limit or LIMIT),
        cost_estimate=pl.CostEstimate(
            flops=flops, bytes_accessed=moved, transcendentals=transcendentals
        ),
    )(*args)


def low_lanes(rows):
    return lax.broadcasted_iota(jnp.int32, (rows, 128), 1) < HD


def document_features(place, lengths, spots, feat):
    flip = place[0]
    lane = lax.broadcasted_iota(jnp.int32, (RUN, 128), 1)
    last = lane == HD + 8
    lane_row = lax.broadcasted_iota(jnp.int32, (1, 128), 1)
    starts, ends = jnp.zeros((1, 128), jnp.int32), jnp.zeros((1, 128), jnp.int32)
    start = jnp.int32(0)
    for d in range(8):
        end = start + lengths[0, d]
        starts = jnp.where(lane_row == HD + d, start, starts)
        ends = jnp.where(lane_row == HD + d, end, ends)
        start = end

    def one(block, carry):
        half = lax.rem(block, 2)
        run = (block - half) + jnp.where(half == flip, 0, 1)
        pos = run * RUN + lax.broadcasted_iota(jnp.int32, (RUN, RUN), 0)
        hit = jnp.where(pos == spots[...], 1.0, 0.0).astype(BF)
        other = 1.0 - dot(hit, jnp.ones((RUN, 128), BF))
        pos128 = run * RUN + lax.broadcasted_iota(jnp.int32, (RUN, 128), 0)
        member = (pos128 >= starts) & (pos128 < ends)
        row = jnp.where(last, other, jnp.where(member, 1.0, 0.0))
        at = pl.ds(pl.multiple_of(block * RUN, RUN), RUN)
        feat[at, :] = row.astype(BF)
        return carry

    lax.fori_loop(0, 2 * NSEC, one, 0)


def project_kernel(place, lengths, tok, wq, wk, wv, cot, spots, mine, theirs, feat, *scratch):
    tok_v, wk_v, wv_v, wq_v, cot_v, sems = scratch
    pairs = ((tok, tok_v), (wk, wk_v), (wv, wv_v), (wq, wq_v), (cot, cot_v))
    copies = [pltpu.make_async_copy(a, b, sems.at[i]) for i, (a, b) in enumerate(pairs)]
    for copy in copies:
        copy.start()
    document_features(place, lengths, spots, feat)
    first = place[0] == 0
    copies[0].wait()
    t = tok_v[...]
    copies[1].wait()
    k = dot(t, wk_v[...]).astype(BF)
    copies[2].wait()
    v = dot(t, wv_v[...]).astype(BF)
    copies[3].wait()
    q = dot(t, wq_v[...]).astype(BF)
    copies[4].wait()
    c = cot_v[...]
    kv0 = jnp.concatenate([k[:, :HD], v[:, :HD]], axis=1)
    kv1 = jnp.concatenate([k[:, HD:], v[:, HD:]], axis=1)
    qc0 = jnp.concatenate([q[:, :HD], c[:, :HD]], axis=1)
    qc1 = jnp.concatenate([q[:, HD:], c[:, HD:]], axis=1)

    @pl.when(first)
    def _():
        mine[:RUN] = kv0
        mine[RUN:] = qc0
        theirs[:RUN] = kv1
        theirs[RUN:] = qc1

    @pl.when(jnp.logical_not(first))
    def _():
        mine[:RUN] = kv1
        mine[RUN:] = qc1
        theirs[:RUN] = kv0
        theirs[RUN:] = qc0


def places(section, flip, along):
    shape = (1, SEC) if along == 1 else (SEC, 1)
    i = lax.broadcasted_iota(jnp.int32, shape, along)
    half = jnp.where(i >= RUN, 1 - flip, flip)
    return section * SEC + half * RUN + lax.bitwise_and(i, RUN - 1)


def section_at(own, offset):
    return lax.rem(own + offset + NSEC, NSEC)


def part_of(pieces, r, part):
    at = slice(part * RUN, (part + 1) * RUN)
    return jnp.concatenate([pieces[2 * r][at], pieces[2 * r + 1][at]], axis=0)


def features_at(feat, section):
    return feat[pl.ds(pl.multiple_of(section * SEC, SEC), SEC), :]


def join_key(kv, feat):
    lane = lax.broadcasted_iota(jnp.int32, kv.shape, 1)
    base = jnp.where(lane < HD + 8, 1.0, 0.0).astype(BF)
    sign = jnp.where(lane == HD + 8, 1.0, jnp.where(lane < HD + 8, -1.0, 0.0)).astype(BF)
    return jnp.where(lane < HD, kv, (base + sign * feat) * jnp.asarray(NEG, BF))


def join_query(qc, feat):
    low = lax.broadcasted_iota(jnp.int32, qc.shape, 1) < HD
    return jnp.where(low, qc * jnp.asarray(1.0 / math.sqrt(HD), BF), feat)


def less_global(joined):
    lane = lax.broadcasted_iota(jnp.int32, joined.shape, 1)
    return jnp.where(lane == HD + 8, jnp.zeros_like(joined), joined)


def right_half(rows):
    low = lax.broadcasted_iota(jnp.int32, rows.shape, 1) < HD
    return jnp.where(low, jnp.zeros_like(rows), rows)


def forward_kernel(chunk, place, *refs):
    pieces, (feat, att_out, column_out, stats) = refs[: 2 * NSEC], refs[2 * NSEC :]
    flip, own = place[0], place[1]
    own_qc = part_of(pieces, 0, 1)
    joined = join_query(own_qc, features_at(feat, own))
    near_rows = less_global(joined)
    row_places = places(own, flip, 0)
    count = SEC // chunk
    state = [None] * count
    for r, offset in enumerate(OFFSETS):
        section = section_at(own, offset)
        kv = part_of(pieces, r, 0)
        kp = join_key(kv, features_at(feat, section))
        for c in range(count):
            rows = slice(c * chunk, (c + 1) * chunk)
            s = dot(joined[rows], kp, NT)
            if r < 3:
                away = row_places[rows] - places(section, flip, 1)
                s = jnp.where(jnp.abs(away) <= HALF, dot(near_rows[rows], kp, NT), s)
            new_peak = jnp.max(s, axis=1, keepdims=True)
            if r > 0:
                peak, total, acc = state[c]
                new_peak = jnp.maximum(peak, new_peak)
                keep = jnp.exp(peak - new_peak)
            e = jnp.exp(s - new_peak)
            new_total = jnp.sum(e, axis=1, keepdims=True)
            new_acc = dot(e.astype(BF), kv)
            if r > 0:
                new_total, new_acc = keep * total + new_total, keep * acc + new_acc
            state[c] = new_peak, new_total, new_acc
    for c in range(count):
        rows = slice(c * chunk, (c + 1) * chunk)
        peak, total, acc = state[c]
        att = (acc / total).astype(BF)
        att_out[rows] = att
        log_total = peak + jnp.log(total)
        cot = right_half(own_qc[rows]).astype(F32)
        delta = jnp.sum(att.astype(F32) * cot, axis=1, keepdims=True)
        lanes = lax.broadcasted_iota(jnp.int32, (chunk, 128), 1)
        column = jnp.where(lanes == 0, log_total, delta)
        column_out[rows] = column
        turned = column.T
        for k in range(chunk // 128):
            at = c * (chunk // 128) + k
            for copy in range(NSEC):
                stats[copy, at : at + 1] = turned[0:1, k * 128 : (k + 1) * 128]
                stats[copy, 4 + at : 5 + at] = turned[1:2, k * 128 : (k + 1) * 128]


def queries_kernel(chunk, place, *refs):
    pieces, (feat, att, column, packed, packed_other) = refs[: 2 * NSEC], refs[2 * NSEC :]
    flip, own = place[0], place[1]
    own_qc = part_of(pieces, 0, 1)
    joined = join_query(own_qc, features_at(feat, own))
    near_rows, cot = less_global(joined), right_half(own_qc)
    row_places = places(own, flip, 0)
    count = SEC // chunk
    grads = [None] * count
    for r, offset in enumerate(OFFSETS):
        section = section_at(own, offset)
        kv = part_of(pieces, r, 0)
        kp = join_key(kv, features_at(feat, section))
        for c in range(count):
            rows = slice(c * chunk, (c + 1) * chunk)
            s = dot(joined[rows], kp, NT)
            if r < 3:
                away = row_places[rows] - places(section, flip, 1)
                s = jnp.where(jnp.abs(away) <= HALF, dot(near_rows[rows], kp, NT), s)
            p = jnp.exp(s - column[rows, 0:1])
            ds = p * (dot(cot[rows], kv, NT) - column[rows, 1:2])
            grad = dot(ds.astype(BF), kv)
            grads[c] = grad if r == 0 else grads[c] + grad
    grad = jnp.concatenate(grads, axis=0) if count > 1 else grads[0]
    grad = (grad * (1.0 / math.sqrt(HD))).astype(BF)
    out = jnp.where(low_lanes(SEC), grad, att[...])
    packed[...] = out[:RUN]
    packed_other[...] = out[RUN:]


def keys_kernel(chunk, place, *refs):
    pieces, (feat, stats, packed, packed_other, stats_s, sems) = refs[: 2 * NSEC], refs[2 * NSEC :]
    flip, own = place[0], place[1]
    copies = []
    for r, offset in enumerate(OFFSETS):
        at = pl.multiple_of(section_at(own, offset) * 8, 8)
        to = stats_s.at[pl.ds(r * 8, 8)]
        copies.append(pltpu.make_async_copy(stats.at[pl.ds(at, 8)], to, sems.at[r]))
        copies[-1].start()
    own_kv = part_of(pieces, 0, 0)
    joined = join_key(own_kv, features_at(feat, own))
    near_keys, value = less_global(joined), right_half(own_kv)
    key_places = places(own, flip, 0)
    count = SEC // chunk
    state = [None] * count
    for copy in copies:
        copy.wait()
    for r, offset in enumerate(OFFSETS):
        section = section_at(own, offset)
        qc = part_of(pieces, r, 1)
        qp = join_query(qc, features_at(feat, section))
        st = stats_s[r * 8 : r * 8 + 8]
        log_total = jnp.concatenate([st[i : i + 1] for i in range(4)], axis=1)
        delta = jnp.concatenate([st[i : i + 1] for i in range(4, 8)], axis=1)
        for c in range(count):
            rows = slice(c * chunk, (c + 1) * chunk)
            s = dot(joined[rows], qp, NT)
            if r < 3:
                away = key_places[rows] - places(section, flip, 1)
                s = jnp.where(jnp.abs(away) <= HALF, dot(near_keys[rows], qp, NT), s)
            p = jnp.exp(s - log_total)
            ds = p * (dot(value[rows], qc, NT) - delta)
            both = dot(ds.astype(BF), qc), dot(p.astype(BF), qc)
            state[c] = both if r == 0 else (state[c][0] + both[0], state[c][1] + both[1])
    key_acc = jnp.concatenate([x[0] for x in state], axis=0) if count > 1 else state[0][0]
    value_acc = jnp.concatenate([x[1] for x in state], axis=0) if count > 1 else state[0][1]
    out = jnp.where(low_lanes(SEC), key_acc * (1.0 / math.sqrt(HD)), value_acc).astype(BF)
    packed[...] = out[:RUN]
    packed_other[...] = out[RUN:]


def weights_kernel(tok, tok_other, first, first_sent, second, second_sent, out):
    qa = dot(tok[...], first[...], TN) + dot(tok_other[...], first_sent[...], TN)
    kv = dot(tok[...], second[...], TN) + dot(tok_other[...], second_sent[...], TN)
    for p in range(16):
        out[p, :64] = kv[p * 64 : (p + 1) * 64].astype(BF)
        upper = qa[p * 32 : (p + 1) * 32, :HD]
        lower = qa[512 + p * 32 : 512 + (p + 1) * 32, :HD]
        out[p, 64:96] = jnp.concatenate([upper, lower], axis=1).astype(BF)


def sum_kernel(parts, out):
    total = parts[0].astype(F32)
    for p in range(1, 16):
        total = total + parts[p].astype(F32)
    total = total.astype(BF)
    for p in range(32):
        out[p] = total


def input_kernel(place, first, first_other, second, second_other, wq, wk, wv, att, keep, send):
    swap = place[0] != 0
    core = place[2]
    a, b, c, d = first[...], first_other[...], second[...], second_other[...]
    a, b = jnp.where(swap, b, a), jnp.where(swap, a, b)
    c, d = jnp.where(swap, d, c), jnp.where(swap, c, d)
    dq = jnp.concatenate([a[:, :HD], b[:, :HD]], axis=1)
    att[...] = jnp.concatenate([a[:, HD:], b[:, HD:]], axis=1)
    dk = jnp.concatenate([c[:, :HD], d[:, :HD]], axis=1)
    dv = jnp.concatenate([c[:, HD:], d[:, HD:]], axis=1)
    grad = dot(dq, wq[...], NT) + dot(dk, wk[...], NT) + dot(dv, wv[...], NT)
    for y in range(4):
        low, high = grad[y * 64 : y * 64 + 32], grad[y * 64 + 32 : y * 64 + 64]
        keep[y] = jnp.where(core == 0, low, high)
        send[y] = jnp.where(core == 0, high, low).astype(BF)


def assemble_kernel(parts, gq, gk, gv):
    for p in range(16):
        a, b = parts[2 * p].astype(F32), parts[2 * p + 1].astype(F32)
        low = jnp.concatenate([a[:, :HD], b[:, :HD]], axis=1)
        high = jnp.concatenate([a[:, HD:], b[:, HD:]], axis=1)
        gk[p * 64 : (p + 1) * 64] = low[:64]
        gv[p * 64 : (p + 1) * 64] = high[:64]
        gq[p * 32 : (p + 1) * 32] = low[64:]
        gq[512 + p * 32 : 512 + (p + 1) * 32] = high[64:]


def shift(a, step):
    return lax.ppermute(a, Z, [(i, (i + step) % NSEC) for i in range(NSEC)])


def swap(a):
    return lax.ppermute(a, "xh", [(0, 1), (1, 0)])


def on_device(tokens, wq, wk, wv, cotangent, doc_lengths, global_positions):
    shape = jax.ShapeDtypeStruct
    tok, cot = tokens[0], cotangent[0]
    xh, z, y, core = (lax.axis_index(a) for a in ("xh", Z, "y", "core"))
    place = jnp.stack([xh, z, core]).astype(jnp.int32)
    weight = pltpu.VMEM((1024, 128), BF)
    mine, theirs, feat = call(
        project_kernel,
        (shape((SEC, 128), BF),) * 2 + (shape((NSEC * SEC, 128), BF),),
        (place, doc_lengths, tok, wq, wk, wv, cot, global_positions),
        scratch=(
            pltpu.VMEM((RUN, 1024), BF),
            weight,
            weight,
            weight,
            pltpu.VMEM((RUN, 128), BF),
            pltpu.SemaphoreType.DMA((5,)),
        ),
        flops=6 * 256 * 1024 * 128,
        smem=2,
        manual=5,
        limit=64 << 20,
    )
    other = swap(theirs)
    tok_other = swap(tok)
    pairs = SEC * SEC * NSEC
    wide = shape((SEC, 128), F32)

    tie = lax.optimization_barrier
    lower_a, upper_a = [mine, shift(mine, 1)], [mine, shift(mine, -1)]
    lower_b, upper_b = [other, shift(other, 1)], [other, shift(other, -1)]
    for x, step in ((lower_a, 1), (upper_a, -1), (lower_b, 1), (upper_b, -1)):
        x.append(shift(x[1], step))
    for x, step in ((lower_a, 1), (upper_a, -1), (lower_b, 1), (upper_b, -1)):
        x.append(shift(x[2], step))
    far = (shift(lower_a[3], 1), shift(upper_b[3], -1))
    pieces = (mine, other)
    for i in (1, 2, 3):
        pieces += (lower_a[i], lower_b[i], upper_a[i], upper_b[i])
    pieces += far
    att_rows, column, stats = call(
        functools.partial(forward_kernel, CHUNK),
        (shape((SEC, 128), BF), wide, shape((NSEC, 8, 128), F32)),
        (place, *pieces, feat),
        flops=2 * 128 * 2 * pairs,
        transcendentals=pairs,
    )
    all_stats = lax.all_to_all(stats, Z, 0, 0, tiled=True).reshape(NSEC * 8, 128)
    half = shape((RUN, 128), BF)
    first, first_sent = call(
        functools.partial(queries_kernel, CHUNK),
        (half, half),
        (place, *pieces, feat, att_rows, column),
        flops=2 * 128 * 3 * pairs,
        transcendentals=pairs,
    )
    all_stats, first, first_sent = lax.optimization_barrier((all_stats, first, first_sent))
    first_other = swap(first_sent)
    second, second_sent = call(
        functools.partial(keys_kernel, CHUNK),
        (half, half),
        (place, *pieces, feat, all_stats),
        scratch=(pltpu.VMEM((NSEC * 8, 128), F32), pltpu.SemaphoreType.DMA((NSEC,))),
        flops=2 * 128 * 4 * pairs,
        transcendentals=pairs,
    )
    second, second_sent, first_other = lax.optimization_barrier((second, second_sent, first_other))
    second_other = swap(second_sent)
    partial = call(
        weights_kernel,
        shape((16, 96, 128), BF),
        (tok, tok_other, first, first_sent, second, second_sent),
        flops=2 * 512 * 1024 * 256,
        smem=0,
    )
    partial = lax.all_to_all(partial, ("b",) + Z, 0, 0, tiled=True)
    partial, second_other = tie((partial, second_other))
    total = call(sum_kernel, shape((32, 96, 128), BF), (partial,), smem=0)
    att, keep, send = call(
        input_kernel,
        (half, shape((4, 32, 1024), F32), shape((4, 32, 1024), BF)),
        (place, first, first_other, second, second_other, wq, wk, wv),
        flops=6 * 256 * 1024 * 128,
    )
    arrived = lax.ppermute(send, "core", [(0, 1), (1, 0)])
    both = keep + arrived.astype(F32)
    share = lax.dynamic_index_in_dim(both, y, 0, False)
    both_bf = both.astype(BF)
    for k in (1, 2, 3):
        out = lax.dynamic_index_in_dim(both_bf, lax.bitwise_xor(y, k), 0, False)
        share = share + lax.ppermute(out, "y", [(i, i ^ k) for i in range(4)]).astype(F32)
    total = lax.all_to_all(total, ("b",) + CTX, 0, 0, tiled=True)
    gq, gk, gv = call(assemble_kernel, (shape((1024, 128), F32),) * 3, (total,), smem=0)
    return att[None], share.astype(BF)[None], gq, gk, gv


def solution(mesh):
    devices = mesh.devices.reshape(2, 2, 2, 2, 2, 4, 2)
    fine = Mesh(devices, ("b",) + CTX + TP)
    in_specs = (
        P("b", CTX, None),
        P(None, TP),
        P(None, TP),
        P(None, TP),
        P("b", CTX, TP),
        P("b", None),
        P("b", None),
    )
    out_specs = (
        P("b", CTX, TP),
        P("b", CTX + TP, None),
        P(None, TP),
        P(None, TP),
        P(None, TP),
    )
    return jax.shard_map(
        on_device, mesh=fine, in_specs=in_specs, out_specs=out_specs, check_vma=False
    )
```

time: 128 us -> 116 us (0.906)
  Pallas kernels: 42.5 us -> 29.8 us
  starting transfers between devices: 58.6 us -> 56.6 us
  waiting for transfers between devices: 23.1 us -> 25.1 us
    pallas_call x8, Pallas kernels: 42.5 us -> 29.8 us  [call(): pl.pallas_call(kernel, out_shape=outs, in_specs=specs, out_specs=jax.tree...]
    all_to_all x1, waiting for transfers between devices: 0.01 us -> 2.62 us  [on_device(): lax.all_to_all(stats, Z, 0, 0, tiled=True).reshape(NSEC * 8, 128)]
    all_to_all x1, starting transfers between devices: 7.32 us -> 5.04 us  [on_device(): partial = lax.all_to_all(partial, ('b',) + Z, 0, 0, tiled=True)]
  transfers between devices with their start and end apart: 25 -> 25, of which waited for: 11 -> 11; matrix products, arithmetic and copies ran while one was open for 1% -> 1% of each run, Pallas kernels for 26% -> 17%
where the time goes in v4:
time: 116 us
  starting transfers between devices  56.6 us (49%)
  Pallas kernels  29.8 us (26%)
  waiting for transfers between devices  25.1 us (22%)
  local copies, waits for them, and re-layouts  1.9 us (2%)
  other arithmetic  1.32 us (1%)
    pallas_call x8, Pallas kernels, call(): pl.pallas_call(kernel, out_shape=outs, in_specs=specs, out_specs=jax.tree...  29.8 us
    ppermute x14, starting transfers between devices, shift(): return lax.ppermute(a, Z, [(i, (i + step) % NSEC) for i in range(NSEC)])  25.9 us
    ppermute x4, starting transfers between devices, swap(): return lax.ppermute(a, 'xh', [(0, 1), (1, 0)])  11.2 us
    all_to_all x1, starting transfers between devices, on_device(): total = lax.all_to_all(total, ('b',) + CTX, 0, 0, tiled=True)  5.89 us
    ppermute x4, waiting for transfers between devices, swap(): return lax.ppermute(a, 'xh', [(0, 1), (1, 0)])  5.77 us
    all_to_all x1, starting transfers between devices, on_device(): partial = lax.all_to_all(partial, ('b',) + Z, 0, 0, tiled=True)  5.04 us
    all_to_all x1, waiting for transfers between devices, on_device(): partial = lax.all_to_all(partial, ('b',) + Z, 0, 0, tiled=True)  4.46 us
    all_to_all x1, starting transfers between devices, on_device(): lax.all_to_all(stats, Z, 0, 0, tiled=True).reshape(NSEC * 8, 128)  4.39 us
  transfers between devices with their start and end apart: 25, of which 11 were waited for; matrix products, arithmetic and copies ran while one was open for 1% of the time, Pallas kernels for 17%

profile of v4, /device:TPU:8, one launch (start us, length us, event | category | flops | bytes accessed | tf_op | source)
XLA Modules:
  0.0 115.6 jit_solution(395574784665708253)
XLA Ops:
  0.6 0.6 pad_add_fusion.place
  1.2 5.7 %shard_map.110 = (bf16[512,128]{1,0:T(8,128)(2,1)}, bf16[512,128]{1,0:T(8,128)(2,1)}, bf16[4096,128]{1,0:T(8,128)(2,1)}) custom-call(s32[3]{0:T(128)} %pad_add_fusion.place, s32[1,8]{1,0:T(1,128)} %lengths.1, bf16[256,1024]{1,0:T(8,128)(2,1)} %bitcast.25, bf16[1024,128]{1,0:T(8,128)(2,1)} %wq.3, bf16[1024,128]{1,0:T(8,128)(2,1)} %wk.3, ...), custom_call_target="tpu_custom_call" | custom-call | flops 201326592 | bytes 1377324 | tf_op jit(solution)/shard_map/pallas_call | solution.py:43
  6.9 3.1 %collective-permute-start = (bf16[512,128]{1,0:T(8,128)(2,1)}, bf16[512,128]{1,0:T(8,128)(2,1)S(1)}, u32[]{:S(2)}, u32[]{:S(2)}) collective-permute-start(bf16[512,128]{1,0:T(8,128)(2,1)} %get-tuple-element.30), channel_id=1, source_target_pairs={{0,8},{8,0},{1,9},{9,1},{2,10},{10,2},{3,11},{11,3},{4,12},{12,4},... | collective-permute-start | bytes 393224 | tf_op jit(solution)/shard_map/ppermute | solution.py:341
  10.1 1.9 %collective-permute-start.1 = (bf16[512,128]{1,0:T(8,128)(2,1)}, bf16[512,128]{1,0:T(8,128)(2,1)S(1)}, u32[]{:S(2)}, u32[]{:S(2)}) collective-permute-start(bf16[512,128]{1,0:T(8,128)(2,1)} %get-tuple-element.29.refs_0_), channel_id=1, source_target_pairs={{0,16},{16,32},{32,48},{48,64},{64,80},{80,96},{96,112},{112,0},{1... | collective-permute-start | bytes 393224 | tf_op jit(solution)/shard_map/ppermute | solution.py:337
  12.0 2.0 %collective-permute-done.refs_1_ = bf16[512,128]{1,0:T(8,128)(2,1)S(1)} collective-permute-done((bf16[512,128]{1,0:T(8,128)(2,1)}, bf16[512,128]{1,0:T(8,128)(2,1)S(1)}, u32[]{:S(2)}, u32[]{:S(2)}) %collective-permute-start) | collective-permute-done | bytes 131104 | tf_op jit(solution)/shard_map/ppermute | solution.py:341
  14.0 5.9 %collective-permute-start.4 = (bf16[512,128]{1,0:T(8,128)(2,1)S(1)}, bf16[512,128]{1,0:T(8,128)(2,1)S(1)}, u32[]{:S(2)}, u32[]{:S(2)}) collective-permute-start(bf16[512,128]{1,0:T(8,128)(2,1)S(1)} %collective-permute-done.refs_1_), channel_id=1, source_target_pairs={{0,112},{16,0},{32,16},{48,32},{64,48},{80,64},{96,80},{112,96},{1... | collective-permute-start | bytes 393224 | tf_op jit(solution)/shard_map/ppermute | solution.py:337
  19.8 1.0 collective-permute-start.3
  20.8 1.0 collective-permute-start.2
  21.9 0.0 collective-permute-start.5
  21.9 1.2 %collective-permute-done.4.refs_5_ = bf16[512,128]{1,0:T(8,128)(2,1)S(1)} collective-permute-done((bf16[512,128]{1,0:T(8,128)(2,1)S(1)}, bf16[512,128]{1,0:T(8,128)(2,1)S(1)}, u32[]{:S(2)}, u32[]{:S(2)}) %collective-permute-start.4) | collective-permute-done | bytes 131104 | tf_op jit(solution)/shard_map/ppermute | solution.py:337
  23.1 3.7 %collective-permute-start.8 = (bf16[512,128]{1,0:T(8,128)(2,1)S(1)}, bf16[512,128]{1,0:T(8,128)(2,1)S(1)}, u32[]{:S(2)}, u32[]{:S(2)}) collective-permute-start(bf16[512,128]{1,0:T(8,128)(2,1)S(1)} %collective-permute-done.4.refs_5_), channel_id=1, source_target_pairs={{0,112},{16,0},{32,16},{48,32},{64,48},{80,64},{96,80},{112,96},{1... | collective-permute-start | bytes 393224 | tf_op jit(solution)/shard_map/ppermute | solution.py:337
  26.8 1.9 %collective-permute-start.7 = (bf16[512,128]{1,0:T(8,128)(2,1)S(1)}, bf16[512,128]{1,0:T(8,128)(2,1)S(1)}, u32[]{:S(2)}, u32[]{:S(2)}) collective-permute-start(bf16[512,128]{1,0:T(8,128)(2,1)S(1)} %collective-permute-done.3.refs_4_), channel_id=1, source_target_pairs={{0,112},{16,0},{32,16},{48,32},{64,48},{80,64},{96,80},{112,96},{1... | collective-permute-start | bytes 393224 | tf_op jit(solution)/shard_map/ppermute | solution.py:337
  28.8 0.1 collective-permute-start.6
  28.9 0.1 collective-permute-start.9
  28.9 0.4 collective-permute-done.8.refs_9_
  29.3 3.7 %collective-permute-start.12 = (bf16[512,128]{1,0:T(8,128)(2,1)S(1)}, bf16[512,128]{1,0:T(8,128)(2,1)S(1)}, u32[]{:S(2)}, u32[]{:S(2)}) collective-permute-start(bf16[512,128]{1,0:T(8,128)(2,1)S(1)} %collective-permute-done.8.refs_9_), channel_id=1, source_target_pairs={{0,112},{16,0},{32,16},{48,32},{64,48},{80,64},{96,80},{112,96},{1... | collective-permute-start | bytes 393224 | tf_op jit(solution)/shard_map/ppermute | solution.py:337
  33.0 3.3 %collective-permute-start.11 = (bf16[512,128]{1,0:T(8,128)(2,1)S(1)}, bf16[512,128]{1,0:T(8,128)(2,1)S(1)}, u32[]{:S(2)}, u32[]{:S(2)}) collective-permute-start(bf16[512,128]{1,0:T(8,128)(2,1)S(1)} %collective-permute-done.7.refs_8_), channel_id=1, source_target_pairs={{0,112},{16,0},{32,16},{48,32},{64,48},{80,64},{96,80},{112,96},{1... | collective-permute-start | bytes 393224 | tf_op jit(solution)/shard_map/ppermute | solution.py:337
  36.3 1.5 %collective-permute-done.9.refs_10_ = bf16[512,128]{1,0:T(8,128)(2,1)S(1)} collective-permute-done((bf16[512,128]{1,0:T(8,128)(2,1)S(1)}, bf16[512,128]{1,0:T(8,128)(2,1)S(1)}, u32[]{:S(2)}, u32[]{:S(2)}) %collective-permute-start.9) | collective-permute-done | bytes 131104 | tf_op jit(solution)/shard_map/ppermute | solution.py:337
  37.8 3.2 %collective-permute-start.14 = (bf16[512,128]{1,0:T(8,128)(2,1)S(1)}, bf16[512,128]{1,0:T(8,128)(2,1)S(1)}, u32[]{:S(2)}, u32[]{:S(2)}) collective-permute-start(bf16[512,128]{1,0:T(8,128)(2,1)S(1)} %collective-permute-done.12.refs_13_), channel_id=1, source_target_pairs={{0,112},{16,0},{32,16},{48,32},{64,48},{80,64},{96,80},{112,96},{1... | collective-permute-start | bytes 393224 | tf_op jit(solution)/shard_map/ppermute | solution.py:337
  41.0 3.0 %collective-permute-start.16 = (bf16[256,1024]{1,0:T(8,128)(2,1)}, bf16[256,1024]{1,0:T(8,128)(2,1)S(1)}, u32[]{:S(2)}, u32[]{:S(2)}) collective-permute-start(bf16[256,1024]{1,0:T(8,128)(2,1)} %bitcast.26), channel_id=1, source_target_pairs={{0,8},{8,0},{1,9},{9,1},{2,10},{10,2},{3,11},{11,3},{4,12},{12,4},... | collective-permute-start | bytes 1572872 | tf_op jit(solution)/shard_map/ppermute | solution.py:341
  44.1 0.0 copy-start.7
  44.1 0.0 copy-start.5
  44.1 0.9 copy-done.5
  45.1 6.2 %shard_map.111 = (bf16[512,128]{1,0:T(8,128)(2,1)S(1)}, f32[512,128]{1,0:T(8,128)S(1)}, f32[8,8,128]{2,1,0:T(8,128)}) custom-call(s32[3]{0:T(128)S(1)} %copy-done.4, bf16[512,128]{1,0:T(8,128)(2,1)S(1)} %copy-done.5, bf16[512,128]{1,0:T(8,128)(2,1)S(1)} %collective-permute-done.refs_1_, bf16[512,128]{1,0:T(8,128)(2,1)S(1)} %collective-permute-done.1.refs_2_, ...), custom_call_target="tpu_custom_call" | custom-call | flops 1073741824 | bytes 3145740 | tf_op jit(solution)/shard_map/pallas_call | solution.py:43
  51.2 4.4 %all-to-all-start = ((f32[8,8,128]{2,1,0:T(8,128)}), f32[8,8,128]{2,1,0:T(8,128)S(1)}, u32[]{:S(2)}, u32[]{:S(2)}) async-start(f32[8,8,128]{2,1,0:T(8,128)} %get-tuple-element.32), calls=%async_computation | async-start | bytes 65536 | tf_op jit(solution)/shard_map/all_to_all | solution.py:391
  55.6 5.4 %shard_map.112 = (bf16[256,128]{1,0:T(8,128)(2,1)S(1)}, bf16[256,128]{1,0:T(8,128)(2,1)S(1)}) custom-call(s32[3]{0:T(128)S(1)} %copy-done.4, bf16[512,128]{1,0:T(8,128)(2,1)S(1)} %copy-done.6, bf16[512,128]{1,0:T(8,128)(2,1)S(1)} %collective-permute-done.refs_1_, bf16[512,128]{1,0:T(8,128)(2,1)S(1)} %collective-permute-done.1.refs_2_, ...), custom_call_target="tpu_custom_call" | custom-call | flops 1610612736 | bytes 3538956 | tf_op jit(solution)/shard_map/pallas_call | solution.py:43
  61.0 2.6 %all-to-all-done = f32[8,8,128]{2,1,0:T(8,128)S(1)} async-done(((f32[8,8,128]{2,1,0:T(8,128)}), f32[8,8,128]{2,1,0:T(8,128)S(1)}, u32[]{:S(2)}, u32[]{:S(2)}) %all-to-all-start) | async-done | bytes 32800 | tf_op jit(solution)/shard_map/all_to_all | solution.py:391
  63.7 3.0 %collective-permute-start.15 = (bf16[256,128]{1,0:T(8,128)(2,1)S(1)}, bf16[256,128]{1,0:T(8,128)(2,1)S(1)}, u32[]{:S(2)}, u32[]{:S(2)}) collective-permute-start(bf16[256,128]{1,0:T(8,128)(2,1)S(1)} %get-tuple-element.41.first_sent), channel_id=1, source_target_pairs={{0,8},{8,0},{1,9},{9,1},{2,10},{10,2},{3,11},{11,3},{4,12},{12,4},... | collective-permute-start | bytes 196616 | tf_op jit(solution)/shard_map/ppermute | solution.py:341
  66.7 0.9 copy-done.8
  67.6 6.8 %shard_map.113 = (bf16[256,128]{1,0:T(8,128)(2,1)S(1)}, bf16[256,128]{1,0:T(8,128)(2,1)S(1)}) custom-call(s32[3]{0:T(128)S(1)} %copy-done.4, bf16[512,128]{1,0:T(8,128)(2,1)S(1)} %copy-done.6, bf16[512,128]{1,0:T(8,128)(2,1)S(1)} %collective-permute-done.refs_1_, bf16[512,128]{1,0:T(8,128)(2,1)S(1)} %collective-permute-done.1.refs_2_, ...), custom_call_target="tpu_custom_call" | custom-call | flops 2147483648 | bytes 3178508 | tf_op jit(solution)/shard_map/pallas_call | solution.py:43
  74.4 1.6 %shard_map.114 = bf16[16,96,128]{2,1,0:T(8,128)(2,1)} custom-call(bf16[256,1024]{1,0:T(8,128)(2,1)S(1)} %bitcast.27, bf16[256,1024]{1,0:T(8,128)(2,1)S(1)} %collective-permute-done.16.tok_other, bf16[256,128]{1,0:T(8,128)(2,1)S(1)} %get-tuple-element.37.first, bf16[256,128]{1,0:T(8,128)(2,1)S(1)} %get-tuple-element.41.first_sent, ...), custom_call_target="tpu_custom_call" | custom-call | flops 268435456 | bytes 1310720 | tf_op jit(solution)/shard_map/pallas_call | solution.py:43
  76.0 5.0 %all-to-all-start.1 = ((bf16[16,96,128]{2,1,0:T(8,128)(2,1)}), bf16[16,96,128]{2,1,0:T(8,128)(2,1)S(1)}, u32[]{:S(2)}, u32[]{:S(2)}) async-start(bf16[16,96,128]{2,1,0:T(8,128)(2,1)} %shard_map.114), calls=%async_computation.1 | async-start | bytes 786432 | tf_op jit(solution)/shard_map/all_to_all | solution.py:419
  81.1 2.1 %collective-permute-start.17 = (bf16[256,128]{1,0:T(8,128)(2,1)S(1)}, bf16[256,128]{1,0:T(8,128)(2,1)S(1)}, u32[]{:S(2)}, u32[]{:S(2)}) collective-permute-start(bf16[256,128]{1,0:T(8,128)(2,1)S(1)} %get-tuple-element.44.second_sent), channel_id=1, source_target_pairs={{0,8},{8,0},{1,9},{9,1},{2,10},{10,2},{3,11},{11,3},{4,12},{12,4},... | collective-permute-start | bytes 196616 | tf_op jit(solution)/shard_map/ppermute | solution.py:341
  83.2 3.8 %collective-permute-done.17.second_other = bf16[256,128]{1,0:T(8,128)(2,1)S(1)} collective-permute-done((bf16[256,128]{1,0:T(8,128)(2,1)S(1)}, bf16[256,128]{1,0:T(8,128)(2,1)S(1)}, u32[]{:S(2)}, u32[]{:S(2)}) %collective-permute-start.17) | collective-permute-done | bytes 65568 | tf_op jit(solution)/shard_map/ppermute | solution.py:341
  86.9 4.5 %all-to-all-done.1.parts = bf16[16,96,128]{2,1,0:T(8,128)(2,1)S(1)} async-done(((bf16[16,96,128]{2,1,0:T(8,128)(2,1)}), bf16[16,96,128]{2,1,0:T(8,128)(2,1)S(1)}, u32[]{:S(2)}, u32[]{:S(2)}) %all-to-all-start.1) | async-done | bytes 393248 | tf_op jit(solution)/shard_map/all_to_all | solution.py:419
  91.4 1.0 shard_map.116
  92.4 5.9 %all-to-all-start.2 = ((bf16[32,96,128]{2,1,0:T(8,128)(2,1)}), bf16[32,96,128]{2,1,0:T(8,128)(2,1)S(1)}, u32[]{:S(2)}, u32[]{:S(2)}) async-start(bf16[32,96,128]{2,1,0:T(8,128)(2,1)} %shard_map.116), calls=%async_computation.2 | async-start | bytes 1572864 | tf_op jit(solution)/shard_map/all_to_all | solution.py:435
  98.3 1.7 %shard_map.115 = (bf16[256,128]{1,0:T(8,128)(2,1)}, f32[4,32,1024]{2,1,0:T(8,128)S(1)}, bf16[4,32,1024]{2,1,0:T(8,128)(2,1)S(1)}) custom-call(s32[3]{0:T(128)S(1)} %copy-done.4, bf16[256,128]{1,0:T(8,128)(2,1)S(1)} %get-tuple-element.37.first, bf16[256,128]{1,0:T(8,128)(2,1)S(1)} %collective-permute-done.15.first_other, ...), custom_call_target="tpu_custom_call" | custom-call | flops 201326592 | bytes 1048588 | tf_op jit(solution)/shard_map/pallas_call | solution.py:43
  100.0 1.5 %collective-permute-done.18 = bf16[4,32,1024]{2,1,0:T(8,128)(2,1)S(1)} collective-permute-done((bf16[4,32,1024]{2,1,0:T(8,128)(2,1)S(1)}, bf16[4,32,1024]{2,1,0:T(8,128)(2,1)S(1)}, u32[]{:S(2)}, u32[]{:S(2)}) %collective-permute-start.18) | collective-permute-done | bytes 262176 | tf_op jit(solution)/shard_map/ppermute | solution.py:428
  101.6 0.1 fusion.4
  101.7 1.7 %collective-permute-start.21 = (bf16[32,1024]{1,0:T(8,128)(2,1)S(1)}, bf16[32,1024]{1,0:T(8,128)(2,1)S(1)}, u32[]{:S(2)}, u32[]{:S(2)}) collective-permute-start(bf16[32,1024]{1,0:T(8,128)(2,1)S(1)} %get-tuple-element.56), channel_id=1, source_target_pairs={{0,6},{2,4},{4,2},{6,0},{1,7},{3,5},{5,3},{7,1},{8,14},{10,12},{12... | collective-permute-start | bytes 196616 | tf_op jit(solution)/shard_map/ppermute | solution.py:434
  103.3 0.9 collective-permute-start.20
  104.3 1.6 %collective-permute-start.19 = (bf16[32,1024]{1,0:T(8,128)(2,1)S(1)}, bf16[32,1024]{1,0:T(8,128)(2,1)S(1)}, u32[]{:S(2)}, u32[]{:S(2)}) collective-permute-start(bf16[32,1024]{1,0:T(8,128)(2,1)S(1)} %get-tuple-element.55), channel_id=1, source_target_pairs={{0,2},{2,0},{4,6},{6,4},{1,3},{3,1},{5,7},{7,5},{8,10},{10,8},{12,... | collective-permute-start | bytes 196616 | tf_op jit(solution)/shard_map/ppermute | solution.py:434
  105.9 0.2 collective-permute-done.21
  106.0 3.7 %collective-permute-done.20 = bf16[32,1024]{1,0:T(8,128)(2,1)S(1)} collective-permute-done((bf16[32,1024]{1,0:T(8,128)(2,1)S(1)}, bf16[32,1024]{1,0:T(8,128)(2,1)S(1)}, u32[]{:S(2)}, u32[]{:S(2)}) %collective-permute-start.20) | collective-permute-done | bytes 65568 | tf_op jit(solution)/shard_map/ppermute | solution.py:434
  109.7 0.7 fusion.3
  110.4 3.8 %all-to-all-done.2.parts = bf16[32,96,128]{2,1,0:T(8,128)(2,1)S(1)} async-done(((bf16[32,96,128]{2,1,0:T(8,128)(2,1)}), bf16[32,96,128]{2,1,0:T(8,128)(2,1)S(1)}, u32[]{:S(2)}, u32[]{:S(2)}) %all-to-all-start.2) | async-done | bytes 786464 | tf_op jit(solution)/shard_map/all_to_all | solution.py:435
  114.2 1.4 %shard_map.117 = (f32[1024,128]{1,0:T(8,128)}, f32[1024,128]{1,0:T(8,128)}, f32[1024,128]{1,0:T(8,128)}) custom-call(bf16[32,96,128]{2,1,0:T(8,128)(2,1)S(1)} %all-to-all-done.2.parts), custom_call_target="tpu_custom_call" | custom-call | bytes 786432 | tf_op jit(solution)/shard_map/pallas_call | solution.py:43
  (32 shorter events, 0.1 us)
Async XLA Ops:
  6.9 7.0 %collective-permute-start = (bf16[512,128]{1,0:T(8,128)(2,1)}, bf16[512,128]{1,0:T(8,128)(2,1)S(1)}, u32[]{:S(2)}, u32[]{:S(2)}) collective-permute-start(bf16[512,128]{1,0:T(8,128)(2,1)} %get-tuple-element.30), channel_id=1, source_target_pairs={{0,8},{8,0},{1,9},{9,1},{2,10},{10,2},{3,11},{11,3},{4,12},{12,4},... | collective-permute-start | bytes 393224 | tf_op jit(solution)/shard_map/ppermute | solution.py:341
  10.1 34.1 %copy-start.4 = (s32[3]{0:T(128)S(1)}, s32[3]{0:T(128)}, u32[]{:S(2)}) copy-start(s32[3]{0:T(128)} %pad_add_fusion.place) | copy-start | bytes 40
  10.1 11.8 %collective-permute-start.1 = (bf16[512,128]{1,0:T(8,128)(2,1)}, bf16[512,128]{1,0:T(8,128)(2,1)S(1)}, u32[]{:S(2)}, u32[]{:S(2)}) collective-permute-start(bf16[512,128]{1,0:T(8,128)(2,1)} %get-tuple-element.29.refs_0_), channel_id=1, source_target_pairs={{0,16},{16,32},{32,48},{48,64},{64,80},{80,96},{96,112},{112,0},{1... | collective-permute-start | bytes 393224 | tf_op jit(solution)/shard_map/ppermute | solution.py:337
  14.0 9.1 %collective-permute-start.4 = (bf16[512,128]{1,0:T(8,128)(2,1)S(1)}, bf16[512,128]{1,0:T(8,128)(2,1)S(1)}, u32[]{:S(2)}, u32[]{:S(2)}) collective-permute-start(bf16[512,128]{1,0:T(8,128)(2,1)S(1)} %collective-permute-done.refs_1_), channel_id=1, source_target_pairs={{0,112},{16,0},{32,16},{48,32},{64,48},{80,64},{96,80},{112,96},{1... | collective-permute-start | bytes 393224 | tf_op jit(solution)/shard_map/ppermute | solution.py:337
  19.8 7.0 %collective-permute-start.3 = (bf16[512,128]{1,0:T(8,128)(2,1)}, bf16[512,128]{1,0:T(8,128)(2,1)S(1)}, u32[]{:S(2)}, u32[]{:S(2)}) collective-permute-start(bf16[512,128]{1,0:T(8,128)(2,1)} %get-tuple-element.29.refs_0_), channel_id=1, source_target_pairs={{0,112},{16,0},{32,16},{48,32},{64,48},{80,64},{96,80},{112,96},{1... | collective-permute-start | bytes 393224 | tf_op jit(solution)/shard_map/ppermute | solution.py:337
  20.8 7.9 %collective-permute-start.2 = (bf16[512,128]{1,0:T(8,128)(2,1)S(1)}, bf16[512,128]{1,0:T(8,128)(2,1)S(1)}, u32[]{:S(2)}, u32[]{:S(2)}) collective-permute-start(bf16[512,128]{1,0:T(8,128)(2,1)S(1)} %collective-permute-done.refs_1_), channel_id=1, source_target_pairs={{0,16},{16,32},{32,48},{48,64},{64,80},{80,96},{96,112},{112,0},{1... | collective-permute-start | bytes 393224 | tf_op jit(solution)/shard_map/ppermute | solution.py:337
  21.9 7.0 %collective-permute-start.5 = (bf16[512,128]{1,0:T(8,128)(2,1)S(1)}, bf16[512,128]{1,0:T(8,128)(2,1)S(1)}, u32[]{:S(2)}, u32[]{:S(2)}) collective-permute-start(bf16[512,128]{1,0:T(8,128)(2,1)S(1)} %collective-permute-done.1.refs_2_), channel_id=1, source_target_pairs={{0,16},{16,32},{32,48},{48,64},{64,80},{80,96},{96,112},{112,0},{1... | collective-permute-start | bytes 393224 | tf_op jit(solution)/shard_map/ppermute | solution.py:337
  23.1 6.2 %collective-permute-start.8 = (bf16[512,128]{1,0:T(8,128)(2,1)S(1)}, bf16[512,128]{1,0:T(8,128)(2,1)S(1)}, u32[]{:S(2)}, u32[]{:S(2)}) collective-permute-start(bf16[512,128]{1,0:T(8,128)(2,1)S(1)} %collective-permute-done.4.refs_5_), channel_id=1, source_target_pairs={{0,112},{16,0},{32,16},{48,32},{64,48},{80,64},{96,80},{112,96},{1... | collective-permute-start | bytes 393224 | tf_op jit(solution)/shard_map/ppermute | solution.py:337
  26.8 6.2 %collective-permute-start.7 = (bf16[512,128]{1,0:T(8,128)(2,1)S(1)}, bf16[512,128]{1,0:T(8,128)(2,1)S(1)}, u32[]{:S(2)}, u32[]{:S(2)}) collective-permute-start(bf16[512,128]{1,0:T(8,128)(2,1)S(1)} %collective-permute-done.3.refs_4_), channel_id=1, source_target_pairs={{0,112},{16,0},{32,16},{48,32},{64,48},{80,64},{96,80},{112,96},{1... | collective-permute-start | bytes 393224 | tf_op jit(solution)/shard_map/ppermute | solution.py:337
  28.8 7.6 %collective-permute-start.6 = (bf16[512,128]{1,0:T(8,128)(2,1)S(1)}, bf16[512,128]{1,0:T(8,128)(2,1)S(1)}, u32[]{:S(2)}, u32[]{:S(2)}) collective-permute-start(bf16[512,128]{1,0:T(8,128)(2,1)S(1)} %collective-permute-done.2.refs_3_), channel_id=1, source_target_pairs={{0,16},{16,32},{32,48},{48,64},{64,80},{80,96},{96,112},{112,0},{1... | collective-permute-start | bytes 393224 | tf_op jit(solution)/shard_map/ppermute | solution.py:337
  28.9 8.9 %collective-permute-start.9 = (bf16[512,128]{1,0:T(8,128)(2,1)S(1)}, bf16[512,128]{1,0:T(8,128)(2,1)S(1)}, u32[]{:S(2)}, u32[]{:S(2)}) collective-permute-start(bf16[512,128]{1,0:T(8,128)(2,1)S(1)} %collective-permute-done.5.refs_6_), channel_id=1, source_target_pairs={{0,16},{16,32},{32,48},{48,64},{64,80},{80,96},{96,112},{112,0},{1... | collective-permute-start | bytes 393224 | tf_op jit(solution)/shard_map/ppermute | solution.py:337
  29.3 8.5 %collective-permute-start.12 = (bf16[512,128]{1,0:T(8,128)(2,1)S(1)}, bf16[512,128]{1,0:T(8,128)(2,1)S(1)}, u32[]{:S(2)}, u32[]{:S(2)}) collective-permute-start(bf16[512,128]{1,0:T(8,128)(2,1)S(1)} %collective-permute-done.8.refs_9_), channel_id=1, source_target_pairs={{0,112},{16,0},{32,16},{48,32},{64,48},{80,64},{96,80},{112,96},{1... | collective-permute-start | bytes 393224 | tf_op jit(solution)/shard_map/ppermute | solution.py:337
  33.0 11.1 %collective-permute-start.11 = (bf16[512,128]{1,0:T(8,128)(2,1)S(1)}, bf16[512,128]{1,0:T(8,128)(2,1)S(1)}, u32[]{:S(2)}, u32[]{:S(2)}) collective-permute-start(bf16[512,128]{1,0:T(8,128)(2,1)S(1)} %collective-permute-done.7.refs_8_), channel_id=1, source_target_pairs={{0,112},{16,0},{32,16},{48,32},{64,48},{80,64},{96,80},{112,96},{1... | collective-permute-start | bytes 393224 | tf_op jit(solution)/shard_map/ppermute | solution.py:337
  36.3 7.7 %collective-permute-start.10 = (bf16[512,128]{1,0:T(8,128)(2,1)S(1)}, bf16[512,128]{1,0:T(8,128)(2,1)S(1)}, u32[]{:S(2)}, u32[]{:S(2)}) collective-permute-start(bf16[512,128]{1,0:T(8,128)(2,1)S(1)} %collective-permute-done.6.refs_7_), channel_id=1, source_target_pairs={{0,16},{16,32},{32,48},{48,64},{64,80},{80,96},{96,112},{112,0},{1... | collective-permute-start | bytes 393224 | tf_op jit(solution)/shard_map/ppermute | solution.py:337
  37.8 6.3 %collective-permute-start.13 = (bf16[512,128]{1,0:T(8,128)(2,1)S(1)}, bf16[512,128]{1,0:T(8,128)(2,1)S(1)}, u32[]{:S(2)}, u32[]{:S(2)}) collective-permute-start(bf16[512,128]{1,0:T(8,128)(2,1)S(1)} %collective-permute-done.9.refs_10_), channel_id=1, source_target_pairs={{0,16},{16,32},{32,48},{48,64},{64,80},{80,96},{96,112},{112,0},{1... | collective-permute-start | bytes 393224 | tf_op jit(solution)/shard_map/ppermute | solution.py:337
  37.8 6.3 %collective-permute-start.14 = (bf16[512,128]{1,0:T(8,128)(2,1)S(1)}, bf16[512,128]{1,0:T(8,128)(2,1)S(1)}, u32[]{:S(2)}, u32[]{:S(2)}) collective-permute-start(bf16[512,128]{1,0:T(8,128)(2,1)S(1)} %collective-permute-done.12.refs_13_), channel_id=1, source_target_pairs={{0,112},{16,0},{32,16},{48,32},{64,48},{80,64},{96,80},{112,96},{1... | collective-permute-start | bytes 393224 | tf_op jit(solution)/shard_map/ppermute | solution.py:337
  41.0 33.4 %collective-permute-start.16 = (bf16[256,1024]{1,0:T(8,128)(2,1)}, bf16[256,1024]{1,0:T(8,128)(2,1)S(1)}, u32[]{:S(2)}, u32[]{:S(2)}) collective-permute-start(bf16[256,1024]{1,0:T(8,128)(2,1)} %bitcast.26), channel_id=1, source_target_pairs={{0,8},{8,0},{1,9},{9,1},{2,10},{10,2},{3,11},{11,3},{4,12},{12,4},... | collective-permute-start | bytes 1572872 | tf_op jit(solution)/shard_map/ppermute | solution.py:341
  44.1 11.5 %copy-start.7 = (bf16[512,128]{1,0:T(8,128)(2,1)}, bf16[512,128]{1,0:T(8,128)(2,1)S(1)}, u32[]{:S(2)}) copy-start(bf16[512,128]{1,0:T(8,128)(2,1)S(1)} %collective-permute-done.14.refs_15_) | copy-start | bytes 393220
  44.1 1.0 copy-start.5
  45.1 10.6 %copy-start.6 = (bf16[512,128]{1,0:T(8,128)(2,1)S(1)}, bf16[512,128]{1,0:T(8,128)(2,1)}, u32[]{:S(2)}) copy-start(bf16[512,128]{1,0:T(8,128)(2,1)} %get-tuple-element.29.refs_0_) | copy-start | bytes 393220
  51.2 12.4 %all-to-all-start = ((f32[8,8,128]{2,1,0:T(8,128)}), f32[8,8,128]{2,1,0:T(8,128)S(1)}, u32[]{:S(2)}, u32[]{:S(2)}) async-start(f32[8,8,128]{2,1,0:T(8,128)} %get-tuple-element.32), calls=%async_computation | async-start | bytes 65536 | tf_op jit(solution)/shard_map/all_to_all | solution.py:391
  63.7 10.8 %copy-start = (bf16[1,256,1024]{2,1,0:T(8,128)(2,1)S(1)}, bf16[1,256,1024]{2,1,0:T(8,128)(2,1)}, u32[]{:S(2)}) copy-start(bf16[1,256,1024]{2,1,0:T(8,128)(2,1)} %param.7) | copy-start | bytes 1572868
  63.7 10.8 %collective-permute-start.15 = (bf16[256,128]{1,0:T(8,128)(2,1)S(1)}, bf16[256,128]{1,0:T(8,128)(2,1)S(1)}, u32[]{:S(2)}, u32[]{:S(2)}) collective-permute-start(bf16[256,128]{1,0:T(8,128)(2,1)S(1)} %get-tuple-element.41.first_sent), channel_id=1, source_target_pairs={{0,8},{8,0},{1,9},{9,1},{2,10},{10,2},{3,11},{11,3},{4,12},{12,4},... | collective-permute-start | bytes 196616 | tf_op jit(solution)/shard_map/ppermute | solution.py:341
  66.7 0.9 copy-start.8
  76.0 15.4 %all-to-all-start.1 = ((bf16[16,96,128]{2,1,0:T(8,128)(2,1)}), bf16[16,96,128]{2,1,0:T(8,128)(2,1)S(1)}, u32[]{:S(2)}, u32[]{:S(2)}) async-start(bf16[16,96,128]{2,1,0:T(8,128)(2,1)} %shard_map.114), calls=%async_computation.1 | async-start | bytes 786432 | tf_op jit(solution)/shard_map/all_to_all | solution.py:419
  81.1 5.9 %collective-permute-start.17 = (bf16[256,128]{1,0:T(8,128)(2,1)S(1)}, bf16[256,128]{1,0:T(8,128)(2,1)S(1)}, u32[]{:S(2)}, u32[]{:S(2)}) collective-permute-start(bf16[256,128]{1,0:T(8,128)(2,1)S(1)} %get-tuple-element.44.second_sent), channel_id=1, source_target_pairs={{0,8},{8,0},{1,9},{9,1},{2,10},{10,2},{3,11},{11,3},{4,12},{12,4},... | collective-permute-start | bytes 196616 | tf_op jit(solution)/shard_map/ppermute | solution.py:341
  92.3 5.9 %copy-start.1 = (bf16[1024,128]{1,0:T(8,128)(2,1)S(1)}, bf16[1024,128]{1,0:T(8,128)(2,1)}, u32[]{:S(2)}) copy-start(bf16[1024,128]{1,0:T(8,128)(2,1)} %wq.3) | copy-start | bytes 786436
  92.3 5.9 %copy-start.2 = (bf16[1024,128]{1,0:T(8,128)(2,1)S(1)}, bf16[1024,128]{1,0:T(8,128)(2,1)}, u32[]{:S(2)}) copy-start(bf16[1024,128]{1,0:T(8,128)(2,1)} %wk.3) | copy-start | bytes 786436
  92.3 5.9 %copy-start.3 = (bf16[1024,128]{1,0:T(8,128)(2,1)S(1)}, bf16[1024,128]{1,0:T(8,128)(2,1)}, u32[]{:S(2)}) copy-start(bf16[1024,128]{1,0:T(8,128)(2,1)} %wv.3) | copy-start | bytes 786436
  92.4 21.8 %all-to-all-start.2 = ((bf16[32,96,128]{2,1,0:T(8,128)(2,1)}), bf16[32,96,128]{2,1,0:T(8,128)(2,1)S(1)}, u32[]{:S(2)}, u32[]{:S(2)}) async-start(bf16[32,96,128]{2,1,0:T(8,128)(2,1)} %shard_map.116), calls=%async_computation.2 | async-start | bytes 1572864 | tf_op jit(solution)/shard_map/all_to_all | solution.py:435
  100.0 1.5 %collective-permute-start.18 = (bf16[4,32,1024]{2,1,0:T(8,128)(2,1)S(1)}, bf16[4,32,1024]{2,1,0:T(8,128)(2,1)S(1)}, u32[]{:S(2)}, u32[]{:S(2)}) collective-permute-start(bf16[4,32,1024]{2,1,0:T(8,128)(2,1)S(1)} %get-tuple-element.48), channel_id=1, source_target_pairs={{0,1},{1,0},{2,3},{3,2},{4,5},{5,4},{6,7},{7,6},{8,9},{9,8},{10,11... | collective-permute-start | bytes 786440 | tf_op jit(solution)/shard_map/ppermute | solution.py:428
  101.7 4.4 %collective-permute-start.21 = (bf16[32,1024]{1,0:T(8,128)(2,1)S(1)}, bf16[32,1024]{1,0:T(8,128)(2,1)S(1)}, u32[]{:S(2)}, u32[]{:S(2)}) collective-permute-start(bf16[32,1024]{1,0:T(8,128)(2,1)S(1)} %get-tuple-element.56), channel_id=1, source_target_pairs={{0,6},{2,4},{4,2},{6,0},{1,7},{3,5},{5,3},{7,1},{8,14},{10,12},{12... | collective-permute-start | bytes 196616 | tf_op jit(solution)/shard_map/ppermute | solution.py:434
  103.3 6.4 %collective-permute-start.20 = (bf16[32,1024]{1,0:T(8,128)(2,1)S(1)}, bf16[32,1024]{1,0:T(8,128)(2,1)S(1)}, u32[]{:S(2)}, u32[]{:S(2)}) collective-permute-start(bf16[32,1024]{1,0:T(8,128)(2,1)S(1)} %get-tuple-element.57), channel_id=1, source_target_pairs={{0,4},{2,6},{4,0},{6,2},{1,5},{3,7},{5,1},{7,3},{8,12},{10,14},{12... | collective-permute-start | bytes 196616 | tf_op jit(solution)/shard_map/ppermute | solution.py:434
  104.3 5.4 %collective-permute-start.19 = (bf16[32,1024]{1,0:T(8,128)(2,1)S(1)}, bf16[32,1024]{1,0:T(8,128)(2,1)S(1)}, u32[]{:S(2)}, u32[]{:S(2)}) collective-permute-start(bf16[32,1024]{1,0:T(8,128)(2,1)S(1)} %get-tuple-element.55), channel_id=1, source_target_pairs={{0,2},{2,0},{4,6},{6,4},{1,3},{3,1},{5,7},{7,5},{8,10},{10,8},{12,... | collective-permute-start | bytes 196616 | tf_op jit(solution)/shard_map/ppermute | solution.py:434

commit v5 on v4

--- a/solution.py
+++ b/solution.py
@@ -17,6 +17,7 @@
 NEG = -1e30
 LIMIT = 51 << 20
 CHUNK = 512
+FEATURE_LIMIT = 64 << 20
 BF = jnp.bfloat16
 F32 = jnp.float32
 
@@ -57,7 +58,7 @@
     return lax.broadcasted_iota(jnp.int32, (rows, 128), 1) < HD
 
 
-def document_features(place, lengths, spots, feat):
+def feature_kernel(place, lengths, spots, feat):
     flip = place[0]
     lane = lax.broadcasted_iota(jnp.int32, (RUN, 128), 1)
     last = lane == HD + 8
@@ -74,8 +75,8 @@
         half = lax.rem(block, 2)
         run = (block - half) + jnp.where(half == flip, 0, 1)
         pos = run * RUN + lax.broadcasted_iota(jnp.int32, (RUN, RUN), 0)
-        hit = jnp.where(pos == spots[...], 1.0, 0.0).astype(BF)
-        other = 1.0 - dot(hit, jnp.ones((RUN, 128), BF))
+        hit = jnp.max(jnp.where(pos == spots[...], 1.0, 0.0), axis=1, keepdims=True)
+        other = 1.0 - hit
         pos128 = run * RUN + lax.broadcasted_iota(jnp.int32, (RUN, 128), 0)
         member = (pos128 >= starts) & (pos128 < ends)
         row = jnp.where(last, other, jnp.where(member, 1.0, 0.0))
@@ -86,13 +87,12 @@
     lax.fori_loop(0, 2 * NSEC, one, 0)
 
 
-def project_kernel(place, lengths, tok, wq, wk, wv, cot, spots, mine, theirs, feat, *scratch):
+def project_kernel(place, tok, wq, wk, wv, cot, mine, theirs, *scratch):
     tok_v, wk_v, wv_v, wq_v, cot_v, sems = scratch
     pairs = ((tok, tok_v), (wk, wk_v), (wv, wv_v), (wq, wq_v), (cot, cot_v))
     copies = [pltpu.make_async_copy(a, b, sems.at[i]) for i, (a, b) in enumerate(pairs)]
     for copy in copies:
         copy.start()
-    document_features(place, lengths, spots, feat)
     first = place[0] == 0
     copies[0].wait()
     t = tok_v[...]
@@ -245,8 +245,8 @@
     packed_other[...] = out[RUN:]
 
 
-def keys_kernel(chunk, place, *refs):
-    pieces, (feat, stats, packed, packed_other, stats_s, sems) = refs[: 2 * NSEC], refs[2 * NSEC :]
+def keys_kernel(half, place, *refs):
+    pieces, (feat, stats, *given, packed, stats_s, sems) = refs[: 2 * NSEC], refs[2 * NSEC :]
     flip, own = place[0], place[1]
     copies = []
     for r, offset in enumerate(OFFSETS):
@@ -254,12 +254,11 @@
         to = stats_s.at[pl.ds(r * 8, 8)]
         copies.append(pltpu.make_async_copy(stats.at[pl.ds(at, 8)], to, sems.at[r]))
         copies[-1].start()
-    own_kv = part_of(pieces, 0, 0)
-    joined = join_key(own_kv, features_at(feat, own))
+    own_kv = pieces[half][:RUN]
+    joined = join_key(own_kv, features_at(feat, own)[half * RUN : (half + 1) * RUN])
     near_keys, value = less_global(joined), right_half(own_kv)
-    key_places = places(own, flip, 0)
-    count = SEC // chunk
-    state = [None] * count
+    key_places = places(own, flip, 0)[half * RUN : (half + 1) * RUN]
+    state = None
     for copy in copies:
         copy.wait()
     for r, offset in enumerate(OFFSETS):
@@ -269,26 +268,25 @@
         st = stats_s[r * 8 : r * 8 + 8]
         log_total = jnp.concatenate([st[i : i + 1] for i in range(4)], axis=1)
         delta = jnp.concatenate([st[i : i + 1] for i in range(4, 8)], axis=1)
-        for c in range(count):
-            rows = slice(c * chunk, (c + 1) * chunk)
-            s = dot(joined[rows], qp, NT)
-            if r < 3:
-                away = key_places[rows] - places(section, flip, 1)
-                s = jnp.where(jnp.abs(away) <= HALF, dot(near_keys[rows], qp, NT), s)
-            p = jnp.exp(s - log_total)
-            ds = p * (dot(value[rows], qc, NT) - delta)
-            both = dot(ds.astype(BF), qc), dot(p.astype(BF), qc)
-            state[c] = both if r == 0 else (state[c][0] + both[0], state[c][1] + both[1])
-    key_acc = jnp.concatenate([x[0] for x in state], axis=0) if count > 1 else state[0][0]
-    value_acc = jnp.concatenate([x[1] for x in state], axis=0) if count > 1 else state[0][1]
-    out = jnp.where(low_lanes(SEC), key_acc * (1.0 / math.sqrt(HD)), value_acc).astype(BF)
-    packed[...] = out[:RUN]
-    packed_other[...] = out[RUN:]
-
-
-def weights_kernel(tok, tok_other, first, first_sent, second, second_sent, out):
-    qa = dot(tok[...], first[...], TN) + dot(tok_other[...], first_sent[...], TN)
-    kv = dot(tok[...], second[...], TN) + dot(tok_other[...], second_sent[...], TN)
+        s = dot(joined, qp, NT)
+        if r < 3:
+            away = key_places - places(section, flip, 1)
+            s = jnp.where(jnp.abs(away) <= HALF, dot(near_keys, qp, NT), s)
+        p = jnp.exp(s - log_total)
+        ds = p * (dot(value, qc, NT) - delta)
+        both = dot(ds.astype(BF), qc), dot(p.astype(BF), qc)
+        state = both if r == 0 else (state[0] + both[0], state[1] + both[1])
+    out = jnp.where(low_lanes(RUN), state[0] * (1.0 / math.sqrt(HD)), state[1]).astype(BF)
+    if half == 1:
+        packed[:RUN] = given[0][...]
+        packed[RUN:] = out
+    else:
+        packed[...] = out
+
+
+def weights_kernel(tok, tok_other, first, second, sent, out):
+    qa = dot(tok[...], first[...], TN) + dot(tok_other[...], sent[:RUN], TN)
+    kv = dot(tok[...], second[...], TN) + dot(tok_other[...], sent[RUN:], TN)
     for p in range(16):
         out[p, :64] = kv[p * 64 : (p + 1) * 64].astype(BF)
         upper = qa[p * 32 : (p + 1) * 32, :HD]
@@ -305,10 +303,10 @@
         out[p] = total
 
 
-def input_kernel(place, first, first_other, second, second_other, wq, wk, wv, att, keep, send):
+def input_kernel(place, first, second, arrived, wq, wk, wv, att, keep, send):
     swap = place[0] != 0
     core = place[2]
-    a, b, c, d = first[...], first_other[...], second[...], second_other[...]
+    a, b, c, d = first[...], arrived[:RUN], second[...], arrived[RUN:]
     a, b = jnp.where(swap, b, a), jnp.where(swap, a, b)
     c, d = jnp.where(swap, d, c), jnp.where(swap, c, d)
     dq = jnp.concatenate([a[:, :HD], b[:, :HD]], axis=1)
@@ -347,10 +345,10 @@
     xh, z, y, core = (lax.axis_index(a) for a in ("xh", Z, "y", "core"))
     place = jnp.stack([xh, z, core]).astype(jnp.int32)
     weight = pltpu.VMEM((1024, 128), BF)
-    mine, theirs, feat = call(
+    mine, theirs = call(
         project_kernel,
-        (shape((SEC, 128), BF),) * 2 + (shape((NSEC * SEC, 128), BF),),
-        (place, doc_lengths, tok, wq, wk, wv, cot, global_positions),
+        (shape((SEC, 128), BF),) * 2,
+        (place, tok, wq, wk, wv, cot),
         scratch=(
             pltpu.VMEM((RUN, 1024), BF),
             weight,
@@ -360,7 +358,6 @@
             pltpu.SemaphoreType.DMA((5,)),
         ),
         flops=6 * 256 * 1024 * 128,
-        smem=2,
         manual=5,
         limit=64 << 20,
     )
@@ -371,6 +368,15 @@
 
     tie = lax.optimization_barrier
     lower_a, upper_a = [mine, shift(mine, 1)], [mine, shift(mine, -1)]
+    late, mine = tie((place, mine))
+    feat = call(
+        feature_kernel,
+        shape((NSEC * SEC, 128), BF),
+        (late, doc_lengths, global_positions),
+        smem=2,
+        limit=FEATURE_LIMIT,
+    )
+    other, feat = tie((other, feat))
     lower_b, upper_b = [other, shift(other, 1)], [other, shift(other, -1)]
     for x, step in ((lower_a, 1), (upper_a, -1), (lower_b, 1), (upper_b, -1)):
         x.append(shift(x[1], step))
@@ -397,35 +403,40 @@
         flops=2 * 128 * 3 * pairs,
         transcendentals=pairs,
     )
-    all_stats, first, first_sent = lax.optimization_barrier((all_stats, first, first_sent))
-    first_other = swap(first_sent)
-    second, second_sent = call(
-        functools.partial(keys_kernel, CHUNK),
-        (half, half),
-        (place, *pieces, feat, all_stats),
-        scratch=(pltpu.VMEM((NSEC * 8, 128), F32), pltpu.SemaphoreType.DMA((NSEC,))),
-        flops=2 * 128 * 4 * pairs,
-        transcendentals=pairs,
-    )
-    second, second_sent, first_other = lax.optimization_barrier((second, second_sent, first_other))
-    second_other = swap(second_sent)
+    all_stats, first, first_sent = tie((all_stats, first, first_sent))
+
+    def keys(half, stats, given, out):
+        return call(
+            functools.partial(keys_kernel, half),
+            out,
+            (place, *pieces, feat, stats, *given),
+            scratch=(pltpu.VMEM((NSEC * 8, 128), F32), pltpu.SemaphoreType.DMA((NSEC,))),
+            flops=2 * 128 * 2 * pairs,
+            transcendentals=pairs // 2,
+        )
+
+    sent = keys(1, all_stats, (first_sent,), shape((SEC, 128), BF))
+    all_stats, sent = tie((all_stats, sent))
+    back = swap(sent)
+    second = keys(0, all_stats, (), half)
     partial = call(
         weights_kernel,
         shape((16, 96, 128), BF),
-        (tok, tok_other, first, first_sent, second, second_sent),
+        (tok, tok_other, first, second, sent),
         flops=2 * 512 * 1024 * 256,
         smem=0,
     )
+    partial, back = tie((partial, back))
     partial = lax.all_to_all(partial, ("b",) + Z, 0, 0, tiled=True)
-    partial, second_other = tie((partial, second_other))
-    total = call(sum_kernel, shape((32, 96, 128), BF), (partial,), smem=0)
     att, keep, send = call(
         input_kernel,
         (half, shape((4, 32, 1024), F32), shape((4, 32, 1024), BF)),
-        (place, first, first_other, second, second_other, wq, wk, wv),
+        (place, first, second, back, wq, wk, wv),
         flops=6 * 256 * 1024 * 128,
     )
     arrived = lax.ppermute(send, "core", [(0, 1), (1, 0)])
+    partial, arrived = tie((partial, arrived))
+    total = call(sum_kernel, shape((32, 96, 128), BF), (partial,), smem=0)
     both = keep + arrived.astype(F32)
     share = lax.dynamic_index_in_dim(both, y, 0, False)
     both_bf = both.astype(BF)

time: 116 us -> 121 us (1.043)
  Pallas kernels: 29.8 us -> 33.8 us
  waiting for transfers between devices: 25.1 us -> 28.7 us
  starting transfers between devices: 56.6 us -> 53.5 us
    all_to_all x1, waiting for transfers between devices: 3.79 us -> 11.4 us  [on_device(): total = lax.all_to_all(total, ('b',) + CTX, 0, 0, tiled=True)]
    ppermute x4 -> x3, waiting for transfers between devices: 5.77 us -> 0.01 us  [swap(): return lax.ppermute(a, 'xh', [(0, 1), (1, 0)])]
    pallas_call x8 -> x10, Pallas kernels: 29.8 us -> 33.8 us  [call(): pl.pallas_call(kernel, out_shape=outs, in_specs=specs, out_specs=jax.tree...]
    all_to_all x1, waiting for transfers between devices: 4.46 us -> 6.99 us  [on_device(): partial = lax.all_to_all(partial, ('b',) + Z, 0, 0, tiled=True)]
    ppermute x4 -> x3, starting transfers between devices: 11.2 us -> 8.84 us  [swap(): return lax.ppermute(a, 'xh', [(0, 1), (1, 0)])]
    ppermute x14, starting transfers between devices: 25.9 us -> 23.8 us  [shift(): return lax.ppermute(a, Z, [(i, (i + step) % NSEC) for i in range(NSEC)])]
  transfers between devices with their start and end apart: 25 -> 24, of which waited for: 11 -> 10; matrix products, arithmetic and copies ran while one was open for 1% -> 1% of each run, Pallas kernels for 17% -> 23%
where the time goes in v5:
time: 121 us; the launch traced here: 120 us
  starting transfers between devices  53.5 us (44%)
  Pallas kernels  33.8 us (28%)
  waiting for transfers between devices  28.7 us (24%)
  local copies, waits for them, and re-layouts  2.24 us (2%)
  other arithmetic  1.32 us (1%)
    pallas_call x10, Pallas kernels, call(): pl.pallas_call(kernel, out_shape=outs, in_specs=specs, out_specs=jax.tree...  33.8 us
    ppermute x14, starting transfers between devices, shift(): return lax.ppermute(a, Z, [(i, (i + step) % NSEC) for i in range(NSEC)])  23.8 us
    all_to_all x1, waiting for transfers between devices, on_device(): total = lax.all_to_all(total, ('b',) + CTX, 0, 0, tiled=True)  11.4 us
    ppermute x3, starting transfers between devices, swap(): return lax.ppermute(a, 'xh', [(0, 1), (1, 0)])  8.84 us
    all_to_all x1, waiting for transfers between devices, on_device(): partial = lax.all_to_all(partial, ('b',) + Z, 0, 0, tiled=True)  6.99 us
    all_to_all x1, starting transfers between devices, on_device(): total = lax.all_to_all(total, ('b',) + CTX, 0, 0, tiled=True)  5.82 us
    all_to_all x1, starting transfers between devices, on_device(): partial = lax.all_to_all(partial, ('b',) + Z, 0, 0, tiled=True)  5.5 us
    all_to_all x1, starting transfers between devices, on_device(): lax.all_to_all(stats, Z, 0, 0, tiled=True).reshape(NSEC * 8, 128)  5.36 us
  transfers between devices with their start and end apart: 24, of which 10 were waited for; matrix products, arithmetic and copies ran while one was open for 1% of the time, Pallas kernels for 23%

profile of v5, /device:TPU:8, one launch (start us, length us, event | category | flops | bytes accessed | tf_op | source)
XLA Modules:
  0.0 120.3 jit_solution(13010934751176183360)
XLA Ops:
  0.6 0.6 pad_add_fusion.place
  1.2 3.5 %shard_map.110 = (bf16[512,128]{1,0:T(8,128)(2,1)}, bf16[512,128]{1,0:T(8,128)(2,1)}) custom-call(s32[3]{0:T(128)} %pad_add_fusion.place, bf16[256,1024]{1,0:T(8,128)(2,1)} %bitcast.25, bf16[1024,128]{1,0:T(8,128)(2,1)} %wq.3, bf16[1024,128]{1,0:T(8,128)(2,1)} %wk.3, bf16[1024,128]{1,0:T(8,128)(2,1)} %wv.3, bf16[256,128]{1,0:T(8,128)(2,1)} %bitcast.30), custom_call_target="tpu_custom_call" | custom-call | flops 201326592 | bytes 1376268 | tf_op jit(solution)/shard_map/pallas_call | solution.py:44
  4.8 3.1 %collective-permute-start = (bf16[512,128]{1,0:T(8,128)(2,1)}, bf16[512,128]{1,0:T(8,128)(2,1)}, u32[]{:S(2)}, u32[]{:S(2)}) collective-permute-start(bf16[512,128]{1,0:T(8,128)(2,1)} %get-tuple-element.33), channel_id=1, source_target_pairs={{0,8},{8,0},{1,9},{9,1},{2,10},{10,2},{3,11},{11,3},{4,12},{12,4},... | collective-permute-start | bytes 393224 | tf_op jit(solution)/shard_map/ppermute | solution.py:339
  7.9 1.9 %collective-permute-start.1 = (bf16[512,128]{1,0:T(8,128)(2,1)}, bf16[512,128]{1,0:T(8,128)(2,1)}, u32[]{:S(2)}, u32[]{:S(2)}) collective-permute-start(bf16[512,128]{1,0:T(8,128)(2,1)} %get-tuple-element.32.refs_0_), channel_id=1, source_target_pairs={{0,16},{16,32},{32,48},{48,64},{64,80},{80,96},{96,112},{112,0},{1... | collective-permute-start | bytes 393224 | tf_op jit(solution)/shard_map/ppermute | solution.py:335
  9.8 3.5 %shard_map.111.refs_16_ = bf16[4096,128]{1,0:T(8,128)(2,1)} custom-call(s32[3]{0:T(128)} %pad_add_fusion.place, s32[1,8]{1,0:T(1,128)} %lengths.1, s32[1,256]{1,0:T(1,128)} %spots.1), custom_call_target="tpu_custom_call" | custom-call | bytes 1068 | tf_op jit(solution)/shard_map/pallas_call | solution.py:44
  13.4 4.4 %collective-permute-start.4 = (bf16[512,128]{1,0:T(8,128)(2,1)}, bf16[512,128]{1,0:T(8,128)(2,1)S(1)}, u32[]{:S(2)}, u32[]{:S(2)}) collective-permute-start(bf16[512,128]{1,0:T(8,128)(2,1)} %collective-permute-done.refs_1_), channel_id=1, source_target_pairs={{0,112},{16,0},{32,16},{48,32},{64,48},{80,64},{96,80},{112,96},{1... | collective-permute-start | bytes 393224 | tf_op jit(solution)/shard_map/ppermute | solution.py:335
  17.8 1.5 %collective-permute-start.3 = (bf16[512,128]{1,0:T(8,128)(2,1)}, bf16[512,128]{1,0:T(8,128)(2,1)S(1)}, u32[]{:S(2)}, u32[]{:S(2)}) collective-permute-start(bf16[512,128]{1,0:T(8,128)(2,1)} %get-tuple-element.32.refs_0_), channel_id=1, source_target_pairs={{0,112},{16,0},{32,16},{48,32},{64,48},{80,64},{96,80},{112,96},{1... | collective-permute-start | bytes 393224 | tf_op jit(solution)/shard_map/ppermute | solution.py:335
  19.3 0.5 collective-permute-start.2
  19.8 0.0 collective-permute-start.5
  19.8 1.7 %collective-permute-done.4.refs_5_ = bf16[512,128]{1,0:T(8,128)(2,1)S(1)} collective-permute-done((bf16[512,128]{1,0:T(8,128)(2,1)}, bf16[512,128]{1,0:T(8,128)(2,1)S(1)}, u32[]{:S(2)}, u32[]{:S(2)}) %collective-permute-start.4) | collective-permute-done | bytes 131104 | tf_op jit(solution)/shard_map/ppermute | solution.py:335
  21.6 3.6 %collective-permute-start.8 = (bf16[512,128]{1,0:T(8,128)(2,1)S(1)}, bf16[512,128]{1,0:T(8,128)(2,1)S(1)}, u32[]{:S(2)}, u32[]{:S(2)}) collective-permute-start(bf16[512,128]{1,0:T(8,128)(2,1)S(1)} %collective-permute-done.4.refs_5_), channel_id=1, source_target_pairs={{0,112},{16,0},{32,16},{48,32},{64,48},{80,64},{96,80},{112,96},{1... | collective-permute-start | bytes 393224 | tf_op jit(solution)/shard_map/ppermute | solution.py:335
  25.1 2.0 %collective-permute-start.7 = (bf16[512,128]{1,0:T(8,128)(2,1)S(1)}, bf16[512,128]{1,0:T(8,128)(2,1)S(1)}, u32[]{:S(2)}, u32[]{:S(2)}) collective-permute-start(bf16[512,128]{1,0:T(8,128)(2,1)S(1)} %collective-permute-done.3.refs_4_), channel_id=1, source_target_pairs={{0,112},{16,0},{32,16},{48,32},{64,48},{80,64},{96,80},{112,96},{1... | collective-permute-start | bytes 393224 | tf_op jit(solution)/shard_map/ppermute | solution.py:335
  27.1 0.1 collective-permute-start.6
  27.2 0.5 collective-permute-done.5.refs_6_
  27.7 0.2 collective-permute-done.8.refs_9_
  27.8 3.7 %collective-permute-start.12 = (bf16[512,128]{1,0:T(8,128)(2,1)S(1)}, bf16[512,128]{1,0:T(8,128)(2,1)S(1)}, u32[]{:S(2)}, u32[]{:S(2)}) collective-permute-start(bf16[512,128]{1,0:T(8,128)(2,1)S(1)} %collective-permute-done.8.refs_9_), channel_id=1, source_target_pairs={{0,112},{16,0},{32,16},{48,32},{64,48},{80,64},{96,80},{112,96},{1... | collective-permute-start | bytes 393224 | tf_op jit(solution)/shard_map/ppermute | solution.py:335
  31.5 2.8 %collective-permute-start.11 = (bf16[512,128]{1,0:T(8,128)(2,1)S(1)}, bf16[512,128]{1,0:T(8,128)(2,1)S(1)}, u32[]{:S(2)}, u32[]{:S(2)}) collective-permute-start(bf16[512,128]{1,0:T(8,128)(2,1)S(1)} %collective-permute-done.7.refs_8_), channel_id=1, source_target_pairs={{0,112},{16,0},{32,16},{48,32},{64,48},{80,64},{96,80},{112,96},{1... | collective-permute-start | bytes 393224 | tf_op jit(solution)/shard_map/ppermute | solution.py:335
  34.4 1.0 collective-permute-done.9.refs_10_
  35.4 3.2 %collective-permute-start.14 = (bf16[512,128]{1,0:T(8,128)(2,1)S(1)}, bf16[512,128]{1,0:T(8,128)(2,1)S(1)}, u32[]{:S(2)}, u32[]{:S(2)}) collective-permute-start(bf16[512,128]{1,0:T(8,128)(2,1)S(1)} %collective-permute-done.12.refs_13_), channel_id=1, source_target_pairs={{0,112},{16,0},{32,16},{48,32},{64,48},{80,64},{96,80},{112,96},{1... | collective-permute-start | bytes 393224 | tf_op jit(solution)/shard_map/ppermute | solution.py:335
  38.7 3.6 %collective-permute-start.15 = (bf16[256,1024]{1,0:T(8,128)(2,1)}, bf16[256,1024]{1,0:T(8,128)(2,1)S(1)}, u32[]{:S(2)}, u32[]{:S(2)}) collective-permute-start(bf16[256,1024]{1,0:T(8,128)(2,1)} %bitcast.26), channel_id=1, source_target_pairs={{0,8},{8,0},{1,9},{9,1},{2,10},{10,2},{3,11},{11,3},{4,12},{12,4},... | collective-permute-start | bytes 1572872 | tf_op jit(solution)/shard_map/ppermute | solution.py:339
  42.2 0.0 copy-start.4
  42.3 0.6 copy-done.4
  42.9 0.9 copy-done.6
  43.8 6.2 %shard_map.112 = (bf16[512,128]{1,0:T(8,128)(2,1)S(1)}, f32[512,128]{1,0:T(8,128)S(1)}, f32[8,8,128]{2,1,0:T(8,128)}) custom-call(s32[3]{0:T(128)S(1)} %copy-done.4, bf16[512,128]{1,0:T(8,128)(2,1)S(1)} %copy-done.6, bf16[512,128]{1,0:T(8,128)(2,1)} %collective-permute-done.refs_1_, bf16[512,128]{1,0:T(8,128)(2,1)} %collective-permute-done.1.refs_2_, ...), custom_call_target="tpu_custom_call" | custom-call | flops 1073741824 | bytes 3145740 | tf_op jit(solution)/shard_map/pallas_call | solution.py:44
  50.0 5.4 %all-to-all-start = ((f32[8,8,128]{2,1,0:T(8,128)}), f32[8,8,128]{2,1,0:T(8,128)S(1)}, u32[]{:S(2)}, u32[]{:S(2)}) async-start(f32[8,8,128]{2,1,0:T(8,128)} %get-tuple-element.37), calls=%async_computation | async-start | bytes 65536 | tf_op jit(solution)/shard_map/all_to_all | solution.py:397
  55.4 0.6 copy-done.5
  56.0 5.4 %shard_map.113 = (bf16[256,128]{1,0:T(8,128)(2,1)S(1)}, bf16[256,128]{1,0:T(8,128)(2,1)S(1)}) custom-call(s32[3]{0:T(128)S(1)} %copy-done.5, bf16[512,128]{1,0:T(8,128)(2,1)S(1)} %copy-done.7, bf16[512,128]{1,0:T(8,128)(2,1)} %collective-permute-done.refs_1_, bf16[512,128]{1,0:T(8,128)(2,1)} %collective-permute-done.1.refs_2_, ...), custom_call_target="tpu_custom_call" | custom-call | flops 1610612736 | bytes 3538956 | tf_op jit(solution)/shard_map/pallas_call | solution.py:44
  61.4 2.0 %all-to-all-done = f32[8,8,128]{2,1,0:T(8,128)S(1)} async-done(((f32[8,8,128]{2,1,0:T(8,128)}), f32[8,8,128]{2,1,0:T(8,128)S(1)}, u32[]{:S(2)}, u32[]{:S(2)}) %all-to-all-start) | async-done | bytes 32800 | tf_op jit(solution)/shard_map/all_to_all | solution.py:397
  63.4 4.7 %shard_map.114.sent = bf16[512,128]{1,0:T(8,128)(2,1)S(1)} custom-call(s32[3]{0:T(128)S(1)} %copy-done.5, bf16[512,128]{1,0:T(8,128)(2,1)S(1)} %copy-done.7, bf16[512,128]{1,0:T(8,128)(2,1)} %collective-permute-done.refs_1_, bf16[512,128]{1,0:T(8,128)(2,1)} %collective-permute-done.1.refs_2_, bf16[512,128]{1,0:T(8,128)(2,1)S(1)} %collective-permute-done.2.refs_3_, ...), custom_call_target="tpu_custom_call" | custom-call | flops 1073741824 | bytes 3244044 | tf_op jit(solution)/shard_map/pallas_call | solution.py:44
  68.1 0.0 copy-start
  68.1 2.2 %collective-permute-start.16 = (bf16[512,128]{1,0:T(8,128)(2,1)S(1)}, bf16[512,128]{1,0:T(8,128)(2,1)S(1)}, u32[]{:S(2)}, u32[]{:S(2)}) collective-permute-start(bf16[512,128]{1,0:T(8,128)(2,1)S(1)} %shard_map.114.sent), channel_id=1, source_target_pairs={{0,8},{8,0},{1,9},{9,1},{2,10},{10,2},{3,11},{11,3},{4,12},{12,4},... | collective-permute-start | bytes 393224 | tf_op jit(solution)/shard_map/ppermute | solution.py:339
  70.3 4.7 %shard_map.115.second = bf16[256,128]{1,0:T(8,128)(2,1)S(1)} custom-call(s32[3]{0:T(128)S(1)} %copy-done.5, bf16[512,128]{1,0:T(8,128)(2,1)S(1)} %copy-done.7, bf16[512,128]{1,0:T(8,128)(2,1)} %collective-permute-done.refs_1_, bf16[512,128]{1,0:T(8,128)(2,1)} %collective-permute-done.1.refs_2_, bf16[512,128]{1,0:T(8,128)(2,1)S(1)} %collective-permute-done.2.refs_3_, ...), custom_call_target="tpu_custom_call" | custom-call | flops 1073741824 | bytes 3178508 | tf_op jit(solution)/shard_map/pallas_call | solution.py:44
  75.0 1.6 %shard_map.116 = bf16[16,96,128]{2,1,0:T(8,128)(2,1)} custom-call(bf16[256,1024]{1,0:T(8,128)(2,1)S(1)} %bitcast.27, bf16[256,1024]{1,0:T(8,128)(2,1)S(1)} %collective-permute-done.15.tok_other, bf16[256,128]{1,0:T(8,128)(2,1)S(1)} %get-tuple-element.42.first, bf16[256,128]{1,0:T(8,128)(2,1)S(1)} %shard_map.115.second, bf16[512,128]{1,0:T(8,128)(2,1)S(1)} %shard_map.114.sent), custom_call_target="tpu_custom_call" | custom-call | flops 268435456 | bytes 1310720 | tf_op jit(solution)/shard_map/pallas_call | solution.py:44
  76.6 5.5 %all-to-all-start.1 = ((bf16[16,96,128]{2,1,0:T(8,128)(2,1)}), bf16[16,96,128]{2,1,0:T(8,128)(2,1)S(1)}, u32[]{:S(2)}, u32[]{:S(2)}) async-start(bf16[16,96,128]{2,1,0:T(8,128)(2,1)} %shard_map.116), calls=%async_computation.1 | async-start | bytes 786432 | tf_op jit(solution)/shard_map/all_to_all | solution.py:430
  82.2 1.7 %shard_map.117 = (bf16[256,128]{1,0:T(8,128)(2,1)}, f32[4,32,1024]{2,1,0:T(8,128)S(1)}, bf16[4,32,1024]{2,1,0:T(8,128)(2,1)S(1)}) custom-call(s32[3]{0:T(128)S(1)} %copy-done.5, bf16[256,128]{1,0:T(8,128)(2,1)S(1)} %get-tuple-element.42.first, bf16[256,128]{1,0:T(8,128)(2,1)S(1)} %shard_map.115.second, bf16[512,128]{1,0:T(8,128)(2,1)S(1)} %collective-permute-done.16.arrived, ...), custom_call_target="tpu_custom_call" | custom-call | flops 201326592 | bytes 1048588 | tf_op jit(solution)/shard_map/pallas_call | solution.py:44
  83.9 1.5 %collective-permute-done.17 = bf16[4,32,1024]{2,1,0:T(8,128)(2,1)S(1)} collective-permute-done((bf16[4,32,1024]{2,1,0:T(8,128)(2,1)S(1)}, bf16[4,32,1024]{2,1,0:T(8,128)(2,1)S(1)}, u32[]{:S(2)}, u32[]{:S(2)}) %collective-permute-start.17) | collective-permute-done | bytes 262176 | tf_op jit(solution)/shard_map/ppermute | solution.py:437
  85.4 7.0 %all-to-all-done.1.parts = bf16[16,96,128]{2,1,0:T(8,128)(2,1)S(1)} async-done(((bf16[16,96,128]{2,1,0:T(8,128)(2,1)}), bf16[16,96,128]{2,1,0:T(8,128)(2,1)S(1)}, u32[]{:S(2)}, u32[]{:S(2)}) %all-to-all-start.1) | async-done | bytes 393248 | tf_op jit(solution)/shard_map/all_to_all | solution.py:430
  92.4 1.0 shard_map.118
  93.4 5.8 %all-to-all-start.2 = ((bf16[32,96,128]{2,1,0:T(8,128)(2,1)}), bf16[32,96,128]{2,1,0:T(8,128)(2,1)S(1)}, u32[]{:S(2)}, u32[]{:S(2)}) async-start(bf16[32,96,128]{2,1,0:T(8,128)(2,1)} %shard_map.118), calls=%async_computation.2 | async-start | bytes 1572864 | tf_op jit(solution)/shard_map/all_to_all | solution.py:446
  99.2 0.1 fusion.4
  99.4 1.7 %collective-permute-start.20 = (bf16[32,1024]{1,0:T(8,128)(2,1)S(1)}, bf16[32,1024]{1,0:T(8,128)(2,1)S(1)}, u32[]{:S(2)}, u32[]{:S(2)}) collective-permute-start(bf16[32,1024]{1,0:T(8,128)(2,1)S(1)} %get-tuple-element.60), channel_id=1, source_target_pairs={{0,6},{2,4},{4,2},{6,0},{1,7},{3,5},{5,3},{7,1},{8,14},{10,12},{12... | collective-permute-start | bytes 196616 | tf_op jit(solution)/shard_map/ppermute | solution.py:445
  101.0 0.9 collective-permute-start.19
  102.0 1.6 %collective-permute-start.18 = (bf16[32,1024]{1,0:T(8,128)(2,1)S(1)}, bf16[32,1024]{1,0:T(8,128)(2,1)S(1)}, u32[]{:S(2)}, u32[]{:S(2)}) collective-permute-start(bf16[32,1024]{1,0:T(8,128)(2,1)S(1)} %get-tuple-element.59), channel_id=1, source_target_pairs={{0,2},{2,0},{4,6},{6,4},{1,3},{3,1},{5,7},{7,5},{8,10},{10,8},{12,... | collective-permute-start | bytes 196616 | tf_op jit(solution)/shard_map/ppermute | solution.py:445
  103.5 0.2 collective-permute-done.20
  103.7 3.1 %collective-permute-done.19 = bf16[32,1024]{1,0:T(8,128)(2,1)S(1)} collective-permute-done((bf16[32,1024]{1,0:T(8,128)(2,1)S(1)}, bf16[32,1024]{1,0:T(8,128)(2,1)S(1)}, u32[]{:S(2)}, u32[]{:S(2)}) %collective-permute-start.19) | collective-permute-done | bytes 65568 | tf_op jit(solution)/shard_map/ppermute | solution.py:445
  106.8 0.7 fusion.3
  107.5 11.4 %all-to-all-done.2.parts = bf16[32,96,128]{2,1,0:T(8,128)(2,1)S(1)} async-done(((bf16[32,96,128]{2,1,0:T(8,128)(2,1)}), bf16[32,96,128]{2,1,0:T(8,128)(2,1)S(1)}, u32[]{:S(2)}, u32[]{:S(2)}) %all-to-all-start.2) | async-done | bytes 786464 | tf_op jit(solution)/shard_map/all_to_all | solution.py:446
  118.9 1.4 %shard_map.119 = (f32[1024,128]{1,0:T(8,128)}, f32[1024,128]{1,0:T(8,128)}, f32[1024,128]{1,0:T(8,128)}) custom-call(bf16[32,96,128]{2,1,0:T(8,128)(2,1)S(1)} %all-to-all-done.2.parts), custom_call_target="tpu_custom_call" | custom-call | bytes 786432 | tf_op jit(solution)/shard_map/pallas_call | solution.py:44
  (30 shorter events, 0.1 us)
Async XLA Ops:
  4.8 8.6 %collective-permute-start = (bf16[512,128]{1,0:T(8,128)(2,1)}, bf16[512,128]{1,0:T(8,128)(2,1)}, u32[]{:S(2)}, u32[]{:S(2)}) collective-permute-start(bf16[512,128]{1,0:T(8,128)(2,1)} %get-tuple-element.33), channel_id=1, source_target_pairs={{0,8},{8,0},{1,9},{9,1},{2,10},{10,2},{3,11},{11,3},{4,12},{12,4},... | collective-permute-start | bytes 393224 | tf_op jit(solution)/shard_map/ppermute | solution.py:339
  7.9 11.9 %collective-permute-start.1 = (bf16[512,128]{1,0:T(8,128)(2,1)}, bf16[512,128]{1,0:T(8,128)(2,1)}, u32[]{:S(2)}, u32[]{:S(2)}) collective-permute-start(bf16[512,128]{1,0:T(8,128)(2,1)} %get-tuple-element.32.refs_0_), channel_id=1, source_target_pairs={{0,16},{16,32},{32,48},{48,64},{64,80},{80,96},{96,112},{112,0},{1... | collective-permute-start | bytes 393224 | tf_op jit(solution)/shard_map/ppermute | solution.py:335
  13.4 8.2 %collective-permute-start.4 = (bf16[512,128]{1,0:T(8,128)(2,1)}, bf16[512,128]{1,0:T(8,128)(2,1)S(1)}, u32[]{:S(2)}, u32[]{:S(2)}) collective-permute-start(bf16[512,128]{1,0:T(8,128)(2,1)} %collective-permute-done.refs_1_), channel_id=1, source_target_pairs={{0,112},{16,0},{32,16},{48,32},{64,48},{80,64},{96,80},{112,96},{1... | collective-permute-start | bytes 393224 | tf_op jit(solution)/shard_map/ppermute | solution.py:335
  17.8 7.4 %collective-permute-start.3 = (bf16[512,128]{1,0:T(8,128)(2,1)}, bf16[512,128]{1,0:T(8,128)(2,1)S(1)}, u32[]{:S(2)}, u32[]{:S(2)}) collective-permute-start(bf16[512,128]{1,0:T(8,128)(2,1)} %get-tuple-element.32.refs_0_), channel_id=1, source_target_pairs={{0,112},{16,0},{32,16},{48,32},{64,48},{80,64},{96,80},{112,96},{1... | collective-permute-start | bytes 393224 | tf_op jit(solution)/shard_map/ppermute | solution.py:335
  19.3 7.8 %collective-permute-start.2 = (bf16[512,128]{1,0:T(8,128)(2,1)}, bf16[512,128]{1,0:T(8,128)(2,1)S(1)}, u32[]{:S(2)}, u32[]{:S(2)}) collective-permute-start(bf16[512,128]{1,0:T(8,128)(2,1)} %collective-permute-done.refs_1_), channel_id=1, source_target_pairs={{0,16},{16,32},{32,48},{48,64},{64,80},{80,96},{96,112},{112,0},{1... | collective-permute-start | bytes 393224 | tf_op jit(solution)/shard_map/ppermute | solution.py:335
  19.8 7.9 %collective-permute-start.5 = (bf16[512,128]{1,0:T(8,128)(2,1)}, bf16[512,128]{1,0:T(8,128)(2,1)S(1)}, u32[]{:S(2)}, u32[]{:S(2)}) collective-permute-start(bf16[512,128]{1,0:T(8,128)(2,1)} %collective-permute-done.1.refs_2_), channel_id=1, source_target_pairs={{0,16},{16,32},{32,48},{48,64},{64,80},{80,96},{96,112},{112,0},{1... | collective-permute-start | bytes 393224 | tf_op jit(solution)/shard_map/ppermute | solution.py:335
  21.6 6.3 %collective-permute-start.8 = (bf16[512,128]{1,0:T(8,128)(2,1)S(1)}, bf16[512,128]{1,0:T(8,128)(2,1)S(1)}, u32[]{:S(2)}, u32[]{:S(2)}) collective-permute-start(bf16[512,128]{1,0:T(8,128)(2,1)S(1)} %collective-permute-done.4.refs_5_), channel_id=1, source_target_pairs={{0,112},{16,0},{32,16},{48,32},{64,48},{80,64},{96,80},{112,96},{1... | collective-permute-start | bytes 393224 | tf_op jit(solution)/shard_map/ppermute | solution.py:335
  25.1 6.4 %collective-permute-start.7 = (bf16[512,128]{1,0:T(8,128)(2,1)S(1)}, bf16[512,128]{1,0:T(8,128)(2,1)S(1)}, u32[]{:S(2)}, u32[]{:S(2)}) collective-permute-start(bf16[512,128]{1,0:T(8,128)(2,1)S(1)} %collective-permute-done.3.refs_4_), channel_id=1, source_target_pairs={{0,112},{16,0},{32,16},{48,32},{64,48},{80,64},{96,80},{112,96},{1... | collective-permute-start | bytes 393224 | tf_op jit(solution)/shard_map/ppermute | solution.py:335
  27.1 7.3 %collective-permute-start.6 = (bf16[512,128]{1,0:T(8,128)(2,1)S(1)}, bf16[512,128]{1,0:T(8,128)(2,1)S(1)}, u32[]{:S(2)}, u32[]{:S(2)}) collective-permute-start(bf16[512,128]{1,0:T(8,128)(2,1)S(1)} %collective-permute-done.2.refs_3_), channel_id=1, source_target_pairs={{0,16},{16,32},{32,48},{48,64},{64,80},{80,96},{96,112},{112,0},{1... | collective-permute-start | bytes 393224 | tf_op jit(solution)/shard_map/ppermute | solution.py:335
  27.7 7.7 %collective-permute-start.9 = (bf16[512,128]{1,0:T(8,128)(2,1)S(1)}, bf16[512,128]{1,0:T(8,128)(2,1)S(1)}, u32[]{:S(2)}, u32[]{:S(2)}) collective-permute-start(bf16[512,128]{1,0:T(8,128)(2,1)S(1)} %collective-permute-done.5.refs_6_), channel_id=1, source_target_pairs={{0,16},{16,32},{32,48},{48,64},{64,80},{80,96},{96,112},{112,0},{1... | collective-permute-start | bytes 393224 | tf_op jit(solution)/shard_map/ppermute | solution.py:335
  27.8 7.6 %collective-permute-start.12 = (bf16[512,128]{1,0:T(8,128)(2,1)S(1)}, bf16[512,128]{1,0:T(8,128)(2,1)S(1)}, u32[]{:S(2)}, u32[]{:S(2)}) collective-permute-start(bf16[512,128]{1,0:T(8,128)(2,1)S(1)} %collective-permute-done.8.refs_9_), channel_id=1, source_target_pairs={{0,112},{16,0},{32,16},{48,32},{64,48},{80,64},{96,80},{112,96},{1... | collective-permute-start | bytes 393224 | tf_op jit(solution)/shard_map/ppermute | solution.py:335
  31.5 10.7 %collective-permute-start.11 = (bf16[512,128]{1,0:T(8,128)(2,1)S(1)}, bf16[512,128]{1,0:T(8,128)(2,1)S(1)}, u32[]{:S(2)}, u32[]{:S(2)}) collective-permute-start(bf16[512,128]{1,0:T(8,128)(2,1)S(1)} %collective-permute-done.7.refs_8_), channel_id=1, source_target_pairs={{0,112},{16,0},{32,16},{48,32},{64,48},{80,64},{96,80},{112,96},{1... | collective-permute-start | bytes 393224 | tf_op jit(solution)/shard_map/ppermute | solution.py:335
  34.4 7.8 %collective-permute-start.10 = (bf16[512,128]{1,0:T(8,128)(2,1)S(1)}, bf16[512,128]{1,0:T(8,128)(2,1)S(1)}, u32[]{:S(2)}, u32[]{:S(2)}) collective-permute-start(bf16[512,128]{1,0:T(8,128)(2,1)S(1)} %collective-permute-done.6.refs_7_), channel_id=1, source_target_pairs={{0,16},{16,32},{32,48},{48,64},{64,80},{80,96},{96,112},{112,0},{1... | collective-permute-start | bytes 393224 | tf_op jit(solution)/shard_map/ppermute | solution.py:335
  35.4 6.8 %collective-permute-start.13 = (bf16[512,128]{1,0:T(8,128)(2,1)S(1)}, bf16[512,128]{1,0:T(8,128)(2,1)S(1)}, u32[]{:S(2)}, u32[]{:S(2)}) collective-permute-start(bf16[512,128]{1,0:T(8,128)(2,1)S(1)} %collective-permute-done.9.refs_10_), channel_id=1, source_target_pairs={{0,16},{16,32},{32,48},{48,64},{64,80},{80,96},{96,112},{112,0},{1... | collective-permute-start | bytes 393224 | tf_op jit(solution)/shard_map/ppermute | solution.py:335
  35.4 6.8 %collective-permute-start.14 = (bf16[512,128]{1,0:T(8,128)(2,1)S(1)}, bf16[512,128]{1,0:T(8,128)(2,1)S(1)}, u32[]{:S(2)}, u32[]{:S(2)}) collective-permute-start(bf16[512,128]{1,0:T(8,128)(2,1)S(1)} %collective-permute-done.12.refs_13_), channel_id=1, source_target_pairs={{0,112},{16,0},{32,16},{48,32},{64,48},{80,64},{96,80},{112,96},{1... | collective-permute-start | bytes 393224 | tf_op jit(solution)/shard_map/ppermute | solution.py:335
  38.7 36.4 %collective-permute-start.15 = (bf16[256,1024]{1,0:T(8,128)(2,1)}, bf16[256,1024]{1,0:T(8,128)(2,1)S(1)}, u32[]{:S(2)}, u32[]{:S(2)}) collective-permute-start(bf16[256,1024]{1,0:T(8,128)(2,1)} %bitcast.26), channel_id=1, source_target_pairs={{0,8},{8,0},{1,9},{9,1},{2,10},{10,2},{3,11},{11,3},{4,12},{12,4},... | collective-permute-start | bytes 1572872 | tf_op jit(solution)/shard_map/ppermute | solution.py:339
  42.2 0.7 copy-start.4
  42.9 0.9 copy-start.6
  43.8 11.6 %copy-start.7 = (bf16[512,128]{1,0:T(8,128)(2,1)S(1)}, bf16[512,128]{1,0:T(8,128)(2,1)}, u32[]{:S(2)}) copy-start(bf16[512,128]{1,0:T(8,128)(2,1)} %get-tuple-element.32.refs_0_) | copy-start | bytes 393220
  50.0 13.4 %all-to-all-start = ((f32[8,8,128]{2,1,0:T(8,128)}), f32[8,8,128]{2,1,0:T(8,128)S(1)}, u32[]{:S(2)}, u32[]{:S(2)}) async-start(f32[8,8,128]{2,1,0:T(8,128)} %get-tuple-element.37), calls=%async_computation | async-start | bytes 65536 | tf_op jit(solution)/shard_map/all_to_all | solution.py:397
  55.4 0.7 copy-start.5
  68.1 6.9 %copy-start = (bf16[1,256,1024]{2,1,0:T(8,128)(2,1)S(1)}, bf16[1,256,1024]{2,1,0:T(8,128)(2,1)}, u32[]{:S(2)}) copy-start(bf16[1,256,1024]{2,1,0:T(8,128)(2,1)} %param.7) | copy-start | bytes 1572868
  68.1 8.5 %collective-permute-start.16 = (bf16[512,128]{1,0:T(8,128)(2,1)S(1)}, bf16[512,128]{1,0:T(8,128)(2,1)S(1)}, u32[]{:S(2)}, u32[]{:S(2)}) collective-permute-start(bf16[512,128]{1,0:T(8,128)(2,1)S(1)} %shard_map.114.sent), channel_id=1, source_target_pairs={{0,8},{8,0},{1,9},{9,1},{2,10},{10,2},{3,11},{11,3},{4,12},{12,4},... | collective-permute-start | bytes 393224 | tf_op jit(solution)/shard_map/ppermute | solution.py:339
  76.6 5.5 %copy-start.1 = (bf16[1024,128]{1,0:T(8,128)(2,1)S(1)}, bf16[1024,128]{1,0:T(8,128)(2,1)}, u32[]{:S(2)}) copy-start(bf16[1024,128]{1,0:T(8,128)(2,1)} %wq.3) | copy-start | bytes 786436
  76.6 5.5 %copy-start.2 = (bf16[1024,128]{1,0:T(8,128)(2,1)S(1)}, bf16[1024,128]{1,0:T(8,128)(2,1)}, u32[]{:S(2)}) copy-start(bf16[1024,128]{1,0:T(8,128)(2,1)} %wk.3) | copy-start | bytes 786436
  76.6 5.5 %copy-start.3 = (bf16[1024,128]{1,0:T(8,128)(2,1)S(1)}, bf16[1024,128]{1,0:T(8,128)(2,1)}, u32[]{:S(2)}) copy-start(bf16[1024,128]{1,0:T(8,128)(2,1)} %wv.3) | copy-start | bytes 786436
  76.6 15.8 %all-to-all-start.1 = ((bf16[16,96,128]{2,1,0:T(8,128)(2,1)}), bf16[16,96,128]{2,1,0:T(8,128)(2,1)S(1)}, u32[]{:S(2)}, u32[]{:S(2)}) async-start(bf16[16,96,128]{2,1,0:T(8,128)(2,1)} %shard_map.116), calls=%async_computation.1 | async-start | bytes 786432 | tf_op jit(solution)/shard_map/all_to_all | solution.py:430
  83.9 1.5 %collective-permute-start.17 = (bf16[4,32,1024]{2,1,0:T(8,128)(2,1)S(1)}, bf16[4,32,1024]{2,1,0:T(8,128)(2,1)S(1)}, u32[]{:S(2)}, u32[]{:S(2)}) collective-permute-start(bf16[4,32,1024]{2,1,0:T(8,128)(2,1)S(1)} %get-tuple-element.51), channel_id=1, source_target_pairs={{0,1},{1,0},{2,3},{3,2},{4,5},{5,4},{6,7},{7,6},{8,9},{9,8},{10,11... | collective-permute-start | bytes 786440 | tf_op jit(solution)/shard_map/ppermute | solution.py:437
  93.4 25.5 %all-to-all-start.2 = ((bf16[32,96,128]{2,1,0:T(8,128)(2,1)}), bf16[32,96,128]{2,1,0:T(8,128)(2,1)S(1)}, u32[]{:S(2)}, u32[]{:S(2)}) async-start(bf16[32,96,128]{2,1,0:T(8,128)(2,1)} %shard_map.118), calls=%async_computation.2 | async-start | bytes 1572864 | tf_op jit(solution)/shard_map/all_to_all | solution.py:446
  99.4 4.4 %collective-permute-start.20 = (bf16[32,1024]{1,0:T(8,128)(2,1)S(1)}, bf16[32,1024]{1,0:T(8,128)(2,1)S(1)}, u32[]{:S(2)}, u32[]{:S(2)}) collective-permute-start(bf16[32,1024]{1,0:T(8,128)(2,1)S(1)} %get-tuple-element.60), channel_id=1, source_target_pairs={{0,6},{2,4},{4,2},{6,0},{1,7},{3,5},{5,3},{7,1},{8,14},{10,12},{12... | collective-permute-start | bytes 196616 | tf_op jit(solution)/shard_map/ppermute | solution.py:445
  101.0 5.8 %collective-permute-start.19 = (bf16[32,1024]{1,0:T(8,128)(2,1)S(1)}, bf16[32,1024]{1,0:T(8,128)(2,1)S(1)}, u32[]{:S(2)}, u32[]{:S(2)}) collective-permute-start(bf16[32,1024]{1,0:T(8,128)(2,1)S(1)} %get-tuple-element.61), channel_id=1, source_target_pairs={{0,4},{2,6},{4,0},{6,2},{1,5},{3,7},{5,1},{7,3},{8,12},{10,14},{12... | collective-permute-start | bytes 196616 | tf_op jit(solution)/shard_map/ppermute | solution.py:445
  102.0 4.8 %collective-permute-start.18 = (bf16[32,1024]{1,0:T(8,128)(2,1)S(1)}, bf16[32,1024]{1,0:T(8,128)(2,1)S(1)}, u32[]{:S(2)}, u32[]{:S(2)}) collective-permute-start(bf16[32,1024]{1,0:T(8,128)(2,1)S(1)} %get-tuple-element.59), channel_id=1, source_target_pairs={{0,2},{2,0},{4,6},{6,4},{1,3},{3,1},{5,7},{7,5},{8,10},{10,8},{12,... | collective-permute-start | bytes 196616 | tf_op jit(solution)/shard_map/ppermute | solution.py:445

commit v6 on v4

--- a/solution.py
+++ b/solution.py
@@ -17,6 +17,7 @@
 NEG = -1e30
 LIMIT = 51 << 20
 CHUNK = 512
+FEATURE_LIMIT = 64 << 20
 BF = jnp.bfloat16
 F32 = jnp.float32
 
@@ -57,7 +58,7 @@
     return lax.broadcasted_iota(jnp.int32, (rows, 128), 1) < HD
 
 
-def document_features(place, lengths, spots, feat):
+def feature_kernel(place, lengths, spots, feat):
     flip = place[0]
     lane = lax.broadcasted_iota(jnp.int32, (RUN, 128), 1)
     last = lane == HD + 8
@@ -74,8 +75,8 @@
         half = lax.rem(block, 2)
         run = (block - half) + jnp.where(half == flip, 0, 1)
         pos = run * RUN + lax.broadcasted_iota(jnp.int32, (RUN, RUN), 0)
-        hit = jnp.where(pos == spots[...], 1.0, 0.0).astype(BF)
-        other = 1.0 - dot(hit, jnp.ones((RUN, 128), BF))
+        hit = jnp.max(jnp.where(pos == spots[...], 1.0, 0.0), axis=1, keepdims=True)
+        other = 1.0 - hit
         pos128 = run * RUN + lax.broadcasted_iota(jnp.int32, (RUN, 128), 0)
         member = (pos128 >= starts) & (pos128 < ends)
         row = jnp.where(last, other, jnp.where(member, 1.0, 0.0))
@@ -86,13 +87,12 @@
     lax.fori_loop(0, 2 * NSEC, one, 0)
 
 
-def project_kernel(place, lengths, tok, wq, wk, wv, cot, spots, mine, theirs, feat, *scratch):
+def project_kernel(place, tok, wq, wk, wv, cot, mine, theirs, *scratch):
     tok_v, wk_v, wv_v, wq_v, cot_v, sems = scratch
     pairs = ((tok, tok_v), (wk, wk_v), (wv, wv_v), (wq, wq_v), (cot, cot_v))
     copies = [pltpu.make_async_copy(a, b, sems.at[i]) for i, (a, b) in enumerate(pairs)]
     for copy in copies:
         copy.start()
-    document_features(place, lengths, spots, feat)
     first = place[0] == 0
     copies[0].wait()
     t = tok_v[...]
@@ -166,53 +166,53 @@
     return jnp.where(low, jnp.zeros_like(rows), rows)
 
 
-def forward_kernel(chunk, place, *refs):
+def near_only(own, flip, r, own_places, near, plain):
+    if r > 2:
+        return plain
+    away = own_places - places(section_at(own, OFFSETS[r]), flip, 1)
+    return jnp.where(jnp.abs(away) <= HALF, near, plain)
+
+
+def forward_kernel(place, *refs):
     pieces, (feat, att_out, column_out, stats) = refs[: 2 * NSEC], refs[2 * NSEC :]
     flip, own = place[0], place[1]
     own_qc = part_of(pieces, 0, 1)
     joined = join_query(own_qc, features_at(feat, own))
     near_rows = less_global(joined)
     row_places = places(own, flip, 0)
-    count = SEC // chunk
-    state = [None] * count
-    for r, offset in enumerate(OFFSETS):
-        section = section_at(own, offset)
-        kv = part_of(pieces, r, 0)
-        kp = join_key(kv, features_at(feat, section))
-        for c in range(count):
-            rows = slice(c * chunk, (c + 1) * chunk)
-            s = dot(joined[rows], kp, NT)
-            if r < 3:
-                away = row_places[rows] - places(section, flip, 1)
-                s = jnp.where(jnp.abs(away) <= HALF, dot(near_rows[rows], kp, NT), s)
-            new_peak = jnp.max(s, axis=1, keepdims=True)
-            if r > 0:
-                peak, total, acc = state[c]
-                new_peak = jnp.maximum(peak, new_peak)
-                keep = jnp.exp(peak - new_peak)
-            e = jnp.exp(s - new_peak)
-            new_total = jnp.sum(e, axis=1, keepdims=True)
-            new_acc = dot(e.astype(BF), kv)
-            if r > 0:
-                new_total, new_acc = keep * total + new_total, keep * acc + new_acc
-            state[c] = new_peak, new_total, new_acc
-    for c in range(count):
-        rows = slice(c * chunk, (c + 1) * chunk)
-        peak, total, acc = state[c]
-        att = (acc / total).astype(BF)
-        att_out[rows] = att
-        log_total = peak + jnp.log(total)
-        cot = right_half(own_qc[rows]).astype(F32)
-        delta = jnp.sum(att.astype(F32) * cot, axis=1, keepdims=True)
-        lanes = lax.broadcasted_iota(jnp.int32, (chunk, 128), 1)
-        column = jnp.where(lanes == 0, log_total, delta)
-        column_out[rows] = column
-        turned = column.T
-        for k in range(chunk // 128):
-            at = c * (chunk // 128) + k
-            for copy in range(NSEC):
-                stats[copy, at : at + 1] = turned[0:1, k * 128 : (k + 1) * 128]
-                stats[copy, 4 + at : 5 + at] = turned[1:2, k * 128 : (k + 1) * 128]
+
+    def products(r):
+        kp = join_key(part_of(pieces, r, 0), features_at(feat, section_at(own, OFFSETS[r])))
+        return dot(joined, kp, NT), dot(near_rows, kp, NT) if r < 3 else None
+
+    ahead = products(0)
+    for r in range(NSEC):
+        plain, near = ahead
+        if r + 1 < NSEC:
+            ahead = products(r + 1)
+        s = near_only(own, flip, r, row_places, near, plain)
+        new_peak = jnp.max(s, axis=1, keepdims=True)
+        if r > 0:
+            new_peak = jnp.maximum(peak, new_peak)
+            keep = jnp.exp(peak - new_peak)
+        e = jnp.exp(s - new_peak)
+        new_total = jnp.sum(e, axis=1, keepdims=True)
+        new_acc = dot(e.astype(BF), part_of(pieces, r, 0))
+        if r > 0:
+            new_total, new_acc = keep * total + new_total, keep * acc + new_acc
+        peak, total, acc = new_peak, new_total, new_acc
+    att = (acc / total).astype(BF)
+    att_out[...] = att
+    cot = right_half(own_qc).astype(F32)
+    delta = jnp.sum(att.astype(F32) * cot, axis=1, keepdims=True)
+    lanes = lax.broadcasted_iota(jnp.int32, (SEC, 128), 1)
+    column = jnp.where(lanes == 0, peak + jnp.log(total), delta)
+    column_out[...] = column
+    turned = column.T
+    for k in range(SEC // 128):
+        for copy in range(NSEC):
+            stats[copy, k : k + 1] = turned[0:1, k * 128 : (k + 1) * 128]
+            stats[copy, 4 + k : 5 + k] = turned[1:2, k * 128 : (k + 1) * 128]
 
 
 def queries_kernel(chunk, place, *refs):
@@ -246,7 +246,7 @@
 
 
 def keys_kernel(chunk, place, *refs):
-    pieces, (feat, stats, packed, packed_other, stats_s, sems) = refs[: 2 * NSEC], refs[2 * NSEC :]
+    pieces, (feat, stats, given, packed, sent, stats_s, sems) = refs[: 2 * NSEC], refs[2 * NSEC :]
     flip, own = place[0], place[1]
     copies = []
     for r, offset in enumerate(OFFSETS):
@@ -283,12 +283,13 @@
     value_acc = jnp.concatenate([x[1] for x in state], axis=0) if count > 1 else state[0][1]
     out = jnp.where(low_lanes(SEC), key_acc * (1.0 / math.sqrt(HD)), value_acc).astype(BF)
     packed[...] = out[:RUN]
-    packed_other[...] = out[RUN:]
-
-
-def weights_kernel(tok, tok_other, first, first_sent, second, second_sent, out):
-    qa = dot(tok[...], first[...], TN) + dot(tok_other[...], first_sent[...], TN)
-    kv = dot(tok[...], second[...], TN) + dot(tok_other[...], second_sent[...], TN)
+    sent[:RUN] = given[...]
+    sent[RUN:] = out[RUN:]
+
+
+def weights_kernel(tok, tok_other, first, second, sent, out):
+    qa = dot(tok[...], first[...], TN) + dot(tok_other[...], sent[:RUN], TN)
+    kv = dot(tok[...], second[...], TN) + dot(tok_other[...], sent[RUN:], TN)
     for p in range(16):
         out[p, :64] = kv[p * 64 : (p + 1) * 64].astype(BF)
         upper = qa[p * 32 : (p + 1) * 32, :HD]
@@ -305,10 +306,10 @@
         out[p] = total
 
 
-def input_kernel(place, first, first_other, second, second_other, wq, wk, wv, att, keep, send):
+def input_kernel(place, first, second, arrived, wq, wk, wv, att, keep, send):
     swap = place[0] != 0
     core = place[2]
-    a, b, c, d = first[...], first_other[...], second[...], second_other[...]
+    a, b, c, d = first[...], arrived[:RUN], second[...], arrived[RUN:]
     a, b = jnp.where(swap, b, a), jnp.where(swap, a, b)
     c, d = jnp.where(swap, d, c), jnp.where(swap, c, d)
     dq = jnp.concatenate([a[:, :HD], b[:, :HD]], axis=1)
@@ -347,10 +348,10 @@
     xh, z, y, core = (lax.axis_index(a) for a in ("xh", Z, "y", "core"))
     place = jnp.stack([xh, z, core]).astype(jnp.int32)
     weight = pltpu.VMEM((1024, 128), BF)
-    mine, theirs, feat = call(
+    mine, theirs = call(
         project_kernel,
-        (shape((SEC, 128), BF),) * 2 + (shape((NSEC * SEC, 128), BF),),
-        (place, doc_lengths, tok, wq, wk, wv, cot, global_positions),
+        (shape((SEC, 128), BF),) * 2,
+        (place, tok, wq, wk, wv, cot),
         scratch=(
             pltpu.VMEM((RUN, 1024), BF),
             weight,
@@ -360,7 +361,6 @@
             pltpu.SemaphoreType.DMA((5,)),
         ),
         flops=6 * 256 * 1024 * 128,
-        smem=2,
         manual=5,
         limit=64 << 20,
     )
@@ -371,6 +371,15 @@
 
     tie = lax.optimization_barrier
     lower_a, upper_a = [mine, shift(mine, 1)], [mine, shift(mine, -1)]
+    late, mine = tie((place, mine))
+    feat = call(
+        feature_kernel,
+        shape((NSEC * SEC, 128), BF),
+        (late, doc_lengths, global_positions),
+        smem=2,
+        limit=FEATURE_LIMIT,
+    )
+    other, feat, lower_a[1], upper_a[1] = tie((other, feat, lower_a[1], upper_a[1]))
     lower_b, upper_b = [other, shift(other, 1)], [other, shift(other, -1)]
     for x, step in ((lower_a, 1), (upper_a, -1), (lower_b, 1), (upper_b, -1)):
         x.append(shift(x[1], step))
@@ -382,7 +391,7 @@
         pieces += (lower_a[i], lower_b[i], upper_a[i], upper_b[i])
     pieces += far
     att_rows, column, stats = call(
-        functools.partial(forward_kernel, CHUNK),
+        forward_kernel,
         (shape((SEC, 128), BF), wide, shape((NSEC, 8, 128), F32)),
         (place, *pieces, feat),
         flops=2 * 128 * 2 * pairs,
@@ -397,35 +406,33 @@
         flops=2 * 128 * 3 * pairs,
         transcendentals=pairs,
     )
-    all_stats, first, first_sent = lax.optimization_barrier((all_stats, first, first_sent))
-    first_other = swap(first_sent)
-    second, second_sent = call(
+    all_stats, first, first_sent = tie((all_stats, first, first_sent))
+    second, sent = call(
         functools.partial(keys_kernel, CHUNK),
-        (half, half),
-        (place, *pieces, feat, all_stats),
+        (half, shape((SEC, 128), BF)),
+        (place, *pieces, feat, all_stats, first_sent),
         scratch=(pltpu.VMEM((NSEC * 8, 128), F32), pltpu.SemaphoreType.DMA((NSEC,))),
         flops=2 * 128 * 4 * pairs,
         transcendentals=pairs,
     )
-    second, second_sent, first_other = lax.optimization_barrier((second, second_sent, first_other))
-    second_other = swap(second_sent)
+    back = swap(sent)
     partial = call(
         weights_kernel,
         shape((16, 96, 128), BF),
-        (tok, tok_other, first, first_sent, second, second_sent),
+        (tok, tok_other, first, second, sent),
         flops=2 * 512 * 1024 * 256,
         smem=0,
     )
     partial = lax.all_to_all(partial, ("b",) + Z, 0, 0, tiled=True)
-    partial, second_other = tie((partial, second_other))
-    total = call(sum_kernel, shape((32, 96, 128), BF), (partial,), smem=0)
     att, keep, send = call(
         input_kernel,
         (half, shape((4, 32, 1024), F32), shape((4, 32, 1024), BF)),
-        (place, first, first_other, second, second_other, wq, wk, wv),
+        (place, first, second, back, wq, wk, wv),
         flops=6 * 256 * 1024 * 128,
     )
+    partial, send = tie((partial, send))
     arrived = lax.ppermute(send, "core", [(0, 1), (1, 0)])
+    total = call(sum_kernel, shape((32, 96, 128), BF), (partial,), smem=0)
     both = keep + arrived.astype(F32)
     share = lax.dynamic_index_in_dim(both, y, 0, False)
     both_bf = both.astype(BF)

time: 116 us -> 116 us (level)
  starting transfers between devices: 56.6 us -> 54.1 us
  Pallas kernels: 29.8 us -> 31.1 us
  waiting for transfers between devices: 25.1 us -> 26.3 us
    ppermute x4 -> x3, starting transfers between devices: 11.2 us -> 5.96 us  [swap(): return lax.ppermute(a, 'xh', [(0, 1), (1, 0)])]
    ppermute x14, waiting for transfers between devices: 3.13 us -> 7.16 us  [shift(): return lax.ppermute(a, Z, [(i, (i + step) % NSEC) for i in range(NSEC)])]
    all_to_all x1, waiting for transfers between devices: 4.46 us -> 1.47 us  [on_device(): partial = lax.all_to_all(partial, ('b',) + Z, 0, 0, tiled=True)]
    all_to_all x1, starting transfers between devices: 5.89 us -> 8.2 us  [on_device(): total = lax.all_to_all(total, ('b',) + CTX, 0, 0, tiled=True)]
    ppermute x14, starting transfers between devices: 25.9 us -> 23.9 us  [shift(): return lax.ppermute(a, Z, [(i, (i + step) % NSEC) for i in range(NSEC)])]
    all_to_all x1, starting transfers between devices: 4.39 us -> 6.15 us  [on_device(): lax.all_to_all(stats, Z, 0, 0, tiled=True).reshape(NSEC * 8, 128)]
    all_to_all x1, waiting for transfers between devices: 3.79 us -> 5.49 us  [on_device(): total = lax.all_to_all(total, ('b',) + CTX, 0, 0, tiled=True)]
    pallas_call x8 -> x9, Pallas kernels: 29.8 us -> 31.1 us  [call(): pl.pallas_call(kernel, out_shape=outs, in_specs=specs, out_specs=jax.tree...]
  transfers between devices with their start and end apart: 25 -> 24, of which waited for: 11 -> 12; matrix products, arithmetic and copies ran while one was open for 1% -> 1% of each run, Pallas kernels for 17% -> 20%
where the time goes in v6:
time: 116 us
  starting transfers between devices  54.1 us (47%)
  Pallas kernels  31.1 us (27%)
  waiting for transfers between devices  26.3 us (23%)
  local copies, waits for them, and re-layouts  2.24 us (2%)
  other arithmetic  1.32 us (1%)
    pallas_call x9, Pallas kernels, call(): pl.pallas_call(kernel, out_shape=outs, in_specs=specs, out_specs=jax.tree...  31.1 us
    ppermute x14, starting transfers between devices, shift(): return lax.ppermute(a, Z, [(i, (i + step) % NSEC) for i in range(NSEC)])  23.9 us
    all_to_all x1, starting transfers between devices, on_device(): total = lax.all_to_all(total, ('b',) + CTX, 0, 0, tiled=True)  8.2 us
    ppermute x14, waiting for transfers between devices, shift(): return lax.ppermute(a, Z, [(i, (i + step) % NSEC) for i in range(NSEC)])  7.16 us
    all_to_all x1, starting transfers between devices, on_device(): lax.all_to_all(stats, Z, 0, 0, tiled=True).reshape(NSEC * 8, 128)  6.15 us
    ppermute x3, starting transfers between devices, swap(): return lax.ppermute(a, 'xh', [(0, 1), (1, 0)])  5.96 us
    all_to_all x1, starting transfers between devices, on_device(): partial = lax.all_to_all(partial, ('b',) + Z, 0, 0, tiled=True)  5.64 us
    all_to_all x1, waiting for transfers between devices, on_device(): total = lax.all_to_all(total, ('b',) + CTX, 0, 0, tiled=True)  5.49 us
  transfers between devices with their start and end apart: 24, of which 12 were waited for; matrix products, arithmetic and copies ran while one was open for 1% of the time, Pallas kernels for 20%

profile of v6, /device:TPU:8, one launch (start us, length us, event | category | flops | bytes accessed | tf_op | source)
XLA Modules:
  0.0 115.8 jit_solution(14130638880797508569)
XLA Ops:
  0.6 0.6 pad_add_fusion.place
  1.2 3.5 %shard_map.110 = (bf16[512,128]{1,0:T(8,128)(2,1)}, bf16[512,128]{1,0:T(8,128)(2,1)}) custom-call(s32[3]{0:T(128)} %pad_add_fusion.place, bf16[256,1024]{1,0:T(8,128)(2,1)} %bitcast.25, bf16[1024,128]{1,0:T(8,128)(2,1)} %wq.3, bf16[1024,128]{1,0:T(8,128)(2,1)} %wk.3, bf16[1024,128]{1,0:T(8,128)(2,1)} %wv.3, bf16[256,128]{1,0:T(8,128)(2,1)} %bitcast.29), custom_call_target="tpu_custom_call" | custom-call | flops 201326592 | bytes 1376268 | tf_op jit(solution)/shard_map/pallas_call | solution.py:44
  4.8 3.1 %collective-permute-start = (bf16[512,128]{1,0:T(8,128)(2,1)}, bf16[512,128]{1,0:T(8,128)(2,1)}, u32[]{:S(2)}, u32[]{:S(2)}) collective-permute-start(bf16[512,128]{1,0:T(8,128)(2,1)} %get-tuple-element.33), channel_id=1, source_target_pairs={{0,8},{8,0},{1,9},{9,1},{2,10},{10,2},{3,11},{11,3},{4,12},{12,4},... | collective-permute-start | bytes 393224 | tf_op jit(solution)/shard_map/ppermute | solution.py:342
  7.9 1.9 %collective-permute-start.1 = (bf16[512,128]{1,0:T(8,128)(2,1)}, bf16[512,128]{1,0:T(8,128)(2,1)}, u32[]{:S(2)}, u32[]{:S(2)}) collective-permute-start(bf16[512,128]{1,0:T(8,128)(2,1)} %get-tuple-element.32.refs_0_), channel_id=1, source_target_pairs={{0,16},{16,32},{32,48},{48,64},{64,80},{80,96},{96,112},{112,0},{1... | collective-permute-start | bytes 393224 | tf_op jit(solution)/shard_map/ppermute | solution.py:338
  9.8 3.9 %collective-permute-start.2 = (bf16[512,128]{1,0:T(8,128)(2,1)}, bf16[512,128]{1,0:T(8,128)(2,1)}, u32[]{:S(2)}, u32[]{:S(2)}) collective-permute-start(bf16[512,128]{1,0:T(8,128)(2,1)} %get-tuple-element.32.refs_0_), channel_id=1, source_target_pairs={{0,112},{16,0},{32,16},{48,32},{64,48},{80,64},{96,80},{112,96},{1... | collective-permute-start | bytes 393224 | tf_op jit(solution)/shard_map/ppermute | solution.py:338
  13.8 3.6 %shard_map.111.refs_16_ = bf16[4096,128]{1,0:T(8,128)(2,1)} custom-call(s32[3]{0:T(128)} %pad_add_fusion.place, s32[1,8]{1,0:T(1,128)} %lengths.1, s32[1,256]{1,0:T(1,128)} %spots.1), custom_call_target="tpu_custom_call" | custom-call | bytes 1068 | tf_op jit(solution)/shard_map/pallas_call | solution.py:44
  17.3 2.9 %collective-permute-start.4 = (bf16[512,128]{1,0:T(8,128)(2,1)}, bf16[512,128]{1,0:T(8,128)(2,1)S(1)}, u32[]{:S(2)}, u32[]{:S(2)}) collective-permute-start(bf16[512,128]{1,0:T(8,128)(2,1)} %collective-permute-done.refs_1_), channel_id=1, source_target_pairs={{0,112},{16,0},{32,16},{48,32},{64,48},{80,64},{96,80},{112,96},{1... | collective-permute-start | bytes 393224 | tf_op jit(solution)/shard_map/ppermute | solution.py:338
  20.3 2.8 %collective-permute-done.4.refs_5_ = bf16[512,128]{1,0:T(8,128)(2,1)S(1)} collective-permute-done((bf16[512,128]{1,0:T(8,128)(2,1)}, bf16[512,128]{1,0:T(8,128)(2,1)S(1)}, u32[]{:S(2)}, u32[]{:S(2)}) %collective-permute-start.4) | collective-permute-done | bytes 131104 | tf_op jit(solution)/shard_map/ppermute | solution.py:338
  23.1 3.6 %collective-permute-start.8 = (bf16[512,128]{1,0:T(8,128)(2,1)S(1)}, bf16[512,128]{1,0:T(8,128)(2,1)S(1)}, u32[]{:S(2)}, u32[]{:S(2)}) collective-permute-start(bf16[512,128]{1,0:T(8,128)(2,1)S(1)} %collective-permute-done.4.refs_5_), channel_id=1, source_target_pairs={{0,112},{16,0},{32,16},{48,32},{64,48},{80,64},{96,80},{112,96},{1... | collective-permute-start | bytes 393224 | tf_op jit(solution)/shard_map/ppermute | solution.py:338
  26.6 0.0 collective-permute-start.7
  26.7 2.0 %collective-permute-start.6 = (bf16[512,128]{1,0:T(8,128)(2,1)S(1)}, bf16[512,128]{1,0:T(8,128)(2,1)S(1)}, u32[]{:S(2)}, u32[]{:S(2)}) collective-permute-start(bf16[512,128]{1,0:T(8,128)(2,1)S(1)} %collective-permute-done.3.refs_3_), channel_id=1, source_target_pairs={{0,16},{16,32},{32,48},{48,64},{64,80},{80,96},{96,112},{112,0},{1... | collective-permute-start | bytes 393224 | tf_op jit(solution)/shard_map/ppermute | solution.py:338
  28.7 0.1 collective-permute-start.9
  28.8 0.7 collective-permute-done.8.refs_9_
  29.5 3.4 %collective-permute-start.12 = (bf16[512,128]{1,0:T(8,128)(2,1)S(1)}, bf16[512,128]{1,0:T(8,128)(2,1)S(1)}, u32[]{:S(2)}, u32[]{:S(2)}) collective-permute-start(bf16[512,128]{1,0:T(8,128)(2,1)S(1)} %collective-permute-done.8.refs_9_), channel_id=1, source_target_pairs={{0,112},{16,0},{32,16},{48,32},{64,48},{80,64},{96,80},{112,96},{1... | collective-permute-start | bytes 393224 | tf_op jit(solution)/shard_map/ppermute | solution.py:338
  32.9 2.8 %collective-permute-start.11 = (bf16[512,128]{1,0:T(8,128)(2,1)S(1)}, bf16[512,128]{1,0:T(8,128)(2,1)S(1)}, u32[]{:S(2)}, u32[]{:S(2)}) collective-permute-start(bf16[512,128]{1,0:T(8,128)(2,1)S(1)} %collective-permute-done.7.refs_8_), channel_id=1, source_target_pairs={{0,112},{16,0},{32,16},{48,32},{64,48},{80,64},{96,80},{112,96},{1... | collective-permute-start | bytes 393224 | tf_op jit(solution)/shard_map/ppermute | solution.py:338
  35.7 0.3 collective-permute-done.9.refs_10_
  35.9 0.7 collective-permute-start.13
  36.6 2.6 %collective-permute-start.14 = (bf16[512,128]{1,0:T(8,128)(2,1)S(1)}, bf16[512,128]{1,0:T(8,128)(2,1)S(1)}, u32[]{:S(2)}, u32[]{:S(2)}) collective-permute-start(bf16[512,128]{1,0:T(8,128)(2,1)S(1)} %collective-permute-done.12.refs_13_), channel_id=1, source_target_pairs={{0,112},{16,0},{32,16},{48,32},{64,48},{80,64},{96,80},{112,96},{1... | collective-permute-start | bytes 393224 | tf_op jit(solution)/shard_map/ppermute | solution.py:338
  39.2 0.7 collective-permute-start.16
  39.9 1.9 %collective-permute-done.10.refs_11_ = bf16[512,128]{1,0:T(8,128)(2,1)S(1)} collective-permute-done((bf16[512,128]{1,0:T(8,128)(2,1)S(1)}, bf16[512,128]{1,0:T(8,128)(2,1)S(1)}, u32[]{:S(2)}, u32[]{:S(2)}) %collective-permute-start.10) | collective-permute-done | bytes 131104 | tf_op jit(solution)/shard_map/ppermute | solution.py:338
  41.8 1.4 %collective-permute-done.13.refs_14_ = bf16[512,128]{1,0:T(8,128)(2,1)S(1)} collective-permute-done((bf16[512,128]{1,0:T(8,128)(2,1)S(1)}, bf16[512,128]{1,0:T(8,128)(2,1)S(1)}, u32[]{:S(2)}, u32[]{:S(2)}) %collective-permute-start.13) | collective-permute-done | bytes 131104 | tf_op jit(solution)/shard_map/ppermute | solution.py:338
  43.3 0.7 copy-done.4
  43.9 0.9 copy-done.6
  44.8 5.7 %shard_map.112 = (bf16[512,128]{1,0:T(8,128)(2,1)S(1)}, f32[512,128]{1,0:T(8,128)S(1)}, f32[8,8,128]{2,1,0:T(8,128)}) custom-call(s32[3]{0:T(128)S(1)} %copy-done.4, bf16[512,128]{1,0:T(8,128)(2,1)S(1)} %copy-done.6, bf16[512,128]{1,0:T(8,128)(2,1)} %collective-permute-done.refs_1_, bf16[512,128]{1,0:T(8,128)(2,1)} %collective-permute-done.1.refs_2_, ...), custom_call_target="tpu_custom_call" | custom-call | flops 1073741824 | bytes 3145740 | tf_op jit(solution)/shard_map/pallas_call | solution.py:44
  50.6 6.2 %all-to-all-start = ((f32[8,8,128]{2,1,0:T(8,128)}), f32[8,8,128]{2,1,0:T(8,128)S(1)}, u32[]{:S(2)}, u32[]{:S(2)}) async-start(f32[8,8,128]{2,1,0:T(8,128)} %get-tuple-element.39), calls=%async_computation | async-start | bytes 65536 | tf_op jit(solution)/shard_map/all_to_all | solution.py:400
  56.7 0.6 copy-done.5
  57.4 5.5 %shard_map.113 = (bf16[256,128]{1,0:T(8,128)(2,1)S(1)}, bf16[256,128]{1,0:T(8,128)(2,1)S(1)}) custom-call(s32[3]{0:T(128)S(1)} %copy-done.5, bf16[512,128]{1,0:T(8,128)(2,1)S(1)} %copy-done.7, bf16[512,128]{1,0:T(8,128)(2,1)} %collective-permute-done.refs_1_, bf16[512,128]{1,0:T(8,128)(2,1)} %collective-permute-done.1.refs_2_, ...), custom_call_target="tpu_custom_call" | custom-call | flops 1610612736 | bytes 3538956 | tf_op jit(solution)/shard_map/pallas_call | solution.py:44
  62.9 1.9 %all-to-all-done = f32[8,8,128]{2,1,0:T(8,128)S(1)} async-done(((f32[8,8,128]{2,1,0:T(8,128)}), f32[8,8,128]{2,1,0:T(8,128)S(1)}, u32[]{:S(2)}, u32[]{:S(2)}) %all-to-all-start) | async-done | bytes 32800 | tf_op jit(solution)/shard_map/all_to_all | solution.py:400
  64.7 7.0 %shard_map.114 = (bf16[256,128]{1,0:T(8,128)(2,1)S(1)}, bf16[512,128]{1,0:T(8,128)(2,1)S(1)}) custom-call(s32[3]{0:T(128)S(1)} %copy-done.5, bf16[512,128]{1,0:T(8,128)(2,1)S(1)} %copy-done.7, bf16[512,128]{1,0:T(8,128)(2,1)} %collective-permute-done.refs_1_, bf16[512,128]{1,0:T(8,128)(2,1)} %collective-permute-done.1.refs_2_, ...), custom_call_target="tpu_custom_call" | custom-call | flops 2147483648 | bytes 3244044 | tf_op jit(solution)/shard_map/pallas_call | solution.py:44
  71.8 1.6 %shard_map.116 = bf16[16,96,128]{2,1,0:T(8,128)(2,1)} custom-call(bf16[256,1024]{1,0:T(8,128)(2,1)S(1)} %bitcast.27, bf16[256,1024]{1,0:T(8,128)(2,1)S(1)} %collective-permute-done.16.tok_other, bf16[256,128]{1,0:T(8,128)(2,1)S(1)} %get-tuple-element.44.first, bf16[256,128]{1,0:T(8,128)(2,1)S(1)} %get-tuple-element.47.second, ...), custom_call_target="tpu_custom_call" | custom-call | flops 268435456 | bytes 1310720 | tf_op jit(solution)/shard_map/pallas_call | solution.py:44
  73.4 5.6 %all-to-all-start.1 = ((bf16[16,96,128]{2,1,0:T(8,128)(2,1)}), bf16[16,96,128]{2,1,0:T(8,128)(2,1)S(1)}, u32[]{:S(2)}, u32[]{:S(2)}) async-start(bf16[16,96,128]{2,1,0:T(8,128)(2,1)} %shard_map.116), calls=%async_computation.1 | async-start | bytes 786432 | tf_op jit(solution)/shard_map/all_to_all | solution.py:426
  79.0 2.1 %collective-permute-start.15 = (bf16[512,128]{1,0:T(8,128)(2,1)S(1)}, bf16[512,128]{1,0:T(8,128)(2,1)S(1)}, u32[]{:S(2)}, u32[]{:S(2)}) collective-permute-start(bf16[512,128]{1,0:T(8,128)(2,1)S(1)} %get-tuple-element.48.sent), channel_id=1, source_target_pairs={{0,8},{8,0},{1,9},{9,1},{2,10},{10,2},{3,11},{11,3},{4,12},{12,4},... | collective-permute-start | bytes 393224 | tf_op jit(solution)/shard_map/ppermute | solution.py:342
  81.1 5.0 %collective-permute-done.15.arrived = bf16[512,128]{1,0:T(8,128)(2,1)S(1)} collective-permute-done((bf16[512,128]{1,0:T(8,128)(2,1)S(1)}, bf16[512,128]{1,0:T(8,128)(2,1)S(1)}, u32[]{:S(2)}, u32[]{:S(2)}) %collective-permute-start.15) | collective-permute-done | bytes 131104 | tf_op jit(solution)/shard_map/ppermute | solution.py:342
  86.1 1.7 %shard_map.115 = (bf16[256,128]{1,0:T(8,128)(2,1)}, f32[4,32,1024]{2,1,0:T(8,128)S(1)}, bf16[4,32,1024]{2,1,0:T(8,128)(2,1)S(1)}) custom-call(s32[3]{0:T(128)S(1)} %copy-done.5, bf16[256,128]{1,0:T(8,128)(2,1)S(1)} %get-tuple-element.44.first, bf16[256,128]{1,0:T(8,128)(2,1)S(1)} %get-tuple-element.47.second, ...), custom_call_target="tpu_custom_call" | custom-call | flops 201326592 | bytes 1048588 | tf_op jit(solution)/shard_map/pallas_call | solution.py:44
  87.9 1.5 %all-to-all-done.1.parts = bf16[16,96,128]{2,1,0:T(8,128)(2,1)S(1)} async-done(((bf16[16,96,128]{2,1,0:T(8,128)(2,1)}), bf16[16,96,128]{2,1,0:T(8,128)(2,1)S(1)}, u32[]{:S(2)}, u32[]{:S(2)}) %all-to-all-start.1) | async-done | bytes 393248 | tf_op jit(solution)/shard_map/all_to_all | solution.py:426
  89.3 1.0 shard_map.117
  90.3 8.2 %all-to-all-start.2 = ((bf16[32,96,128]{2,1,0:T(8,128)(2,1)}), bf16[32,96,128]{2,1,0:T(8,128)(2,1)S(1)}, u32[]{:S(2)}, u32[]{:S(2)}) async-start(bf16[32,96,128]{2,1,0:T(8,128)(2,1)} %shard_map.117), calls=%async_computation.2 | async-start | bytes 1572864 | tf_op jit(solution)/shard_map/all_to_all | solution.py:442
  98.5 0.1 collective-permute-start.17
  98.6 1.5 %collective-permute-done.17 = bf16[4,32,1024]{2,1,0:T(8,128)(2,1)S(1)} collective-permute-done((bf16[4,32,1024]{2,1,0:T(8,128)(2,1)S(1)}, bf16[4,32,1024]{2,1,0:T(8,128)(2,1)S(1)}, u32[]{:S(2)}, u32[]{:S(2)}) %collective-permute-start.17) | collective-permute-done | bytes 262176 | tf_op jit(solution)/shard_map/ppermute | solution.py:434
  100.1 0.1 fusion.4
  100.3 1.7 %collective-permute-start.20 = (bf16[32,1024]{1,0:T(8,128)(2,1)S(1)}, bf16[32,1024]{1,0:T(8,128)(2,1)S(1)}, u32[]{:S(2)}, u32[]{:S(2)}) collective-permute-start(bf16[32,1024]{1,0:T(8,128)(2,1)S(1)} %get-tuple-element.60), channel_id=1, source_target_pairs={{0,6},{2,4},{4,2},{6,0},{1,7},{3,5},{5,3},{7,1},{8,14},{10,12},{12... | collective-permute-start | bytes 196616 | tf_op jit(solution)/shard_map/ppermute | solution.py:441
  101.9 0.9 collective-permute-start.19
  102.8 1.6 %collective-permute-start.18 = (bf16[32,1024]{1,0:T(8,128)(2,1)S(1)}, bf16[32,1024]{1,0:T(8,128)(2,1)S(1)}, u32[]{:S(2)}, u32[]{:S(2)}) collective-permute-start(bf16[32,1024]{1,0:T(8,128)(2,1)S(1)} %get-tuple-element.59), channel_id=1, source_target_pairs={{0,2},{2,0},{4,6},{6,4},{1,3},{3,1},{5,7},{7,5},{8,10},{10,8},{12,... | collective-permute-start | bytes 196616 | tf_op jit(solution)/shard_map/ppermute | solution.py:441
  104.4 0.2 collective-permute-done.20
  104.6 3.7 %collective-permute-done.19 = bf16[32,1024]{1,0:T(8,128)(2,1)S(1)} collective-permute-done((bf16[32,1024]{1,0:T(8,128)(2,1)S(1)}, bf16[32,1024]{1,0:T(8,128)(2,1)S(1)}, u32[]{:S(2)}, u32[]{:S(2)}) %collective-permute-start.19) | collective-permute-done | bytes 65568 | tf_op jit(solution)/shard_map/ppermute | solution.py:441
  108.3 0.7 fusion.3
  108.9 5.5 %all-to-all-done.2.parts = bf16[32,96,128]{2,1,0:T(8,128)(2,1)S(1)} async-done(((bf16[32,96,128]{2,1,0:T(8,128)(2,1)}), bf16[32,96,128]{2,1,0:T(8,128)(2,1)S(1)}, u32[]{:S(2)}, u32[]{:S(2)}) %all-to-all-start.2) | async-done | bytes 786464 | tf_op jit(solution)/shard_map/all_to_all | solution.py:442
  114.4 1.4 %shard_map.118 = (f32[1024,128]{1,0:T(8,128)}, f32[1024,128]{1,0:T(8,128)}, f32[1024,128]{1,0:T(8,128)}) custom-call(bf16[32,96,128]{2,1,0:T(8,128)(2,1)S(1)} %all-to-all-done.2.parts), custom_call_target="tpu_custom_call" | custom-call | bytes 786432 | tf_op jit(solution)/shard_map/pallas_call | solution.py:44
  (29 shorter events, 0.1 us)
Async XLA Ops:
  4.8 12.5 %collective-permute-start = (bf16[512,128]{1,0:T(8,128)(2,1)}, bf16[512,128]{1,0:T(8,128)(2,1)}, u32[]{:S(2)}, u32[]{:S(2)}) collective-permute-start(bf16[512,128]{1,0:T(8,128)(2,1)} %get-tuple-element.33), channel_id=1, source_target_pairs={{0,8},{8,0},{1,9},{9,1},{2,10},{10,2},{3,11},{11,3},{4,12},{12,4},... | collective-permute-start | bytes 393224 | tf_op jit(solution)/shard_map/ppermute | solution.py:342
  7.9 9.4 %collective-permute-start.1 = (bf16[512,128]{1,0:T(8,128)(2,1)}, bf16[512,128]{1,0:T(8,128)(2,1)}, u32[]{:S(2)}, u32[]{:S(2)}) collective-permute-start(bf16[512,128]{1,0:T(8,128)(2,1)} %get-tuple-element.32.refs_0_), channel_id=1, source_target_pairs={{0,16},{16,32},{32,48},{48,64},{64,80},{80,96},{96,112},{112,0},{1... | collective-permute-start | bytes 393224 | tf_op jit(solution)/shard_map/ppermute | solution.py:338
  9.8 7.5 %collective-permute-start.2 = (bf16[512,128]{1,0:T(8,128)(2,1)}, bf16[512,128]{1,0:T(8,128)(2,1)}, u32[]{:S(2)}, u32[]{:S(2)}) collective-permute-start(bf16[512,128]{1,0:T(8,128)(2,1)} %get-tuple-element.32.refs_0_), channel_id=1, source_target_pairs={{0,112},{16,0},{32,16},{48,32},{64,48},{80,64},{96,80},{112,96},{1... | collective-permute-start | bytes 393224 | tf_op jit(solution)/shard_map/ppermute | solution.py:338
  17.3 5.8 %collective-permute-start.4 = (bf16[512,128]{1,0:T(8,128)(2,1)}, bf16[512,128]{1,0:T(8,128)(2,1)S(1)}, u32[]{:S(2)}, u32[]{:S(2)}) collective-permute-start(bf16[512,128]{1,0:T(8,128)(2,1)} %collective-permute-done.refs_1_), channel_id=1, source_target_pairs={{0,112},{16,0},{32,16},{48,32},{64,48},{80,64},{96,80},{112,96},{1... | collective-permute-start | bytes 393224 | tf_op jit(solution)/shard_map/ppermute | solution.py:338
  20.2 6.4 %collective-permute-start.3 = (bf16[512,128]{1,0:T(8,128)(2,1)}, bf16[512,128]{1,0:T(8,128)(2,1)S(1)}, u32[]{:S(2)}, u32[]{:S(2)}) collective-permute-start(bf16[512,128]{1,0:T(8,128)(2,1)} %collective-permute-done.refs_1_), channel_id=1, source_target_pairs={{0,16},{16,32},{32,48},{48,64},{64,80},{80,96},{96,112},{112,0},{1... | collective-permute-start | bytes 393224 | tf_op jit(solution)/shard_map/ppermute | solution.py:338
  20.2 8.4 %collective-permute-start.5 = (bf16[512,128]{1,0:T(8,128)(2,1)}, bf16[512,128]{1,0:T(8,128)(2,1)S(1)}, u32[]{:S(2)}, u32[]{:S(2)}) collective-permute-start(bf16[512,128]{1,0:T(8,128)(2,1)} %collective-permute-done.1.refs_2_), channel_id=1, source_target_pairs={{0,16},{16,32},{32,48},{48,64},{64,80},{80,96},{96,112},{112,0},{1... | collective-permute-start | bytes 393224 | tf_op jit(solution)/shard_map/ppermute | solution.py:338
  23.1 6.4 %collective-permute-start.8 = (bf16[512,128]{1,0:T(8,128)(2,1)S(1)}, bf16[512,128]{1,0:T(8,128)(2,1)S(1)}, u32[]{:S(2)}, u32[]{:S(2)}) collective-permute-start(bf16[512,128]{1,0:T(8,128)(2,1)S(1)} %collective-permute-done.4.refs_5_), channel_id=1, source_target_pairs={{0,112},{16,0},{32,16},{48,32},{64,48},{80,64},{96,80},{112,96},{1... | collective-permute-start | bytes 393224 | tf_op jit(solution)/shard_map/ppermute | solution.py:338
  26.6 6.2 %collective-permute-start.7 = (bf16[512,128]{1,0:T(8,128)(2,1)}, bf16[512,128]{1,0:T(8,128)(2,1)S(1)}, u32[]{:S(2)}, u32[]{:S(2)}) collective-permute-start(bf16[512,128]{1,0:T(8,128)(2,1)} %collective-permute-done.2.refs_4_), channel_id=1, source_target_pairs={{0,112},{16,0},{32,16},{48,32},{64,48},{80,64},{96,80},{112,96},{1... | collective-permute-start | bytes 393224 | tf_op jit(solution)/shard_map/ppermute | solution.py:338
  26.7 9.0 %collective-permute-start.6 = (bf16[512,128]{1,0:T(8,128)(2,1)S(1)}, bf16[512,128]{1,0:T(8,128)(2,1)S(1)}, u32[]{:S(2)}, u32[]{:S(2)}) collective-permute-start(bf16[512,128]{1,0:T(8,128)(2,1)S(1)} %collective-permute-done.3.refs_3_), channel_id=1, source_target_pairs={{0,16},{16,32},{32,48},{48,64},{64,80},{80,96},{96,112},{112,0},{1... | collective-permute-start | bytes 393224 | tf_op jit(solution)/shard_map/ppermute | solution.py:338
  28.7 7.3 %collective-permute-start.9 = (bf16[512,128]{1,0:T(8,128)(2,1)S(1)}, bf16[512,128]{1,0:T(8,128)(2,1)S(1)}, u32[]{:S(2)}, u32[]{:S(2)}) collective-permute-start(bf16[512,128]{1,0:T(8,128)(2,1)S(1)} %collective-permute-done.5.refs_6_), channel_id=1, source_target_pairs={{0,16},{16,32},{32,48},{48,64},{64,80},{80,96},{96,112},{112,0},{1... | collective-permute-start | bytes 393224 | tf_op jit(solution)/shard_map/ppermute | solution.py:338
  29.5 7.1 %collective-permute-start.12 = (bf16[512,128]{1,0:T(8,128)(2,1)S(1)}, bf16[512,128]{1,0:T(8,128)(2,1)S(1)}, u32[]{:S(2)}, u32[]{:S(2)}) collective-permute-start(bf16[512,128]{1,0:T(8,128)(2,1)S(1)} %collective-permute-done.8.refs_9_), channel_id=1, source_target_pairs={{0,112},{16,0},{32,16},{48,32},{64,48},{80,64},{96,80},{112,96},{1... | collective-permute-start | bytes 393224 | tf_op jit(solution)/shard_map/ppermute | solution.py:338
  32.9 7.0 %collective-permute-start.11 = (bf16[512,128]{1,0:T(8,128)(2,1)S(1)}, bf16[512,128]{1,0:T(8,128)(2,1)S(1)}, u32[]{:S(2)}, u32[]{:S(2)}) collective-permute-start(bf16[512,128]{1,0:T(8,128)(2,1)S(1)} %collective-permute-done.7.refs_8_), channel_id=1, source_target_pairs={{0,112},{16,0},{32,16},{48,32},{64,48},{80,64},{96,80},{112,96},{1... | collective-permute-start | bytes 393224 | tf_op jit(solution)/shard_map/ppermute | solution.py:338
  35.7 6.2 %collective-permute-start.10 = (bf16[512,128]{1,0:T(8,128)(2,1)S(1)}, bf16[512,128]{1,0:T(8,128)(2,1)S(1)}, u32[]{:S(2)}, u32[]{:S(2)}) collective-permute-start(bf16[512,128]{1,0:T(8,128)(2,1)S(1)} %collective-permute-done.6.refs_7_), channel_id=1, source_target_pairs={{0,16},{16,32},{32,48},{48,64},{64,80},{80,96},{96,112},{112,0},{1... | collective-permute-start | bytes 393224 | tf_op jit(solution)/shard_map/ppermute | solution.py:338
  35.9 7.3 %collective-permute-start.13 = (bf16[512,128]{1,0:T(8,128)(2,1)S(1)}, bf16[512,128]{1,0:T(8,128)(2,1)S(1)}, u32[]{:S(2)}, u32[]{:S(2)}) collective-permute-start(bf16[512,128]{1,0:T(8,128)(2,1)S(1)} %collective-permute-done.9.refs_10_), channel_id=1, source_target_pairs={{0,16},{16,32},{32,48},{48,64},{64,80},{80,96},{96,112},{112,0},{1... | collective-permute-start | bytes 393224 | tf_op jit(solution)/shard_map/ppermute | solution.py:338
  36.6 6.7 %collective-permute-start.14 = (bf16[512,128]{1,0:T(8,128)(2,1)S(1)}, bf16[512,128]{1,0:T(8,128)(2,1)S(1)}, u32[]{:S(2)}, u32[]{:S(2)}) collective-permute-start(bf16[512,128]{1,0:T(8,128)(2,1)S(1)} %collective-permute-done.12.refs_13_), channel_id=1, source_target_pairs={{0,112},{16,0},{32,16},{48,32},{64,48},{80,64},{96,80},{112,96},{1... | collective-permute-start | bytes 393224 | tf_op jit(solution)/shard_map/ppermute | solution.py:338
  39.2 32.6 %collective-permute-start.16 = (bf16[256,1024]{1,0:T(8,128)(2,1)}, bf16[256,1024]{1,0:T(8,128)(2,1)S(1)}, u32[]{:S(2)}, u32[]{:S(2)}) collective-permute-start(bf16[256,1024]{1,0:T(8,128)(2,1)} %bitcast.26), channel_id=1, source_target_pairs={{0,8},{8,0},{1,9},{9,1},{2,10},{10,2},{3,11},{11,3},{4,12},{12,4},... | collective-permute-start | bytes 1572872 | tf_op jit(solution)/shard_map/ppermute | solution.py:342
  43.3 0.7 copy-start.4
  43.9 0.9 copy-start.6
  44.8 11.9 %copy-start.7 = (bf16[512,128]{1,0:T(8,128)(2,1)S(1)}, bf16[512,128]{1,0:T(8,128)(2,1)}, u32[]{:S(2)}) copy-start(bf16[512,128]{1,0:T(8,128)(2,1)} %get-tuple-element.32.refs_0_) | copy-start | bytes 393220
  50.6 14.2 %all-to-all-start = ((f32[8,8,128]{2,1,0:T(8,128)}), f32[8,8,128]{2,1,0:T(8,128)S(1)}, u32[]{:S(2)}, u32[]{:S(2)}) async-start(f32[8,8,128]{2,1,0:T(8,128)} %get-tuple-element.39), calls=%async_computation | async-start | bytes 65536 | tf_op jit(solution)/shard_map/all_to_all | solution.py:400
  56.7 0.7 copy-start.5
  64.7 7.0 %copy-start = (bf16[1,256,1024]{2,1,0:T(8,128)(2,1)S(1)}, bf16[1,256,1024]{2,1,0:T(8,128)(2,1)}, u32[]{:S(2)}) copy-start(bf16[1,256,1024]{2,1,0:T(8,128)(2,1)} %param.7) | copy-start | bytes 1572868
  73.4 12.7 %copy-start.1 = (bf16[1024,128]{1,0:T(8,128)(2,1)S(1)}, bf16[1024,128]{1,0:T(8,128)(2,1)}, u32[]{:S(2)}) copy-start(bf16[1024,128]{1,0:T(8,128)(2,1)} %wq.3) | copy-start | bytes 786436
  73.4 12.7 %copy-start.2 = (bf16[1024,128]{1,0:T(8,128)(2,1)S(1)}, bf16[1024,128]{1,0:T(8,128)(2,1)}, u32[]{:S(2)}) copy-start(bf16[1024,128]{1,0:T(8,128)(2,1)} %wk.3) | copy-start | bytes 786436
  73.4 12.7 %copy-start.3 = (bf16[1024,128]{1,0:T(8,128)(2,1)S(1)}, bf16[1024,128]{1,0:T(8,128)(2,1)}, u32[]{:S(2)}) copy-start(bf16[1024,128]{1,0:T(8,128)(2,1)} %wv.3) | copy-start | bytes 786436
  73.4 16.0 %all-to-all-start.1 = ((bf16[16,96,128]{2,1,0:T(8,128)(2,1)}), bf16[16,96,128]{2,1,0:T(8,128)(2,1)S(1)}, u32[]{:S(2)}, u32[]{:S(2)}) async-start(bf16[16,96,128]{2,1,0:T(8,128)(2,1)} %shard_map.116), calls=%async_computation.1 | async-start | bytes 786432 | tf_op jit(solution)/shard_map/all_to_all | solution.py:426
  79.0 7.1 %collective-permute-start.15 = (bf16[512,128]{1,0:T(8,128)(2,1)S(1)}, bf16[512,128]{1,0:T(8,128)(2,1)S(1)}, u32[]{:S(2)}, u32[]{:S(2)}) collective-permute-start(bf16[512,128]{1,0:T(8,128)(2,1)S(1)} %get-tuple-element.48.sent), channel_id=1, source_target_pairs={{0,8},{8,0},{1,9},{9,1},{2,10},{10,2},{3,11},{11,3},{4,12},{12,4},... | collective-permute-start | bytes 393224 | tf_op jit(solution)/shard_map/ppermute | solution.py:342
  90.3 24.1 %all-to-all-start.2 = ((bf16[32,96,128]{2,1,0:T(8,128)(2,1)}), bf16[32,96,128]{2,1,0:T(8,128)(2,1)S(1)}, u32[]{:S(2)}, u32[]{:S(2)}) async-start(bf16[32,96,128]{2,1,0:T(8,128)(2,1)} %shard_map.117), calls=%async_computation.2 | async-start | bytes 1572864 | tf_op jit(solution)/shard_map/all_to_all | solution.py:442
  98.5 1.6 %collective-permute-start.17 = (bf16[4,32,1024]{2,1,0:T(8,128)(2,1)S(1)}, bf16[4,32,1024]{2,1,0:T(8,128)(2,1)S(1)}, u32[]{:S(2)}, u32[]{:S(2)}) collective-permute-start(bf16[4,32,1024]{2,1,0:T(8,128)(2,1)S(1)} %get-tuple-element.52), channel_id=1, source_target_pairs={{0,1},{1,0},{2,3},{3,2},{4,5},{5,4},{6,7},{7,6},{8,9},{9,8},{10,11... | collective-permute-start | bytes 786440 | tf_op jit(solution)/shard_map/ppermute | solution.py:434
  100.3 4.4 %collective-permute-start.20 = (bf16[32,1024]{1,0:T(8,128)(2,1)S(1)}, bf16[32,1024]{1,0:T(8,128)(2,1)S(1)}, u32[]{:S(2)}, u32[]{:S(2)}) collective-permute-start(bf16[32,1024]{1,0:T(8,128)(2,1)S(1)} %get-tuple-element.60), channel_id=1, source_target_pairs={{0,6},{2,4},{4,2},{6,0},{1,7},{3,5},{5,3},{7,1},{8,14},{10,12},{12... | collective-permute-start | bytes 196616 | tf_op jit(solution)/shard_map/ppermute | solution.py:441
  101.9 6.4 %collective-permute-start.19 = (bf16[32,1024]{1,0:T(8,128)(2,1)S(1)}, bf16[32,1024]{1,0:T(8,128)(2,1)S(1)}, u32[]{:S(2)}, u32[]{:S(2)}) collective-permute-start(bf16[32,1024]{1,0:T(8,128)(2,1)S(1)} %get-tuple-element.61), channel_id=1, source_target_pairs={{0,4},{2,6},{4,0},{6,2},{1,5},{3,7},{5,1},{7,3},{8,12},{10,14},{12... | collective-permute-start | bytes 196616 | tf_op jit(solution)/shard_map/ppermute | solution.py:441
  102.8 5.4 %collective-permute-start.18 = (bf16[32,1024]{1,0:T(8,128)(2,1)S(1)}, bf16[32,1024]{1,0:T(8,128)(2,1)S(1)}, u32[]{:S(2)}, u32[]{:S(2)}) collective-permute-start(bf16[32,1024]{1,0:T(8,128)(2,1)S(1)} %get-tuple-element.59), channel_id=1, source_target_pairs={{0,2},{2,0},{4,6},{6,4},{1,3},{3,1},{5,7},{7,5},{8,10},{10,8},{12,... | collective-permute-start | bytes 196616 | tf_op jit(solution)/shard_map/ppermute | solution.py:441

commit v7 on v6

--- a/solution.py
+++ b/solution.py
@@ -17,6 +17,7 @@
 NEG = -1e30
 LIMIT = 51 << 20
 CHUNK = 512
+SPLIT = 7
 FEATURE_LIMIT = 64 << 20
 BF = jnp.bfloat16
 F32 = jnp.float32
@@ -87,13 +88,13 @@
     lax.fori_loop(0, 2 * NSEC, one, 0)
 
 
-def project_kernel(place, tok, wq, wk, wv, cot, mine, theirs, *scratch):
+def project_kernel(tok, wq, wk, wv, cot, mine, theirs, *scratch):
     tok_v, wk_v, wv_v, wq_v, cot_v, sems = scratch
     pairs = ((tok, tok_v), (wk, wk_v), (wv, wv_v), (wq, wq_v), (cot, cot_v))
     copies = [pltpu.make_async_copy(a, b, sems.at[i]) for i, (a, b) in enumerate(pairs)]
     for copy in copies:
         copy.start()
-    first = place[0] == 0
+    first = lax.axis_index("xh") == 0
     copies[0].wait()
     t = tok_v[...]
     copies[1].wait()
@@ -173,22 +174,27 @@
     return jnp.where(jnp.abs(away) <= HALF, near, plain)
 
 
-def forward_kernel(place, *refs):
-    pieces, (feat, att_out, column_out, stats) = refs[: 2 * NSEC], refs[2 * NSEC :]
+def forward_kernel(lo, hi, place, own_a, own_b, feat, *refs):
+    pieces, refs = refs[: 2 * (hi - lo)], list(refs[2 * (hi - lo) :])
     flip, own = place[0], place[1]
-    own_qc = part_of(pieces, 0, 1)
+    own_qc = part_of((own_a, own_b), 0, 1)
     joined = join_query(own_qc, features_at(feat, own))
     near_rows = less_global(joined)
     row_places = places(own, flip, 0)
+    lanes = lax.broadcasted_iota(jnp.int32, (SEC, 128), 1)
+    if lo > 0:
+        acc_in, peak_in = refs.pop(0), refs.pop(0)
+        peak, total, acc = peak_in[:, 0:1], peak_in[:, 1:2], acc_in[...]
 
     def products(r):
-        kp = join_key(part_of(pieces, r, 0), features_at(feat, section_at(own, OFFSETS[r])))
+        kv = part_of(pieces, r - lo, 0)
+        kp = join_key(kv, features_at(feat, section_at(own, OFFSETS[r])))
         return dot(joined, kp, NT), dot(near_rows, kp, NT) if r < 3 else None
 
-    ahead = products(0)
-    for r in range(NSEC):
+    ahead = products(lo)
+    for r in range(lo, hi):
         plain, near = ahead
-        if r + 1 < NSEC:
+        if r + 1 < hi:
             ahead = products(r + 1)
         s = near_only(own, flip, r, row_places, near, plain)
         new_peak = jnp.max(s, axis=1, keepdims=True)
@@ -197,15 +203,20 @@
             keep = jnp.exp(peak - new_peak)
         e = jnp.exp(s - new_peak)
         new_total = jnp.sum(e, axis=1, keepdims=True)
-        new_acc = dot(e.astype(BF), part_of(pieces, r, 0))
+        new_acc = dot(e.astype(BF), part_of(pieces, r - lo, 0))
         if r > 0:
             new_total, new_acc = keep * total + new_total, keep * acc + new_acc
         peak, total, acc = new_peak, new_total, new_acc
+    if hi < NSEC:
+        acc_out, peak_out = refs
+        acc_out[...] = acc
+        peak_out[...] = jnp.where(lanes == 0, peak, total)
+        return
+    att_out, column_out, stats = refs
     att = (acc / total).astype(BF)
     att_out[...] = att
     cot = right_half(own_qc).astype(F32)
     delta = jnp.sum(att.astype(F32) * cot, axis=1, keepdims=True)
-    lanes = lax.broadcasted_iota(jnp.int32, (SEC, 128), 1)
     column = jnp.where(lanes == 0, peak + jnp.log(total), delta)
     column_out[...] = column
     turned = column.T
@@ -351,7 +362,7 @@
     mine, theirs = call(
         project_kernel,
         (shape((SEC, 128), BF),) * 2,
-        (place, tok, wq, wk, wv, cot),
+        (tok, wq, wk, wv, cot),
         scratch=(
             pltpu.VMEM((RUN, 1024), BF),
             weight,
@@ -361,6 +372,7 @@
             pltpu.SemaphoreType.DMA((5,)),
         ),
         flops=6 * 256 * 1024 * 128,
+        smem=0,
         manual=5,
         limit=64 << 20,
     )
@@ -390,12 +402,20 @@
     for i in (1, 2, 3):
         pieces += (lower_a[i], lower_b[i], upper_a[i], upper_b[i])
     pieces += far
+    state = call(
+        functools.partial(forward_kernel, 0, SPLIT),
+        (wide, wide),
+        (place, mine, other, feat, *pieces[: 2 * SPLIT]),
+        flops=2 * 128 * 2 * pairs * SPLIT // NSEC,
+        transcendentals=pairs * SPLIT // NSEC,
+    )
+    tok_other, *state = tie((tok_other, *state))
     att_rows, column, stats = call(
-        forward_kernel,
+        functools.partial(forward_kernel, SPLIT, NSEC),
         (shape((SEC, 128), BF), wide, shape((NSEC, 8, 128), F32)),
-        (place, *pieces, feat),
-        flops=2 * 128 * 2 * pairs,
-        transcendentals=pairs,
+        (place, mine, other, feat, *pieces[2 * SPLIT :], *state),
+        flops=2 * 128 * 2 * pairs * (NSEC - SPLIT) // NSEC,
+        transcendentals=pairs * (NSEC - SPLIT) // NSEC,
     )
     all_stats = lax.all_to_all(stats, Z, 0, 0, tiled=True).reshape(NSEC * 8, 128)
     half = shape((RUN, 128), BF)

time: 116 us -> 118 us (1.017)
  Pallas kernels: 31.1 us -> 34.4 us
  starting transfers between devices: 54.1 us -> 51.4 us
    pallas_call x9 -> x10, Pallas kernels: 31.1 us -> 34.4 us  [call(): pl.pallas_call(kernel, out_shape=outs, in_specs=specs, out_specs=jax.tree...]
    all_to_all x1, starting transfers between devices: 6.15 us -> 3.72 us  [on_device(): lax.all_to_all(stats, Z, 0, 0, tiled=True).reshape(NSEC * 8, 128)]
    ppermute x14, starting transfers between devices: 23.9 us -> 21.7 us  [shift(): return lax.ppermute(a, Z, [(i, (i + step) % NSEC) for i in range(NSEC)])]
    all_to_all x1, starting transfers between devices: 5.64 us -> 7.09 us  [on_device(): partial = lax.all_to_all(partial, ('b',) + Z, 0, 0, tiled=True)]
    all_to_all x1, waiting for transfers between devices: 5.49 us -> 6.83 us  [on_device(): total = lax.all_to_all(total, ('b',) + CTX, 0, 0, tiled=True)]
    ppermute x3, waiting for transfers between devices: 4.97 us -> 3.77 us  [swap(): return lax.ppermute(a, 'xh', [(0, 1), (1, 0)])]
  transfers between devices with their start and end apart: 24 -> 24, of which waited for: 12 -> 14; matrix products, arithmetic and copies ran while one was open for 1% -> 1% of each run, Pallas kernels for 20% -> 13%
where the time goes in v7:
time: 118 us; the launch traced here: 117 us
  starting transfers between devices  51.4 us (44%)
  Pallas kernels  34.4 us (29%)
  waiting for transfers between devices  26.7 us (23%)
  local copies, waits for them, and re-layouts  2.3 us (2%)
  other arithmetic  1.4 us (1%)
    pallas_call x10, Pallas kernels, call(): pl.pallas_call(kernel, out_shape=outs, in_specs=specs, out_specs=jax.tree...  34.4 us
    ppermute x14, starting transfers between devices, shift(): return lax.ppermute(a, Z, [(i, (i + step) % NSEC) for i in range(NSEC)])  21.7 us
    all_to_all x1, starting transfers between devices, on_device(): total = lax.all_to_all(total, ('b',) + CTX, 0, 0, tiled=True)  8.78 us
    all_to_all x1, starting transfers between devices, on_device(): partial = lax.all_to_all(partial, ('b',) + Z, 0, 0, tiled=True)  7.09 us
    all_to_all x1, waiting for transfers between devices, on_device(): total = lax.all_to_all(total, ('b',) + CTX, 0, 0, tiled=True)  6.83 us
    ppermute x14, waiting for transfers between devices, shift(): return lax.ppermute(a, Z, [(i, (i + step) % NSEC) for i in range(NSEC)])  6.79 us
    ppermute x3, starting transfers between devices, swap(): return lax.ppermute(a, 'xh', [(0, 1), (1, 0)])  6.48 us
    ppermute x3, waiting for transfers between devices, on_device(): lax.ppermute(out, 'y', [(i, i ^ k) for i in range(4)]).astype(F32)  4.09 us
  transfers between devices with their start and end apart: 24, of which 14 were waited for; matrix products, arithmetic and copies ran while one was open for 1% of the time, Pallas kernels for 13%

profile of v7, /device:TPU:8, one launch (start us, length us, event | category | flops | bytes accessed | tf_op | source)
XLA Modules:
  0.0 117.1 jit_solution(7809525354185553015)
XLA Ops:
  0.6 2.9 %shard_map.110 = (bf16[512,128]{1,0:T(8,128)(2,1)}, bf16[512,128]{1,0:T(8,128)(2,1)}) custom-call(bf16[256,1024]{1,0:T(8,128)(2,1)} %bitcast.25, bf16[1024,128]{1,0:T(8,128)(2,1)} %wq.3, bf16[1024,128]{1,0:T(8,128)(2,1)} %wk.3, bf16[1024,128]{1,0:T(8,128)(2,1)} %wv.3, bf16[256,128]{1,0:T(8,128)(2,1)} %bitcast.29), custom_call_target="tpu_custom_call" | custom-call | flops 201326592 | bytes 1376256 | tf_op jit(solution)/shard_map/pallas_call | solution.py:45
  3.5 2.0 %collective-permute-start.1 = (bf16[512,128]{1,0:T(8,128)(2,1)}, bf16[512,128]{1,0:T(8,128)(2,1)}, u32[]{:S(2)}, u32[]{:S(2)}) collective-permute-start(bf16[512,128]{1,0:T(8,128)(2,1)} %get-tuple-element.37.own_a.refs_0_), channel_id=1, source_target_pairs={{0,16},{16,32},{32,48},{48,64},{64,80},{80,96},{96,112},{112,0},{1... | collective-permute-start | bytes 393224 | tf_op jit(solution)/shard_map/ppermute | solution.py:349
  5.5 4.0 %collective-permute-start.2 = (bf16[512,128]{1,0:T(8,128)(2,1)}, bf16[512,128]{1,0:T(8,128)(2,1)}, u32[]{:S(2)}, u32[]{:S(2)}) collective-permute-start(bf16[512,128]{1,0:T(8,128)(2,1)} %get-tuple-element.37.own_a.refs_0_), channel_id=1, source_target_pairs={{0,112},{16,0},{32,16},{48,32},{64,48},{80,64},{96,80},{112,96},{1... | collective-permute-start | bytes 393224 | tf_op jit(solution)/shard_map/ppermute | solution.py:349
  9.5 3.0 %collective-permute-start = (bf16[512,128]{1,0:T(8,128)(2,1)}, bf16[512,128]{1,0:T(8,128)(2,1)}, u32[]{:S(2)}, u32[]{:S(2)}) collective-permute-start(bf16[512,128]{1,0:T(8,128)(2,1)} %get-tuple-element.38), channel_id=1, source_target_pairs={{0,8},{8,0},{1,9},{9,1},{2,10},{10,2},{3,11},{11,3},{4,12},{12,4},... | collective-permute-start | bytes 393224 | tf_op jit(solution)/shard_map/ppermute | solution.py:353
  12.6 0.5 collective-permute-start.10
  13.1 0.7 pad_add_fusion.place
  13.7 3.5 %shard_map.111.feat.refs_16_ = bf16[4096,128]{1,0:T(8,128)(2,1)} custom-call(s32[3]{0:T(128)} %pad_add_fusion.place, s32[1,8]{1,0:T(1,128)} %lengths.1, s32[1,256]{1,0:T(1,128)} %spots.1), custom_call_target="tpu_custom_call" | custom-call | bytes 1068 | tf_op jit(solution)/shard_map/pallas_call | solution.py:45
  17.3 2.0 %collective-permute-start.6 = (bf16[512,128]{1,0:T(8,128)(2,1)}, bf16[512,128]{1,0:T(8,128)(2,1)S(1)}, u32[]{:S(2)}, u32[]{:S(2)}) collective-permute-start(bf16[512,128]{1,0:T(8,128)(2,1)} %collective-permute-done.own_b.refs_1_), channel_id=1, source_target_pairs={{0,112},{16,0},{32,16},{48,32},{64,48},{80,64},{96,80},{112,96},{1... | collective-permute-start | bytes 393224 | tf_op jit(solution)/shard_map/ppermute | solution.py:349
  19.5 3.1 %collective-permute-done.6.refs_5_ = bf16[512,128]{1,0:T(8,128)(2,1)S(1)} collective-permute-done((bf16[512,128]{1,0:T(8,128)(2,1)}, bf16[512,128]{1,0:T(8,128)(2,1)S(1)}, u32[]{:S(2)}, u32[]{:S(2)}) %collective-permute-start.6) | collective-permute-done | bytes 131104 | tf_op jit(solution)/shard_map/ppermute | solution.py:349
  22.6 3.1 %collective-permute-start.7 = (bf16[512,128]{1,0:T(8,128)(2,1)S(1)}, bf16[512,128]{1,0:T(8,128)(2,1)S(1)}, u32[]{:S(2)}, u32[]{:S(2)}) collective-permute-start(bf16[512,128]{1,0:T(8,128)(2,1)S(1)} %collective-permute-done.6.refs_5_), channel_id=1, source_target_pairs={{0,112},{16,0},{32,16},{48,32},{64,48},{80,64},{96,80},{112,96},{1... | collective-permute-start | bytes 393224 | tf_op jit(solution)/shard_map/ppermute | solution.py:349
  25.7 0.2 collective-permute-done.11.refs_3_
  26.0 1.8 %collective-permute-start.12 = (bf16[512,128]{1,0:T(8,128)(2,1)S(1)}, bf16[512,128]{1,0:T(8,128)(2,1)S(1)}, u32[]{:S(2)}, u32[]{:S(2)}) collective-permute-start(bf16[512,128]{1,0:T(8,128)(2,1)S(1)} %collective-permute-done.11.refs_3_), channel_id=1, source_target_pairs={{0,16},{16,32},{32,48},{48,64},{64,80},{80,96},{96,112},{112,0},{1... | collective-permute-start | bytes 393224 | tf_op jit(solution)/shard_map/ppermute | solution.py:349
  27.8 1.0 collective-permute-done.7.refs_9_
  28.9 3.0 %collective-permute-start.8 = (bf16[512,128]{1,0:T(8,128)(2,1)S(1)}, bf16[512,128]{1,0:T(8,128)(2,1)S(1)}, u32[]{:S(2)}, u32[]{:S(2)}) collective-permute-start(bf16[512,128]{1,0:T(8,128)(2,1)S(1)} %collective-permute-done.7.refs_9_), channel_id=1, source_target_pairs={{0,112},{16,0},{32,16},{48,32},{64,48},{80,64},{96,80},{112,96},{1... | collective-permute-start | bytes 393224 | tf_op jit(solution)/shard_map/ppermute | solution.py:349
  31.9 1.7 %collective-permute-start.15 = (bf16[512,128]{1,0:T(8,128)(2,1)S(1)}, bf16[512,128]{1,0:T(8,128)(2,1)S(1)}, u32[]{:S(2)}, u32[]{:S(2)}) collective-permute-start(bf16[512,128]{1,0:T(8,128)(2,1)S(1)} %collective-permute-done.13.refs_8_), channel_id=1, source_target_pairs={{0,112},{16,0},{32,16},{48,32},{64,48},{80,64},{96,80},{112,96},{1... | collective-permute-start | bytes 393224 | tf_op jit(solution)/shard_map/ppermute | solution.py:349
  33.6 0.3 collective-permute-start.14
  33.9 0.3 collective-permute-done.4.refs_10_
  34.2 0.6 collective-permute-start.5
  34.8 0.4 collective-permute-done.8.refs_13_
  35.2 2.9 %collective-permute-start.9 = (bf16[512,128]{1,0:T(8,128)(2,1)S(1)}, bf16[512,128]{1,0:T(8,128)(2,1)S(1)}, u32[]{:S(2)}, u32[]{:S(2)}) collective-permute-start(bf16[512,128]{1,0:T(8,128)(2,1)S(1)} %collective-permute-done.8.refs_13_), channel_id=1, source_target_pairs={{0,112},{16,0},{32,16},{48,32},{64,48},{80,64},{96,80},{112,96},{1... | collective-permute-start | bytes 393224 | tf_op jit(solution)/shard_map/ppermute | solution.py:349
  38.1 1.7 %collective-permute-done.14.refs_11_ = bf16[512,128]{1,0:T(8,128)(2,1)S(1)} collective-permute-done((bf16[512,128]{1,0:T(8,128)(2,1)S(1)}, bf16[512,128]{1,0:T(8,128)(2,1)S(1)}, u32[]{:S(2)}, u32[]{:S(2)}) %collective-permute-start.14) | collective-permute-done | bytes 131104 | tf_op jit(solution)/shard_map/ppermute | solution.py:349
  39.8 0.9 copy-done.5
  40.7 0.7 copy-done.7
  41.4 4.6 %shard_map.112 = (f32[512,128]{1,0:T(8,128)S(1)}, f32[512,128]{1,0:T(8,128)S(1)}) custom-call(s32[3]{0:T(128)S(1)} %copy-done.7, bf16[512,128]{1,0:T(8,128)(2,1)S(1)} %copy-done.5, bf16[512,128]{1,0:T(8,128)(2,1)} %collective-permute-done.own_b.refs_1_, bf16[4096,128]{1,0:T(8,128)(2,1)} %shard_map.111.feat.refs_16_, bf16[512,128]{1,0:T(8,128)(2,1)S(1)} %copy-done.5, ...), custom_call_target="tpu_custom_call" | custom-call | flops 939524096 | bytes 3145740 | tf_op jit(solution)/shard_map/pallas_call | solution.py:45
  46.0 4.2 %shard_map.113 = (bf16[512,128]{1,0:T(8,128)(2,1)S(1)}, f32[512,128]{1,0:T(8,128)S(1)}, f32[8,8,128]{2,1,0:T(8,128)}) custom-call(s32[3]{0:T(128)S(1)} %copy-done.7, bf16[512,128]{1,0:T(8,128)(2,1)S(1)} %copy-done.5, bf16[512,128]{1,0:T(8,128)(2,1)} %collective-permute-done.own_b.refs_1_, bf16[4096,128]{1,0:T(8,128)(2,1)S(1)} %copy-done, ...), custom_call_target="tpu_custom_call" | custom-call | flops 134217728 | bytes 2097164 | tf_op jit(solution)/shard_map/pallas_call | solution.py:45
  50.2 3.7 %all-to-all-start = ((f32[8,8,128]{2,1,0:T(8,128)}), f32[8,8,128]{2,1,0:T(8,128)S(1)}, u32[]{:S(2)}, u32[]{:S(2)}) async-start(f32[8,8,128]{2,1,0:T(8,128)} %get-tuple-element.48), calls=%async_computation | async-start | bytes 65536 | tf_op jit(solution)/shard_map/all_to_all | solution.py:420
  53.9 0.7 copy-done.8
  54.6 5.5 %shard_map.114 = (bf16[256,128]{1,0:T(8,128)(2,1)S(1)}, bf16[256,128]{1,0:T(8,128)(2,1)S(1)}) custom-call(s32[3]{0:T(128)S(1)} %copy-done.8, bf16[512,128]{1,0:T(8,128)(2,1)S(1)} %copy-done.6, bf16[512,128]{1,0:T(8,128)(2,1)} %collective-permute-done.own_b.refs_1_, bf16[512,128]{1,0:T(8,128)(2,1)} %collective-permute-done.1.refs_2_, ...), custom_call_target="tpu_custom_call" | custom-call | flops 1610612736 | bytes 3538956 | tf_op jit(solution)/shard_map/pallas_call | solution.py:45
  60.1 1.9 %all-to-all-done = f32[8,8,128]{2,1,0:T(8,128)S(1)} async-done(((f32[8,8,128]{2,1,0:T(8,128)}), f32[8,8,128]{2,1,0:T(8,128)S(1)}, u32[]{:S(2)}, u32[]{:S(2)}) %all-to-all-start) | async-done | bytes 32800 | tf_op jit(solution)/shard_map/all_to_all | solution.py:420
  61.9 7.0 %shard_map.115 = (bf16[256,128]{1,0:T(8,128)(2,1)S(1)}, bf16[512,128]{1,0:T(8,128)(2,1)S(1)}) custom-call(s32[3]{0:T(128)S(1)} %copy-done.8, bf16[512,128]{1,0:T(8,128)(2,1)S(1)} %copy-done.6, bf16[512,128]{1,0:T(8,128)(2,1)} %collective-permute-done.own_b.refs_1_, bf16[512,128]{1,0:T(8,128)(2,1)} %collective-permute-done.1.refs_2_, ...), custom_call_target="tpu_custom_call" | custom-call | flops 2147483648 | bytes 3244044 | tf_op jit(solution)/shard_map/pallas_call | solution.py:45
  69.0 2.6 %shard_map.117 = bf16[16,96,128]{2,1,0:T(8,128)(2,1)} custom-call(bf16[256,1024]{1,0:T(8,128)(2,1)S(1)} %bitcast.27, bf16[256,1024]{1,0:T(8,128)(2,1)} %collective-permute-done.10.tok_other, bf16[256,128]{1,0:T(8,128)(2,1)S(1)} %get-tuple-element.53.first, bf16[256,128]{1,0:T(8,128)(2,1)S(1)} %get-tuple-element.56.second, ...), custom_call_target="tpu_custom_call" | custom-call | flops 268435456 | bytes 1310720 | tf_op jit(solution)/shard_map/pallas_call | solution.py:45
  71.6 7.1 %all-to-all-start.1 = ((bf16[16,96,128]{2,1,0:T(8,128)(2,1)}), bf16[16,96,128]{2,1,0:T(8,128)(2,1)S(1)}, u32[]{:S(2)}, u32[]{:S(2)}) async-start(bf16[16,96,128]{2,1,0:T(8,128)(2,1)} %shard_map.117), calls=%async_computation.1 | async-start | bytes 786432 | tf_op jit(solution)/shard_map/all_to_all | solution.py:446
  78.7 2.9 %collective-permute-start.16 = (bf16[512,128]{1,0:T(8,128)(2,1)S(1)}, bf16[512,128]{1,0:T(8,128)(2,1)S(1)}, u32[]{:S(2)}, u32[]{:S(2)}) collective-permute-start(bf16[512,128]{1,0:T(8,128)(2,1)S(1)} %get-tuple-element.57.sent), channel_id=1, source_target_pairs={{0,8},{8,0},{1,9},{9,1},{2,10},{10,2},{3,11},{11,3},{4,12},{12,4},... | collective-permute-start | bytes 393224 | tf_op jit(solution)/shard_map/ppermute | solution.py:353
  81.6 3.8 %collective-permute-done.16.arrived = bf16[512,128]{1,0:T(8,128)(2,1)S(1)} collective-permute-done((bf16[512,128]{1,0:T(8,128)(2,1)S(1)}, bf16[512,128]{1,0:T(8,128)(2,1)S(1)}, u32[]{:S(2)}, u32[]{:S(2)}) %collective-permute-start.16) | collective-permute-done | bytes 131104 | tf_op jit(solution)/shard_map/ppermute | solution.py:353
  85.4 1.7 %shard_map.116 = (bf16[256,128]{1,0:T(8,128)(2,1)}, f32[4,32,1024]{2,1,0:T(8,128)S(1)}, bf16[4,32,1024]{2,1,0:T(8,128)(2,1)S(1)}) custom-call(s32[3]{0:T(128)S(1)} %copy-done.8, bf16[256,128]{1,0:T(8,128)(2,1)S(1)} %get-tuple-element.53.first, bf16[256,128]{1,0:T(8,128)(2,1)S(1)} %get-tuple-element.56.second, ...), custom_call_target="tpu_custom_call" | custom-call | flops 201326592 | bytes 1048588 | tf_op jit(solution)/shard_map/pallas_call | solution.py:45
  87.1 1.8 %all-to-all-done.1.parts = bf16[16,96,128]{2,1,0:T(8,128)(2,1)S(1)} async-done(((bf16[16,96,128]{2,1,0:T(8,128)(2,1)}), bf16[16,96,128]{2,1,0:T(8,128)(2,1)S(1)}, u32[]{:S(2)}, u32[]{:S(2)}) %all-to-all-start.1) | async-done | bytes 393248 | tf_op jit(solution)/shard_map/all_to_all | solution.py:446
  89.0 1.0 shard_map.118
  90.0 8.8 %all-to-all-start.2 = ((bf16[32,96,128]{2,1,0:T(8,128)(2,1)}), bf16[32,96,128]{2,1,0:T(8,128)(2,1)S(1)}, u32[]{:S(2)}, u32[]{:S(2)}) async-start(bf16[32,96,128]{2,1,0:T(8,128)(2,1)} %shard_map.118), calls=%async_computation.2 | async-start | bytes 1572864 | tf_op jit(solution)/shard_map/all_to_all | solution.py:462
  98.9 1.5 %collective-permute-done.17 = bf16[4,32,1024]{2,1,0:T(8,128)(2,1)S(1)} collective-permute-done((bf16[4,32,1024]{2,1,0:T(8,128)(2,1)S(1)}, bf16[4,32,1024]{2,1,0:T(8,128)(2,1)S(1)}, u32[]{:S(2)}, u32[]{:S(2)}) %collective-permute-start.17) | collective-permute-done | bytes 262176 | tf_op jit(solution)/shard_map/ppermute | solution.py:454
  100.5 0.5 collective-permute-start.18
  101.0 2.6 %collective-permute-start.19 = (bf16[32,1024]{1,0:T(8,128)(2,1)S(1)}, bf16[32,1024]{1,0:T(8,128)(2,1)S(1)}, u32[]{:S(2)}, u32[]{:S(2)}) collective-permute-start(bf16[32,1024]{1,0:T(8,128)(2,1)S(1)} %get-tuple-element.71), channel_id=1, source_target_pairs={{0,4},{2,6},{4,0},{6,2},{1,5},{3,7},{5,1},{7,3},{8,12},{10,14},{12... | collective-permute-start | bytes 196616 | tf_op jit(solution)/shard_map/ppermute | solution.py:461
  103.6 0.5 collective-permute-start.20
  104.1 0.8 collective-permute-done.18
  104.8 2.4 %collective-permute-done.19 = bf16[32,1024]{1,0:T(8,128)(2,1)S(1)} collective-permute-done((bf16[32,1024]{1,0:T(8,128)(2,1)S(1)}, bf16[32,1024]{1,0:T(8,128)(2,1)S(1)}, u32[]{:S(2)}, u32[]{:S(2)}) %collective-permute-start.19) | collective-permute-done | bytes 65568 | tf_op jit(solution)/shard_map/ppermute | solution.py:461
  107.2 0.9 collective-permute-done.20
  108.2 0.7 fusion.3
  108.8 6.8 %all-to-all-done.2.parts = bf16[32,96,128]{2,1,0:T(8,128)(2,1)S(1)} async-done(((bf16[32,96,128]{2,1,0:T(8,128)(2,1)}), bf16[32,96,128]{2,1,0:T(8,128)(2,1)S(1)}, u32[]{:S(2)}, u32[]{:S(2)}) %all-to-all-start.2) | async-done | bytes 786464 | tf_op jit(solution)/shard_map/all_to_all | solution.py:462
  115.6 1.4 %shard_map.119 = (f32[1024,128]{1,0:T(8,128)}, f32[1024,128]{1,0:T(8,128)}, f32[1024,128]{1,0:T(8,128)}) custom-call(bf16[32,96,128]{2,1,0:T(8,128)(2,1)S(1)} %all-to-all-done.2.parts), custom_call_target="tpu_custom_call" | custom-call | bytes 786432 | tf_op jit(solution)/shard_map/pallas_call | solution.py:45
  (32 shorter events, 0.5 us)
Async XLA Ops:
  3.5 13.8 %collective-permute-start.1 = (bf16[512,128]{1,0:T(8,128)(2,1)}, bf16[512,128]{1,0:T(8,128)(2,1)}, u32[]{:S(2)}, u32[]{:S(2)}) collective-permute-start(bf16[512,128]{1,0:T(8,128)(2,1)} %get-tuple-element.37.own_a.refs_0_), channel_id=1, source_target_pairs={{0,16},{16,32},{32,48},{48,64},{64,80},{80,96},{96,112},{112,0},{1... | collective-permute-start | bytes 393224 | tf_op jit(solution)/shard_map/ppermute | solution.py:349
  5.5 11.8 %collective-permute-start.2 = (bf16[512,128]{1,0:T(8,128)(2,1)}, bf16[512,128]{1,0:T(8,128)(2,1)}, u32[]{:S(2)}, u32[]{:S(2)}) collective-permute-start(bf16[512,128]{1,0:T(8,128)(2,1)} %get-tuple-element.37.own_a.refs_0_), channel_id=1, source_target_pairs={{0,112},{16,0},{32,16},{48,32},{64,48},{80,64},{96,80},{112,96},{1... | collective-permute-start | bytes 393224 | tf_op jit(solution)/shard_map/ppermute | solution.py:349
  9.5 7.8 %collective-permute-start = (bf16[512,128]{1,0:T(8,128)(2,1)}, bf16[512,128]{1,0:T(8,128)(2,1)}, u32[]{:S(2)}, u32[]{:S(2)}) collective-permute-start(bf16[512,128]{1,0:T(8,128)(2,1)} %get-tuple-element.38), channel_id=1, source_target_pairs={{0,8},{8,0},{1,9},{9,1},{2,10},{10,2},{3,11},{11,3},{4,12},{12,4},... | collective-permute-start | bytes 393224 | tf_op jit(solution)/shard_map/ppermute | solution.py:353
  12.6 33.4 %collective-permute-start.10 = (bf16[256,1024]{1,0:T(8,128)(2,1)}, bf16[256,1024]{1,0:T(8,128)(2,1)}, u32[]{:S(2)}, u32[]{:S(2)}) collective-permute-start(bf16[256,1024]{1,0:T(8,128)(2,1)} %bitcast.26), channel_id=1, source_target_pairs={{0,8},{8,0},{1,9},{9,1},{2,10},{10,2},{3,11},{11,3},{4,12},{12,4},... | collective-permute-start | bytes 1572872 | tf_op jit(solution)/shard_map/ppermute | solution.py:353
  17.3 28.7 %copy-start = (bf16[4096,128]{1,0:T(8,128)(2,1)S(1)}, bf16[4096,128]{1,0:T(8,128)(2,1)}, u32[]{:S(2)}) copy-start(bf16[4096,128]{1,0:T(8,128)(2,1)} %shard_map.111.feat.refs_16_) | copy-start | bytes 3145732
  17.3 5.3 %collective-permute-start.6 = (bf16[512,128]{1,0:T(8,128)(2,1)}, bf16[512,128]{1,0:T(8,128)(2,1)S(1)}, u32[]{:S(2)}, u32[]{:S(2)}) collective-permute-start(bf16[512,128]{1,0:T(8,128)(2,1)} %collective-permute-done.own_b.refs_1_), channel_id=1, source_target_pairs={{0,112},{16,0},{32,16},{48,32},{64,48},{80,64},{96,80},{112,96},{1... | collective-permute-start | bytes 393224 | tf_op jit(solution)/shard_map/ppermute | solution.py:349
  19.3 6.7 %collective-permute-start.11 = (bf16[512,128]{1,0:T(8,128)(2,1)}, bf16[512,128]{1,0:T(8,128)(2,1)S(1)}, u32[]{:S(2)}, u32[]{:S(2)}) collective-permute-start(bf16[512,128]{1,0:T(8,128)(2,1)} %collective-permute-done.own_b.refs_1_), channel_id=1, source_target_pairs={{0,16},{16,32},{32,48},{48,64},{64,80},{80,96},{96,112},{112,0},{1... | collective-permute-start | bytes 393224 | tf_op jit(solution)/shard_map/ppermute | solution.py:349
  19.4 8.3 %collective-permute-start.3 = (bf16[512,128]{1,0:T(8,128)(2,1)}, bf16[512,128]{1,0:T(8,128)(2,1)S(1)}, u32[]{:S(2)}, u32[]{:S(2)}) collective-permute-start(bf16[512,128]{1,0:T(8,128)(2,1)} %collective-permute-done.1.refs_2_), channel_id=1, source_target_pairs={{0,16},{16,32},{32,48},{48,64},{64,80},{80,96},{96,112},{112,0},{1... | collective-permute-start | bytes 393224 | tf_op jit(solution)/shard_map/ppermute | solution.py:349
  22.6 6.3 %collective-permute-start.7 = (bf16[512,128]{1,0:T(8,128)(2,1)S(1)}, bf16[512,128]{1,0:T(8,128)(2,1)S(1)}, u32[]{:S(2)}, u32[]{:S(2)}) collective-permute-start(bf16[512,128]{1,0:T(8,128)(2,1)S(1)} %collective-permute-done.6.refs_5_), channel_id=1, source_target_pairs={{0,112},{16,0},{32,16},{48,32},{64,48},{80,64},{96,80},{112,96},{1... | collective-permute-start | bytes 393224 | tf_op jit(solution)/shard_map/ppermute | solution.py:349
  25.7 6.2 %collective-permute-start.13 = (bf16[512,128]{1,0:T(8,128)(2,1)}, bf16[512,128]{1,0:T(8,128)(2,1)S(1)}, u32[]{:S(2)}, u32[]{:S(2)}) collective-permute-start(bf16[512,128]{1,0:T(8,128)(2,1)} %collective-permute-done.2.refs_4_), channel_id=1, source_target_pairs={{0,112},{16,0},{32,16},{48,32},{64,48},{80,64},{96,80},{112,96},{1... | collective-permute-start | bytes 393224 | tf_op jit(solution)/shard_map/ppermute | solution.py:349
  26.0 7.6 %collective-permute-start.12 = (bf16[512,128]{1,0:T(8,128)(2,1)S(1)}, bf16[512,128]{1,0:T(8,128)(2,1)S(1)}, u32[]{:S(2)}, u32[]{:S(2)}) collective-permute-start(bf16[512,128]{1,0:T(8,128)(2,1)S(1)} %collective-permute-done.11.refs_3_), channel_id=1, source_target_pairs={{0,16},{16,32},{32,48},{48,64},{64,80},{80,96},{96,112},{112,0},{1... | collective-permute-start | bytes 393224 | tf_op jit(solution)/shard_map/ppermute | solution.py:349
  27.7 6.4 %collective-permute-start.4 = (bf16[512,128]{1,0:T(8,128)(2,1)S(1)}, bf16[512,128]{1,0:T(8,128)(2,1)S(1)}, u32[]{:S(2)}, u32[]{:S(2)}) collective-permute-start(bf16[512,128]{1,0:T(8,128)(2,1)S(1)} %collective-permute-done.3.refs_6_), channel_id=1, source_target_pairs={{0,16},{16,32},{32,48},{48,64},{64,80},{80,96},{96,112},{112,0},{1... | collective-permute-start | bytes 393224 | tf_op jit(solution)/shard_map/ppermute | solution.py:349
  28.9 6.3 %collective-permute-start.8 = (bf16[512,128]{1,0:T(8,128)(2,1)S(1)}, bf16[512,128]{1,0:T(8,128)(2,1)S(1)}, u32[]{:S(2)}, u32[]{:S(2)}) collective-permute-start(bf16[512,128]{1,0:T(8,128)(2,1)S(1)} %collective-permute-done.7.refs_9_), channel_id=1, source_target_pairs={{0,112},{16,0},{32,16},{48,32},{64,48},{80,64},{96,80},{112,96},{1... | collective-permute-start | bytes 393224 | tf_op jit(solution)/shard_map/ppermute | solution.py:349
  31.9 6.2 %collective-permute-start.15 = (bf16[512,128]{1,0:T(8,128)(2,1)S(1)}, bf16[512,128]{1,0:T(8,128)(2,1)S(1)}, u32[]{:S(2)}, u32[]{:S(2)}) collective-permute-start(bf16[512,128]{1,0:T(8,128)(2,1)S(1)} %collective-permute-done.13.refs_8_), channel_id=1, source_target_pairs={{0,112},{16,0},{32,16},{48,32},{64,48},{80,64},{96,80},{112,96},{1... | collective-permute-start | bytes 393224 | tf_op jit(solution)/shard_map/ppermute | solution.py:349
  33.6 6.2 %collective-permute-start.14 = (bf16[512,128]{1,0:T(8,128)(2,1)S(1)}, bf16[512,128]{1,0:T(8,128)(2,1)S(1)}, u32[]{:S(2)}, u32[]{:S(2)}) collective-permute-start(bf16[512,128]{1,0:T(8,128)(2,1)S(1)} %collective-permute-done.12.refs_7_), channel_id=1, source_target_pairs={{0,16},{16,32},{32,48},{48,64},{64,80},{80,96},{96,112},{112,0},{1... | collective-permute-start | bytes 393224 | tf_op jit(solution)/shard_map/ppermute | solution.py:349
  34.2 11.8 %collective-permute-start.5 = (bf16[512,128]{1,0:T(8,128)(2,1)S(1)}, bf16[512,128]{1,0:T(8,128)(2,1)S(1)}, u32[]{:S(2)}, u32[]{:S(2)}) collective-permute-start(bf16[512,128]{1,0:T(8,128)(2,1)S(1)} %collective-permute-done.4.refs_10_), channel_id=1, source_target_pairs={{0,16},{16,32},{32,48},{48,64},{64,80},{80,96},{96,112},{112,0},{1... | collective-permute-start | bytes 393224 | tf_op jit(solution)/shard_map/ppermute | solution.py:349
  35.2 10.8 %collective-permute-start.9 = (bf16[512,128]{1,0:T(8,128)(2,1)S(1)}, bf16[512,128]{1,0:T(8,128)(2,1)S(1)}, u32[]{:S(2)}, u32[]{:S(2)}) collective-permute-start(bf16[512,128]{1,0:T(8,128)(2,1)S(1)} %collective-permute-done.8.refs_13_), channel_id=1, source_target_pairs={{0,112},{16,0},{32,16},{48,32},{64,48},{80,64},{96,80},{112,96},{1... | collective-permute-start | bytes 393224 | tf_op jit(solution)/shard_map/ppermute | solution.py:349
  39.8 0.9 copy-start.5
  40.7 0.7 copy-start.7
  45.9 8.0 %copy-start.6 = (bf16[512,128]{1,0:T(8,128)(2,1)S(1)}, bf16[512,128]{1,0:T(8,128)(2,1)}, u32[]{:S(2)}) copy-start(bf16[512,128]{1,0:T(8,128)(2,1)} %get-tuple-element.37.own_a.refs_0_) | copy-start | bytes 393220
  50.2 11.7 %all-to-all-start = ((f32[8,8,128]{2,1,0:T(8,128)}), f32[8,8,128]{2,1,0:T(8,128)S(1)}, u32[]{:S(2)}, u32[]{:S(2)}) async-start(f32[8,8,128]{2,1,0:T(8,128)} %get-tuple-element.48), calls=%async_computation | async-start | bytes 65536 | tf_op jit(solution)/shard_map/all_to_all | solution.py:420
  53.9 0.7 copy-start.8
  61.9 7.0 %copy-start.1 = (bf16[1,256,1024]{2,1,0:T(8,128)(2,1)S(1)}, bf16[1,256,1024]{2,1,0:T(8,128)(2,1)}, u32[]{:S(2)}) copy-start(bf16[1,256,1024]{2,1,0:T(8,128)(2,1)} %param.7) | copy-start | bytes 1572868
  71.6 13.8 %copy-start.2 = (bf16[1024,128]{1,0:T(8,128)(2,1)S(1)}, bf16[1024,128]{1,0:T(8,128)(2,1)}, u32[]{:S(2)}) copy-start(bf16[1024,128]{1,0:T(8,128)(2,1)} %wq.3) | copy-start | bytes 786436
  71.6 13.8 %copy-start.3 = (bf16[1024,128]{1,0:T(8,128)(2,1)S(1)}, bf16[1024,128]{1,0:T(8,128)(2,1)}, u32[]{:S(2)}) copy-start(bf16[1024,128]{1,0:T(8,128)(2,1)} %wk.3) | copy-start | bytes 786436
  71.6 13.8 %copy-start.4 = (bf16[1024,128]{1,0:T(8,128)(2,1)S(1)}, bf16[1024,128]{1,0:T(8,128)(2,1)}, u32[]{:S(2)}) copy-start(bf16[1024,128]{1,0:T(8,128)(2,1)} %wv.3) | copy-start | bytes 786436
  71.6 17.4 %all-to-all-start.1 = ((bf16[16,96,128]{2,1,0:T(8,128)(2,1)}), bf16[16,96,128]{2,1,0:T(8,128)(2,1)S(1)}, u32[]{:S(2)}, u32[]{:S(2)}) async-start(bf16[16,96,128]{2,1,0:T(8,128)(2,1)} %shard_map.117), calls=%async_computation.1 | async-start | bytes 786432 | tf_op jit(solution)/shard_map/all_to_all | solution.py:446
  78.7 6.7 %collective-permute-start.16 = (bf16[512,128]{1,0:T(8,128)(2,1)S(1)}, bf16[512,128]{1,0:T(8,128)(2,1)S(1)}, u32[]{:S(2)}, u32[]{:S(2)}) collective-permute-start(bf16[512,128]{1,0:T(8,128)(2,1)S(1)} %get-tuple-element.57.sent), channel_id=1, source_target_pairs={{0,8},{8,0},{1,9},{9,1},{2,10},{10,2},{3,11},{11,3},{4,12},{12,4},... | collective-permute-start | bytes 393224 | tf_op jit(solution)/shard_map/ppermute | solution.py:353
  90.0 25.7 %all-to-all-start.2 = ((bf16[32,96,128]{2,1,0:T(8,128)(2,1)}), bf16[32,96,128]{2,1,0:T(8,128)(2,1)S(1)}, u32[]{:S(2)}, u32[]{:S(2)}) async-start(bf16[32,96,128]{2,1,0:T(8,128)(2,1)} %shard_map.118), calls=%async_computation.2 | async-start | bytes 1572864 | tf_op jit(solution)/shard_map/all_to_all | solution.py:462
  98.8 1.6 %collective-permute-start.17 = (bf16[4,32,1024]{2,1,0:T(8,128)(2,1)S(1)}, bf16[4,32,1024]{2,1,0:T(8,128)(2,1)S(1)}, u32[]{:S(2)}, u32[]{:S(2)}) collective-permute-start(bf16[4,32,1024]{2,1,0:T(8,128)(2,1)S(1)} %get-tuple-element.62), channel_id=1, source_target_pairs={{0,1},{1,0},{2,3},{3,2},{4,5},{5,4},{6,7},{7,6},{8,9},{9,8},{10,11... | collective-permute-start | bytes 786440 | tf_op jit(solution)/shard_map/ppermute | solution.py:454
  100.5 4.4 %collective-permute-start.18 = (bf16[32,1024]{1,0:T(8,128)(2,1)S(1)}, bf16[32,1024]{1,0:T(8,128)(2,1)S(1)}, u32[]{:S(2)}, u32[]{:S(2)}) collective-permute-start(bf16[32,1024]{1,0:T(8,128)(2,1)S(1)} %get-tuple-element.69), channel_id=1, source_target_pairs={{0,2},{2,0},{4,6},{6,4},{1,3},{3,1},{5,7},{7,5},{8,10},{10,8},{12,... | collective-permute-start | bytes 196616 | tf_op jit(solution)/shard_map/ppermute | solution.py:461
  101.0 6.2 %collective-permute-start.19 = (bf16[32,1024]{1,0:T(8,128)(2,1)S(1)}, bf16[32,1024]{1,0:T(8,128)(2,1)S(1)}, u32[]{:S(2)}, u32[]{:S(2)}) collective-permute-start(bf16[32,1024]{1,0:T(8,128)(2,1)S(1)} %get-tuple-element.71), channel_id=1, source_target_pairs={{0,4},{2,6},{4,0},{6,2},{1,5},{3,7},{5,1},{7,3},{8,12},{10,14},{12... | collective-permute-start | bytes 196616 | tf_op jit(solution)/shard_map/ppermute | solution.py:461
  103.6 4.5 %collective-permute-start.20 = (bf16[32,1024]{1,0:T(8,128)(2,1)S(1)}, bf16[32,1024]{1,0:T(8,128)(2,1)S(1)}, u32[]{:S(2)}, u32[]{:S(2)}) collective-permute-start(bf16[32,1024]{1,0:T(8,128)(2,1)S(1)} %get-tuple-element.70), channel_id=1, source_target_pairs={{0,6},{2,4},{4,2},{6,0},{1,7},{3,5},{5,3},{7,1},{8,14},{10,12},{12... | collective-permute-start | bytes 196616 | tf_op jit(solution)/shard_map/ppermute | solution.py:461

commit v8 on v6

--- a/solution.py
+++ b/solution.py
@@ -87,13 +87,13 @@
     lax.fori_loop(0, 2 * NSEC, one, 0)
 
 
-def project_kernel(place, tok, wq, wk, wv, cot, mine, theirs, *scratch):
+def project_kernel(tok, wq, wk, wv, cot, mine, theirs, *scratch):
     tok_v, wk_v, wv_v, wq_v, cot_v, sems = scratch
     pairs = ((tok, tok_v), (wk, wk_v), (wv, wv_v), (wq, wq_v), (cot, cot_v))
     copies = [pltpu.make_async_copy(a, b, sems.at[i]) for i, (a, b) in enumerate(pairs)]
     for copy in copies:
         copy.start()
-    first = place[0] == 0
+    first = lax.axis_index("xh") == 0
     copies[0].wait()
     t = tok_v[...]
     copies[1].wait()
@@ -351,7 +351,7 @@
     mine, theirs = call(
         project_kernel,
         (shape((SEC, 128), BF),) * 2,
-        (place, tok, wq, wk, wv, cot),
+        (tok, wq, wk, wv, cot),
         scratch=(
             pltpu.VMEM((RUN, 1024), BF),
             weight,
@@ -361,6 +361,7 @@
             pltpu.SemaphoreType.DMA((5,)),
         ),
         flops=6 * 256 * 1024 * 128,
+        smem=0,
         manual=5,
         limit=64 << 20,
     )
@@ -390,6 +391,7 @@
     for i in (1, 2, 3):
         pieces += (lower_a[i], lower_b[i], upper_a[i], upper_b[i])
     pieces += far
+    tok_other, feat = tie((tok_other, feat))
     att_rows, column, stats = call(
         forward_kernel,
         (shape((SEC, 128), BF), wide, shape((NSEC, 8, 128), F32)),

time: 116 us -> 117 us (level)
  waiting for transfers between devices: 26.3 us -> 29.4 us
  starting transfers between devices: 54.1 us -> 51.5 us
    all_to_all x1, waiting for transfers between devices: 5.49 us -> 7.37 us  [on_device(): total = lax.all_to_all(total, ('b',) + CTX, 0, 0, tiled=True)]
    ppermute x14, starting transfers between devices: 23.9 us -> 22.1 us  [shift(): return lax.ppermute(a, Z, [(i, (i + step) % NSEC) for i in range(NSEC)])]
  transfers between devices with their start and end apart: 24 -> 24, of which waited for: 12 -> 13; matrix products, arithmetic and copies ran while one was open for 1% -> 1% of each run, Pallas kernels for 20% -> 9%
where the time goes in v8:
time: 117 us
  starting transfers between devices  51.5 us (44%)
  Pallas kernels  31.4 us (27%)
  waiting for transfers between devices  29.4 us (25%)
  local copies, waits for them, and re-layouts  2.25 us (2%)
  other arithmetic  1.38 us (1%)
    pallas_call x9, Pallas kernels, call(): pl.pallas_call(kernel, out_shape=outs, in_specs=specs, out_specs=jax.tree...  31.4 us
    ppermute x14, starting transfers between devices, shift(): return lax.ppermute(a, Z, [(i, (i + step) % NSEC) for i in range(NSEC)])  22.1 us
    all_to_all x1, starting transfers between devices, on_device(): total = lax.all_to_all(total, ('b',) + CTX, 0, 0, tiled=True)  7.8 us
    ppermute x14, waiting for transfers between devices, shift(): return lax.ppermute(a, Z, [(i, (i + step) % NSEC) for i in range(NSEC)])  7.67 us
    all_to_all x1, waiting for transfers between devices, on_device(): total = lax.all_to_all(total, ('b',) + CTX, 0, 0, tiled=True)  7.37 us
    all_to_all x1, starting transfers between devices, on_device(): lax.all_to_all(stats, Z, 0, 0, tiled=True).reshape(NSEC * 8, 128)  6.52 us
    ppermute x3, waiting for transfers between devices, swap(): return lax.ppermute(a, 'xh', [(0, 1), (1, 0)])  5.9 us
    all_to_all x1, starting transfers between devices, on_device(): partial = lax.all_to_all(partial, ('b',) + Z, 0, 0, tiled=True)  5.72 us
  transfers between devices with their start and end apart: 24, of which 13 were waited for; matrix products, arithmetic and copies ran while one was open for 1% of the time, Pallas kernels for 9%

profile of v8, /device:TPU:8, one launch (start us, length us, event | category | flops | bytes accessed | tf_op | source)
XLA Modules:
  0.0 116.7 jit_solution(2275659875710672862)
XLA Ops:
  0.6 2.9 %shard_map.110 = (bf16[512,128]{1,0:T(8,128)(2,1)}, bf16[512,128]{1,0:T(8,128)(2,1)}) custom-call(bf16[256,1024]{1,0:T(8,128)(2,1)} %bitcast.25, bf16[1024,128]{1,0:T(8,128)(2,1)} %wq.3, bf16[1024,128]{1,0:T(8,128)(2,1)} %wk.3, bf16[1024,128]{1,0:T(8,128)(2,1)} %wv.3, bf16[256,128]{1,0:T(8,128)(2,1)} %bitcast.29), custom_call_target="tpu_custom_call" | custom-call | flops 201326592 | bytes 1376256 | tf_op jit(solution)/shard_map/pallas_call | solution.py:44
  3.5 3.1 %collective-permute-start = (bf16[512,128]{1,0:T(8,128)(2,1)}, bf16[512,128]{1,0:T(8,128)(2,1)}, u32[]{:S(2)}, u32[]{:S(2)}) collective-permute-start(bf16[512,128]{1,0:T(8,128)(2,1)} %get-tuple-element.35), channel_id=1, source_target_pairs={{0,8},{8,0},{1,9},{9,1},{2,10},{10,2},{3,11},{11,3},{4,12},{12,4},... | collective-permute-start | bytes 393224 | tf_op jit(solution)/shard_map/ppermute | solution.py:342
  6.6 1.9 %collective-permute-start.1 = (bf16[512,128]{1,0:T(8,128)(2,1)}, bf16[512,128]{1,0:T(8,128)(2,1)}, u32[]{:S(2)}, u32[]{:S(2)}) collective-permute-start(bf16[512,128]{1,0:T(8,128)(2,1)} %get-tuple-element.34.refs_0_), channel_id=1, source_target_pairs={{0,16},{16,32},{32,48},{48,64},{64,80},{80,96},{96,112},{112,0},{1... | collective-permute-start | bytes 393224 | tf_op jit(solution)/shard_map/ppermute | solution.py:338
  8.6 3.9 %collective-permute-start.2 = (bf16[512,128]{1,0:T(8,128)(2,1)}, bf16[512,128]{1,0:T(8,128)(2,1)}, u32[]{:S(2)}, u32[]{:S(2)}) collective-permute-start(bf16[512,128]{1,0:T(8,128)(2,1)} %get-tuple-element.34.refs_0_), channel_id=1, source_target_pairs={{0,112},{16,0},{32,16},{48,32},{64,48},{80,64},{96,80},{112,96},{1... | collective-permute-start | bytes 393224 | tf_op jit(solution)/shard_map/ppermute | solution.py:338
  12.5 0.5 collective-permute-start.15
  13.0 0.6 pad_add_fusion.place
  13.6 3.6 %shard_map.111.refs_16_ = bf16[4096,128]{1,0:T(8,128)(2,1)} custom-call(s32[3]{0:T(128)} %pad_add_fusion.place, s32[1,8]{1,0:T(1,128)} %lengths.1, s32[1,256]{1,0:T(1,128)} %spots.1), custom_call_target="tpu_custom_call" | custom-call | bytes 1068 | tf_op jit(solution)/shard_map/pallas_call | solution.py:44
  17.2 2.1 %collective-permute-start.4 = (bf16[512,128]{1,0:T(8,128)(2,1)}, bf16[512,128]{1,0:T(8,128)(2,1)S(1)}, u32[]{:S(2)}, u32[]{:S(2)}) collective-permute-start(bf16[512,128]{1,0:T(8,128)(2,1)} %collective-permute-done.refs_1_), channel_id=1, source_target_pairs={{0,112},{16,0},{32,16},{48,32},{64,48},{80,64},{96,80},{112,96},{1... | collective-permute-start | bytes 393224 | tf_op jit(solution)/shard_map/ppermute | solution.py:338
  19.4 3.1 %collective-permute-done.4.refs_5_ = bf16[512,128]{1,0:T(8,128)(2,1)S(1)} collective-permute-done((bf16[512,128]{1,0:T(8,128)(2,1)}, bf16[512,128]{1,0:T(8,128)(2,1)S(1)}, u32[]{:S(2)}, u32[]{:S(2)}) %collective-permute-start.4) | collective-permute-done | bytes 131104 | tf_op jit(solution)/shard_map/ppermute | solution.py:338
  22.5 3.2 %collective-permute-start.8 = (bf16[512,128]{1,0:T(8,128)(2,1)S(1)}, bf16[512,128]{1,0:T(8,128)(2,1)S(1)}, u32[]{:S(2)}, u32[]{:S(2)}) collective-permute-start(bf16[512,128]{1,0:T(8,128)(2,1)S(1)} %collective-permute-done.4.refs_5_), channel_id=1, source_target_pairs={{0,112},{16,0},{32,16},{48,32},{64,48},{80,64},{96,80},{112,96},{1... | collective-permute-start | bytes 393224 | tf_op jit(solution)/shard_map/ppermute | solution.py:338
  25.7 0.2 collective-permute-done.3.refs_3_
  26.0 1.8 %collective-permute-start.6 = (bf16[512,128]{1,0:T(8,128)(2,1)S(1)}, bf16[512,128]{1,0:T(8,128)(2,1)S(1)}, u32[]{:S(2)}, u32[]{:S(2)}) collective-permute-start(bf16[512,128]{1,0:T(8,128)(2,1)S(1)} %collective-permute-done.3.refs_3_), channel_id=1, source_target_pairs={{0,16},{16,32},{32,48},{48,64},{64,80},{80,96},{96,112},{112,0},{1... | collective-permute-start | bytes 393224 | tf_op jit(solution)/shard_map/ppermute | solution.py:338
  27.7 0.1 collective-permute-start.9
  27.8 0.9 collective-permute-done.8.refs_9_
  28.7 3.2 %collective-permute-start.12 = (bf16[512,128]{1,0:T(8,128)(2,1)S(1)}, bf16[512,128]{1,0:T(8,128)(2,1)S(1)}, u32[]{:S(2)}, u32[]{:S(2)}) collective-permute-start(bf16[512,128]{1,0:T(8,128)(2,1)S(1)} %collective-permute-done.8.refs_9_), channel_id=1, source_target_pairs={{0,112},{16,0},{32,16},{48,32},{64,48},{80,64},{96,80},{112,96},{1... | collective-permute-start | bytes 393224 | tf_op jit(solution)/shard_map/ppermute | solution.py:338
  31.9 1.7 %collective-permute-start.11 = (bf16[512,128]{1,0:T(8,128)(2,1)S(1)}, bf16[512,128]{1,0:T(8,128)(2,1)S(1)}, u32[]{:S(2)}, u32[]{:S(2)}) collective-permute-start(bf16[512,128]{1,0:T(8,128)(2,1)S(1)} %collective-permute-done.7.refs_8_), channel_id=1, source_target_pairs={{0,112},{16,0},{32,16},{48,32},{64,48},{80,64},{96,80},{112,96},{1... | collective-permute-start | bytes 393224 | tf_op jit(solution)/shard_map/ppermute | solution.py:338
  33.6 0.3 collective-permute-start.10
  33.9 0.3 collective-permute-done.9.refs_10_
  34.2 0.8 collective-permute-start.13
  35.0 3.0 %collective-permute-start.14 = (bf16[512,128]{1,0:T(8,128)(2,1)S(1)}, bf16[512,128]{1,0:T(8,128)(2,1)S(1)}, u32[]{:S(2)}, u32[]{:S(2)}) collective-permute-start(bf16[512,128]{1,0:T(8,128)(2,1)S(1)} %collective-permute-done.12.refs_13_), channel_id=1, source_target_pairs={{0,112},{16,0},{32,16},{48,32},{64,48},{80,64},{96,80},{112,96},{1... | collective-permute-start | bytes 393224 | tf_op jit(solution)/shard_map/ppermute | solution.py:338
  38.1 1.7 %collective-permute-done.10.refs_11_ = bf16[512,128]{1,0:T(8,128)(2,1)S(1)} collective-permute-done((bf16[512,128]{1,0:T(8,128)(2,1)S(1)}, bf16[512,128]{1,0:T(8,128)(2,1)S(1)}, u32[]{:S(2)}, u32[]{:S(2)}) %collective-permute-start.10) | collective-permute-done | bytes 131104 | tf_op jit(solution)/shard_map/ppermute | solution.py:338
  39.8 1.4 %collective-permute-done.13.refs_14_ = bf16[512,128]{1,0:T(8,128)(2,1)S(1)} collective-permute-done((bf16[512,128]{1,0:T(8,128)(2,1)S(1)}, bf16[512,128]{1,0:T(8,128)(2,1)S(1)}, u32[]{:S(2)}, u32[]{:S(2)}) %collective-permute-start.13) | collective-permute-done | bytes 131104 | tf_op jit(solution)/shard_map/ppermute | solution.py:338
  41.2 0.7 copy-done.4
  41.9 0.9 copy-done.6
  42.8 5.7 %shard_map.112 = (bf16[512,128]{1,0:T(8,128)(2,1)S(1)}, f32[512,128]{1,0:T(8,128)S(1)}, f32[8,8,128]{2,1,0:T(8,128)}) custom-call(s32[3]{0:T(128)S(1)} %copy-done.4, bf16[512,128]{1,0:T(8,128)(2,1)S(1)} %copy-done.6, bf16[512,128]{1,0:T(8,128)(2,1)} %collective-permute-done.refs_1_, bf16[512,128]{1,0:T(8,128)(2,1)} %collective-permute-done.1.refs_2_, ...), custom_call_target="tpu_custom_call" | custom-call | flops 1073741824 | bytes 3145740 | tf_op jit(solution)/shard_map/pallas_call | solution.py:44
  48.5 6.5 %all-to-all-start = ((f32[8,8,128]{2,1,0:T(8,128)}), f32[8,8,128]{2,1,0:T(8,128)S(1)}, u32[]{:S(2)}, u32[]{:S(2)}) async-start(f32[8,8,128]{2,1,0:T(8,128)} %get-tuple-element.42), calls=%async_computation | async-start | bytes 65536 | tf_op jit(solution)/shard_map/all_to_all | solution.py:402
  55.0 0.6 copy-done.5
  55.7 5.5 %shard_map.113 = (bf16[256,128]{1,0:T(8,128)(2,1)S(1)}, bf16[256,128]{1,0:T(8,128)(2,1)S(1)}) custom-call(s32[3]{0:T(128)S(1)} %copy-done.5, bf16[512,128]{1,0:T(8,128)(2,1)S(1)} %copy-done.7, bf16[512,128]{1,0:T(8,128)(2,1)} %collective-permute-done.refs_1_, bf16[512,128]{1,0:T(8,128)(2,1)} %collective-permute-done.1.refs_2_, ...), custom_call_target="tpu_custom_call" | custom-call | flops 1610612736 | bytes 3538956 | tf_op jit(solution)/shard_map/pallas_call | solution.py:44
  61.2 1.9 %all-to-all-done = f32[8,8,128]{2,1,0:T(8,128)S(1)} async-done(((f32[8,8,128]{2,1,0:T(8,128)}), f32[8,8,128]{2,1,0:T(8,128)S(1)}, u32[]{:S(2)}, u32[]{:S(2)}) %all-to-all-start) | async-done | bytes 32800 | tf_op jit(solution)/shard_map/all_to_all | solution.py:402
  63.0 7.0 %shard_map.114 = (bf16[256,128]{1,0:T(8,128)(2,1)S(1)}, bf16[512,128]{1,0:T(8,128)(2,1)S(1)}) custom-call(s32[3]{0:T(128)S(1)} %copy-done.5, bf16[512,128]{1,0:T(8,128)(2,1)S(1)} %copy-done.7, bf16[512,128]{1,0:T(8,128)(2,1)} %collective-permute-done.refs_1_, bf16[512,128]{1,0:T(8,128)(2,1)} %collective-permute-done.1.refs_2_, ...), custom_call_target="tpu_custom_call" | custom-call | flops 2147483648 | bytes 3244044 | tf_op jit(solution)/shard_map/pallas_call | solution.py:44
  70.1 2.6 %shard_map.116 = bf16[16,96,128]{2,1,0:T(8,128)(2,1)} custom-call(bf16[256,1024]{1,0:T(8,128)(2,1)S(1)} %bitcast.27, bf16[256,1024]{1,0:T(8,128)(2,1)} %collective-permute-done.15.tok_other, bf16[256,128]{1,0:T(8,128)(2,1)S(1)} %get-tuple-element.47.first, bf16[256,128]{1,0:T(8,128)(2,1)S(1)} %get-tuple-element.50.second, ...), custom_call_target="tpu_custom_call" | custom-call | flops 268435456 | bytes 1310720 | tf_op jit(solution)/shard_map/pallas_call | solution.py:44
  72.7 5.7 %all-to-all-start.1 = ((bf16[16,96,128]{2,1,0:T(8,128)(2,1)}), bf16[16,96,128]{2,1,0:T(8,128)(2,1)S(1)}, u32[]{:S(2)}, u32[]{:S(2)}) async-start(bf16[16,96,128]{2,1,0:T(8,128)(2,1)} %shard_map.116), calls=%async_computation.1 | async-start | bytes 786432 | tf_op jit(solution)/shard_map/all_to_all | solution.py:428
  78.4 1.4 %collective-permute-start.16 = (bf16[512,128]{1,0:T(8,128)(2,1)S(1)}, bf16[512,128]{1,0:T(8,128)(2,1)S(1)}, u32[]{:S(2)}, u32[]{:S(2)}) collective-permute-start(bf16[512,128]{1,0:T(8,128)(2,1)S(1)} %get-tuple-element.51.sent), channel_id=1, source_target_pairs={{0,8},{8,0},{1,9},{9,1},{2,10},{10,2},{3,11},{11,3},{4,12},{12,4},... | collective-permute-start | bytes 393224 | tf_op jit(solution)/shard_map/ppermute | solution.py:342
  79.9 5.9 %collective-permute-done.16.arrived = bf16[512,128]{1,0:T(8,128)(2,1)S(1)} collective-permute-done((bf16[512,128]{1,0:T(8,128)(2,1)S(1)}, bf16[512,128]{1,0:T(8,128)(2,1)S(1)}, u32[]{:S(2)}, u32[]{:S(2)}) %collective-permute-start.16) | collective-permute-done | bytes 131104 | tf_op jit(solution)/shard_map/ppermute | solution.py:342
  85.8 1.7 %shard_map.115 = (bf16[256,128]{1,0:T(8,128)(2,1)}, f32[4,32,1024]{2,1,0:T(8,128)S(1)}, bf16[4,32,1024]{2,1,0:T(8,128)(2,1)S(1)}) custom-call(s32[3]{0:T(128)S(1)} %copy-done.5, bf16[256,128]{1,0:T(8,128)(2,1)S(1)} %get-tuple-element.47.first, bf16[256,128]{1,0:T(8,128)(2,1)S(1)} %get-tuple-element.50.second, ...), custom_call_target="tpu_custom_call" | custom-call | flops 201326592 | bytes 1048588 | tf_op jit(solution)/shard_map/pallas_call | solution.py:44
  87.5 1.2 %all-to-all-done.1.parts = bf16[16,96,128]{2,1,0:T(8,128)(2,1)S(1)} async-done(((bf16[16,96,128]{2,1,0:T(8,128)(2,1)}), bf16[16,96,128]{2,1,0:T(8,128)(2,1)S(1)}, u32[]{:S(2)}, u32[]{:S(2)}) %all-to-all-start.1) | async-done | bytes 393248 | tf_op jit(solution)/shard_map/all_to_all | solution.py:428
  88.7 1.0 shard_map.117
  89.7 7.8 %all-to-all-start.2 = ((bf16[32,96,128]{2,1,0:T(8,128)(2,1)}), bf16[32,96,128]{2,1,0:T(8,128)(2,1)S(1)}, u32[]{:S(2)}, u32[]{:S(2)}) async-start(bf16[32,96,128]{2,1,0:T(8,128)(2,1)} %shard_map.117), calls=%async_computation.2 | async-start | bytes 1572864 | tf_op jit(solution)/shard_map/all_to_all | solution.py:444
  97.5 0.1 collective-permute-start.17
  97.6 1.5 %collective-permute-done.17 = bf16[4,32,1024]{2,1,0:T(8,128)(2,1)S(1)} collective-permute-done((bf16[4,32,1024]{2,1,0:T(8,128)(2,1)S(1)}, bf16[4,32,1024]{2,1,0:T(8,128)(2,1)S(1)}, u32[]{:S(2)}, u32[]{:S(2)}) %collective-permute-start.17) | collective-permute-done | bytes 262176 | tf_op jit(solution)/shard_map/ppermute | solution.py:436
  99.3 1.7 %collective-permute-start.20 = (bf16[32,1024]{1,0:T(8,128)(2,1)S(1)}, bf16[32,1024]{1,0:T(8,128)(2,1)S(1)}, u32[]{:S(2)}, u32[]{:S(2)}) collective-permute-start(bf16[32,1024]{1,0:T(8,128)(2,1)S(1)} %get-tuple-element.64), channel_id=1, source_target_pairs={{0,6},{2,4},{4,2},{6,0},{1,7},{3,5},{5,3},{7,1},{8,14},{10,12},{12... | collective-permute-start | bytes 196616 | tf_op jit(solution)/shard_map/ppermute | solution.py:443
  100.9 0.9 collective-permute-start.19
  101.9 1.6 %collective-permute-start.18 = (bf16[32,1024]{1,0:T(8,128)(2,1)S(1)}, bf16[32,1024]{1,0:T(8,128)(2,1)S(1)}, u32[]{:S(2)}, u32[]{:S(2)}) collective-permute-start(bf16[32,1024]{1,0:T(8,128)(2,1)S(1)} %get-tuple-element.63), channel_id=1, source_target_pairs={{0,2},{2,0},{4,6},{6,4},{1,3},{3,1},{5,7},{7,5},{8,10},{10,8},{12,... | collective-permute-start | bytes 196616 | tf_op jit(solution)/shard_map/ppermute | solution.py:443
  103.4 0.2 collective-permute-done.20
  103.6 3.7 %collective-permute-done.19 = bf16[32,1024]{1,0:T(8,128)(2,1)S(1)} collective-permute-done((bf16[32,1024]{1,0:T(8,128)(2,1)S(1)}, bf16[32,1024]{1,0:T(8,128)(2,1)S(1)}, u32[]{:S(2)}, u32[]{:S(2)}) %collective-permute-start.19) | collective-permute-done | bytes 65568 | tf_op jit(solution)/shard_map/ppermute | solution.py:443
  107.3 0.7 fusion.3
  107.9 7.4 %all-to-all-done.2.parts = bf16[32,96,128]{2,1,0:T(8,128)(2,1)S(1)} async-done(((bf16[32,96,128]{2,1,0:T(8,128)(2,1)}), bf16[32,96,128]{2,1,0:T(8,128)(2,1)S(1)}, u32[]{:S(2)}, u32[]{:S(2)}) %all-to-all-start.2) | async-done | bytes 786464 | tf_op jit(solution)/shard_map/all_to_all | solution.py:444
  115.3 1.4 %shard_map.118 = (f32[1024,128]{1,0:T(8,128)}, f32[1024,128]{1,0:T(8,128)}, f32[1024,128]{1,0:T(8,128)}) custom-call(bf16[32,96,128]{2,1,0:T(8,128)(2,1)S(1)} %all-to-all-done.2.parts), custom_call_target="tpu_custom_call" | custom-call | bytes 786432 | tf_op jit(solution)/shard_map/pallas_call | solution.py:44
  (29 shorter events, 0.3 us)
Async XLA Ops:
  3.5 13.7 %collective-permute-start = (bf16[512,128]{1,0:T(8,128)(2,1)}, bf16[512,128]{1,0:T(8,128)(2,1)}, u32[]{:S(2)}, u32[]{:S(2)}) collective-permute-start(bf16[512,128]{1,0:T(8,128)(2,1)} %get-tuple-element.35), channel_id=1, source_target_pairs={{0,8},{8,0},{1,9},{9,1},{2,10},{10,2},{3,11},{11,3},{4,12},{12,4},... | collective-permute-start | bytes 393224 | tf_op jit(solution)/shard_map/ppermute | solution.py:342
  6.6 10.6 %collective-permute-start.1 = (bf16[512,128]{1,0:T(8,128)(2,1)}, bf16[512,128]{1,0:T(8,128)(2,1)}, u32[]{:S(2)}, u32[]{:S(2)}) collective-permute-start(bf16[512,128]{1,0:T(8,128)(2,1)} %get-tuple-element.34.refs_0_), channel_id=1, source_target_pairs={{0,16},{16,32},{32,48},{48,64},{64,80},{80,96},{96,112},{112,0},{1... | collective-permute-start | bytes 393224 | tf_op jit(solution)/shard_map/ppermute | solution.py:338
  8.6 8.7 %collective-permute-start.2 = (bf16[512,128]{1,0:T(8,128)(2,1)}, bf16[512,128]{1,0:T(8,128)(2,1)}, u32[]{:S(2)}, u32[]{:S(2)}) collective-permute-start(bf16[512,128]{1,0:T(8,128)(2,1)} %get-tuple-element.34.refs_0_), channel_id=1, source_target_pairs={{0,112},{16,0},{32,16},{48,32},{64,48},{80,64},{96,80},{112,96},{1... | collective-permute-start | bytes 393224 | tf_op jit(solution)/shard_map/ppermute | solution.py:338
  12.5 25.6 %collective-permute-start.15 = (bf16[256,1024]{1,0:T(8,128)(2,1)}, bf16[256,1024]{1,0:T(8,128)(2,1)}, u32[]{:S(2)}, u32[]{:S(2)}) collective-permute-start(bf16[256,1024]{1,0:T(8,128)(2,1)} %bitcast.26), channel_id=1, source_target_pairs={{0,8},{8,0},{1,9},{9,1},{2,10},{10,2},{3,11},{11,3},{4,12},{12,4},... | collective-permute-start | bytes 1572872 | tf_op jit(solution)/shard_map/ppermute | solution.py:342
  17.2 5.3 %collective-permute-start.4 = (bf16[512,128]{1,0:T(8,128)(2,1)}, bf16[512,128]{1,0:T(8,128)(2,1)S(1)}, u32[]{:S(2)}, u32[]{:S(2)}) collective-permute-start(bf16[512,128]{1,0:T(8,128)(2,1)} %collective-permute-done.refs_1_), channel_id=1, source_target_pairs={{0,112},{16,0},{32,16},{48,32},{64,48},{80,64},{96,80},{112,96},{1... | collective-permute-start | bytes 393224 | tf_op jit(solution)/shard_map/ppermute | solution.py:338
  19.3 6.7 %collective-permute-start.3 = (bf16[512,128]{1,0:T(8,128)(2,1)}, bf16[512,128]{1,0:T(8,128)(2,1)S(1)}, u32[]{:S(2)}, u32[]{:S(2)}) collective-permute-start(bf16[512,128]{1,0:T(8,128)(2,1)} %collective-permute-done.refs_1_), channel_id=1, source_target_pairs={{0,16},{16,32},{32,48},{48,64},{64,80},{80,96},{96,112},{112,0},{1... | collective-permute-start | bytes 393224 | tf_op jit(solution)/shard_map/ppermute | solution.py:338
  19.3 8.4 %collective-permute-start.5 = (bf16[512,128]{1,0:T(8,128)(2,1)}, bf16[512,128]{1,0:T(8,128)(2,1)S(1)}, u32[]{:S(2)}, u32[]{:S(2)}) collective-permute-start(bf16[512,128]{1,0:T(8,128)(2,1)} %collective-permute-done.1.refs_2_), channel_id=1, source_target_pairs={{0,16},{16,32},{32,48},{48,64},{64,80},{80,96},{96,112},{112,0},{1... | collective-permute-start | bytes 393224 | tf_op jit(solution)/shard_map/ppermute | solution.py:338
  22.5 6.2 %collective-permute-start.8 = (bf16[512,128]{1,0:T(8,128)(2,1)S(1)}, bf16[512,128]{1,0:T(8,128)(2,1)S(1)}, u32[]{:S(2)}, u32[]{:S(2)}) collective-permute-start(bf16[512,128]{1,0:T(8,128)(2,1)S(1)} %collective-permute-done.4.refs_5_), channel_id=1, source_target_pairs={{0,112},{16,0},{32,16},{48,32},{64,48},{80,64},{96,80},{112,96},{1... | collective-permute-start | bytes 393224 | tf_op jit(solution)/shard_map/ppermute | solution.py:338
  25.7 6.2 %collective-permute-start.7 = (bf16[512,128]{1,0:T(8,128)(2,1)}, bf16[512,128]{1,0:T(8,128)(2,1)S(1)}, u32[]{:S(2)}, u32[]{:S(2)}) collective-permute-start(bf16[512,128]{1,0:T(8,128)(2,1)} %collective-permute-done.2.refs_4_), channel_id=1, source_target_pairs={{0,112},{16,0},{32,16},{48,32},{64,48},{80,64},{96,80},{112,96},{1... | collective-permute-start | bytes 393224 | tf_op jit(solution)/shard_map/ppermute | solution.py:338
  26.0 7.6 %collective-permute-start.6 = (bf16[512,128]{1,0:T(8,128)(2,1)S(1)}, bf16[512,128]{1,0:T(8,128)(2,1)S(1)}, u32[]{:S(2)}, u32[]{:S(2)}) collective-permute-start(bf16[512,128]{1,0:T(8,128)(2,1)S(1)} %collective-permute-done.3.refs_3_), channel_id=1, source_target_pairs={{0,16},{16,32},{32,48},{48,64},{64,80},{80,96},{96,112},{112,0},{1... | collective-permute-start | bytes 393224 | tf_op jit(solution)/shard_map/ppermute | solution.py:338
  27.7 6.4 %collective-permute-start.9 = (bf16[512,128]{1,0:T(8,128)(2,1)S(1)}, bf16[512,128]{1,0:T(8,128)(2,1)S(1)}, u32[]{:S(2)}, u32[]{:S(2)}) collective-permute-start(bf16[512,128]{1,0:T(8,128)(2,1)S(1)} %collective-permute-done.5.refs_6_), channel_id=1, source_target_pairs={{0,16},{16,32},{32,48},{48,64},{64,80},{80,96},{96,112},{112,0},{1... | collective-permute-start | bytes 393224 | tf_op jit(solution)/shard_map/ppermute | solution.py:338
  28.7 6.3 %collective-permute-start.12 = (bf16[512,128]{1,0:T(8,128)(2,1)S(1)}, bf16[512,128]{1,0:T(8,128)(2,1)S(1)}, u32[]{:S(2)}, u32[]{:S(2)}) collective-permute-start(bf16[512,128]{1,0:T(8,128)(2,1)S(1)} %collective-permute-done.8.refs_9_), channel_id=1, source_target_pairs={{0,112},{16,0},{32,16},{48,32},{64,48},{80,64},{96,80},{112,96},{1... | collective-permute-start | bytes 393224 | tf_op jit(solution)/shard_map/ppermute | solution.py:338
  31.9 6.2 %collective-permute-start.11 = (bf16[512,128]{1,0:T(8,128)(2,1)S(1)}, bf16[512,128]{1,0:T(8,128)(2,1)S(1)}, u32[]{:S(2)}, u32[]{:S(2)}) collective-permute-start(bf16[512,128]{1,0:T(8,128)(2,1)S(1)} %collective-permute-done.7.refs_8_), channel_id=1, source_target_pairs={{0,112},{16,0},{32,16},{48,32},{64,48},{80,64},{96,80},{112,96},{1... | collective-permute-start | bytes 393224 | tf_op jit(solution)/shard_map/ppermute | solution.py:338
  33.6 6.2 %collective-permute-start.10 = (bf16[512,128]{1,0:T(8,128)(2,1)S(1)}, bf16[512,128]{1,0:T(8,128)(2,1)S(1)}, u32[]{:S(2)}, u32[]{:S(2)}) collective-permute-start(bf16[512,128]{1,0:T(8,128)(2,1)S(1)} %collective-permute-done.6.refs_7_), channel_id=1, source_target_pairs={{0,16},{16,32},{32,48},{48,64},{64,80},{80,96},{96,112},{112,0},{1... | collective-permute-start | bytes 393224 | tf_op jit(solution)/shard_map/ppermute | solution.py:338
  34.2 7.0 %collective-permute-start.13 = (bf16[512,128]{1,0:T(8,128)(2,1)S(1)}, bf16[512,128]{1,0:T(8,128)(2,1)S(1)}, u32[]{:S(2)}, u32[]{:S(2)}) collective-permute-start(bf16[512,128]{1,0:T(8,128)(2,1)S(1)} %collective-permute-done.9.refs_10_), channel_id=1, source_target_pairs={{0,16},{16,32},{32,48},{48,64},{64,80},{80,96},{96,112},{112,0},{1... | collective-permute-start | bytes 393224 | tf_op jit(solution)/shard_map/ppermute | solution.py:338
  35.0 6.2 %collective-permute-start.14 = (bf16[512,128]{1,0:T(8,128)(2,1)S(1)}, bf16[512,128]{1,0:T(8,128)(2,1)S(1)}, u32[]{:S(2)}, u32[]{:S(2)}) collective-permute-start(bf16[512,128]{1,0:T(8,128)(2,1)S(1)} %collective-permute-done.12.refs_13_), channel_id=1, source_target_pairs={{0,112},{16,0},{32,16},{48,32},{64,48},{80,64},{96,80},{112,96},{1... | collective-permute-start | bytes 393224 | tf_op jit(solution)/shard_map/ppermute | solution.py:338
  41.2 0.7 copy-start.4
  41.9 0.9 copy-start.6
  42.8 12.3 %copy-start.7 = (bf16[512,128]{1,0:T(8,128)(2,1)S(1)}, bf16[512,128]{1,0:T(8,128)(2,1)}, u32[]{:S(2)}) copy-start(bf16[512,128]{1,0:T(8,128)(2,1)} %get-tuple-element.34.refs_0_) | copy-start | bytes 393220
  48.5 14.5 %all-to-all-start = ((f32[8,8,128]{2,1,0:T(8,128)}), f32[8,8,128]{2,1,0:T(8,128)S(1)}, u32[]{:S(2)}, u32[]{:S(2)}) async-start(f32[8,8,128]{2,1,0:T(8,128)} %get-tuple-element.42), calls=%async_computation | async-start | bytes 65536 | tf_op jit(solution)/shard_map/all_to_all | solution.py:402
  55.0 0.7 copy-start.5
  63.0 7.0 %copy-start = (bf16[1,256,1024]{2,1,0:T(8,128)(2,1)S(1)}, bf16[1,256,1024]{2,1,0:T(8,128)(2,1)}, u32[]{:S(2)}) copy-start(bf16[1,256,1024]{2,1,0:T(8,128)(2,1)} %param.7) | copy-start | bytes 1572868
  72.7 13.1 %copy-start.1 = (bf16[1024,128]{1,0:T(8,128)(2,1)S(1)}, bf16[1024,128]{1,0:T(8,128)(2,1)}, u32[]{:S(2)}) copy-start(bf16[1024,128]{1,0:T(8,128)(2,1)} %wq.3) | copy-start | bytes 786436
  72.7 13.1 %copy-start.2 = (bf16[1024,128]{1,0:T(8,128)(2,1)S(1)}, bf16[1024,128]{1,0:T(8,128)(2,1)}, u32[]{:S(2)}) copy-start(bf16[1024,128]{1,0:T(8,128)(2,1)} %wk.3) | copy-start | bytes 786436
  72.7 13.1 %copy-start.3 = (bf16[1024,128]{1,0:T(8,128)(2,1)S(1)}, bf16[1024,128]{1,0:T(8,128)(2,1)}, u32[]{:S(2)}) copy-start(bf16[1024,128]{1,0:T(8,128)(2,1)} %wv.3) | copy-start | bytes 786436
  72.7 16.0 %all-to-all-start.1 = ((bf16[16,96,128]{2,1,0:T(8,128)(2,1)}), bf16[16,96,128]{2,1,0:T(8,128)(2,1)S(1)}, u32[]{:S(2)}, u32[]{:S(2)}) async-start(bf16[16,96,128]{2,1,0:T(8,128)(2,1)} %shard_map.116), calls=%async_computation.1 | async-start | bytes 786432 | tf_op jit(solution)/shard_map/all_to_all | solution.py:428
  78.4 7.3 %collective-permute-start.16 = (bf16[512,128]{1,0:T(8,128)(2,1)S(1)}, bf16[512,128]{1,0:T(8,128)(2,1)S(1)}, u32[]{:S(2)}, u32[]{:S(2)}) collective-permute-start(bf16[512,128]{1,0:T(8,128)(2,1)S(1)} %get-tuple-element.51.sent), channel_id=1, source_target_pairs={{0,8},{8,0},{1,9},{9,1},{2,10},{10,2},{3,11},{11,3},{4,12},{12,4},... | collective-permute-start | bytes 393224 | tf_op jit(solution)/shard_map/ppermute | solution.py:342
  89.7 25.6 %all-to-all-start.2 = ((bf16[32,96,128]{2,1,0:T(8,128)(2,1)}), bf16[32,96,128]{2,1,0:T(8,128)(2,1)S(1)}, u32[]{:S(2)}, u32[]{:S(2)}) async-start(bf16[32,96,128]{2,1,0:T(8,128)(2,1)} %shard_map.117), calls=%async_computation.2 | async-start | bytes 1572864 | tf_op jit(solution)/shard_map/all_to_all | solution.py:444
  97.5 1.6 %collective-permute-start.17 = (bf16[4,32,1024]{2,1,0:T(8,128)(2,1)S(1)}, bf16[4,32,1024]{2,1,0:T(8,128)(2,1)S(1)}, u32[]{:S(2)}, u32[]{:S(2)}) collective-permute-start(bf16[4,32,1024]{2,1,0:T(8,128)(2,1)S(1)} %get-tuple-element.56), channel_id=1, source_target_pairs={{0,1},{1,0},{2,3},{3,2},{4,5},{5,4},{6,7},{7,6},{8,9},{9,8},{10,11... | collective-permute-start | bytes 786440 | tf_op jit(solution)/shard_map/ppermute | solution.py:436
  99.3 4.4 %collective-permute-start.20 = (bf16[32,1024]{1,0:T(8,128)(2,1)S(1)}, bf16[32,1024]{1,0:T(8,128)(2,1)S(1)}, u32[]{:S(2)}, u32[]{:S(2)}) collective-permute-start(bf16[32,1024]{1,0:T(8,128)(2,1)S(1)} %get-tuple-element.64), channel_id=1, source_target_pairs={{0,6},{2,4},{4,2},{6,0},{1,7},{3,5},{5,3},{7,1},{8,14},{10,12},{12... | collective-permute-start | bytes 196616 | tf_op jit(solution)/shard_map/ppermute | solution.py:443
  100.9 6.4 %collective-permute-start.19 = (bf16[32,1024]{1,0:T(8,128)(2,1)S(1)}, bf16[32,1024]{1,0:T(8,128)(2,1)S(1)}, u32[]{:S(2)}, u32[]{:S(2)}) collective-permute-start(bf16[32,1024]{1,0:T(8,128)(2,1)S(1)} %get-tuple-element.65), channel_id=1, source_target_pairs={{0,4},{2,6},{4,0},{6,2},{1,5},{3,7},{5,1},{7,3},{8,12},{10,14},{12... | collective-permute-start | bytes 196616 | tf_op jit(solution)/shard_map/ppermute | solution.py:443
  101.9 5.4 %collective-permute-start.18 = (bf16[32,1024]{1,0:T(8,128)(2,1)S(1)}, bf16[32,1024]{1,0:T(8,128)(2,1)S(1)}, u32[]{:S(2)}, u32[]{:S(2)}) collective-permute-start(bf16[32,1024]{1,0:T(8,128)(2,1)S(1)} %get-tuple-element.63), channel_id=1, source_target_pairs={{0,2},{2,0},{4,6},{6,4},{1,3},{3,1},{5,7},{7,5},{8,10},{10,8},{12,... | collective-permute-start | bytes 196616 | tf_op jit(solution)/shard_map/ppermute | solution.py:443

commit v9 on v8

--- a/solution.py
+++ b/solution.py
@@ -391,7 +391,6 @@
     for i in (1, 2, 3):
         pieces += (lower_a[i], lower_b[i], upper_a[i], upper_b[i])
     pieces += far
-    tok_other, feat = tie((tok_other, feat))
     att_rows, column, stats = call(
         forward_kernel,
         (shape((SEC, 128), BF), wide, shape((NSEC, 8, 128), F32)),

time: 117 us -> 115 us (0.983)
  waiting for transfers between devices: 29.4 us -> 26.7 us
  starting transfers between devices: 51.5 us -> 53.1 us
    all_to_all x1, waiting for transfers between devices: 7.37 us -> 5.49 us  [on_device(): total = lax.all_to_all(total, ('b',) + CTX, 0, 0, tiled=True)]
  transfers between devices with their start and end apart: 24 -> 24, of which waited for: 13 -> 14; matrix products, arithmetic and copies ran while one was open for 1% -> 1% of each run, Pallas kernels for 9% -> 21%
where the time goes in v9:
time: 115 us; the launch traced here: 114 us
  starting transfers between devices  53.1 us (46%)
  Pallas kernels  30.4 us (26%)
  waiting for transfers between devices  26.7 us (23%)
  local copies, waits for them, and re-layouts  2.08 us (2%)
  other arithmetic  1.29 us (1%)
    pallas_call x9, Pallas kernels, call(): pl.pallas_call(kernel, out_shape=outs, in_specs=specs, out_specs=jax.tree...  30.4 us
    ppermute x14, starting transfers between devices, shift(): return lax.ppermute(a, Z, [(i, (i + step) % NSEC) for i in range(NSEC)])  22.6 us
    all_to_all x1, starting transfers between devices, on_device(): total = lax.all_to_all(total, ('b',) + CTX, 0, 0, tiled=True)  8.18 us
    ppermute x14, waiting for transfers between devices, shift(): return lax.ppermute(a, Z, [(i, (i + step) % NSEC) for i in range(NSEC)])  7.47 us
    all_to_all x1, starting transfers between devices, on_device(): lax.all_to_all(stats, Z, 0, 0, tiled=True).reshape(NSEC * 8, 128)  6.53 us
    ppermute x3, starting transfers between devices, swap(): return lax.ppermute(a, 'xh', [(0, 1), (1, 0)])  6.01 us
    all_to_all x1, starting transfers between devices, on_device(): partial = lax.all_to_all(partial, ('b',) + Z, 0, 0, tiled=True)  5.55 us
    all_to_all x1, waiting for transfers between devices, on_device(): total = lax.all_to_all(total, ('b',) + CTX, 0, 0, tiled=True)  5.49 us
  transfers between devices with their start and end apart: 24, of which 14 were waited for; matrix products, arithmetic and copies ran while one was open for 1% of the time, Pallas kernels for 21%

profile of v9, /device:TPU:8, one launch (start us, length us, event | category | flops | bytes accessed | tf_op | source)
XLA Modules:
  0.0 114.4 jit_solution(18307575120951755696)
XLA Ops:
  0.6 2.9 %shard_map.110 = (bf16[512,128]{1,0:T(8,128)(2,1)}, bf16[512,128]{1,0:T(8,128)(2,1)}) custom-call(bf16[256,1024]{1,0:T(8,128)(2,1)} %bitcast.25, bf16[1024,128]{1,0:T(8,128)(2,1)} %wq.3, bf16[1024,128]{1,0:T(8,128)(2,1)} %wk.3, bf16[1024,128]{1,0:T(8,128)(2,1)} %wv.3, bf16[256,128]{1,0:T(8,128)(2,1)} %bitcast.29), custom_call_target="tpu_custom_call" | custom-call | flops 201326592 | bytes 1376256 | tf_op jit(solution)/shard_map/pallas_call | solution.py:44
  3.5 3.1 %collective-permute-start = (bf16[512,128]{1,0:T(8,128)(2,1)}, bf16[512,128]{1,0:T(8,128)(2,1)}, u32[]{:S(2)}, u32[]{:S(2)}) collective-permute-start(bf16[512,128]{1,0:T(8,128)(2,1)} %get-tuple-element.33), channel_id=1, source_target_pairs={{0,8},{8,0},{1,9},{9,1},{2,10},{10,2},{3,11},{11,3},{4,12},{12,4},... | collective-permute-start | bytes 393224 | tf_op jit(solution)/shard_map/ppermute | solution.py:342
  6.6 1.9 %collective-permute-start.1 = (bf16[512,128]{1,0:T(8,128)(2,1)}, bf16[512,128]{1,0:T(8,128)(2,1)}, u32[]{:S(2)}, u32[]{:S(2)}) collective-permute-start(bf16[512,128]{1,0:T(8,128)(2,1)} %get-tuple-element.32.refs_0_), channel_id=1, source_target_pairs={{0,16},{16,32},{32,48},{48,64},{64,80},{80,96},{96,112},{112,0},{1... | collective-permute-start | bytes 393224 | tf_op jit(solution)/shard_map/ppermute | solution.py:338
  8.6 3.9 %collective-permute-start.2 = (bf16[512,128]{1,0:T(8,128)(2,1)}, bf16[512,128]{1,0:T(8,128)(2,1)}, u32[]{:S(2)}, u32[]{:S(2)}) collective-permute-start(bf16[512,128]{1,0:T(8,128)(2,1)} %get-tuple-element.32.refs_0_), channel_id=1, source_target_pairs={{0,112},{16,0},{32,16},{48,32},{64,48},{80,64},{96,80},{112,96},{1... | collective-permute-start | bytes 393224 | tf_op jit(solution)/shard_map/ppermute | solution.py:338
  12.5 0.6 pad_add_fusion.place
  13.1 3.6 %shard_map.111.refs_16_ = bf16[4096,128]{1,0:T(8,128)(2,1)} custom-call(s32[3]{0:T(128)} %pad_add_fusion.place, s32[1,8]{1,0:T(1,128)} %lengths.1, s32[1,256]{1,0:T(1,128)} %spots.1), custom_call_target="tpu_custom_call" | custom-call | bytes 1068 | tf_op jit(solution)/shard_map/pallas_call | solution.py:44
  16.6 2.4 %collective-permute-start.4 = (bf16[512,128]{1,0:T(8,128)(2,1)}, bf16[512,128]{1,0:T(8,128)(2,1)S(1)}, u32[]{:S(2)}, u32[]{:S(2)}) collective-permute-start(bf16[512,128]{1,0:T(8,128)(2,1)} %collective-permute-done.refs_1_), channel_id=1, source_target_pairs={{0,112},{16,0},{32,16},{48,32},{64,48},{80,64},{96,80},{112,96},{1... | collective-permute-start | bytes 393224 | tf_op jit(solution)/shard_map/ppermute | solution.py:338
  19.0 2.9 %collective-permute-done.4.refs_5_ = bf16[512,128]{1,0:T(8,128)(2,1)S(1)} collective-permute-done((bf16[512,128]{1,0:T(8,128)(2,1)}, bf16[512,128]{1,0:T(8,128)(2,1)S(1)}, u32[]{:S(2)}, u32[]{:S(2)}) %collective-permute-start.4) | collective-permute-done | bytes 131104 | tf_op jit(solution)/shard_map/ppermute | solution.py:338
  21.9 3.5 %collective-permute-start.8 = (bf16[512,128]{1,0:T(8,128)(2,1)S(1)}, bf16[512,128]{1,0:T(8,128)(2,1)S(1)}, u32[]{:S(2)}, u32[]{:S(2)}) collective-permute-start(bf16[512,128]{1,0:T(8,128)(2,1)S(1)} %collective-permute-done.4.refs_5_), channel_id=1, source_target_pairs={{0,112},{16,0},{32,16},{48,32},{64,48},{80,64},{96,80},{112,96},{1... | collective-permute-start | bytes 393224 | tf_op jit(solution)/shard_map/ppermute | solution.py:338
  25.4 0.3 collective-permute-done.3.refs_3_
  25.7 1.7 %collective-permute-start.6 = (bf16[512,128]{1,0:T(8,128)(2,1)S(1)}, bf16[512,128]{1,0:T(8,128)(2,1)S(1)}, u32[]{:S(2)}, u32[]{:S(2)}) collective-permute-start(bf16[512,128]{1,0:T(8,128)(2,1)S(1)} %collective-permute-done.3.refs_3_), channel_id=1, source_target_pairs={{0,16},{16,32},{32,48},{48,64},{64,80},{80,96},{96,112},{112,0},{1... | collective-permute-start | bytes 393224 | tf_op jit(solution)/shard_map/ppermute | solution.py:338
  27.4 0.1 collective-permute-done.5.refs_6_
  27.6 0.7 collective-permute-done.8.refs_9_
  28.2 3.4 %collective-permute-start.12 = (bf16[512,128]{1,0:T(8,128)(2,1)S(1)}, bf16[512,128]{1,0:T(8,128)(2,1)S(1)}, u32[]{:S(2)}, u32[]{:S(2)}) collective-permute-start(bf16[512,128]{1,0:T(8,128)(2,1)S(1)} %collective-permute-done.8.refs_9_), channel_id=1, source_target_pairs={{0,112},{16,0},{32,16},{48,32},{64,48},{80,64},{96,80},{112,96},{1... | collective-permute-start | bytes 393224 | tf_op jit(solution)/shard_map/ppermute | solution.py:338
  31.6 2.5 %collective-permute-start.11 = (bf16[512,128]{1,0:T(8,128)(2,1)S(1)}, bf16[512,128]{1,0:T(8,128)(2,1)S(1)}, u32[]{:S(2)}, u32[]{:S(2)}) collective-permute-start(bf16[512,128]{1,0:T(8,128)(2,1)S(1)} %collective-permute-done.7.refs_8_), channel_id=1, source_target_pairs={{0,112},{16,0},{32,16},{48,32},{64,48},{80,64},{96,80},{112,96},{1... | collective-permute-start | bytes 393224 | tf_op jit(solution)/shard_map/ppermute | solution.py:338
  34.1 0.5 collective-permute-done.9.refs_10_
  34.6 0.2 collective-permute-start.13
  34.8 3.0 %collective-permute-start.14 = (bf16[512,128]{1,0:T(8,128)(2,1)S(1)}, bf16[512,128]{1,0:T(8,128)(2,1)S(1)}, u32[]{:S(2)}, u32[]{:S(2)}) collective-permute-start(bf16[512,128]{1,0:T(8,128)(2,1)S(1)} %collective-permute-done.12.refs_13_), channel_id=1, source_target_pairs={{0,112},{16,0},{32,16},{48,32},{64,48},{80,64},{96,80},{112,96},{1... | collective-permute-start | bytes 393224 | tf_op jit(solution)/shard_map/ppermute | solution.py:338
  37.8 0.8 collective-permute-start.16
  38.7 1.6 %collective-permute-done.10.refs_11_ = bf16[512,128]{1,0:T(8,128)(2,1)S(1)} collective-permute-done((bf16[512,128]{1,0:T(8,128)(2,1)S(1)}, bf16[512,128]{1,0:T(8,128)(2,1)S(1)}, u32[]{:S(2)}, u32[]{:S(2)}) %collective-permute-start.10) | collective-permute-done | bytes 131104 | tf_op jit(solution)/shard_map/ppermute | solution.py:338
  40.2 1.4 %collective-permute-done.13.refs_14_ = bf16[512,128]{1,0:T(8,128)(2,1)S(1)} collective-permute-done((bf16[512,128]{1,0:T(8,128)(2,1)S(1)}, bf16[512,128]{1,0:T(8,128)(2,1)S(1)}, u32[]{:S(2)}, u32[]{:S(2)}) %collective-permute-start.13) | collective-permute-done | bytes 131104 | tf_op jit(solution)/shard_map/ppermute | solution.py:338
  41.7 0.6 copy-done.4
  42.2 0.9 copy-done.6
  43.1 5.7 %shard_map.112 = (bf16[512,128]{1,0:T(8,128)(2,1)S(1)}, f32[512,128]{1,0:T(8,128)S(1)}, f32[8,8,128]{2,1,0:T(8,128)}) custom-call(s32[3]{0:T(128)S(1)} %copy-done.4, bf16[512,128]{1,0:T(8,128)(2,1)S(1)} %copy-done.6, bf16[512,128]{1,0:T(8,128)(2,1)} %collective-permute-done.refs_1_, bf16[512,128]{1,0:T(8,128)(2,1)} %collective-permute-done.1.refs_2_, ...), custom_call_target="tpu_custom_call" | custom-call | flops 1073741824 | bytes 3145740 | tf_op jit(solution)/shard_map/pallas_call | solution.py:44
  48.9 6.5 %all-to-all-start = ((f32[8,8,128]{2,1,0:T(8,128)}), f32[8,8,128]{2,1,0:T(8,128)S(1)}, u32[]{:S(2)}, u32[]{:S(2)}) async-start(f32[8,8,128]{2,1,0:T(8,128)} %get-tuple-element.39), calls=%async_computation | async-start | bytes 65536 | tf_op jit(solution)/shard_map/all_to_all | solution.py:401
  55.4 0.6 copy-done.5
  56.0 5.5 %shard_map.113 = (bf16[256,128]{1,0:T(8,128)(2,1)S(1)}, bf16[256,128]{1,0:T(8,128)(2,1)S(1)}) custom-call(s32[3]{0:T(128)S(1)} %copy-done.5, bf16[512,128]{1,0:T(8,128)(2,1)S(1)} %copy-done.7, bf16[512,128]{1,0:T(8,128)(2,1)} %collective-permute-done.refs_1_, bf16[512,128]{1,0:T(8,128)(2,1)} %collective-permute-done.1.refs_2_, ...), custom_call_target="tpu_custom_call" | custom-call | flops 1610612736 | bytes 3538956 | tf_op jit(solution)/shard_map/pallas_call | solution.py:44
  61.5 1.9 %all-to-all-done = f32[8,8,128]{2,1,0:T(8,128)S(1)} async-done(((f32[8,8,128]{2,1,0:T(8,128)}), f32[8,8,128]{2,1,0:T(8,128)S(1)}, u32[]{:S(2)}, u32[]{:S(2)}) %all-to-all-start) | async-done | bytes 32800 | tf_op jit(solution)/shard_map/all_to_all | solution.py:401
  63.4 7.0 %shard_map.114 = (bf16[256,128]{1,0:T(8,128)(2,1)S(1)}, bf16[512,128]{1,0:T(8,128)(2,1)S(1)}) custom-call(s32[3]{0:T(128)S(1)} %copy-done.5, bf16[512,128]{1,0:T(8,128)(2,1)S(1)} %copy-done.7, bf16[512,128]{1,0:T(8,128)(2,1)} %collective-permute-done.refs_1_, bf16[512,128]{1,0:T(8,128)(2,1)} %collective-permute-done.1.refs_2_, ...), custom_call_target="tpu_custom_call" | custom-call | flops 2147483648 | bytes 3244044 | tf_op jit(solution)/shard_map/pallas_call | solution.py:44
  70.5 1.6 %shard_map.116 = bf16[16,96,128]{2,1,0:T(8,128)(2,1)} custom-call(bf16[256,1024]{1,0:T(8,128)(2,1)S(1)} %bitcast.27, bf16[256,1024]{1,0:T(8,128)(2,1)S(1)} %collective-permute-done.16.tok_other, bf16[256,128]{1,0:T(8,128)(2,1)S(1)} %get-tuple-element.44.first, bf16[256,128]{1,0:T(8,128)(2,1)S(1)} %get-tuple-element.47.second, ...), custom_call_target="tpu_custom_call" | custom-call | flops 268435456 | bytes 1310720 | tf_op jit(solution)/shard_map/pallas_call | solution.py:44
  72.0 5.5 %all-to-all-start.1 = ((bf16[16,96,128]{2,1,0:T(8,128)(2,1)}), bf16[16,96,128]{2,1,0:T(8,128)(2,1)S(1)}, u32[]{:S(2)}, u32[]{:S(2)}) async-start(bf16[16,96,128]{2,1,0:T(8,128)(2,1)} %shard_map.116), calls=%async_computation.1 | async-start | bytes 786432 | tf_op jit(solution)/shard_map/all_to_all | solution.py:427
  77.6 2.1 %collective-permute-start.15 = (bf16[512,128]{1,0:T(8,128)(2,1)S(1)}, bf16[512,128]{1,0:T(8,128)(2,1)S(1)}, u32[]{:S(2)}, u32[]{:S(2)}) collective-permute-start(bf16[512,128]{1,0:T(8,128)(2,1)S(1)} %get-tuple-element.48.sent), channel_id=1, source_target_pairs={{0,8},{8,0},{1,9},{9,1},{2,10},{10,2},{3,11},{11,3},{4,12},{12,4},... | collective-permute-start | bytes 393224 | tf_op jit(solution)/shard_map/ppermute | solution.py:342
  79.7 5.0 %collective-permute-done.15.arrived = bf16[512,128]{1,0:T(8,128)(2,1)S(1)} collective-permute-done((bf16[512,128]{1,0:T(8,128)(2,1)S(1)}, bf16[512,128]{1,0:T(8,128)(2,1)S(1)}, u32[]{:S(2)}, u32[]{:S(2)}) %collective-permute-start.15) | collective-permute-done | bytes 131104 | tf_op jit(solution)/shard_map/ppermute | solution.py:342
  84.7 1.7 %shard_map.115 = (bf16[256,128]{1,0:T(8,128)(2,1)}, f32[4,32,1024]{2,1,0:T(8,128)S(1)}, bf16[4,32,1024]{2,1,0:T(8,128)(2,1)S(1)}) custom-call(s32[3]{0:T(128)S(1)} %copy-done.5, bf16[256,128]{1,0:T(8,128)(2,1)S(1)} %get-tuple-element.44.first, bf16[256,128]{1,0:T(8,128)(2,1)S(1)} %get-tuple-element.47.second, ...), custom_call_target="tpu_custom_call" | custom-call | flops 201326592 | bytes 1048588 | tf_op jit(solution)/shard_map/pallas_call | solution.py:44
  86.4 1.5 %all-to-all-done.1.parts = bf16[16,96,128]{2,1,0:T(8,128)(2,1)S(1)} async-done(((bf16[16,96,128]{2,1,0:T(8,128)(2,1)}), bf16[16,96,128]{2,1,0:T(8,128)(2,1)S(1)}, u32[]{:S(2)}, u32[]{:S(2)}) %all-to-all-start.1) | async-done | bytes 393248 | tf_op jit(solution)/shard_map/all_to_all | solution.py:427
  87.9 1.0 shard_map.117
  88.9 8.2 %all-to-all-start.2 = ((bf16[32,96,128]{2,1,0:T(8,128)(2,1)}), bf16[32,96,128]{2,1,0:T(8,128)(2,1)S(1)}, u32[]{:S(2)}, u32[]{:S(2)}) async-start(bf16[32,96,128]{2,1,0:T(8,128)(2,1)} %shard_map.117), calls=%async_computation.2 | async-start | bytes 1572864 | tf_op jit(solution)/shard_map/all_to_all | solution.py:443
  97.1 0.1 collective-permute-start.17
  97.2 1.5 %collective-permute-done.17 = bf16[4,32,1024]{2,1,0:T(8,128)(2,1)S(1)} collective-permute-done((bf16[4,32,1024]{2,1,0:T(8,128)(2,1)S(1)}, bf16[4,32,1024]{2,1,0:T(8,128)(2,1)S(1)}, u32[]{:S(2)}, u32[]{:S(2)}) %collective-permute-start.17) | collective-permute-done | bytes 262176 | tf_op jit(solution)/shard_map/ppermute | solution.py:435
  98.7 0.1 fusion.4
  98.8 1.7 %collective-permute-start.20 = (bf16[32,1024]{1,0:T(8,128)(2,1)S(1)}, bf16[32,1024]{1,0:T(8,128)(2,1)S(1)}, u32[]{:S(2)}, u32[]{:S(2)}) collective-permute-start(bf16[32,1024]{1,0:T(8,128)(2,1)S(1)} %get-tuple-element.60), channel_id=1, source_target_pairs={{0,6},{2,4},{4,2},{6,0},{1,7},{3,5},{5,3},{7,1},{8,14},{10,12},{12... | collective-permute-start | bytes 196616 | tf_op jit(solution)/shard_map/ppermute | solution.py:442
  100.5 0.9 collective-permute-start.19
  101.4 1.6 %collective-permute-start.18 = (bf16[32,1024]{1,0:T(8,128)(2,1)S(1)}, bf16[32,1024]{1,0:T(8,128)(2,1)S(1)}, u32[]{:S(2)}, u32[]{:S(2)}) collective-permute-start(bf16[32,1024]{1,0:T(8,128)(2,1)S(1)} %get-tuple-element.59), channel_id=1, source_target_pairs={{0,2},{2,0},{4,6},{6,4},{1,3},{3,1},{5,7},{7,5},{8,10},{10,8},{12,... | collective-permute-start | bytes 196616 | tf_op jit(solution)/shard_map/ppermute | solution.py:442
  103.0 0.2 collective-permute-done.20
  103.2 3.7 %collective-permute-done.19 = bf16[32,1024]{1,0:T(8,128)(2,1)S(1)} collective-permute-done((bf16[32,1024]{1,0:T(8,128)(2,1)S(1)}, bf16[32,1024]{1,0:T(8,128)(2,1)S(1)}, u32[]{:S(2)}, u32[]{:S(2)}) %collective-permute-start.19) | collective-permute-done | bytes 65568 | tf_op jit(solution)/shard_map/ppermute | solution.py:442
  106.8 0.7 fusion.3
  107.5 5.5 %all-to-all-done.2.parts = bf16[32,96,128]{2,1,0:T(8,128)(2,1)S(1)} async-done(((bf16[32,96,128]{2,1,0:T(8,128)(2,1)}), bf16[32,96,128]{2,1,0:T(8,128)(2,1)S(1)}, u32[]{:S(2)}, u32[]{:S(2)}) %all-to-all-start.2) | async-done | bytes 786464 | tf_op jit(solution)/shard_map/all_to_all | solution.py:443
  113.0 1.4 %shard_map.118 = (f32[1024,128]{1,0:T(8,128)}, f32[1024,128]{1,0:T(8,128)}, f32[1024,128]{1,0:T(8,128)}) custom-call(bf16[32,96,128]{2,1,0:T(8,128)(2,1)S(1)} %all-to-all-done.2.parts), custom_call_target="tpu_custom_call" | custom-call | bytes 786432 | tf_op jit(solution)/shard_map/pallas_call | solution.py:44
  (29 shorter events, 0.1 us)
Async XLA Ops:
  3.5 13.1 %collective-permute-start = (bf16[512,128]{1,0:T(8,128)(2,1)}, bf16[512,128]{1,0:T(8,128)(2,1)}, u32[]{:S(2)}, u32[]{:S(2)}) collective-permute-start(bf16[512,128]{1,0:T(8,128)(2,1)} %get-tuple-element.33), channel_id=1, source_target_pairs={{0,8},{8,0},{1,9},{9,1},{2,10},{10,2},{3,11},{11,3},{4,12},{12,4},... | collective-permute-start | bytes 393224 | tf_op jit(solution)/shard_map/ppermute | solution.py:342
  6.6 10.0 %collective-permute-start.1 = (bf16[512,128]{1,0:T(8,128)(2,1)}, bf16[512,128]{1,0:T(8,128)(2,1)}, u32[]{:S(2)}, u32[]{:S(2)}) collective-permute-start(bf16[512,128]{1,0:T(8,128)(2,1)} %get-tuple-element.32.refs_0_), channel_id=1, source_target_pairs={{0,16},{16,32},{32,48},{48,64},{64,80},{80,96},{96,112},{112,0},{1... | collective-permute-start | bytes 393224 | tf_op jit(solution)/shard_map/ppermute | solution.py:338
  8.6 8.1 %collective-permute-start.2 = (bf16[512,128]{1,0:T(8,128)(2,1)}, bf16[512,128]{1,0:T(8,128)(2,1)}, u32[]{:S(2)}, u32[]{:S(2)}) collective-permute-start(bf16[512,128]{1,0:T(8,128)(2,1)} %get-tuple-element.32.refs_0_), channel_id=1, source_target_pairs={{0,112},{16,0},{32,16},{48,32},{64,48},{80,64},{96,80},{112,96},{1... | collective-permute-start | bytes 393224 | tf_op jit(solution)/shard_map/ppermute | solution.py:338
  16.6 5.3 %collective-permute-start.4 = (bf16[512,128]{1,0:T(8,128)(2,1)}, bf16[512,128]{1,0:T(8,128)(2,1)S(1)}, u32[]{:S(2)}, u32[]{:S(2)}) collective-permute-start(bf16[512,128]{1,0:T(8,128)(2,1)} %collective-permute-done.refs_1_), channel_id=1, source_target_pairs={{0,112},{16,0},{32,16},{48,32},{64,48},{80,64},{96,80},{112,96},{1... | collective-permute-start | bytes 393224 | tf_op jit(solution)/shard_map/ppermute | solution.py:338
  19.0 6.7 %collective-permute-start.3 = (bf16[512,128]{1,0:T(8,128)(2,1)}, bf16[512,128]{1,0:T(8,128)(2,1)S(1)}, u32[]{:S(2)}, u32[]{:S(2)}) collective-permute-start(bf16[512,128]{1,0:T(8,128)(2,1)} %collective-permute-done.refs_1_), channel_id=1, source_target_pairs={{0,16},{16,32},{32,48},{48,64},{64,80},{80,96},{96,112},{112,0},{1... | collective-permute-start | bytes 393224 | tf_op jit(solution)/shard_map/ppermute | solution.py:338
  19.0 8.6 %collective-permute-start.5 = (bf16[512,128]{1,0:T(8,128)(2,1)}, bf16[512,128]{1,0:T(8,128)(2,1)S(1)}, u32[]{:S(2)}, u32[]{:S(2)}) collective-permute-start(bf16[512,128]{1,0:T(8,128)(2,1)} %collective-permute-done.1.refs_2_), channel_id=1, source_target_pairs={{0,16},{16,32},{32,48},{48,64},{64,80},{80,96},{96,112},{112,0},{1... | collective-permute-start | bytes 393224 | tf_op jit(solution)/shard_map/ppermute | solution.py:338
  21.9 6.3 %collective-permute-start.8 = (bf16[512,128]{1,0:T(8,128)(2,1)S(1)}, bf16[512,128]{1,0:T(8,128)(2,1)S(1)}, u32[]{:S(2)}, u32[]{:S(2)}) collective-permute-start(bf16[512,128]{1,0:T(8,128)(2,1)S(1)} %collective-permute-done.4.refs_5_), channel_id=1, source_target_pairs={{0,112},{16,0},{32,16},{48,32},{64,48},{80,64},{96,80},{112,96},{1... | collective-permute-start | bytes 393224 | tf_op jit(solution)/shard_map/ppermute | solution.py:338
  25.4 6.2 %collective-permute-start.7 = (bf16[512,128]{1,0:T(8,128)(2,1)}, bf16[512,128]{1,0:T(8,128)(2,1)S(1)}, u32[]{:S(2)}, u32[]{:S(2)}) collective-permute-start(bf16[512,128]{1,0:T(8,128)(2,1)} %collective-permute-done.2.refs_4_), channel_id=1, source_target_pairs={{0,112},{16,0},{32,16},{48,32},{64,48},{80,64},{96,80},{112,96},{1... | collective-permute-start | bytes 393224 | tf_op jit(solution)/shard_map/ppermute | solution.py:338
  25.7 8.4 %collective-permute-start.6 = (bf16[512,128]{1,0:T(8,128)(2,1)S(1)}, bf16[512,128]{1,0:T(8,128)(2,1)S(1)}, u32[]{:S(2)}, u32[]{:S(2)}) collective-permute-start(bf16[512,128]{1,0:T(8,128)(2,1)S(1)} %collective-permute-done.3.refs_3_), channel_id=1, source_target_pairs={{0,16},{16,32},{32,48},{48,64},{64,80},{80,96},{96,112},{112,0},{1... | collective-permute-start | bytes 393224 | tf_op jit(solution)/shard_map/ppermute | solution.py:338
  27.5 7.1 %collective-permute-start.9 = (bf16[512,128]{1,0:T(8,128)(2,1)S(1)}, bf16[512,128]{1,0:T(8,128)(2,1)S(1)}, u32[]{:S(2)}, u32[]{:S(2)}) collective-permute-start(bf16[512,128]{1,0:T(8,128)(2,1)S(1)} %collective-permute-done.5.refs_6_), channel_id=1, source_target_pairs={{0,16},{16,32},{32,48},{48,64},{64,80},{80,96},{96,112},{112,0},{1... | collective-permute-start | bytes 393224 | tf_op jit(solution)/shard_map/ppermute | solution.py:338
  28.2 6.6 %collective-permute-start.12 = (bf16[512,128]{1,0:T(8,128)(2,1)S(1)}, bf16[512,128]{1,0:T(8,128)(2,1)S(1)}, u32[]{:S(2)}, u32[]{:S(2)}) collective-permute-start(bf16[512,128]{1,0:T(8,128)(2,1)S(1)} %collective-permute-done.8.refs_9_), channel_id=1, source_target_pairs={{0,112},{16,0},{32,16},{48,32},{64,48},{80,64},{96,80},{112,96},{1... | collective-permute-start | bytes 393224 | tf_op jit(solution)/shard_map/ppermute | solution.py:338
  31.6 7.1 %collective-permute-start.11 = (bf16[512,128]{1,0:T(8,128)(2,1)S(1)}, bf16[512,128]{1,0:T(8,128)(2,1)S(1)}, u32[]{:S(2)}, u32[]{:S(2)}) collective-permute-start(bf16[512,128]{1,0:T(8,128)(2,1)S(1)} %collective-permute-done.7.refs_8_), channel_id=1, source_target_pairs={{0,112},{16,0},{32,16},{48,32},{64,48},{80,64},{96,80},{112,96},{1... | collective-permute-start | bytes 393224 | tf_op jit(solution)/shard_map/ppermute | solution.py:338
  34.1 6.2 %collective-permute-start.10 = (bf16[512,128]{1,0:T(8,128)(2,1)S(1)}, bf16[512,128]{1,0:T(8,128)(2,1)S(1)}, u32[]{:S(2)}, u32[]{:S(2)}) collective-permute-start(bf16[512,128]{1,0:T(8,128)(2,1)S(1)} %collective-permute-done.6.refs_7_), channel_id=1, source_target_pairs={{0,16},{16,32},{32,48},{48,64},{64,80},{80,96},{96,112},{112,0},{1... | collective-permute-start | bytes 393224 | tf_op jit(solution)/shard_map/ppermute | solution.py:338
  34.6 7.0 %collective-permute-start.13 = (bf16[512,128]{1,0:T(8,128)(2,1)S(1)}, bf16[512,128]{1,0:T(8,128)(2,1)S(1)}, u32[]{:S(2)}, u32[]{:S(2)}) collective-permute-start(bf16[512,128]{1,0:T(8,128)(2,1)S(1)} %collective-permute-done.9.refs_10_), channel_id=1, source_target_pairs={{0,16},{16,32},{32,48},{48,64},{64,80},{80,96},{96,112},{112,0},{1... | collective-permute-start | bytes 393224 | tf_op jit(solution)/shard_map/ppermute | solution.py:338
  34.8 6.8 %collective-permute-start.14 = (bf16[512,128]{1,0:T(8,128)(2,1)S(1)}, bf16[512,128]{1,0:T(8,128)(2,1)S(1)}, u32[]{:S(2)}, u32[]{:S(2)}) collective-permute-start(bf16[512,128]{1,0:T(8,128)(2,1)S(1)} %collective-permute-done.12.refs_13_), channel_id=1, source_target_pairs={{0,112},{16,0},{32,16},{48,32},{64,48},{80,64},{96,80},{112,96},{1... | collective-permute-start | bytes 393224 | tf_op jit(solution)/shard_map/ppermute | solution.py:338
  37.8 32.6 %collective-permute-start.16 = (bf16[256,1024]{1,0:T(8,128)(2,1)}, bf16[256,1024]{1,0:T(8,128)(2,1)S(1)}, u32[]{:S(2)}, u32[]{:S(2)}) collective-permute-start(bf16[256,1024]{1,0:T(8,128)(2,1)} %bitcast.26), channel_id=1, source_target_pairs={{0,8},{8,0},{1,9},{9,1},{2,10},{10,2},{3,11},{11,3},{4,12},{12,4},... | collective-permute-start | bytes 1572872 | tf_op jit(solution)/shard_map/ppermute | solution.py:342
  41.7 0.6 copy-start.4
  42.2 0.9 copy-start.6
  43.1 12.3 %copy-start.7 = (bf16[512,128]{1,0:T(8,128)(2,1)S(1)}, bf16[512,128]{1,0:T(8,128)(2,1)}, u32[]{:S(2)}) copy-start(bf16[512,128]{1,0:T(8,128)(2,1)} %get-tuple-element.32.refs_0_) | copy-start | bytes 393220
  48.9 14.6 %all-to-all-start = ((f32[8,8,128]{2,1,0:T(8,128)}), f32[8,8,128]{2,1,0:T(8,128)S(1)}, u32[]{:S(2)}, u32[]{:S(2)}) async-start(f32[8,8,128]{2,1,0:T(8,128)} %get-tuple-element.39), calls=%async_computation | async-start | bytes 65536 | tf_op jit(solution)/shard_map/all_to_all | solution.py:401
  55.4 0.6 copy-start.5
  63.4 7.0 %copy-start = (bf16[1,256,1024]{2,1,0:T(8,128)(2,1)S(1)}, bf16[1,256,1024]{2,1,0:T(8,128)(2,1)}, u32[]{:S(2)}) copy-start(bf16[1,256,1024]{2,1,0:T(8,128)(2,1)} %param.7) | copy-start | bytes 1572868
  72.0 12.7 %copy-start.1 = (bf16[1024,128]{1,0:T(8,128)(2,1)S(1)}, bf16[1024,128]{1,0:T(8,128)(2,1)}, u32[]{:S(2)}) copy-start(bf16[1024,128]{1,0:T(8,128)(2,1)} %wq.3) | copy-start | bytes 786436
  72.0 12.7 %copy-start.2 = (bf16[1024,128]{1,0:T(8,128)(2,1)S(1)}, bf16[1024,128]{1,0:T(8,128)(2,1)}, u32[]{:S(2)}) copy-start(bf16[1024,128]{1,0:T(8,128)(2,1)} %wk.3) | copy-start | bytes 786436
  72.0 12.7 %copy-start.3 = (bf16[1024,128]{1,0:T(8,128)(2,1)S(1)}, bf16[1024,128]{1,0:T(8,128)(2,1)}, u32[]{:S(2)}) copy-start(bf16[1024,128]{1,0:T(8,128)(2,1)} %wv.3) | copy-start | bytes 786436
  72.0 15.9 %all-to-all-start.1 = ((bf16[16,96,128]{2,1,0:T(8,128)(2,1)}), bf16[16,96,128]{2,1,0:T(8,128)(2,1)S(1)}, u32[]{:S(2)}, u32[]{:S(2)}) async-start(bf16[16,96,128]{2,1,0:T(8,128)(2,1)} %shard_map.116), calls=%async_computation.1 | async-start | bytes 786432 | tf_op jit(solution)/shard_map/all_to_all | solution.py:427
  77.6 7.1 %collective-permute-start.15 = (bf16[512,128]{1,0:T(8,128)(2,1)S(1)}, bf16[512,128]{1,0:T(8,128)(2,1)S(1)}, u32[]{:S(2)}, u32[]{:S(2)}) collective-permute-start(bf16[512,128]{1,0:T(8,128)(2,1)S(1)} %get-tuple-element.48.sent), channel_id=1, source_target_pairs={{0,8},{8,0},{1,9},{9,1},{2,10},{10,2},{3,11},{11,3},{4,12},{12,4},... | collective-permute-start | bytes 393224 | tf_op jit(solution)/shard_map/ppermute | solution.py:342
  88.9 24.1 %all-to-all-start.2 = ((bf16[32,96,128]{2,1,0:T(8,128)(2,1)}), bf16[32,96,128]{2,1,0:T(8,128)(2,1)S(1)}, u32[]{:S(2)}, u32[]{:S(2)}) async-start(bf16[32,96,128]{2,1,0:T(8,128)(2,1)} %shard_map.117), calls=%async_computation.2 | async-start | bytes 1572864 | tf_op jit(solution)/shard_map/all_to_all | solution.py:443
  97.1 1.6 %collective-permute-start.17 = (bf16[4,32,1024]{2,1,0:T(8,128)(2,1)S(1)}, bf16[4,32,1024]{2,1,0:T(8,128)(2,1)S(1)}, u32[]{:S(2)}, u32[]{:S(2)}) collective-permute-start(bf16[4,32,1024]{2,1,0:T(8,128)(2,1)S(1)} %get-tuple-element.52), channel_id=1, source_target_pairs={{0,1},{1,0},{2,3},{3,2},{4,5},{5,4},{6,7},{7,6},{8,9},{9,8},{10,11... | collective-permute-start | bytes 786440 | tf_op jit(solution)/shard_map/ppermute | solution.py:435
  98.8 4.4 %collective-permute-start.20 = (bf16[32,1024]{1,0:T(8,128)(2,1)S(1)}, bf16[32,1024]{1,0:T(8,128)(2,1)S(1)}, u32[]{:S(2)}, u32[]{:S(2)}) collective-permute-start(bf16[32,1024]{1,0:T(8,128)(2,1)S(1)} %get-tuple-element.60), channel_id=1, source_target_pairs={{0,6},{2,4},{4,2},{6,0},{1,7},{3,5},{5,3},{7,1},{8,14},{10,12},{12... | collective-permute-start | bytes 196616 | tf_op jit(solution)/shard_map/ppermute | solution.py:442
  100.5 6.4 %collective-permute-start.19 = (bf16[32,1024]{1,0:T(8,128)(2,1)S(1)}, bf16[32,1024]{1,0:T(8,128)(2,1)S(1)}, u32[]{:S(2)}, u32[]{:S(2)}) collective-permute-start(bf16[32,1024]{1,0:T(8,128)(2,1)S(1)} %get-tuple-element.61), channel_id=1, source_target_pairs={{0,4},{2,6},{4,0},{6,2},{1,5},{3,7},{5,1},{7,3},{8,12},{10,14},{12... | collective-permute-start | bytes 196616 | tf_op jit(solution)/shard_map/ppermute | solution.py:442
  101.4 5.4 %collective-permute-start.18 = (bf16[32,1024]{1,0:T(8,128)(2,1)S(1)}, bf16[32,1024]{1,0:T(8,128)(2,1)S(1)}, u32[]{:S(2)}, u32[]{:S(2)}) collective-permute-start(bf16[32,1024]{1,0:T(8,128)(2,1)S(1)} %get-tuple-element.59), channel_id=1, source_target_pairs={{0,2},{2,0},{4,6},{6,4},{1,3},{3,1},{5,7},{7,5},{8,10},{10,8},{12,... | collective-permute-start | bytes 196616 | tf_op jit(solution)/shard_map/ppermute | solution.py:442

commit v10 on v9

--- a/solution.py
+++ b/solution.py
@@ -17,7 +17,7 @@
 NEG = -1e30
 LIMIT = 51 << 20
 CHUNK = 512
-FEATURE_LIMIT = 64 << 20
+FEATURE_LIMIT = 63 << 20
 BF = jnp.bfloat16
 F32 = jnp.float32
 
@@ -363,7 +363,7 @@
         flops=6 * 256 * 1024 * 128,
         smem=0,
         manual=5,
-        limit=64 << 20,
+        limit=63 << 20,
     )
     other = swap(theirs)
     tok_other = swap(tok)

time: 115 us -> 114 us (level)
  transfers between devices with their start and end apart: 24 -> 24, of which waited for: 14 -> 14; matrix products, arithmetic and copies ran while one was open for 1% -> 1% of each run, Pallas kernels for 21% -> 20%
where the time goes in v10:
time: 114 us; the launch traced here: 113 us
  starting transfers between devices  52.3 us (46%)
  Pallas kernels  30 us (26%)
  waiting for transfers between devices  27.1 us (24%)
  local copies, waits for them, and re-layouts  1.69 us (1%)
  other arithmetic  1.37 us (1%)
    pallas_call x9, Pallas kernels, call(): pl.pallas_call(kernel, out_shape=outs, in_specs=specs, out_specs=jax.tree...  30 us
    ppermute x14, starting transfers between devices, shift(): return lax.ppermute(a, Z, [(i, (i + step) % NSEC) for i in range(NSEC)])  21.6 us
    all_to_all x1, starting transfers between devices, on_device(): total = lax.all_to_all(total, ('b',) + CTX, 0, 0, tiled=True)  8.19 us
    ppermute x14, waiting for transfers between devices, shift(): return lax.ppermute(a, Z, [(i, (i + step) % NSEC) for i in range(NSEC)])  8.09 us
    all_to_all x1, starting transfers between devices, on_device(): lax.all_to_all(stats, Z, 0, 0, tiled=True).reshape(NSEC * 8, 128)  6.72 us
    ppermute x3, starting transfers between devices, swap(): return lax.ppermute(a, 'xh', [(0, 1), (1, 0)])  5.82 us
    all_to_all x1, starting transfers between devices, on_device(): partial = lax.all_to_all(partial, ('b',) + Z, 0, 0, tiled=True)  5.74 us
    all_to_all x1, waiting for transfers between devices, on_device(): total = lax.all_to_all(total, ('b',) + CTX, 0, 0, tiled=True)  5.49 us
  transfers between devices with their start and end apart: 24, of which 14 were waited for; matrix products, arithmetic and copies ran while one was open for 1% of the time, Pallas kernels for 20%

profile of v10, /device:TPU:8, one launch (start us, length us, event | category | flops | bytes accessed | tf_op | source)
XLA Modules:
  0.0 113.3 jit_solution(12062432502793640086)
XLA Ops:
  0.6 2.9 %shard_map.110 = (bf16[512,128]{1,0:T(8,128)(2,1)}, bf16[512,128]{1,0:T(8,128)(2,1)}) custom-call(bf16[256,1024]{1,0:T(8,128)(2,1)} %bitcast.25, bf16[1024,128]{1,0:T(8,128)(2,1)} %wq.3, bf16[1024,128]{1,0:T(8,128)(2,1)} %wk.3, bf16[1024,128]{1,0:T(8,128)(2,1)} %wv.3, bf16[256,128]{1,0:T(8,128)(2,1)} %bitcast.29), custom_call_target="tpu_custom_call" | custom-call | flops 201326592 | bytes 1376256 | tf_op jit(solution)/shard_map/pallas_call | solution.py:44
  3.5 3.1 %collective-permute-start = (bf16[512,128]{1,0:T(8,128)(2,1)}, bf16[512,128]{1,0:T(8,128)(2,1)S(1)}, u32[]{:S(2)}, u32[]{:S(2)}) collective-permute-start(bf16[512,128]{1,0:T(8,128)(2,1)} %get-tuple-element.33), channel_id=1, source_target_pairs={{0,8},{8,0},{1,9},{9,1},{2,10},{10,2},{3,11},{11,3},{4,12},{12,4},... | collective-permute-start | bytes 393224 | tf_op jit(solution)/shard_map/ppermute | solution.py:342
  6.6 1.9 %collective-permute-start.1 = (bf16[512,128]{1,0:T(8,128)(2,1)}, bf16[512,128]{1,0:T(8,128)(2,1)S(1)}, u32[]{:S(2)}, u32[]{:S(2)}) collective-permute-start(bf16[512,128]{1,0:T(8,128)(2,1)} %get-tuple-element.32.refs_0_), channel_id=1, source_target_pairs={{0,16},{16,32},{32,48},{48,64},{64,80},{80,96},{96,112},{112,0},{1... | collective-permute-start | bytes 393224 | tf_op jit(solution)/shard_map/ppermute | solution.py:338
  8.6 3.9 %collective-permute-start.2 = (bf16[512,128]{1,0:T(8,128)(2,1)}, bf16[512,128]{1,0:T(8,128)(2,1)}, u32[]{:S(2)}, u32[]{:S(2)}) collective-permute-start(bf16[512,128]{1,0:T(8,128)(2,1)} %get-tuple-element.32.refs_0_), channel_id=1, source_target_pairs={{0,112},{16,0},{32,16},{48,32},{64,48},{80,64},{96,80},{112,96},{1... | collective-permute-start | bytes 393224 | tf_op jit(solution)/shard_map/ppermute | solution.py:338
  12.5 0.6 pad_add_fusion.place
  13.1 3.7 %shard_map.111.refs_16_ = bf16[4096,128]{1,0:T(8,128)(2,1)} custom-call(s32[3]{0:T(128)} %pad_add_fusion.place, s32[1,8]{1,0:T(1,128)} %lengths.1, s32[1,256]{1,0:T(1,128)} %spots.1), custom_call_target="tpu_custom_call" | custom-call | bytes 1068 | tf_op jit(solution)/shard_map/pallas_call | solution.py:44
  16.8 2.2 %collective-permute-start.4 = (bf16[512,128]{1,0:T(8,128)(2,1)S(1)}, bf16[512,128]{1,0:T(8,128)(2,1)S(1)}, u32[]{:S(2)}, u32[]{:S(2)}) collective-permute-start(bf16[512,128]{1,0:T(8,128)(2,1)S(1)} %collective-permute-done.refs_1_), channel_id=1, source_target_pairs={{0,112},{16,0},{32,16},{48,32},{64,48},{80,64},{96,80},{112,96},{1... | collective-permute-start | bytes 393224 | tf_op jit(solution)/shard_map/ppermute | solution.py:338
  19.0 0.0 collective-permute-start.3
  19.0 2.9 %collective-permute-done.4.refs_5_ = bf16[512,128]{1,0:T(8,128)(2,1)S(1)} collective-permute-done((bf16[512,128]{1,0:T(8,128)(2,1)S(1)}, bf16[512,128]{1,0:T(8,128)(2,1)S(1)}, u32[]{:S(2)}, u32[]{:S(2)}) %collective-permute-start.4) | collective-permute-done | bytes 131104 | tf_op jit(solution)/shard_map/ppermute | solution.py:338
  21.9 3.3 %collective-permute-start.8 = (bf16[512,128]{1,0:T(8,128)(2,1)S(1)}, bf16[512,128]{1,0:T(8,128)(2,1)S(1)}, u32[]{:S(2)}, u32[]{:S(2)}) collective-permute-start(bf16[512,128]{1,0:T(8,128)(2,1)S(1)} %collective-permute-done.4.refs_5_), channel_id=1, source_target_pairs={{0,112},{16,0},{32,16},{48,32},{64,48},{80,64},{96,80},{112,96},{1... | collective-permute-start | bytes 393224 | tf_op jit(solution)/shard_map/ppermute | solution.py:338
  25.2 0.0 collective-permute-start.7
  25.2 0.5 collective-permute-done.3.refs_3_
  25.7 1.5 %collective-permute-start.6 = (bf16[512,128]{1,0:T(8,128)(2,1)S(1)}, bf16[512,128]{1,0:T(8,128)(2,1)S(1)}, u32[]{:S(2)}, u32[]{:S(2)}) collective-permute-start(bf16[512,128]{1,0:T(8,128)(2,1)S(1)} %collective-permute-done.3.refs_3_), channel_id=1, source_target_pairs={{0,16},{16,32},{32,48},{48,64},{64,80},{80,96},{96,112},{112,0},{1... | collective-permute-start | bytes 393224 | tf_op jit(solution)/shard_map/ppermute | solution.py:338
  27.2 0.3 collective-permute-done.5.refs_6_
  27.5 0.7 collective-permute-done.8.refs_9_
  28.2 3.1 %collective-permute-start.12 = (bf16[512,128]{1,0:T(8,128)(2,1)S(1)}, bf16[512,128]{1,0:T(8,128)(2,1)S(1)}, u32[]{:S(2)}, u32[]{:S(2)}) collective-permute-start(bf16[512,128]{1,0:T(8,128)(2,1)S(1)} %collective-permute-done.8.refs_9_), channel_id=1, source_target_pairs={{0,112},{16,0},{32,16},{48,32},{64,48},{80,64},{96,80},{112,96},{1... | collective-permute-start | bytes 393224 | tf_op jit(solution)/shard_map/ppermute | solution.py:338
  31.3 2.3 %collective-permute-start.11 = (bf16[512,128]{1,0:T(8,128)(2,1)S(1)}, bf16[512,128]{1,0:T(8,128)(2,1)S(1)}, u32[]{:S(2)}, u32[]{:S(2)}) collective-permute-start(bf16[512,128]{1,0:T(8,128)(2,1)S(1)} %collective-permute-done.7.refs_8_), channel_id=1, source_target_pairs={{0,112},{16,0},{32,16},{48,32},{64,48},{80,64},{96,80},{112,96},{1... | collective-permute-start | bytes 393224 | tf_op jit(solution)/shard_map/ppermute | solution.py:338
  33.7 0.9 collective-permute-done.9.refs_10_
  34.6 3.2 %collective-permute-start.14 = (bf16[512,128]{1,0:T(8,128)(2,1)S(1)}, bf16[512,128]{1,0:T(8,128)(2,1)S(1)}, u32[]{:S(2)}, u32[]{:S(2)}) collective-permute-start(bf16[512,128]{1,0:T(8,128)(2,1)S(1)} %collective-permute-done.12.refs_13_), channel_id=1, source_target_pairs={{0,112},{16,0},{32,16},{48,32},{64,48},{80,64},{96,80},{112,96},{1... | collective-permute-start | bytes 393224 | tf_op jit(solution)/shard_map/ppermute | solution.py:338
  37.8 0.6 collective-permute-start.16
  38.4 1.4 %collective-permute-done.10.refs_11_ = bf16[512,128]{1,0:T(8,128)(2,1)S(1)} collective-permute-done((bf16[512,128]{1,0:T(8,128)(2,1)S(1)}, bf16[512,128]{1,0:T(8,128)(2,1)S(1)}, u32[]{:S(2)}, u32[]{:S(2)}) %collective-permute-start.10) | collective-permute-done | bytes 131104 | tf_op jit(solution)/shard_map/ppermute | solution.py:338
  39.8 1.4 %collective-permute-done.13.refs_14_ = bf16[512,128]{1,0:T(8,128)(2,1)S(1)} collective-permute-done((bf16[512,128]{1,0:T(8,128)(2,1)S(1)}, bf16[512,128]{1,0:T(8,128)(2,1)S(1)}, u32[]{:S(2)}, u32[]{:S(2)}) %collective-permute-start.13) | collective-permute-done | bytes 131104 | tf_op jit(solution)/shard_map/ppermute | solution.py:338
  41.2 5.7 %shard_map.112 = (bf16[512,128]{1,0:T(8,128)(2,1)S(1)}, f32[512,128]{1,0:T(8,128)S(1)}, f32[8,8,128]{2,1,0:T(8,128)}) custom-call(s32[3]{0:T(128)S(1)} %copy-done.4, bf16[512,128]{1,0:T(8,128)(2,1)S(1)} %copy-done.5, bf16[512,128]{1,0:T(8,128)(2,1)S(1)} %collective-permute-done.refs_1_, bf16[512,128]{1,0:T(8,128)(2,1)S(1)} %collective-permute-done.1.refs_2_, ...), custom_call_target="tpu_custom_call" | custom-call | flops 1073741824 | bytes 3145740 | tf_op jit(solution)/shard_map/pallas_call | solution.py:44
  46.9 0.7 copy-done.6
  47.6 6.7 %all-to-all-start = ((f32[8,8,128]{2,1,0:T(8,128)}), f32[8,8,128]{2,1,0:T(8,128)S(1)}, u32[]{:S(2)}, u32[]{:S(2)}) async-start(f32[8,8,128]{2,1,0:T(8,128)} %get-tuple-element.39), calls=%async_computation | async-start | bytes 65536 | tf_op jit(solution)/shard_map/all_to_all | solution.py:401
  54.3 0.9 copy-done.7
  55.3 5.3 %shard_map.113 = (bf16[256,128]{1,0:T(8,128)(2,1)S(1)}, bf16[256,128]{1,0:T(8,128)(2,1)S(1)}) custom-call(s32[3]{0:T(128)S(1)} %copy-done.4, bf16[512,128]{1,0:T(8,128)(2,1)S(1)} %copy-done.5, bf16[512,128]{1,0:T(8,128)(2,1)S(1)} %collective-permute-done.refs_1_, bf16[512,128]{1,0:T(8,128)(2,1)S(1)} %collective-permute-done.1.refs_2_, ...), custom_call_target="tpu_custom_call" | custom-call | flops 1610612736 | bytes 3538956 | tf_op jit(solution)/shard_map/pallas_call | solution.py:44
  60.6 1.8 %all-to-all-done = f32[8,8,128]{2,1,0:T(8,128)S(1)} async-done(((f32[8,8,128]{2,1,0:T(8,128)}), f32[8,8,128]{2,1,0:T(8,128)S(1)}, u32[]{:S(2)}, u32[]{:S(2)}) %all-to-all-start) | async-done | bytes 32800 | tf_op jit(solution)/shard_map/all_to_all | solution.py:401
  62.4 6.8 %shard_map.114 = (bf16[256,128]{1,0:T(8,128)(2,1)S(1)}, bf16[512,128]{1,0:T(8,128)(2,1)S(1)}) custom-call(s32[3]{0:T(128)S(1)} %copy-done.4, bf16[512,128]{1,0:T(8,128)(2,1)S(1)} %copy-done.5, bf16[512,128]{1,0:T(8,128)(2,1)S(1)} %collective-permute-done.refs_1_, bf16[512,128]{1,0:T(8,128)(2,1)S(1)} %collective-permute-done.1.refs_2_, ...), custom_call_target="tpu_custom_call" | custom-call | flops 2147483648 | bytes 3244044 | tf_op jit(solution)/shard_map/pallas_call | solution.py:44
  69.2 1.6 %shard_map.116 = bf16[16,96,128]{2,1,0:T(8,128)(2,1)} custom-call(bf16[256,1024]{1,0:T(8,128)(2,1)S(1)} %bitcast.27, bf16[256,1024]{1,0:T(8,128)(2,1)S(1)} %collective-permute-done.16.tok_other, bf16[256,128]{1,0:T(8,128)(2,1)S(1)} %get-tuple-element.44.first, bf16[256,128]{1,0:T(8,128)(2,1)S(1)} %get-tuple-element.47.second, ...), custom_call_target="tpu_custom_call" | custom-call | flops 268435456 | bytes 1310720 | tf_op jit(solution)/shard_map/pallas_call | solution.py:44
  70.7 5.7 %all-to-all-start.1 = ((bf16[16,96,128]{2,1,0:T(8,128)(2,1)}), bf16[16,96,128]{2,1,0:T(8,128)(2,1)S(1)}, u32[]{:S(2)}, u32[]{:S(2)}) async-start(bf16[16,96,128]{2,1,0:T(8,128)(2,1)} %shard_map.116), calls=%async_computation.1 | async-start | bytes 786432 | tf_op jit(solution)/shard_map/all_to_all | solution.py:427
  76.5 2.1 %collective-permute-start.15 = (bf16[512,128]{1,0:T(8,128)(2,1)S(1)}, bf16[512,128]{1,0:T(8,128)(2,1)S(1)}, u32[]{:S(2)}, u32[]{:S(2)}) collective-permute-start(bf16[512,128]{1,0:T(8,128)(2,1)S(1)} %get-tuple-element.48.sent), channel_id=1, source_target_pairs={{0,8},{8,0},{1,9},{9,1},{2,10},{10,2},{3,11},{11,3},{4,12},{12,4},... | collective-permute-start | bytes 393224 | tf_op jit(solution)/shard_map/ppermute | solution.py:342
  78.6 5.0 %collective-permute-done.15.arrived = bf16[512,128]{1,0:T(8,128)(2,1)S(1)} collective-permute-done((bf16[512,128]{1,0:T(8,128)(2,1)S(1)}, bf16[512,128]{1,0:T(8,128)(2,1)S(1)}, u32[]{:S(2)}, u32[]{:S(2)}) %collective-permute-start.15) | collective-permute-done | bytes 131104 | tf_op jit(solution)/shard_map/ppermute | solution.py:342
  83.6 1.7 %shard_map.115 = (bf16[256,128]{1,0:T(8,128)(2,1)}, f32[4,32,1024]{2,1,0:T(8,128)S(1)}, bf16[4,32,1024]{2,1,0:T(8,128)(2,1)S(1)}) custom-call(s32[3]{0:T(128)S(1)} %copy-done.4, bf16[256,128]{1,0:T(8,128)(2,1)S(1)} %get-tuple-element.44.first, bf16[256,128]{1,0:T(8,128)(2,1)S(1)} %get-tuple-element.47.second, ...), custom_call_target="tpu_custom_call" | custom-call | flops 201326592 | bytes 1048588 | tf_op jit(solution)/shard_map/pallas_call | solution.py:44
  85.3 1.5 %all-to-all-done.1.parts = bf16[16,96,128]{2,1,0:T(8,128)(2,1)S(1)} async-done(((bf16[16,96,128]{2,1,0:T(8,128)(2,1)}), bf16[16,96,128]{2,1,0:T(8,128)(2,1)S(1)}, u32[]{:S(2)}, u32[]{:S(2)}) %all-to-all-start.1) | async-done | bytes 393248 | tf_op jit(solution)/shard_map/all_to_all | solution.py:427
  86.8 1.0 shard_map.117
  87.8 8.2 %all-to-all-start.2 = ((bf16[32,96,128]{2,1,0:T(8,128)(2,1)}), bf16[32,96,128]{2,1,0:T(8,128)(2,1)S(1)}, u32[]{:S(2)}, u32[]{:S(2)}) async-start(bf16[32,96,128]{2,1,0:T(8,128)(2,1)} %shard_map.117), calls=%async_computation.2 | async-start | bytes 1572864 | tf_op jit(solution)/shard_map/all_to_all | solution.py:443
  96.0 0.1 collective-permute-start.17
  96.1 1.5 %collective-permute-done.17 = bf16[4,32,1024]{2,1,0:T(8,128)(2,1)S(1)} collective-permute-done((bf16[4,32,1024]{2,1,0:T(8,128)(2,1)S(1)}, bf16[4,32,1024]{2,1,0:T(8,128)(2,1)S(1)}, u32[]{:S(2)}, u32[]{:S(2)}) %collective-permute-start.17) | collective-permute-done | bytes 262176 | tf_op jit(solution)/shard_map/ppermute | solution.py:435
  97.6 0.1 fusion.4
  97.7 1.7 %collective-permute-start.20 = (bf16[32,1024]{1,0:T(8,128)(2,1)S(1)}, bf16[32,1024]{1,0:T(8,128)(2,1)S(1)}, u32[]{:S(2)}, u32[]{:S(2)}) collective-permute-start(bf16[32,1024]{1,0:T(8,128)(2,1)S(1)} %get-tuple-element.60), channel_id=1, source_target_pairs={{0,6},{2,4},{4,2},{6,0},{1,7},{3,5},{5,3},{7,1},{8,14},{10,12},{12... | collective-permute-start | bytes 196616 | tf_op jit(solution)/shard_map/ppermute | solution.py:442
  99.4 0.9 collective-permute-start.19
  100.3 1.6 %collective-permute-start.18 = (bf16[32,1024]{1,0:T(8,128)(2,1)S(1)}, bf16[32,1024]{1,0:T(8,128)(2,1)S(1)}, u32[]{:S(2)}, u32[]{:S(2)}) collective-permute-start(bf16[32,1024]{1,0:T(8,128)(2,1)S(1)} %get-tuple-element.59), channel_id=1, source_target_pairs={{0,2},{2,0},{4,6},{6,4},{1,3},{3,1},{5,7},{7,5},{8,10},{10,8},{12,... | collective-permute-start | bytes 196616 | tf_op jit(solution)/shard_map/ppermute | solution.py:442
  101.9 0.2 collective-permute-done.20
  102.1 3.7 %collective-permute-done.19 = bf16[32,1024]{1,0:T(8,128)(2,1)S(1)} collective-permute-done((bf16[32,1024]{1,0:T(8,128)(2,1)S(1)}, bf16[32,1024]{1,0:T(8,128)(2,1)S(1)}, u32[]{:S(2)}, u32[]{:S(2)}) %collective-permute-start.19) | collective-permute-done | bytes 65568 | tf_op jit(solution)/shard_map/ppermute | solution.py:442
  105.7 0.7 fusion.3
  106.4 5.5 %all-to-all-done.2.parts = bf16[32,96,128]{2,1,0:T(8,128)(2,1)S(1)} async-done(((bf16[32,96,128]{2,1,0:T(8,128)(2,1)}), bf16[32,96,128]{2,1,0:T(8,128)(2,1)S(1)}, u32[]{:S(2)}, u32[]{:S(2)}) %all-to-all-start.2) | async-done | bytes 786464 | tf_op jit(solution)/shard_map/all_to_all | solution.py:443
  111.9 1.4 %shard_map.118 = (f32[1024,128]{1,0:T(8,128)}, f32[1024,128]{1,0:T(8,128)}, f32[1024,128]{1,0:T(8,128)}) custom-call(bf16[32,96,128]{2,1,0:T(8,128)(2,1)S(1)} %all-to-all-done.2.parts), custom_call_target="tpu_custom_call" | custom-call | bytes 786432 | tf_op jit(solution)/shard_map/pallas_call | solution.py:44
  (29 shorter events, 0.1 us)
Async XLA Ops:
  3.5 13.3 %collective-permute-start = (bf16[512,128]{1,0:T(8,128)(2,1)}, bf16[512,128]{1,0:T(8,128)(2,1)S(1)}, u32[]{:S(2)}, u32[]{:S(2)}) collective-permute-start(bf16[512,128]{1,0:T(8,128)(2,1)} %get-tuple-element.33), channel_id=1, source_target_pairs={{0,8},{8,0},{1,9},{9,1},{2,10},{10,2},{3,11},{11,3},{4,12},{12,4},... | collective-permute-start | bytes 393224 | tf_op jit(solution)/shard_map/ppermute | solution.py:342
  6.6 10.2 %collective-permute-start.1 = (bf16[512,128]{1,0:T(8,128)(2,1)}, bf16[512,128]{1,0:T(8,128)(2,1)S(1)}, u32[]{:S(2)}, u32[]{:S(2)}) collective-permute-start(bf16[512,128]{1,0:T(8,128)(2,1)} %get-tuple-element.32.refs_0_), channel_id=1, source_target_pairs={{0,16},{16,32},{32,48},{48,64},{64,80},{80,96},{96,112},{112,0},{1... | collective-permute-start | bytes 393224 | tf_op jit(solution)/shard_map/ppermute | solution.py:338
  8.6 8.3 %collective-permute-start.2 = (bf16[512,128]{1,0:T(8,128)(2,1)}, bf16[512,128]{1,0:T(8,128)(2,1)}, u32[]{:S(2)}, u32[]{:S(2)}) collective-permute-start(bf16[512,128]{1,0:T(8,128)(2,1)} %get-tuple-element.32.refs_0_), channel_id=1, source_target_pairs={{0,112},{16,0},{32,16},{48,32},{64,48},{80,64},{96,80},{112,96},{1... | collective-permute-start | bytes 393224 | tf_op jit(solution)/shard_map/ppermute | solution.py:338
  13.1 24.7 %copy-start = (bf16[1,256,1024]{2,1,0:T(8,128)(2,1)S(1)}, bf16[1,256,1024]{2,1,0:T(8,128)(2,1)}, u32[]{:S(2)}) copy-start(bf16[1,256,1024]{2,1,0:T(8,128)(2,1)} %param.7) | copy-start | bytes 1572868
  13.1 28.1 %copy-start.4 = (s32[3]{0:T(128)S(1)}, s32[3]{0:T(128)}, u32[]{:S(2)}) copy-start(s32[3]{0:T(128)} %pad_add_fusion.place) | copy-start | bytes 40
  13.1 28.1 %copy-start.5 = (bf16[512,128]{1,0:T(8,128)(2,1)S(1)}, bf16[512,128]{1,0:T(8,128)(2,1)}, u32[]{:S(2)}) copy-start(bf16[512,128]{1,0:T(8,128)(2,1)} %get-tuple-element.32.refs_0_) | copy-start | bytes 393220
  16.8 5.0 %collective-permute-start.4 = (bf16[512,128]{1,0:T(8,128)(2,1)S(1)}, bf16[512,128]{1,0:T(8,128)(2,1)S(1)}, u32[]{:S(2)}, u32[]{:S(2)}) collective-permute-start(bf16[512,128]{1,0:T(8,128)(2,1)S(1)} %collective-permute-done.refs_1_), channel_id=1, source_target_pairs={{0,112},{16,0},{32,16},{48,32},{64,48},{80,64},{96,80},{112,96},{1... | collective-permute-start | bytes 393224 | tf_op jit(solution)/shard_map/ppermute | solution.py:338
  19.0 6.7 %collective-permute-start.3 = (bf16[512,128]{1,0:T(8,128)(2,1)S(1)}, bf16[512,128]{1,0:T(8,128)(2,1)S(1)}, u32[]{:S(2)}, u32[]{:S(2)}) collective-permute-start(bf16[512,128]{1,0:T(8,128)(2,1)S(1)} %collective-permute-done.refs_1_), channel_id=1, source_target_pairs={{0,16},{16,32},{32,48},{48,64},{64,80},{80,96},{96,112},{112,0},{1... | collective-permute-start | bytes 393224 | tf_op jit(solution)/shard_map/ppermute | solution.py:338
  19.0 8.6 %collective-permute-start.5 = (bf16[512,128]{1,0:T(8,128)(2,1)S(1)}, bf16[512,128]{1,0:T(8,128)(2,1)S(1)}, u32[]{:S(2)}, u32[]{:S(2)}) collective-permute-start(bf16[512,128]{1,0:T(8,128)(2,1)S(1)} %collective-permute-done.1.refs_2_), channel_id=1, source_target_pairs={{0,16},{16,32},{32,48},{48,64},{64,80},{80,96},{96,112},{112,0},{1... | collective-permute-start | bytes 393224 | tf_op jit(solution)/shard_map/ppermute | solution.py:338
  21.9 6.3 %collective-permute-start.8 = (bf16[512,128]{1,0:T(8,128)(2,1)S(1)}, bf16[512,128]{1,0:T(8,128)(2,1)S(1)}, u32[]{:S(2)}, u32[]{:S(2)}) collective-permute-start(bf16[512,128]{1,0:T(8,128)(2,1)S(1)} %collective-permute-done.4.refs_5_), channel_id=1, source_target_pairs={{0,112},{16,0},{32,16},{48,32},{64,48},{80,64},{96,80},{112,96},{1... | collective-permute-start | bytes 393224 | tf_op jit(solution)/shard_map/ppermute | solution.py:338
  25.2 6.2 %collective-permute-start.7 = (bf16[512,128]{1,0:T(8,128)(2,1)}, bf16[512,128]{1,0:T(8,128)(2,1)S(1)}, u32[]{:S(2)}, u32[]{:S(2)}) collective-permute-start(bf16[512,128]{1,0:T(8,128)(2,1)} %collective-permute-done.2.refs_4_), channel_id=1, source_target_pairs={{0,112},{16,0},{32,16},{48,32},{64,48},{80,64},{96,80},{112,96},{1... | collective-permute-start | bytes 393224 | tf_op jit(solution)/shard_map/ppermute | solution.py:338
  25.7 8.0 %collective-permute-start.6 = (bf16[512,128]{1,0:T(8,128)(2,1)S(1)}, bf16[512,128]{1,0:T(8,128)(2,1)S(1)}, u32[]{:S(2)}, u32[]{:S(2)}) collective-permute-start(bf16[512,128]{1,0:T(8,128)(2,1)S(1)} %collective-permute-done.3.refs_3_), channel_id=1, source_target_pairs={{0,16},{16,32},{32,48},{48,64},{64,80},{80,96},{96,112},{112,0},{1... | collective-permute-start | bytes 393224 | tf_op jit(solution)/shard_map/ppermute | solution.py:338
  27.5 7.1 %collective-permute-start.9 = (bf16[512,128]{1,0:T(8,128)(2,1)S(1)}, bf16[512,128]{1,0:T(8,128)(2,1)S(1)}, u32[]{:S(2)}, u32[]{:S(2)}) collective-permute-start(bf16[512,128]{1,0:T(8,128)(2,1)S(1)} %collective-permute-done.5.refs_6_), channel_id=1, source_target_pairs={{0,16},{16,32},{32,48},{48,64},{64,80},{80,96},{96,112},{112,0},{1... | collective-permute-start | bytes 393224 | tf_op jit(solution)/shard_map/ppermute | solution.py:338
  28.2 6.4 %collective-permute-start.12 = (bf16[512,128]{1,0:T(8,128)(2,1)S(1)}, bf16[512,128]{1,0:T(8,128)(2,1)S(1)}, u32[]{:S(2)}, u32[]{:S(2)}) collective-permute-start(bf16[512,128]{1,0:T(8,128)(2,1)S(1)} %collective-permute-done.8.refs_9_), channel_id=1, source_target_pairs={{0,112},{16,0},{32,16},{48,32},{64,48},{80,64},{96,80},{112,96},{1... | collective-permute-start | bytes 393224 | tf_op jit(solution)/shard_map/ppermute | solution.py:338
  31.3 7.1 %collective-permute-start.11 = (bf16[512,128]{1,0:T(8,128)(2,1)S(1)}, bf16[512,128]{1,0:T(8,128)(2,1)S(1)}, u32[]{:S(2)}, u32[]{:S(2)}) collective-permute-start(bf16[512,128]{1,0:T(8,128)(2,1)S(1)} %collective-permute-done.7.refs_8_), channel_id=1, source_target_pairs={{0,112},{16,0},{32,16},{48,32},{64,48},{80,64},{96,80},{112,96},{1... | collective-permute-start | bytes 393224 | tf_op jit(solution)/shard_map/ppermute | solution.py:338
  33.7 6.2 %collective-permute-start.10 = (bf16[512,128]{1,0:T(8,128)(2,1)S(1)}, bf16[512,128]{1,0:T(8,128)(2,1)S(1)}, u32[]{:S(2)}, u32[]{:S(2)}) collective-permute-start(bf16[512,128]{1,0:T(8,128)(2,1)S(1)} %collective-permute-done.6.refs_7_), channel_id=1, source_target_pairs={{0,16},{16,32},{32,48},{48,64},{64,80},{80,96},{96,112},{112,0},{1... | collective-permute-start | bytes 393224 | tf_op jit(solution)/shard_map/ppermute | solution.py:338
  34.6 6.6 %collective-permute-start.13 = (bf16[512,128]{1,0:T(8,128)(2,1)S(1)}, bf16[512,128]{1,0:T(8,128)(2,1)S(1)}, u32[]{:S(2)}, u32[]{:S(2)}) collective-permute-start(bf16[512,128]{1,0:T(8,128)(2,1)S(1)} %collective-permute-done.9.refs_10_), channel_id=1, source_target_pairs={{0,16},{16,32},{32,48},{48,64},{64,80},{80,96},{96,112},{112,0},{1... | collective-permute-start | bytes 393224 | tf_op jit(solution)/shard_map/ppermute | solution.py:338
  34.6 6.6 %collective-permute-start.14 = (bf16[512,128]{1,0:T(8,128)(2,1)S(1)}, bf16[512,128]{1,0:T(8,128)(2,1)S(1)}, u32[]{:S(2)}, u32[]{:S(2)}) collective-permute-start(bf16[512,128]{1,0:T(8,128)(2,1)S(1)} %collective-permute-done.12.refs_13_), channel_id=1, source_target_pairs={{0,112},{16,0},{32,16},{48,32},{64,48},{80,64},{96,80},{112,96},{1... | collective-permute-start | bytes 393224 | tf_op jit(solution)/shard_map/ppermute | solution.py:338
  37.8 31.3 %collective-permute-start.16 = (bf16[256,1024]{1,0:T(8,128)(2,1)S(1)}, bf16[256,1024]{1,0:T(8,128)(2,1)S(1)}, u32[]{:S(2)}, u32[]{:S(2)}) collective-permute-start(bf16[256,1024]{1,0:T(8,128)(2,1)S(1)} %bitcast.26), channel_id=1, source_target_pairs={{0,8},{8,0},{1,9},{9,1},{2,10},{10,2},{3,11},{11,3},{4,12},{12,4},... | collective-permute-start | bytes 1572872 | tf_op jit(solution)/shard_map/ppermute | solution.py:342
  46.9 0.7 copy-start.6
  47.6 14.7 %all-to-all-start = ((f32[8,8,128]{2,1,0:T(8,128)}), f32[8,8,128]{2,1,0:T(8,128)S(1)}, u32[]{:S(2)}, u32[]{:S(2)}) async-start(f32[8,8,128]{2,1,0:T(8,128)} %get-tuple-element.39), calls=%async_computation | async-start | bytes 65536 | tf_op jit(solution)/shard_map/all_to_all | solution.py:401
  54.3 0.9 copy-start.7
  70.7 12.8 %copy-start.1 = (bf16[1024,128]{1,0:T(8,128)(2,1)S(1)}, bf16[1024,128]{1,0:T(8,128)(2,1)}, u32[]{:S(2)}) copy-start(bf16[1024,128]{1,0:T(8,128)(2,1)} %wq.3) | copy-start | bytes 786436
  70.7 12.8 %copy-start.2 = (bf16[1024,128]{1,0:T(8,128)(2,1)S(1)}, bf16[1024,128]{1,0:T(8,128)(2,1)}, u32[]{:S(2)}) copy-start(bf16[1024,128]{1,0:T(8,128)(2,1)} %wk.3) | copy-start | bytes 786436
  70.7 12.8 %copy-start.3 = (bf16[1024,128]{1,0:T(8,128)(2,1)S(1)}, bf16[1024,128]{1,0:T(8,128)(2,1)}, u32[]{:S(2)}) copy-start(bf16[1024,128]{1,0:T(8,128)(2,1)} %wv.3) | copy-start | bytes 786436
  70.7 16.1 %all-to-all-start.1 = ((bf16[16,96,128]{2,1,0:T(8,128)(2,1)}), bf16[16,96,128]{2,1,0:T(8,128)(2,1)S(1)}, u32[]{:S(2)}, u32[]{:S(2)}) async-start(bf16[16,96,128]{2,1,0:T(8,128)(2,1)} %shard_map.116), calls=%async_computation.1 | async-start | bytes 786432 | tf_op jit(solution)/shard_map/all_to_all | solution.py:427
  76.5 7.1 %collective-permute-start.15 = (bf16[512,128]{1,0:T(8,128)(2,1)S(1)}, bf16[512,128]{1,0:T(8,128)(2,1)S(1)}, u32[]{:S(2)}, u32[]{:S(2)}) collective-permute-start(bf16[512,128]{1,0:T(8,128)(2,1)S(1)} %get-tuple-element.48.sent), channel_id=1, source_target_pairs={{0,8},{8,0},{1,9},{9,1},{2,10},{10,2},{3,11},{11,3},{4,12},{12,4},... | collective-permute-start | bytes 393224 | tf_op jit(solution)/shard_map/ppermute | solution.py:342
  87.8 24.1 %all-to-all-start.2 = ((bf16[32,96,128]{2,1,0:T(8,128)(2,1)}), bf16[32,96,128]{2,1,0:T(8,128)(2,1)S(1)}, u32[]{:S(2)}, u32[]{:S(2)}) async-start(bf16[32,96,128]{2,1,0:T(8,128)(2,1)} %shard_map.117), calls=%async_computation.2 | async-start | bytes 1572864 | tf_op jit(solution)/shard_map/all_to_all | solution.py:443
  96.0 1.6 %collective-permute-start.17 = (bf16[4,32,1024]{2,1,0:T(8,128)(2,1)S(1)}, bf16[4,32,1024]{2,1,0:T(8,128)(2,1)S(1)}, u32[]{:S(2)}, u32[]{:S(2)}) collective-permute-start(bf16[4,32,1024]{2,1,0:T(8,128)(2,1)S(1)} %get-tuple-element.52), channel_id=1, source_target_pairs={{0,1},{1,0},{2,3},{3,2},{4,5},{5,4},{6,7},{7,6},{8,9},{9,8},{10,11... | collective-permute-start | bytes 786440 | tf_op jit(solution)/shard_map/ppermute | solution.py:435
  97.7 4.4 %collective-permute-start.20 = (bf16[32,1024]{1,0:T(8,128)(2,1)S(1)}, bf16[32,1024]{1,0:T(8,128)(2,1)S(1)}, u32[]{:S(2)}, u32[]{:S(2)}) collective-permute-start(bf16[32,1024]{1,0:T(8,128)(2,1)S(1)} %get-tuple-element.60), channel_id=1, source_target_pairs={{0,6},{2,4},{4,2},{6,0},{1,7},{3,5},{5,3},{7,1},{8,14},{10,12},{12... | collective-permute-start | bytes 196616 | tf_op jit(solution)/shard_map/ppermute | solution.py:442
  99.4 6.4 %collective-permute-start.19 = (bf16[32,1024]{1,0:T(8,128)(2,1)S(1)}, bf16[32,1024]{1,0:T(8,128)(2,1)S(1)}, u32[]{:S(2)}, u32[]{:S(2)}) collective-permute-start(bf16[32,1024]{1,0:T(8,128)(2,1)S(1)} %get-tuple-element.61), channel_id=1, source_target_pairs={{0,4},{2,6},{4,0},{6,2},{1,5},{3,7},{5,1},{7,3},{8,12},{10,14},{12... | collective-permute-start | bytes 196616 | tf_op jit(solution)/shard_map/ppermute | solution.py:442
  100.3 5.4 %collective-permute-start.18 = (bf16[32,1024]{1,0:T(8,128)(2,1)S(1)}, bf16[32,1024]{1,0:T(8,128)(2,1)S(1)}, u32[]{:S(2)}, u32[]{:S(2)}) collective-permute-start(bf16[32,1024]{1,0:T(8,128)(2,1)S(1)} %get-tuple-element.59), channel_id=1, source_target_pairs={{0,2},{2,0},{4,6},{6,4},{1,3},{3,1},{5,7},{7,5},{8,10},{10,8},{12,... | collective-permute-start | bytes 196616 | tf_op jit(solution)/shard_map/ppermute | solution.py:442
